TPU v7x, 32 devices: a whole 2x2x4 slice. The times are simulated.
32 devices in a mesh: row: 4 (over y, core), col: 8 (over z, x).
Axes of the slice: x: 2, y: 2, z: 4, core: 2. Of those that a mesh axis runs over, the one named last changes fastest.
Arguments:
- tensor: bfloat16 [128, 384, 4096], P(None, 'col', 'row'), may hold values from -2 to 2
- first_factor: bfloat16 [64, 4096], P(None, ('row', 'col')), may hold values from -0.453125 to 0.453125
- second_factor: bfloat16 [64, 384], P(None, 'col'), may hold values from -1.4799 to 1.4799
Outputs:
- frames: float32 [64, 128], replicated
- mode_one: float32 [64, 4096], P(None, ('row', 'col'))
All inputs are finite; a program needn't handle non-finite values.
Results may differ from a plain program's by a relative error of at most 0.004.
Values may be sent and summed in bfloat16 or wider, within the bound.
No kernel may reach another device: no remote copies, remote signals or barrier semaphores. Data moves between devices by JAX's collectives and lax.ppermute only.
A program may use at most 128 MiB of HBM per device.

v0:
```python
import functools

import jax
import jax.numpy as jnp
from jax import lax
from jax.experimental import pallas as pl
from jax.experimental.pallas import tpu as pltpu
from jax.sharding import PartitionSpec as P

ridge_weight = 0.05
HIGH = lax.Precision.HIGHEST
BOTH = ("row", "col")
F32, BF16 = jnp.float32, jnp.bfloat16
VM = pltpu.VMEM
MIB = 1 << 20
GROUP = 16


def vmem():
    return pl.BlockSpec(memory_space=VM)


def anywhere():
    return pl.BlockSpec(memory_space=pl.ANY)


def smem():
    return pl.BlockSpec(memory_space=pltpu.SMEM)


def shaped(shape, dtype=F32):
    return jax.ShapeDtypeStruct(shape, dtype)


def call(body, outs, ins, operands, name, scratch=(), mib=16, us=1):
    several = isinstance(outs, tuple)
    return pl.pallas_call(
        body,
        out_shape=outs,
        in_specs=ins,
        out_specs=(vmem(),) * len(outs) if several else vmem(),
        scratch_shapes=scratch,
        compiler_params=pltpu.CompilerParams(vmem_limit_bytes=mib * MIB),
        cost_estimate=pl.CostEstimate(flops=0, bytes_accessed=int(us * 3_000_000), transcendentals=0),
        name=name,
    )(*operands)


def dot(a, b, dims, precision=None):
    return lax.dot_general(a, b, (dims, ((), ())), precision=precision, preferred_element_type=F32)


def swap(x, axes, count, offset):
    return lax.ppermute(x, axes, [(n, n ^ offset) for n in range(count)])


def join_body(a_ref, b_ref, out_ref):
    components = a_ref.shape[0]
    half = b_ref.shape[0] // 2
    out_ref[...] = jnp.zeros_like(out_ref)
    out_ref[0, :components, : a_ref.shape[1]] = a_ref[...]
    b = b_ref[...].astype(F32)
    pair = jnp.concatenate([b[:half], b[half:]], axis=1)
    pair = jnp.concatenate([pair, jnp.zeros((-half % 16, 2 * components), F32)], axis=0)
    out_ref[0, components:, :] = pair.astype(BF16)


def join(first, second_turned):
    components, half = first.shape[0], second_turned.shape[0] // 2
    height = components + half + (-half % 16)
    return call(
        join_body,
        shaped((1, height, 128), BF16),
        [vmem()] * 2,
        (first, second_turned),
        "join",
    )


def stack_body(a_ref, b_ref, after_ref, out_ref):
    del after_ref
    count = a_ref.shape[0]
    out_ref[:count] = a_ref[...]
    out_ref[count:] = b_ref[...]


def stack(a, b, after):
    shape = (2 * a.shape[0],) + a.shape[1:]
    specs = [vmem()] * 2 + [anywhere()]
    return call(stack_body, shaped(shape, a.dtype), specs, (a, b, after), "stack", us=0.2)


def add_body(a_ref, b_ref, after_ref, out_ref):
    del after_ref
    out_ref[...] = a_ref[...] + b_ref[...]


def add(a, b, after):
    specs = [vmem()] * 2 + [anywhere()]
    return call(add_body, shaped(a.shape, a.dtype), specs, (a, b, after), "add", us=0.2)


def prepare_body(at, t_ref, b_ref, after_ref, out_ref, wide_ref, slab, sems):
    del after_ref
    blocks = slab.shape[0]

    def fetch(n):
        return pltpu.make_async_copy(
            t_ref.at[pl.ds(n * GROUP, GROUP), pl.ds(at, GROUP)], slab.at[n], sems.at[n]
        )

    for n in range(blocks):
        fetch(n).start()
    for j in range(GROUP):
        wide_ref[j] = jnp.broadcast_to(b_ref[:, at + j : at + j + 1], wide_ref.shape[1:])
    to = lax.broadcasted_iota(jnp.int32, (256, 256), 0)
    of = lax.broadcasted_iota(jnp.int32, (256, 256), 1)
    turn = jnp.where((to // GROUP) + (to % GROUP) * GROUP == of, 1.0, 0.0).astype(BF16)

    def step(n, _):
        fetch(n).wait()
        block = slab[n].reshape(GROUP * GROUP, -1)
        turned = dot(turn, block, ((1,), (0,))).astype(BF16).reshape(GROUP, GROUP, -1)
        out_ref[:, pl.ds(pl.multiple_of(n * GROUP, GROUP), GROUP), :] = turned
        return 0

    lax.fori_loop(0, blocks, step, 0)


def prepare(tensor, second, at, after):
    frames, _, rows = tensor.shape
    components = second.shape[0]
    blocks = frames // GROUP
    return call(
        functools.partial(prepare_body, at),
        (VM((GROUP, frames, rows), BF16), VM((GROUP, components, 128), F32)),
        [anywhere(), vmem(), anywhere()],
        (tensor, second, after),
        "prepare",
        [VM((blocks, GROUP, GROUP, rows), BF16), pltpu.SemaphoreType.DMA((blocks,))],
        us=2,
    )


def place(at, blocks, width, full_ref):
    for offset, block in blocks:
        if len(blocks) == 1:
            full_ref[...] = block.astype(full_ref.dtype)
        else:
            lanes = pl.ds(pl.multiple_of((at ^ offset) * width, width), width)
            full_ref[:, lanes] = block.astype(full_ref.dtype)


def assemble_first_body(offsets, me_ref, *refs):
    stacks, (turned_ref, gram_ref, other_ref), (full_ref, every_ref) = refs[:-6], refs[-5:-2], refs[-2:]
    components = full_ref.shape[0]
    blocks = [s[n] for s in stacks for n in range(s.shape[0])]
    width = blocks[0].shape[1]
    place(me_ref[0], [(o, b[:components]) for o, b in zip(offsets, blocks)], width, full_ref)
    full = full_ref[...]
    gram_ref[...] = dot(full.astype(BF16), full.astype(BF16), ((1,), (1,)))
    turned_ref[...] = full.T.astype(BF16)
    height = blocks[0].shape[0] - components
    for o, b in zip(offsets, blocks):
        every_ref[pl.ds(pl.multiple_of((me_ref[0] ^ o) * height, height), height), :] = b[components:].astype(F32)
    every = every_ref[...].T.astype(BF16)
    both = dot(every, every, ((1,), (1,)))
    other_ref[...] = both[:components, :components] + both[components:, components:]


def assemble_first(me, stacks, after, offsets, components, rows):
    height = stacks[0].shape[1] - components
    square = shaped((components, components))
    return call(
        functools.partial(assemble_first_body, offsets),
        (shaped((rows, components), BF16), square, square),
        [smem()] + [vmem()] * len(stacks) + [anywhere()],
        (me, *stacks, after),
        "assemble_first",
        [VM((components, rows), F32), VM((height * len(offsets), 2 * components), F32)],
    )


def project_body(last, span, turned_ref, second_ref, t_ref, sum_ref, after_ref, out_ref):
    del after_ref
    components = turned_ref.shape[1]
    cols, frames, rows = t_ref.shape
    weights = turned_ref[...]
    total = sum_ref[...]
    for n in range(0, cols, span):
        block = t_ref[n : n + span].reshape(span * frames, rows)
        product = dot(block, weights, ((1,), (0,))).reshape(span, frames, components)
        for s in range(span):
            total = total + product[s] * second_ref[n + s : n + s + 1, :]
    out_ref[...] = total.T if last else total


def project(turned, second_turned, t, total, after, last):
    frames, components = total.shape
    shape = (components, frames) if last else (frames, components)
    return call(
        functools.partial(project_body, last, 8),
        shaped(shape),
        [vmem()] * 4 + [anywhere()],
        (turned, second_turned, t, total, after),
        "project",
        us=1.5,
    )


def eliminate(matrix, start, stop):
    size = matrix.shape[0]
    row_at = lax.broadcasted_iota(jnp.int32, (size, size), 0)
    col_at = lax.broadcasted_iota(jnp.int32, (size, size), 1)
    lane = col_at[:1]
    for k in range(start, stop, 2):
        a = jnp.broadcast_to(matrix[:, k : k + 1], matrix.shape)
        b = jnp.broadcast_to(matrix[:, k + 1 : k + 2], matrix.shape)
        inverse_a = 1.0 / a[k : k + 1]
        low = a[k + 1 : k + 2] * inverse_a
        inverse_b = 1.0 / (b[k + 1 : k + 2] - b[k : k + 1] * low)
        mine = (lane == k) | (lane == k + 1)
        p = jnp.where(mine, jnp.where(lane == k, 1.0, 0.0), matrix[k : k + 1])
        q = jnp.where(mine, jnp.where(lane == k, 0.0, 1.0), matrix[k + 1 : k + 2])
        q = (q - low * p) * inverse_b
        p = p * inverse_a - (b[k : k + 1] * inverse_a) * q
        rest = jnp.where((col_at == k) | (col_at == k + 1), 0.0, matrix) - a * p - b * q
        matrix = jnp.where(row_at == k, p, jnp.where(row_at == k + 1, q, rest))
    return matrix


def ridged(gram):
    row_at = lax.broadcasted_iota(jnp.int32, gram.shape, 0)
    col_at = lax.broadcasted_iota(jnp.int32, gram.shape, 1)
    return gram + jnp.where(row_at == col_at, ridge_weight, 0.0)


def eliminate_body(start, stop, first, *refs):
    *ins, after_ref, out_ref = refs
    del after_ref
    matrix = ridged(ins[0][...] * ins[1][...]) if first else ins[0][...]
    out_ref[...] = eliminate(matrix, start, stop)


def eliminate_part(operands, start, stop, after):
    return call(
        functools.partial(eliminate_body, start, stop, len(operands) == 2),
        shaped(operands[0].shape),
        [vmem()] * len(operands) + [anywhere()],
        (*operands, after),
        "eliminate",
    )


def halve_first(me_ref, sum_ref, keep_ref, send_ref):
    if keep_ref.shape[0] == 0:
        return
    count, _, width = keep_ref.shape
    bit = me_ref[0] & 1
    for n in range(count):
        keep_ref[n] = sum_ref[:, pl.ds(pl.multiple_of((2 * n + bit) * width, width), width)]
        send = sum_ref[:, pl.ds(pl.multiple_of((2 * n + 1 - bit) * width, width), width)]
        send_ref[n] = send.astype(send_ref.dtype)


def halve_body(shift, me_ref, keep_in, got_in, after_ref, keep_ref, send_ref):
    del after_ref
    bit = (me_ref[0] >> shift) & 1
    for n in range(keep_ref.shape[0]):
        mine, other = 2 * n + bit, 2 * n + 1 - bit
        keep_ref[n] = keep_in[mine] + got_in[mine].astype(F32)
        send_ref[n] = (keep_in[other] + got_in[other].astype(F32)).astype(send_ref.dtype)


def halve(me, keep, got, shift, after):
    shape = (keep.shape[0] // 2,) + keep.shape[1:]
    return call(
        functools.partial(halve_body, shift),
        (shaped(shape), shaped(shape, got.dtype)),
        [smem(), vmem(), vmem(), anywhere()],
        (me, keep, got, after),
        "halve",
        us=0.2,
    )


def shares_out(direct, components, rows, width, send_type):
    if not direct:
        return (shaped((components, rows)),)
    shape = (rows // width // 2, components, width)
    return (shaped(shape), shaped(shape, send_type))


def slab_body(groups, me_ref, inverse_ref, summed_ref, *refs):
    t_refs, wide_refs = refs[:groups], refs[groups : 2 * groups]
    frames_ref, gram_ref, z_ref, *outs, sum_ref = refs[2 * groups :]
    components, rows = sum_ref.shape
    frames = dot(inverse_ref[...], summed_ref[...], ((1,), (0,)), HIGH)
    frames_ref[...] = frames
    gram_ref[...] = dot(frames, frames, ((1,), (1,)), HIGH)
    high = frames.astype(BF16)
    low = (frames - high.astype(F32)).astype(BF16)
    both = jnp.concatenate([high, low], axis=0)
    wide = 256

    def chunk(c, _):
        lanes = pl.ds(pl.multiple_of(c * wide, wide), wide)
        total = jnp.zeros((components, wide), F32)
        for g in range(groups):
            t_ref, wide_ref = t_refs[g], wide_refs[g]

            def step(n, total):
                for s in range(8):
                    j = n * 8 + s
                    product = dot(both, t_ref[j, :, lanes], ((1,), (0,)))
                    z = product[:components] + product[components:]
                    z_ref[g * GROUP + j, :, lanes] = z
                    scale = wide_ref[j]
                    total = total + z * jnp.concatenate([scale, scale], axis=1)
                return total

            total = lax.fori_loop(0, GROUP // 8, step, total)
        sum_ref[:, lanes] = total
        return 0

    lax.fori_loop(0, rows // wide, chunk, 0)
    if len(outs) == 1:
        outs[0][...] = sum_ref[...]
    else:
        halve_first(me_ref, sum_ref, *outs)


def slab(me, inverse_first, frame_sum, turned, wides, width, direct):
    _, frames, rows = turned[0].shape
    components = inverse_first.shape[0]
    groups = len(turned)
    return call(
        functools.partial(slab_body, groups),
        (
            shaped((components, frames)),
            shaped((components, components)),
            VM((groups * GROUP, components, rows), F32),
        )
        + shares_out(direct, components, rows, width, F32),
        [smem()] + [vmem()] * (2 + 2 * groups),
        (me, inverse_first, frame_sum, *turned, *wides),
        "slab",
        [VM((components, rows), F32)],
        us=8,
    )


def update_body(inverse_ref, *refs):
    *parts, out_ref = refs
    for n in range(out_ref.shape[0]):
        summed = parts[0][n]
        for part in parts[1:]:
            summed = summed + part[n]
        out_ref[n] = dot(inverse_ref[...], summed, ((1,), (0,)), HIGH).astype(BF16)


def update(inverse_now, parts):
    return call(
        update_body,
        shaped(parts[0].shape, BF16),
        [vmem()] * (1 + len(parts)),
        (inverse_now, *parts),
        "update",
    )


def second_body(offsets, me_ref, *refs):
    *stacks, z_ref, out_ref, full_ref = refs
    cols, components, rows = z_ref.shape
    blocks = [s[n] for s in stacks for n in range(s.shape[0])]
    place(me_ref[0] & 3, list(zip(offsets, blocks)), blocks[0].shape[1], full_ref)
    lane = lax.broadcasted_iota(jnp.int32, (8, 128), 1)

    def step(n, _):
        at = pl.ds(pl.multiple_of(n * 8, 8), 8)
        mine = full_ref[at, :]
        total = jnp.zeros((8, 128), F32)
        for j in range(cols):
            product = z_ref[j, at, :] * mine
            folded = product[:, :128]
            for c in range(1, rows // 128):
                folded = folded + product[:, c * 128 : c * 128 + 128]
            total = jnp.where(lane == j, jnp.sum(folded, axis=1, keepdims=True), total)
        out_ref[at, :] = total
        return 0

    lax.fori_loop(0, components // 8, step, 0)
    full = full_ref[...].astype(BF16)
    gram = dot(full, full, ((1,), (1,)))
    out_ref[...] = jnp.concatenate([out_ref[:, :components], gram], axis=1)


def second(me, stacks, offsets, z):
    cols, components, rows = z.shape
    return call(
        functools.partial(second_body, offsets),
        shaped((components, 2 * components)),
        [smem()] + [vmem()] * (1 + len(stacks)),
        (me, *stacks, z),
        "second",
        [VM((components, rows), F32)],
        us=2,
    )


def mode_body(me_ref, mine_ref, got_ref, gram_frames_ref, z_ref, *refs):
    *outs, sum_ref, new_ref = refs
    cols, components, rows = z_ref.shape
    summed = mine_ref[...] + got_ref[...]
    solver = eliminate(ridged(summed[:, components:] * gram_frames_ref[...]), 0, components)
    new_ref[...] = dot(solver, summed, ((1,), (0,)), HIGH)

    def step(n, _):
        at = pl.ds(pl.multiple_of(n * 8, 8), 8)
        scale = new_ref[at, :]
        total = jnp.zeros((8, rows), F32)
        for j in range(cols):
            total = total + z_ref[j, at, :] * scale[:, j : j + 1]
        sum_ref[at, :] = total
        return 0

    lax.fori_loop(0, components // 8, step, 0)
    if len(outs) == 1:
        outs[0][...] = sum_ref[...]
    else:
        halve_first(me_ref, sum_ref, *outs)


def mode(me, mine, got, gram_frames, z, width, direct):
    cols, components, rows = z.shape
    return call(
        mode_body,
        shares_out(direct, components, rows, width, BF16),
        [smem()] + [vmem()] * 4,
        (me, mine, got, gram_frames, z),
        "mode",
        [VM((components, rows), F32), VM((components, 2 * components), F32)],
        us=5,
    )


def local(tensor, first_factor, second_factor):
    frame_count, col_count, row_count = tensor.shape
    components = first_factor.shape[0]
    row_size, col_size = lax.axis_size("row"), lax.axis_size("col")
    every = row_size * col_size
    width = row_count // col_size
    direct = width % 128 == 0 and col_size == 8
    me = lax.axis_index("col").astype(jnp.int32).reshape(1)
    col_bits = [1 << b for b in range(col_size.bit_length() - 1)]
    row_bits = [col_size << b for b in range(row_size.bit_length() - 1)]
    tensor = pltpu.with_memory_space_constraint(tensor, pltpu.HBM)
    second_values = second_factor.astype(F32)
    second_turned = second_factor.T
    groups = range(0, col_count, GROUP)

    offsets, turned, wides = [0], [], []
    if direct:
        have = join(first_factor, second_turned)
        for n, bit in enumerate((4, 2, 1)):
            got = swap(have, "col", col_size, bit)
            offsets = offsets + [o ^ bit for o in offsets]
            t, w = prepare(tensor, second_values, groups[n], have)
            turned.append(t)
            wides.append(w)
            if n < 2:
                have = stack(have, got, t)
        first_turned, gram_first, gram_second = assemble_first(me, [have, got], t, offsets, components, row_count)
    else:
        full = lax.all_gather(first_factor, "col", axis=1, tiled=True)
        others = lax.all_gather(second_factor, "col", axis=1, tiled=True)
        first_turned = full.T
        gram_first = jnp.dot(full, full.T, preferred_element_type=F32)
        gram_second = jnp.dot(others, others.T, preferred_element_type=F32)
    for at in groups[len(turned) :]:
        t, w = prepare(tensor, second_values, at, second_values)
        turned.append(t)
        wides.append(w)

    total = jnp.zeros((frame_count, components), F32)
    second_flat = second_turned.astype(F32)
    for n, t in enumerate(turned):
        after = gram_first
        if n < len(row_bits):
            got = swap(gram_first, BOTH, every, row_bits[n])
        rows_now = second_flat[n * GROUP : n * GROUP + GROUP]
        total = project(first_turned, rows_now, t, total, after, n == len(turned) - 1)
        if n < len(row_bits):
            gram_first = add(gram_first, got, total)

    state = (gram_first, gram_second)
    bits = row_bits + col_bits
    cuts = components // 4
    for n, bit in enumerate(bits):
        got = swap(total, BOTH, every, bit)
        if n < 4:
            state = (eliminate_part(state, n * cuts, n * cuts + cuts, total),)
        total = add(total, got, state[0])
    frames, gram_frames, z, *outs = slab(me, state[0], total, turned, wides, width, direct)

    state = (gram_second, gram_frames)
    if direct:
        keep, send = outs
        got = swap(send, "col", col_size, 1)
        state = (eliminate_part(state, 0, 24, send),)
        keep, send = halve(me, keep, got, 1, state[0])
        got = swap(send, "col", col_size, 2)
        state = (eliminate_part(state, 24, 44, send),)
        keep = add(keep, got, state[0])
        got = swap(keep, "col", col_size, 4)
        state = (eliminate_part(state, 44, components, keep),)
        have = update(state[0], [keep, got])
        got = swap(have, "col", col_size, 2)
        have = stack(have, got, state[0])
        got = swap(have, "col", col_size, 1)
        stacks = [have, got]
    else:
        state = (eliminate_part(state, 0, components, outs[0]),)
        summed = lax.psum_scatter(outs[0], "col", scatter_dimension=1, tiled=True)
        new = update(state[0], [summed[None]])[0]
        stacks = [lax.all_gather(new, "col", axis=1, tiled=True)[None]]
    part = second(me, stacks, offsets, z)
    for bit in row_bits[:-1]:
        part = part + swap(part, BOTH, every, bit)
    got = swap(part, BOTH, every, row_bits[-1])
    outs = mode(me, part, got, gram_frames, z, width, direct)
    if not direct:
        return (frames, lax.psum_scatter(outs[0], "col", scatter_dimension=1, tiled=True))
    keep, send = outs
    got = swap(send, "col", col_size, 1)
    keep, send = halve(me, keep, got, 1, keep)
    got = swap(send, "col", col_size, 2)
    keep, send = halve(me, keep, got, 2, keep)
    got = swap(send, "col", col_size, 4)
    return (frames, keep[0] + got[0].astype(F32))


def solution(mesh):
    return jax.shard_map(
        local,
        mesh=mesh,
        in_specs=(P(None, "col", "row"), P(None, ("row", "col")), P(None, "col")),
        out_specs=(P(), P(None, ("row", "col"))),
        check_vma=False,
    )
```

profile of v0, /device:TPU:0, one launch (start us, length us, event | category | flops | bytes accessed | tf_op | source)
XLA Modules:
  0.0 108.3 jit_solution(15416150754069795052)
XLA Ops:
  2.1 4.0 %collective-permute-start = (bf16[1,96,128]{2,1,0:T(8,128)(2,1)S(1)}, bf16[1,96,128]{2,1,0:T(8,128)(2,1)S(1)}, u32[]{:S(2)}, u32[]{:S(2)}) collective-permute-start(bf16[1,96,128]{2,1,0:T(8,128)(2,1)S(1)} %join.1.after_ref.a_ref), channel_id=1, source_target_pairs={{0,4},{1,5},{2,6},{3,7},{4,0},{5,1},{6,2},{7,3},{8,12},{9,13},{10,... | collective-permute-start | bytes 73736 | tf_op jit(solution)/shard_map/ppermute | solution.py:54
  6.3 3.6 %prepare.3 = (bf16[16,128,1024]{2,1,0:T(8,128)(2,1)S(1)}, f32[16,64,128]{2,1,0:T(8,128)S(1)}) custom-call(bf16[128,48,1024]{2,1,0:T(8,128)(2,1)} %t_ref.5, f32[64,48]{1,0:T(8,128)S(1)} %convert_element_type.10.b_ref, bf16[1,96,128]{2,1,0:T(8,128)(2,1)S(1)} %join.1.after_ref.a_ref), custom_call_target="tpu_custom_call" | custom-call | bytes 6000000 | tf_op jit(solution)/shard_map/prepare/pallas_call | solution.py:37
  9.9 2.0 %copy-done = bf16[16,128,1024]{2,1,0:T(8,128)(2,1)} copy-done((bf16[16,128,1024]{2,1,0:T(8,128)(2,1)}, bf16[16,128,1024]{2,1,0:T(8,128)(2,1)S(1)}, u32[]{:S(2)}) %copy-start) | copy-done | bytes 4194328
  11.8 1.6 %collective-permute-start.1 = (bf16[2,96,128]{2,1,0:T(8,128)(2,1)S(1)}, bf16[2,96,128]{2,1,0:T(8,128)(2,1)S(1)}, u32[]{:S(2)}, u32[]{:S(2)}) collective-permute-start(bf16[2,96,128]{2,1,0:T(8,128)(2,1)S(1)} %stack.3.after_ref.a_ref), channel_id=1, source_target_pairs={{0,2},{1,3},{2,0},{3,1},{4,6},{5,7},{6,4},{7,5},{8,10},{9,11},{10,... | collective-permute-start | bytes 147464 | tf_op jit(solution)/shard_map/ppermute | solution.py:54
  13.4 3.6 %prepare.4 = (bf16[16,128,1024]{2,1,0:T(8,128)(2,1)S(1)}, f32[16,64,128]{2,1,0:T(8,128)S(1)}) custom-call(bf16[128,48,1024]{2,1,0:T(8,128)(2,1)} %t_ref.5, f32[64,48]{1,0:T(8,128)S(1)} %convert_element_type.10.b_ref, bf16[2,96,128]{2,1,0:T(8,128)(2,1)S(1)} %stack.3.after_ref.a_ref), custom_call_target="tpu_custom_call" | custom-call | bytes 6000000 | tf_op jit(solution)/shard_map/prepare/pallas_call | solution.py:37
  17.0 2.0 %copy-done.2 = bf16[16,128,1024]{2,1,0:T(8,128)(2,1)} copy-done((bf16[16,128,1024]{2,1,0:T(8,128)(2,1)}, bf16[16,128,1024]{2,1,0:T(8,128)(2,1)S(1)}, u32[]{:S(2)}) %copy-start.2) | copy-done | bytes 4194328
  20.5 3.6 %prepare.5 = (bf16[16,128,1024]{2,1,0:T(8,128)(2,1)S(1)}, f32[16,64,128]{2,1,0:T(8,128)S(1)}) custom-call(bf16[128,48,1024]{2,1,0:T(8,128)(2,1)} %t_ref.5, f32[64,48]{1,0:T(8,128)S(1)} %convert_element_type.10.b_ref, bf16[4,96,128]{2,1,0:T(8,128)(2,1)S(1)} %stack.4.after_ref.refs_0_), custom_call_target="tpu_custom_call" | custom-call | bytes 6000000 | tf_op jit(solution)/shard_map/prepare/pallas_call | solution.py:37
  24.6 1.7 %copy-done.1 = bf16[16,128,1024]{2,1,0:T(8,128)(2,1)S(1)} copy-done((bf16[16,128,1024]{2,1,0:T(8,128)(2,1)S(1)}, bf16[16,128,1024]{2,1,0:T(8,128)(2,1)}, u32[]{:S(2)}) %copy-start.1) | copy-done | bytes 4194328
  27.6 1.6 %collective-permute-start.4 = (f32[64,64]{1,0:T(8,128)S(1)}, f32[64,64]{1,0:T(8,128)S(1)}, u32[]{:S(2)}, u32[]{:S(2)}) collective-permute-start(f32[64,64]{1,0:T(8,128)S(1)} %add.21.after_ref.a_ref), channel_id=1, source_target_pairs={{0,16},{1,17},{2,18},{3,19},{4,20},{5,21},{6,22},{7,23},{8,24},{9,... | collective-permute-start | bytes 49160 | tf_op jit(solution)/shard_map/ppermute | solution.py:54
  39.5 2.5 %collective-permute-done.7.b_ref = f32[64,128]{1,0:T(8,128)S(1)} collective-permute-done((f32[64,128]{1,0:T(8,128)S(1)}, f32[64,128]{1,0:T(8,128)S(1)}, u32[]{:S(2)}, u32[]{:S(2)}) %collective-permute-start.7) | collective-permute-done | bytes 32800 | tf_op jit(solution)/shard_map/ppermute | solution.py:54
  43.4 2.5 %collective-permute-done.8.b_ref = f32[64,128]{1,0:T(8,128)S(1)} collective-permute-done((f32[64,128]{1,0:T(8,128)S(1)}, f32[64,128]{1,0:T(8,128)S(1)}, u32[]{:S(2)}, u32[]{:S(2)}) %collective-permute-start.8) | collective-permute-done | bytes 32800 | tf_op jit(solution)/shard_map/ppermute | solution.py:54
  47.4 3.6 %collective-permute-done.9.b_ref = f32[64,128]{1,0:T(8,128)S(1)} collective-permute-done((f32[64,128]{1,0:T(8,128)S(1)}, f32[64,128]{1,0:T(8,128)S(1)}, u32[]{:S(2)}, u32[]{:S(2)}) %collective-permute-start.9) | collective-permute-done | bytes 32800 | tf_op jit(solution)/shard_map/ppermute | solution.py:54
  51.0 8.0 %slab.1 = (f32[64,128]{1,0:T(8,128)}, f32[64,64]{1,0:T(8,128)S(1)}, f32[48,64,1024]{2,1,0:T(8,128)S(1)}, f32[4,64,128]{2,1,0:T(8,128)S(1)}, f32[4,64,128]{2,1,0:T(8,128)S(1)}) custom-call(s32[1]{0:T(128)} %bitcast.me_ref, f32[64,64]{1,0:T(8,128)S(1)} %eliminate.10.after_ref.inverse_ref, f32[64,128]{1,0:T(8,128)S(1)} %add.27.summed_ref, ...), custom_call_target="tpu_custom_call" | custom-call | bytes 24000000 | tf_op jit(solution)/shard_map/slab/pallas_call | solution.py:37
  60.9 3.0 %collective-permute-done.10.got_in = f32[4,64,128]{2,1,0:T(8,128)S(1)} collective-permute-done((f32[4,64,128]{2,1,0:T(8,128)S(1)}, f32[4,64,128]{2,1,0:T(8,128)S(1)}, u32[]{:S(2)}, u32[]{:S(2)}) %collective-permute-start.10) | collective-permute-done | bytes 131104 | tf_op jit(solution)/shard_map/ppermute | solution.py:54
  65.4 2.9 %collective-permute-done.11.b_ref = f32[2,64,128]{2,1,0:T(8,128)S(1)} collective-permute-done((f32[2,64,128]{2,1,0:T(8,128)S(1)}, f32[2,64,128]{2,1,0:T(8,128)S(1)}, u32[]{:S(2)}, u32[]{:S(2)}) %collective-permute-start.11) | collective-permute-done | bytes 65568 | tf_op jit(solution)/shard_map/ppermute | solution.py:54
  70.7 3.2 %collective-permute-done.12.refs_1_ = f32[2,64,128]{2,1,0:T(8,128)S(1)} collective-permute-done((f32[2,64,128]{2,1,0:T(8,128)S(1)}, f32[2,64,128]{2,1,0:T(8,128)S(1)}, u32[]{:S(2)}, u32[]{:S(2)}) %collective-permute-start.12) | collective-permute-done | bytes 65568 | tf_op jit(solution)/shard_map/ppermute | solution.py:54
  74.2 3.9 %collective-permute-done.13.b_ref = bf16[2,64,128]{2,1,0:T(8,128)(2,1)S(1)} collective-permute-done((bf16[2,64,128]{2,1,0:T(8,128)(2,1)S(1)}, bf16[2,64,128]{2,1,0:T(8,128)(2,1)S(1)}, u32[]{:S(2)}, u32[]{:S(2)}) %collective-permute-start.13) | collective-permute-done | bytes 32800 | tf_op jit(solution)/shard_map/ppermute | solution.py:54
  78.6 3.7 %collective-permute-done.14.refs_1_ = bf16[4,64,128]{2,1,0:T(8,128)(2,1)S(1)} collective-permute-done((bf16[4,64,128]{2,1,0:T(8,128)(2,1)S(1)}, bf16[4,64,128]{2,1,0:T(8,128)(2,1)S(1)}, u32[]{:S(2)}, u32[]{:S(2)}) %collective-permute-start.14) | collective-permute-done | bytes 65568 | tf_op jit(solution)/shard_map/ppermute | solution.py:54
  82.3 1.7 %second.1 = f32[64,128]{1,0:T(8,128)S(1)} custom-call(s32[1]{0:T(128)} %bitcast.me_ref, bf16[4,64,128]{2,1,0:T(8,128)(2,1)S(1)} %stack.5.refs_0_, bf16[4,64,128]{2,1,0:T(8,128)(2,1)S(1)} %collective-permute-done.14.refs_1_, f32[48,64,1024]{2,1,0:T(8,128)S(1)} %get-tuple-element.39.refs_2_.z_ref), custom_call_target="tpu_custom_call" | custom-call | bytes 6000000 | tf_op jit(solution)/shard_map/second/pallas_call | solution.py:37
  86.8 2.4 %collective-permute-done.16.got_ref = f32[64,128]{1,0:T(8,128)S(1)} collective-permute-done((f32[64,128]{1,0:T(8,128)S(1)}, f32[64,128]{1,0:T(8,128)S(1)}, u32[]{:S(2)}, u32[]{:S(2)}) %collective-permute-start.16) | collective-permute-done | bytes 32800 | tf_op jit(solution)/shard_map/ppermute | solution.py:54
  89.2 5.4 %mode.1 = (f32[4,64,128]{2,1,0:T(8,128)S(1)}, bf16[4,64,128]{2,1,0:T(8,128)(2,1)S(1)}) custom-call(s32[1]{0:T(128)} %bitcast.me_ref, f32[64,128]{1,0:T(8,128)S(1)} %add.17.mine_ref, f32[64,128]{1,0:T(8,128)S(1)} %collective-permute-done.16.got_ref, f32[64,64]{1,0:T(8,128)S(1)} %get-tuple-element.34.refs_1_.gram_frames_ref, ...), custom_call_target="tpu_custom_call" | custom-call | bytes 15000000 | tf_op jit(solution)/shard_map/mode/pallas_call | solution.py:37
  95.2 3.7 %collective-permute-done.17.got_in = bf16[4,64,128]{2,1,0:T(8,128)(2,1)S(1)} collective-permute-done((bf16[4,64,128]{2,1,0:T(8,128)(2,1)S(1)}, bf16[4,64,128]{2,1,0:T(8,128)(2,1)S(1)}, u32[]{:S(2)}, u32[]{:S(2)}) %collective-permute-start.17) | collective-permute-done | bytes 65568 | tf_op jit(solution)/shard_map/ppermute | solution.py:54
  99.0 3.9 %collective-permute-done.18.got_in = bf16[2,64,128]{2,1,0:T(8,128)(2,1)S(1)} collective-permute-done((bf16[2,64,128]{2,1,0:T(8,128)(2,1)S(1)}, bf16[2,64,128]{2,1,0:T(8,128)(2,1)S(1)}, u32[]{:S(2)}, u32[]{:S(2)}) %collective-permute-start.18) | collective-permute-done | bytes 32800 | tf_op jit(solution)/shard_map/ppermute | solution.py:54
  104.0 3.6 %collective-permute-done.19 = bf16[1,64,128]{2,1,0:T(8,128)(2,1)S(1)} collective-permute-done((bf16[1,64,128]{2,1,0:T(8,128)(2,1)S(1)}, bf16[1,64,128]{2,1,0:T(8,128)(2,1)S(1)}, u32[]{:S(2)}, u32[]{:S(2)}) %collective-permute-start.19) | collective-permute-done | bytes 16416 | tf_op jit(solution)/shard_map/ppermute | solution.py:54
  (70 shorter events, 29.9 us)
Async XLA Ops:
  2.1 7.7 %collective-permute-start = (bf16[1,96,128]{2,1,0:T(8,128)(2,1)S(1)}, bf16[1,96,128]{2,1,0:T(8,128)(2,1)S(1)}, u32[]{:S(2)}, u32[]{:S(2)}) collective-permute-start(bf16[1,96,128]{2,1,0:T(8,128)(2,1)S(1)} %join.1.after_ref.a_ref), channel_id=1, source_target_pairs={{0,4},{1,5},{2,6},{3,7},{4,0},{5,1},{6,2},{7,3},{8,12},{9,13},{10,... | collective-permute-start | bytes 73736 | tf_op jit(solution)/shard_map/ppermute | solution.py:54
  11.8 5.2 %collective-permute-start.1 = (bf16[2,96,128]{2,1,0:T(8,128)(2,1)S(1)}, bf16[2,96,128]{2,1,0:T(8,128)(2,1)S(1)}, u32[]{:S(2)}, u32[]{:S(2)}) collective-permute-start(bf16[2,96,128]{2,1,0:T(8,128)(2,1)S(1)} %stack.3.after_ref.a_ref), channel_id=1, source_target_pairs={{0,2},{1,3},{2,0},{3,1},{4,6},{5,7},{6,4},{7,5},{8,10},{9,11},{10,... | collective-permute-start | bytes 147464 | tf_op jit(solution)/shard_map/ppermute | solution.py:54
  17.0 3.6 %copy-start.5 = (bf16[64,48]{0,1:T(8,128)(2,1)S(1)}, bf16[64,48]{0,1:T(8,128)(2,1)}, u32[]{:S(2)}) copy-start(bf16[64,48]{0,1:T(8,128)(2,1)} %param.5) | copy-start | bytes 18436
  17.0 2.0 %copy-start.2 = (bf16[16,128,1024]{2,1,0:T(8,128)(2,1)}, bf16[16,128,1024]{2,1,0:T(8,128)(2,1)S(1)}, u32[]{:S(2)}) copy-start(bf16[16,128,1024]{2,1,0:T(8,128)(2,1)S(1)} %get-tuple-element.25.after_ref.t_ref.refs_1_) | copy-start | bytes 12582916
  19.0 5.1 %collective-permute-start.2 = (bf16[4,96,128]{2,1,0:T(8,128)(2,1)S(1)}, bf16[4,96,128]{2,1,0:T(8,128)(2,1)S(1)}, u32[]{:S(2)}, u32[]{:S(2)}) collective-permute-start(bf16[4,96,128]{2,1,0:T(8,128)(2,1)S(1)} %stack.4.after_ref.refs_0_), channel_id=1, source_target_pairs={{0,1},{1,0},{2,3},{3,2},{4,5},{5,4},{6,7},{7,6},{8,9},{9,8},{10,11... | collective-permute-start | bytes 294920 | tf_op jit(solution)/shard_map/ppermute | solution.py:54
  24.1 2.2 %copy-start.1 = (bf16[16,128,1024]{2,1,0:T(8,128)(2,1)S(1)}, bf16[16,128,1024]{2,1,0:T(8,128)(2,1)}, u32[]{:S(2)}) copy-start(bf16[16,128,1024]{2,1,0:T(8,128)(2,1)} %copy-done) | copy-start | bytes 12582916
  24.1 5.0 %copy-start.3 = (bf16[16,128,1024]{2,1,0:T(8,128)(2,1)S(1)}, bf16[16,128,1024]{2,1,0:T(8,128)(2,1)}, u32[]{:S(2)}) copy-start(bf16[16,128,1024]{2,1,0:T(8,128)(2,1)} %copy-done.2) | copy-start | bytes 12582916
  24.5 3.0 %collective-permute-start.3 = (f32[64,64]{1,0:T(8,128)S(1)}, f32[64,64]{1,0:T(8,128)S(1)}, u32[]{:S(2)}, u32[]{:S(2)}) collective-permute-start(f32[64,64]{1,0:T(8,128)S(1)} %get-tuple-element.27.after_ref.a_ref), channel_id=1, source_target_pairs={{0,8},{1,9},{2,10},{3,11},{4,12},{5,13},{6,14},{7,15},{8,0},{9,1},... | collective-permute-start | bytes 49160 | tf_op jit(solution)/shard_map/ppermute | solution.py:54
  27.6 4.0 %collective-permute-start.4 = (f32[64,64]{1,0:T(8,128)S(1)}, f32[64,64]{1,0:T(8,128)S(1)}, u32[]{:S(2)}, u32[]{:S(2)}) collective-permute-start(f32[64,64]{1,0:T(8,128)S(1)} %add.21.after_ref.a_ref), channel_id=1, source_target_pairs={{0,16},{1,17},{2,18},{3,19},{4,20},{5,21},{6,22},{7,23},{8,24},{9,... | collective-permute-start | bytes 49160 | tf_op jit(solution)/shard_map/ppermute | solution.py:54
  32.9 1.3 %collective-permute-start.5 = (f32[64,128]{1,0:T(8,128)S(1)}, f32[64,128]{1,0:T(8,128)S(1)}, u32[]{:S(2)}, u32[]{:S(2)}) collective-permute-start(f32[64,128]{1,0:T(8,128)S(1)} %project.5.refs_2_.a_ref), channel_id=1, source_target_pairs={{0,8},{1,9},{2,10},{3,11},{4,12},{5,13},{6,14},{7,15},{8,0},{9,1},... | collective-permute-start | bytes 98312 | tf_op jit(solution)/shard_map/ppermute | solution.py:54
  34.1 3.9 %collective-permute-start.6 = (f32[64,128]{1,0:T(8,128)S(1)}, f32[64,128]{1,0:T(8,128)S(1)}, u32[]{:S(2)}, u32[]{:S(2)}) collective-permute-start(f32[64,128]{1,0:T(8,128)S(1)} %add.23.refs_1_.a_ref), channel_id=1, source_target_pairs={{0,16},{1,17},{2,18},{3,19},{4,20},{5,21},{6,22},{7,23},{8,24},{9,... | collective-permute-start | bytes 98312 | tf_op jit(solution)/shard_map/ppermute | solution.py:54
  38.0 3.9 %collective-permute-start.7 = (f32[64,128]{1,0:T(8,128)S(1)}, f32[64,128]{1,0:T(8,128)S(1)}, u32[]{:S(2)}, u32[]{:S(2)}) collective-permute-start(f32[64,128]{1,0:T(8,128)S(1)} %add.24.refs_1_.a_ref), channel_id=1, source_target_pairs={{0,1},{1,0},{2,3},{3,2},{4,5},{5,4},{6,7},{7,6},{8,9},{9,8},{10,11... | collective-permute-start | bytes 98312 | tf_op jit(solution)/shard_map/ppermute | solution.py:54
  42.0 3.9 %collective-permute-start.8 = (f32[64,128]{1,0:T(8,128)S(1)}, f32[64,128]{1,0:T(8,128)S(1)}, u32[]{:S(2)}, u32[]{:S(2)}) collective-permute-start(f32[64,128]{1,0:T(8,128)S(1)} %add.25.refs_1_.a_ref), channel_id=1, source_target_pairs={{0,2},{1,3},{2,0},{3,1},{4,6},{5,7},{6,4},{7,5},{8,10},{9,11},{10,... | collective-permute-start | bytes 98312 | tf_op jit(solution)/shard_map/ppermute | solution.py:54
  45.9 5.1 %collective-permute-start.9 = (f32[64,128]{1,0:T(8,128)S(1)}, f32[64,128]{1,0:T(8,128)S(1)}, u32[]{:S(2)}, u32[]{:S(2)}) collective-permute-start(f32[64,128]{1,0:T(8,128)S(1)} %add.26.a_ref), channel_id=1, source_target_pairs={{0,4},{1,5},{2,6},{3,7},{4,0},{5,1},{6,2},{7,3},{8,12},{9,13},{10,... | collective-permute-start | bytes 98312 | tf_op jit(solution)/shard_map/ppermute | solution.py:54
  59.0 5.0 %collective-permute-start.10 = (f32[4,64,128]{2,1,0:T(8,128)S(1)}, f32[4,64,128]{2,1,0:T(8,128)S(1)}, u32[]{:S(2)}, u32[]{:S(2)}) collective-permute-start(f32[4,64,128]{2,1,0:T(8,128)S(1)} %get-tuple-element.35.refs_2_), channel_id=1, source_target_pairs={{0,1},{1,0},{2,3},{3,2},{4,5},{5,4},{6,7},{7,6},{8,9},{9,8},{10,11... | collective-permute-start | bytes 393224 | tf_op jit(solution)/shard_map/ppermute | solution.py:54
  63.9 4.3 %collective-permute-start.11 = (f32[2,64,128]{2,1,0:T(8,128)S(1)}, f32[2,64,128]{2,1,0:T(8,128)S(1)}, u32[]{:S(2)}, u32[]{:S(2)}) collective-permute-start(f32[2,64,128]{2,1,0:T(8,128)S(1)} %get-tuple-element.37.refs_1_), channel_id=1, source_target_pairs={{0,2},{1,3},{2,0},{3,1},{4,6},{5,7},{6,4},{7,5},{8,10},{9,11},{10,... | collective-permute-start | bytes 196616 | tf_op jit(solution)/shard_map/ppermute | solution.py:54
  68.3 5.6 %collective-permute-start.12 = (f32[2,64,128]{2,1,0:T(8,128)S(1)}, f32[2,64,128]{2,1,0:T(8,128)S(1)}, u32[]{:S(2)}, u32[]{:S(2)}) collective-permute-start(f32[2,64,128]{2,1,0:T(8,128)S(1)} %add.28.refs_1_.refs_0_), channel_id=1, source_target_pairs={{0,4},{1,5},{2,6},{3,7},{4,0},{5,1},{6,2},{7,3},{8,12},{9,13},{10,... | collective-permute-start | bytes 196616 | tf_op jit(solution)/shard_map/ppermute | solution.py:54
  74.1 4.0 %collective-permute-start.13 = (bf16[2,64,128]{2,1,0:T(8,128)(2,1)S(1)}, bf16[2,64,128]{2,1,0:T(8,128)(2,1)S(1)}, u32[]{:S(2)}, u32[]{:S(2)}) collective-permute-start(bf16[2,64,128]{2,1,0:T(8,128)(2,1)S(1)} %update.1.a_ref), channel_id=1, source_target_pairs={{0,2},{1,3},{2,0},{3,1},{4,6},{5,7},{6,4},{7,5},{8,10},{9,11},{10,... | collective-permute-start | bytes 98312 | tf_op jit(solution)/shard_map/ppermute | solution.py:54
  78.1 4.3 %collective-permute-start.14 = (bf16[4,64,128]{2,1,0:T(8,128)(2,1)S(1)}, bf16[4,64,128]{2,1,0:T(8,128)(2,1)S(1)}, u32[]{:S(2)}, u32[]{:S(2)}) collective-permute-start(bf16[4,64,128]{2,1,0:T(8,128)(2,1)S(1)} %stack.5.refs_0_), channel_id=1, source_target_pairs={{0,1},{1,0},{2,3},{3,2},{4,5},{5,4},{6,7},{7,6},{8,9},{9,8},{10,11... | collective-permute-start | bytes 196616 | tf_op jit(solution)/shard_map/ppermute | solution.py:54
  84.0 1.3 %collective-permute-start.15 = (f32[64,128]{1,0:T(8,128)S(1)}, f32[64,128]{1,0:T(8,128)S(1)}, u32[]{:S(2)}, u32[]{:S(2)}) collective-permute-start(f32[64,128]{1,0:T(8,128)S(1)} %second.1), channel_id=1, source_target_pairs={{0,8},{1,9},{2,10},{3,11},{4,12},{5,13},{6,14},{7,15},{8,0},{9,1},... | collective-permute-start | bytes 98312 | tf_op jit(solution)/shard_map/ppermute | solution.py:54
  85.3 3.9 %collective-permute-start.16 = (f32[64,128]{1,0:T(8,128)S(1)}, f32[64,128]{1,0:T(8,128)S(1)}, u32[]{:S(2)}, u32[]{:S(2)}) collective-permute-start(f32[64,128]{1,0:T(8,128)S(1)} %add.17.mine_ref), channel_id=1, source_target_pairs={{0,16},{1,17},{2,18},{3,19},{4,20},{5,21},{6,22},{7,23},{8,24},{9,... | collective-permute-start | bytes 98312 | tf_op jit(solution)/shard_map/ppermute | solution.py:54
  94.6 4.3 %collective-permute-start.17 = (bf16[4,64,128]{2,1,0:T(8,128)(2,1)S(1)}, bf16[4,64,128]{2,1,0:T(8,128)(2,1)S(1)}, u32[]{:S(2)}, u32[]{:S(2)}) collective-permute-start(bf16[4,64,128]{2,1,0:T(8,128)(2,1)S(1)} %get-tuple-element.41), channel_id=1, source_target_pairs={{0,1},{1,0},{2,3},{3,2},{4,5},{5,4},{6,7},{7,6},{8,9},{9,8},{10,11... | collective-permute-start | bytes 196616 | tf_op jit(solution)/shard_map/ppermute | solution.py:54
  99.0 4.0 %collective-permute-start.18 = (bf16[2,64,128]{2,1,0:T(8,128)(2,1)S(1)}, bf16[2,64,128]{2,1,0:T(8,128)(2,1)S(1)}, u32[]{:S(2)}, u32[]{:S(2)}) collective-permute-start(bf16[2,64,128]{2,1,0:T(8,128)(2,1)S(1)} %get-tuple-element.43), channel_id=1, source_target_pairs={{0,2},{1,3},{2,0},{3,1},{4,6},{5,7},{6,4},{7,5},{8,10},{9,11},{10,... | collective-permute-start | bytes 98312 | tf_op jit(solution)/shard_map/ppermute | solution.py:54
  102.9 4.7 %collective-permute-start.19 = (bf16[1,64,128]{2,1,0:T(8,128)(2,1)S(1)}, bf16[1,64,128]{2,1,0:T(8,128)(2,1)S(1)}, u32[]{:S(2)}, u32[]{:S(2)}) collective-permute-start(bf16[1,64,128]{2,1,0:T(8,128)(2,1)S(1)} %get-tuple-element.45), channel_id=1, source_target_pairs={{0,4},{1,5},{2,6},{3,7},{4,0},{5,1},{6,2},{7,3},{8,12},{9,13},{10,... | collective-permute-start | bytes 49160 | tf_op jit(solution)/shard_map/ppermute | solution.py:54
  (3 other events, 3.4 us)
where the time goes:
time: 109 us; the launch traced here: 108 us
  waiting for transfers between devices  42.9 us (39%)
  Pallas kernels  37.5 us (34%)
  starting transfers between devices  19 us (17%)
  local copies, waits for them, and re-layouts  7.2 us (7%)
    ppermute x20, waiting for transfers between devices, swap(): return lax.ppermute(x, axes, [(n, n ^ offset) for n in range(count)])  42.9 us
    pallas_call x33, Pallas kernels, call(): pl.pallas_call(body, out_shape=outs, in_specs=ins, out_specs=(vmem(),) *...  37.5 us
    ppermute x20, starting transfers between devices, swap(): return lax.ppermute(x, axes, [(n, n ^ offset) for n in range(count)])  19 us
    unnamed x15, local copies, waits for them, and re-layouts  7.19 us
  transfers between devices with their start and end apart: 20, of which 16 were waited for; matrix products, arithmetic and copies ran while one was open for 0% of the time, Pallas kernels for 19%

commit v1 on v0

--- a/solution.py
+++ b/solution.py
@@ -50,68 +50,96 @@
     return lax.dot_general(a, b, (dims, ((), ())), precision=precision, preferred_element_type=F32)
 
 
+def swaps(x, axes, count, bits):
+    offsets = [0]
+    for bit in bits:
+        offsets = offsets + [o ^ bit for o in offsets]
+    return [swap(x, axes, count, o) for o in offsets[1:]]
+
+
 def swap(x, axes, count, offset):
     return lax.ppermute(x, axes, [(n, n ^ offset) for n in range(count)])
 
 
-def join_body(a_ref, b_ref, out_ref):
+def join_body(a_hbm, b_hbm, out_ref, turned_ref, second_ref, a_ref, b_ref, sems):
+    moves = [pltpu.make_async_copy(*pair, sems.at[n]) for n, pair in enumerate(((a_hbm, a_ref), (b_hbm, b_ref)))]
+    for move in moves:
+        move.start()
+    for move in moves:
+        move.wait()
     components = a_ref.shape[0]
     half = b_ref.shape[0] // 2
-    out_ref[...] = jnp.zeros_like(out_ref)
-    out_ref[0, :components, : a_ref.shape[1]] = a_ref[...]
+    out_ref[0, :components, :] = a_ref[...]
     b = b_ref[...].astype(F32)
+    turned_ref[...] = b
+    second_ref[...] = jnp.zeros_like(second_ref)
+    second_ref[:, : b.shape[0]] = b.T
     pair = jnp.concatenate([b[:half], b[half:]], axis=1)
     pair = jnp.concatenate([pair, jnp.zeros((-half % 16, 2 * components), F32)], axis=0)
     out_ref[0, components:, :] = pair.astype(BF16)
 
 
 def join(first, second_turned):
-    components, half = first.shape[0], second_turned.shape[0] // 2
-    height = components + half + (-half % 16)
+    components, width = first.shape
+    cols = second_turned.shape[0]
+    height = components + cols // 2 + (-(cols // 2) % 16)
+    first = pltpu.with_memory_space_constraint(first, pltpu.HBM)
+    second_turned = pltpu.with_memory_space_constraint(second_turned, pltpu.HBM)
     return call(
         join_body,
-        shaped((1, height, 128), BF16),
-        [vmem()] * 2,
+        (shaped((1, height, width), BF16), shaped((cols, components)), shaped((components, 128))),
+        [anywhere()] * 2,
         (first, second_turned),
         "join",
-    )
-
-
-def stack_body(a_ref, b_ref, after_ref, out_ref):
+        [VM(first.shape, BF16), VM(second_turned.shape, BF16), pltpu.SemaphoreType.DMA((2,))],
+    )
+
+
+def stack_body(*refs):
+    *parts, after_ref, out_ref = refs
     del after_ref
-    count = a_ref.shape[0]
-    out_ref[:count] = a_ref[...]
-    out_ref[count:] = b_ref[...]
-
-
-def stack(a, b, after):
-    shape = (2 * a.shape[0],) + a.shape[1:]
-    specs = [vmem()] * 2 + [anywhere()]
-    return call(stack_body, shaped(shape, a.dtype), specs, (a, b, after), "stack", us=0.2)
-
-
-def add_body(a_ref, b_ref, after_ref, out_ref):
+    at = 0
+    for part in parts:
+        out_ref[at : at + part.shape[0]] = part[...]
+        at += part.shape[0]
+
+
+def stack(parts, after):
+    shape = (sum(p.shape[0] for p in parts),) + parts[0].shape[1:]
+    specs = [vmem()] * len(parts) + [anywhere()]
+    return call(stack_body, shaped(shape, parts[0].dtype), specs, (*parts, after), "stack", us=0.2)
+
+
+def paired(values):
+    while len(values) > 1:
+        values = [values[n] + values[n + 1] for n in range(0, len(values), 2)]
+    return values[0]
+
+
+def add_body(*refs):
+    *parts, after_ref, out_ref = refs
     del after_ref
-    out_ref[...] = a_ref[...] + b_ref[...]
-
-
-def add(a, b, after):
-    specs = [vmem()] * 2 + [anywhere()]
-    return call(add_body, shaped(a.shape, a.dtype), specs, (a, b, after), "add", us=0.2)
-
-
-def prepare_body(at, t_ref, b_ref, after_ref, out_ref, wide_ref, slab, sems):
+    out_ref[...] = paired([p[...] for p in parts])
+
+
+def add(parts, after):
+    specs = [vmem()] * len(parts) + [anywhere()]
+    return call(add_body, shaped(parts[0].shape), specs, (*parts, after), "add", us=0.2)
+
+
+def prepare_body(at, t_ref, b_ref, after_ref, out_ref, wide_ref, token_ref, slab, sems):
     del after_ref
-    blocks = slab.shape[0]
+    blocks, _, cols, _ = slab.shape
 
     def fetch(n):
         return pltpu.make_async_copy(
-            t_ref.at[pl.ds(n * GROUP, GROUP), pl.ds(at, GROUP)], slab.at[n], sems.at[n]
+            t_ref.at[pl.ds(n * GROUP, GROUP), pl.ds(at, cols)], slab.at[n], sems.at[n]
         )
 
     for n in range(blocks):
         fetch(n).start()
-    for j in range(GROUP):
+    token_ref[...] = jnp.zeros_like(token_ref)
+    for j in range(cols):
         wide_ref[j] = jnp.broadcast_to(b_ref[:, at + j : at + j + 1], wide_ref.shape[1:])
     to = lax.broadcasted_iota(jnp.int32, (256, 256), 0)
     of = lax.broadcasted_iota(jnp.int32, (256, 256), 1)
@@ -119,26 +147,27 @@
 
     def step(n, _):
         fetch(n).wait()
-        block = slab[n].reshape(GROUP * GROUP, -1)
-        turned = dot(turn, block, ((1,), (0,))).astype(BF16).reshape(GROUP, GROUP, -1)
-        out_ref[:, pl.ds(pl.multiple_of(n * GROUP, GROUP), GROUP), :] = turned
+        for g in range(0, cols, GROUP):
+            block = slab[n, :, g : g + GROUP, :].reshape(GROUP * GROUP, -1)
+            turned = dot(turn, block, ((1,), (0,))).astype(BF16).reshape(GROUP, GROUP, -1)
+            out_ref[g : g + GROUP, pl.ds(pl.multiple_of(n * GROUP, GROUP), GROUP), :] = turned
         return 0
 
     lax.fori_loop(0, blocks, step, 0)
 
 
-def prepare(tensor, second, at, after):
+def prepare(tensor, second, at, cols, after):
     frames, _, rows = tensor.shape
     components = second.shape[0]
     blocks = frames // GROUP
     return call(
         functools.partial(prepare_body, at),
-        (VM((GROUP, frames, rows), BF16), VM((GROUP, components, 128), F32)),
+        (VM((cols, frames, rows), BF16), VM((cols, components, 128), F32), shaped((8, 128))),
         [anywhere(), vmem(), anywhere()],
         (tensor, second, after),
         "prepare",
-        [VM((blocks, GROUP, GROUP, rows), BF16), pltpu.SemaphoreType.DMA((blocks,))],
-        us=2,
+        [VM((blocks, GROUP, cols, rows), BF16), pltpu.SemaphoreType.DMA((blocks,))],
+        us=cols / 8,
     )
 
 
@@ -181,30 +210,36 @@
     )
 
 
-def project_body(last, span, turned_ref, second_ref, t_ref, sum_ref, after_ref, out_ref):
+def project_body(at, base, cols, last, span, turned_ref, second_ref, t_ref, *refs):
+    *sums, after_ref, out_ref = refs
     del after_ref
     components = turned_ref.shape[1]
-    cols, frames, rows = t_ref.shape
+    _, frames, rows = t_ref.shape
     weights = turned_ref[...]
-    total = sum_ref[...]
-    for n in range(0, cols, span):
-        block = t_ref[n : n + span].reshape(span * frames, rows)
+
+    def step(n, total):
+        block = t_ref[pl.ds(base + n * span, span)].reshape(span * frames, rows)
         product = dot(block, weights, ((1,), (0,))).reshape(span, frames, components)
+        scale = second_ref[pl.ds(pl.multiple_of(at + base + n * span, span), span), :]
         for s in range(span):
-            total = total + product[s] * second_ref[n + s : n + s + 1, :]
+            total = total + product[s] * scale[s : s + 1, :]
+        return total
+
+    start = sums[0][...] if sums else jnp.zeros((frames, components), F32)
+    total = lax.fori_loop(0, cols // span, step, start)
     out_ref[...] = total.T if last else total
 
 
-def project(turned, second_turned, t, total, after, last):
-    frames, components = total.shape
+def project(turned, second_turned, t, at, base, cols, sums, after, last):
+    components, frames = turned.shape[1], t.shape[1]
     shape = (components, frames) if last else (frames, components)
     return call(
-        functools.partial(project_body, last, 8),
+        functools.partial(project_body, at, base, cols, last, 8),
         shaped(shape),
-        [vmem()] * 4 + [anywhere()],
-        (turned, second_turned, t, total, after),
+        [vmem()] * (3 + len(sums)) + [anywhere()],
+        (turned, second_turned, t, *sums, after),
         "project",
-        us=1.5,
+        us=cols / 10,
     )
 
 
@@ -263,23 +298,23 @@
         send_ref[n] = send.astype(send_ref.dtype)
 
 
-def halve_body(shift, me_ref, keep_in, got_in, after_ref, keep_ref, send_ref):
+def deal_body(me_ref, keep_in, got_in, after_ref, mine_ref, *outs):
     del after_ref
-    bit = (me_ref[0] >> shift) & 1
-    for n in range(keep_ref.shape[0]):
-        mine, other = 2 * n + bit, 2 * n + 1 - bit
-        keep_ref[n] = keep_in[mine] + got_in[mine].astype(F32)
-        send_ref[n] = (keep_in[other] + got_in[other].astype(F32)).astype(send_ref.dtype)
-
-
-def halve(me, keep, got, shift, after):
-    shape = (keep.shape[0] // 2,) + keep.shape[1:]
-    return call(
-        functools.partial(halve_body, shift),
-        (shaped(shape), shaped(shape, got.dtype)),
+    upper = me_ref[0] >> 1
+    mine_ref[...] = keep_in[upper] + got_in[upper].astype(F32)
+    for n, out in enumerate(outs):
+        at = upper ^ (n + 1)
+        out[...] = (keep_in[at] + got_in[at].astype(F32)).astype(out.dtype)
+
+
+def deal(me, keep, got, after):
+    count, shape = keep.shape[0], keep.shape[1:]
+    return call(
+        deal_body,
+        (shaped(shape),) + (shaped(shape, got.dtype),) * (count - 1),
         [smem(), vmem(), vmem(), anywhere()],
         (me, keep, got, after),
-        "halve",
+        "deal",
         us=0.2,
     )
 
@@ -306,20 +341,21 @@
     def chunk(c, _):
         lanes = pl.ds(pl.multiple_of(c * wide, wide), wide)
         total = jnp.zeros((components, wide), F32)
-        for g in range(groups):
-            t_ref, wide_ref = t_refs[g], wide_refs[g]
-
-            def step(n, total):
+        base = 0
+        for t_ref, wide_ref in zip(t_refs, wide_refs):
+
+            def step(n, total, t_ref=t_ref, wide_ref=wide_ref, base=base):
                 for s in range(8):
                     j = n * 8 + s
                     product = dot(both, t_ref[j, :, lanes], ((1,), (0,)))
                     z = product[:components] + product[components:]
-                    z_ref[g * GROUP + j, :, lanes] = z
+                    z_ref[base + j, :, lanes] = z
                     scale = wide_ref[j]
                     total = total + z * jnp.concatenate([scale, scale], axis=1)
                 return total
 
-            total = lax.fori_loop(0, GROUP // 8, step, total)
+            total = lax.fori_loop(0, t_ref.shape[0] // 8, step, total)
+            base += t_ref.shape[0]
         sum_ref[:, lanes] = total
         return 0
 
@@ -339,7 +375,7 @@
         (
             shaped((components, frames)),
             shaped((components, components)),
-            VM((groups * GROUP, components, rows), F32),
+            VM((sum(t.shape[0] for t in turned), components, rows), F32),
         )
         + shares_out(direct, components, rows, width, F32),
         [smem()] + [vmem()] * (2 + 2 * groups),
@@ -352,17 +388,14 @@
 
 def update_body(inverse_ref, *refs):
     *parts, out_ref = refs
-    for n in range(out_ref.shape[0]):
-        summed = parts[0][n]
-        for part in parts[1:]:
-            summed = summed + part[n]
-        out_ref[n] = dot(inverse_ref[...], summed, ((1,), (0,)), HIGH).astype(BF16)
+    summed = paired([p[...] for p in parts])
+    out_ref[0] = dot(inverse_ref[...], summed, ((1,), (0,)), HIGH).astype(BF16)
 
 
 def update(inverse_now, parts):
     return call(
         update_body,
-        shaped(parts[0].shape, BF16),
+        shaped((1,) + parts[0].shape, BF16),
         [vmem()] * (1 + len(parts)),
         (inverse_now, *parts),
         "update",
@@ -373,7 +406,7 @@
     *stacks, z_ref, out_ref, full_ref = refs
     cols, components, rows = z_ref.shape
     blocks = [s[n] for s in stacks for n in range(s.shape[0])]
-    place(me_ref[0] & 3, list(zip(offsets, blocks)), blocks[0].shape[1], full_ref)
+    place(me_ref[0], list(zip(offsets, blocks)), blocks[0].shape[1], full_ref)
     lane = lax.broadcasted_iota(jnp.int32, (8, 128), 1)
 
     def step(n, _):
@@ -455,76 +488,74 @@
     col_bits = [1 << b for b in range(col_size.bit_length() - 1)]
     row_bits = [col_size << b for b in range(row_size.bit_length() - 1)]
     tensor = pltpu.with_memory_space_constraint(tensor, pltpu.HBM)
-    second_values = second_factor.astype(F32)
-    second_turned = second_factor.T
-    groups = range(0, col_count, GROUP)
-
-    offsets, turned, wides = [0], [], []
+    cuts = [(0, GROUP), (GROUP, col_count - GROUP)]
+
+    turned, wides, gathered = [], [], []
     if direct:
-        have = join(first_factor, second_turned)
-        for n, bit in enumerate((4, 2, 1)):
-            got = swap(have, "col", col_size, bit)
-            offsets = offsets + [o ^ bit for o in offsets]
-            t, w = prepare(tensor, second_values, groups[n], have)
+        have, second_turned, second_values = join(first_factor, second_factor.T)
+        token = have
+        for at, cols in cuts:
+            bits = [2, 4] if gathered else [1]
+            gathered = [have] + swaps(have, "col", col_size, bits)
+            t, w, token = prepare(tensor, second_values, at, cols, have)
             turned.append(t)
             wides.append(w)
-            if n < 2:
-                have = stack(have, got, t)
-        first_turned, gram_first, gram_second = assemble_first(me, [have, got], t, offsets, components, row_count)
+            if len(turned) == 1:
+                have = stack(gathered, token)
+        first_turned, gram_first, gram_second = assemble_first(
+            me, gathered, token, list(range(col_size)), components, row_count
+        )
     else:
+        second_turned = second_factor.T.astype(F32)
+        second_values = second_factor.astype(F32)
+        for at, cols in cuts:
+            t, w, token = prepare(tensor, second_values, at, cols, second_values)
+            turned.append(t)
+            wides.append(w)
         full = lax.all_gather(first_factor, "col", axis=1, tiled=True)
         others = lax.all_gather(second_factor, "col", axis=1, tiled=True)
         first_turned = full.T
         gram_first = jnp.dot(full, full.T, preferred_element_type=F32)
         gram_second = jnp.dot(others, others.T, preferred_element_type=F32)
-    for at in groups[len(turned) :]:
-        t, w = prepare(tensor, second_values, at, second_values)
-        turned.append(t)
-        wides.append(w)
-
-    total = jnp.zeros((frame_count, components), F32)
-    second_flat = second_turned.astype(F32)
-    for n, t in enumerate(turned):
-        after = gram_first
-        if n < len(row_bits):
-            got = swap(gram_first, BOTH, every, row_bits[n])
-        rows_now = second_flat[n * GROUP : n * GROUP + GROUP]
-        total = project(first_turned, rows_now, t, total, after, n == len(turned) - 1)
-        if n < len(row_bits):
-            gram_first = add(gram_first, got, total)
+
+    pieces = [(t, at, base) for (at, cols), t in zip(cuts, turned) for base in range(0, cols, GROUP)]
+    sums = []
+    for n, (t, at, base) in enumerate(pieces):
+        got = [swap(gram_first, BOTH, every, bit) for bit in row_bits[n : n + 1]]
+        last = n == len(pieces) - 1
+        sums = [project(first_turned, second_turned, t, at, base, GROUP, sums, gram_first, last)]
+        if got:
+            gram_first = add([gram_first, *got], sums[0])
+    total = sums[0]
 
     state = (gram_first, gram_second)
-    bits = row_bits + col_bits
-    cuts = components // 4
-    for n, bit in enumerate(bits):
-        got = swap(total, BOTH, every, bit)
-        if n < 4:
-            state = (eliminate_part(state, n * cuts, n * cuts + cuts, total),)
-        total = add(total, got, state[0])
+    half = components // 2
+    bits = row_bits[1:] + col_bits
+    stages = [row_bits[:1]] + [bits[n : n + 2] for n in range(0, len(bits), 2)]
+    for n, pair in enumerate(stages):
+        got = swaps(total, BOTH, every, pair)
+        if n in (1, 2):
+            state = (eliminate_part(state, (n - 1) * half, n * half, total),)
+        total = add([total, *got], state[0])
     frames, gram_frames, z, *outs = slab(me, state[0], total, turned, wides, width, direct)
 
     state = (gram_second, gram_frames)
     if direct:
         keep, send = outs
         got = swap(send, "col", col_size, 1)
-        state = (eliminate_part(state, 0, 24, send),)
-        keep, send = halve(me, keep, got, 1, state[0])
-        got = swap(send, "col", col_size, 2)
-        state = (eliminate_part(state, 24, 44, send),)
-        keep = add(keep, got, state[0])
-        got = swap(keep, "col", col_size, 4)
-        state = (eliminate_part(state, 44, components, keep),)
-        have = update(state[0], [keep, got])
-        got = swap(have, "col", col_size, 2)
-        have = stack(have, got, state[0])
-        got = swap(have, "col", col_size, 1)
-        stacks = [have, got]
+        state = (eliminate_part(state, 0, half, send),)
+        mine, *send = deal(me, keep, got, state[0])
+        parts = [mine] + [swap(x, "col", col_size, 2 * n + 2) for n, x in enumerate(send)]
+        state = (eliminate_part(state, half, components, mine),)
+        new = update(state[0], parts)
+        new = stack([new] + swaps(new, "col", col_size, [2, 4]), new)
+        stacks = [new, swap(new, "col", col_size, 1)]
     else:
         state = (eliminate_part(state, 0, components, outs[0]),)
         summed = lax.psum_scatter(outs[0], "col", scatter_dimension=1, tiled=True)
-        new = update(state[0], [summed[None]])[0]
+        new = update(state[0], [summed])[0]
         stacks = [lax.all_gather(new, "col", axis=1, tiled=True)[None]]
-    part = second(me, stacks, offsets, z)
+    part = second(me, stacks, [0, 2, 4, 6, 1, 3, 5, 7], z)
     for bit in row_bits[:-1]:
         part = part + swap(part, BOTH, every, bit)
     got = swap(part, BOTH, every, row_bits[-1])
@@ -532,12 +563,9 @@
     if not direct:
         return (frames, lax.psum_scatter(outs[0], "col", scatter_dimension=1, tiled=True))
     keep, send = outs
-    got = swap(send, "col", col_size, 1)
-    keep, send = halve(me, keep, got, 1, keep)
-    got = swap(send, "col", col_size, 2)
-    keep, send = halve(me, keep, got, 2, keep)
-    got = swap(send, "col", col_size, 4)
-    return (frames, keep[0] + got[0].astype(F32))
+    mine, *send = deal(me, keep, swap(send, "col", col_size, 1), keep)
+    parts = [swap(x, "col", col_size, 2 * n + 2) for n, x in enumerate(send)]
+    return (frames, paired([mine] + [x.astype(F32) for x in parts]))
 
 
 def solution(mesh):

time: 109 us -> 102 us (0.936)
  waiting for transfers between devices: 42.9 us -> 27.9 us
  starting transfers between devices: 19 us -> 32.8 us
  local copies, waits for them, and re-layouts: 7.2 us -> 1.96 us
    ppermute x20 -> x27, waiting for transfers between devices: 42.9 us -> 27.9 us  [swap(): return lax.ppermute(x, axes, [(n, n ^ offset) for n in range(count)])]
    ppermute x20 -> x27, starting transfers between devices: 19 us -> 32.8 us  [swap(): return lax.ppermute(x, axes, [(n, n ^ offset) for n in range(count)])]
    unnamed x15 -> x4, local copies, waits for them, and re-layouts: 7.19 us -> 1.96 us
    pallas_call x33 -> x24, Pallas kernels: 37.5 us -> 37 us  [call(): pl.pallas_call(body, out_shape=outs, in_specs=ins, out_specs=(vmem(),) *...]
  transfers between devices with their start and end apart: 20 -> 27, of which waited for: 16 -> 14; matrix products, arithmetic and copies ran while one was open for 0% -> 0% of each run, Pallas kernels for 19% -> 19%
where the time goes in v1:
time: 102 us; the launch traced here: 101 us
  Pallas kernels  37 us (36%)
  starting transfers between devices  32.8 us (32%)
  waiting for transfers between devices  27.9 us (27%)
  local copies, waits for them, and re-layouts  1.96 us (2%)
    pallas_call x24, Pallas kernels, call(): pl.pallas_call(body, out_shape=outs, in_specs=ins, out_specs=(vmem(),) *...  37 us
    ppermute x27, starting transfers between devices, swap(): return lax.ppermute(x, axes, [(n, n ^ offset) for n in range(count)])  32.8 us
    ppermute x27, waiting for transfers between devices, swap(): return lax.ppermute(x, axes, [(n, n ^ offset) for n in range(count)])  27.9 us
  transfers between devices with their start and end apart: 27, of which 14 were waited for; matrix products, arithmetic and copies ran while one was open for 0% of the time, Pallas kernels for 19%

profile of v1, /device:TPU:0, one launch (start us, length us, event | category | flops | bytes accessed | tf_op | source)
XLA Modules:
  0.0 101.2 jit_solution(2973041947720619399)
XLA Ops:
  1.5 3.0 %collective-permute-start = (bf16[1,96,128]{2,1,0:T(8,128)(2,1)S(1)}, bf16[1,96,128]{2,1,0:T(8,128)(2,1)S(1)}, u32[]{:S(2)}, u32[]{:S(2)}) collective-permute-start(bf16[1,96,128]{2,1,0:T(8,128)(2,1)S(1)} %get-tuple-element.29.after_ref.refs_0_), channel_id=1, source_target_pairs={{0,1},{1,0},{2,3},{3,2},{4,5},{5,4},{6,7},{7,6},{8,9},{9,8},{10,11... | collective-permute-start | bytes 73736 | tf_op jit(solution)/shard_map/ppermute | solution.py:61
  4.5 3.6 %prepare.2 = (bf16[16,128,1024]{2,1,0:T(8,128)(2,1)S(1)}, f32[16,64,128]{2,1,0:T(8,128)S(1)}, f32[8,128]{1,0:T(8,128)S(1)}) custom-call(bf16[128,48,1024]{2,1,0:T(8,128)(2,1)} %t_ref.3, f32[64,128]{1,0:T(8,128)S(1)} %get-tuple-element.30.b_ref, bf16[1,96,128]{2,1,0:T(8,128)(2,1)S(1)} %get-tuple-element.29.after_ref.refs_0_), custom_call_target="tpu_custom_call" | custom-call | bytes 6000000 | tf_op jit(solution)/shard_map/prepare/pallas_call | solution.py:37
  8.0 2.0 %copy-done = bf16[16,128,1024]{2,1,0:T(8,128)(2,1)} copy-done((bf16[16,128,1024]{2,1,0:T(8,128)(2,1)}, bf16[16,128,1024]{2,1,0:T(8,128)(2,1)S(1)}, u32[]{:S(2)}) %copy-start) | copy-done | bytes 4194328
  10.0 3.7 %collective-permute-start.3 = (bf16[2,96,128]{2,1,0:T(8,128)(2,1)S(1)}, bf16[2,96,128]{2,1,0:T(8,128)(2,1)S(1)}, u32[]{:S(2)}, u32[]{:S(2)}) collective-permute-start(bf16[2,96,128]{2,1,0:T(8,128)(2,1)S(1)} %stack.2.after_ref.refs_0_), channel_id=1, source_target_pairs={{0,6},{1,7},{2,4},{3,5},{4,2},{5,3},{6,0},{7,1},{8,14},{9,15},{10,... | collective-permute-start | bytes 147464 | tf_op jit(solution)/shard_map/ppermute | solution.py:61
  14.5 5.0 %prepare.3 = (bf16[32,128,1024]{2,1,0:T(8,128)(2,1)S(1)}, f32[32,64,128]{2,1,0:T(8,128)S(1)}, f32[8,128]{1,0:T(8,128)S(1)}) custom-call(bf16[128,48,1024]{2,1,0:T(8,128)(2,1)} %t_ref.3, f32[64,128]{1,0:T(8,128)S(1)} %get-tuple-element.30.b_ref, bf16[2,96,128]{2,1,0:T(8,128)(2,1)S(1)} %stack.2.after_ref.refs_0_), custom_call_target="tpu_custom_call" | custom-call | bytes 12000000 | tf_op jit(solution)/shard_map/prepare/pallas_call | solution.py:37
  31.6 1.9 %eliminate.4.refs_4_.refs_0_ = f32[64,64]{1,0:T(8,128)S(1)} custom-call(f32[64,64]{1,0:T(8,128)S(1)} %add.25.refs_1_.refs_2_.refs_0_, f32[64,64]{1,0:T(8,128)S(1)} %get-tuple-element.38.refs_1_.refs_0_, f32[64,128]{1,0:T(8,128)S(1)} %add.26.refs_2_.refs_0_), custom_call_target="tpu_custom_call" | custom-call | bytes 3000000 | tf_op jit(solution)/shard_map/eliminate/pallas_call | solution.py:37
  35.1 3.7 %collective-permute-start.12 = (f32[64,128]{1,0:T(8,128)S(1)}, f32[64,128]{1,0:T(8,128)S(1)}, u32[]{:S(2)}, u32[]{:S(2)}) collective-permute-start(f32[64,128]{1,0:T(8,128)S(1)} %add.27.refs_1_.refs_0_), channel_id=1, source_target_pairs={{0,6},{1,7},{2,4},{3,5},{4,2},{5,3},{6,0},{7,1},{8,14},{9,15},{10,... | collective-permute-start | bytes 98312 | tf_op jit(solution)/shard_map/ppermute | solution.py:61
  39.5 1.9 %eliminate.5.refs_4_.inverse_ref = f32[64,64]{1,0:T(8,128)S(1)} custom-call(f32[64,64]{1,0:T(8,128)S(1)} %eliminate.4.refs_4_.refs_0_, f32[64,128]{1,0:T(8,128)S(1)} %add.27.refs_1_.refs_0_), custom_call_target="tpu_custom_call" | custom-call | bytes 3000000 | tf_op jit(solution)/shard_map/eliminate/pallas_call | solution.py:37
  41.4 2.1 %collective-permute-done.11.refs_2_ = f32[64,128]{1,0:T(8,128)S(1)} collective-permute-done((f32[64,128]{1,0:T(8,128)S(1)}, f32[64,128]{1,0:T(8,128)S(1)}, u32[]{:S(2)}, u32[]{:S(2)}) %collective-permute-start.11) | collective-permute-done | bytes 32800 | tf_op jit(solution)/shard_map/ppermute | solution.py:61
  43.6 8.0 %slab.1 = (f32[64,128]{1,0:T(8,128)}, f32[64,64]{1,0:T(8,128)S(1)}, f32[48,64,1024]{2,1,0:T(8,128)S(1)}, f32[4,64,128]{2,1,0:T(8,128)S(1)}, f32[4,64,128]{2,1,0:T(8,128)S(1)}) custom-call(s32[1]{0:T(128)} %bitcast.me_ref, f32[64,64]{1,0:T(8,128)S(1)} %eliminate.5.refs_4_.inverse_ref, f32[64,128]{1,0:T(8,128)S(1)} %add.28.summed_ref, ...), custom_call_target="tpu_custom_call" | custom-call | bytes 24000000 | tf_op jit(solution)/shard_map/slab/pallas_call | solution.py:37
  52.1 1.9 %eliminate.6.after_ref.refs_0_ = f32[64,64]{1,0:T(8,128)S(1)} custom-call(f32[64,64]{1,0:T(8,128)S(1)} %get-tuple-element.38.refs_1_.refs_0_, f32[64,64]{1,0:T(8,128)S(1)} %get-tuple-element.42.refs_1_.gram_frames_ref, f32[4,64,128]{2,1,0:T(8,128)S(1)} %get-tuple-element.43.refs_2_), custom_call_target="tpu_custom_call" | custom-call | bytes 3000000 | tf_op jit(solution)/shard_map/eliminate/pallas_call | solution.py:37
  54.0 2.5 %collective-permute-done.13.got_in = f32[4,64,128]{2,1,0:T(8,128)S(1)} collective-permute-done((f32[4,64,128]{2,1,0:T(8,128)S(1)}, f32[4,64,128]{2,1,0:T(8,128)S(1)}, u32[]{:S(2)}, u32[]{:S(2)}) %collective-permute-start.13) | collective-permute-done | bytes 131104 | tf_op jit(solution)/shard_map/ppermute | solution.py:61
  56.6 2.1 %collective-permute-start.15 = (f32[64,128]{1,0:T(8,128)S(1)}, f32[64,128]{1,0:T(8,128)S(1)}, u32[]{:S(2)}, u32[]{:S(2)}) collective-permute-start(f32[64,128]{1,0:T(8,128)S(1)} %get-tuple-element.47), channel_id=1, source_target_pairs={{0,4},{1,5},{2,6},{3,7},{4,0},{5,1},{6,2},{7,3},{8,12},{9,13},{10,... | collective-permute-start | bytes 98312 | tf_op jit(solution)/shard_map/ppermute | solution.py:61
  58.7 2.3 %collective-permute-start.16 = (f32[64,128]{1,0:T(8,128)S(1)}, f32[64,128]{1,0:T(8,128)S(1)}, u32[]{:S(2)}, u32[]{:S(2)}) collective-permute-start(f32[64,128]{1,0:T(8,128)S(1)} %get-tuple-element.48), channel_id=1, source_target_pairs={{0,6},{1,7},{2,4},{3,5},{4,2},{5,3},{6,0},{7,1},{8,14},{9,15},{10,... | collective-permute-start | bytes 98312 | tf_op jit(solution)/shard_map/ppermute | solution.py:61
  61.0 1.9 %eliminate.7.inverse_ref = f32[64,64]{1,0:T(8,128)S(1)} custom-call(f32[64,64]{1,0:T(8,128)S(1)} %eliminate.6.after_ref.refs_0_, f32[64,128]{1,0:T(8,128)S(1)} %get-tuple-element.45.refs_1_.refs_0_), custom_call_target="tpu_custom_call" | custom-call | bytes 3000000 | tf_op jit(solution)/shard_map/eliminate/pallas_call | solution.py:37
  62.9 1.8 %collective-permute-done.16.refs_3_ = f32[64,128]{1,0:T(8,128)S(1)} collective-permute-done((f32[64,128]{1,0:T(8,128)S(1)}, f32[64,128]{1,0:T(8,128)S(1)}, u32[]{:S(2)}, u32[]{:S(2)}) %collective-permute-start.16) | collective-permute-done | bytes 32800 | tf_op jit(solution)/shard_map/ppermute | solution.py:61
  64.9 2.1 %collective-permute-start.19 = (bf16[1,64,128]{2,1,0:T(8,128)(2,1)S(1)}, bf16[1,64,128]{2,1,0:T(8,128)(2,1)S(1)}, u32[]{:S(2)}, u32[]{:S(2)}) collective-permute-start(bf16[1,64,128]{2,1,0:T(8,128)(2,1)S(1)} %update.1.refs_0_.refs_4_), channel_id=1, source_target_pairs={{0,6},{1,7},{2,4},{3,5},{4,2},{5,3},{6,0},{7,1},{8,14},{9,15},{10,... | collective-permute-start | bytes 49160 | tf_op jit(solution)/shard_map/ppermute | solution.py:61
  67.0 2.3 %collective-permute-start.17 = (bf16[1,64,128]{2,1,0:T(8,128)(2,1)S(1)}, bf16[1,64,128]{2,1,0:T(8,128)(2,1)S(1)}, u32[]{:S(2)}, u32[]{:S(2)}) collective-permute-start(bf16[1,64,128]{2,1,0:T(8,128)(2,1)S(1)} %update.1.refs_0_.refs_4_), channel_id=1, source_target_pairs={{0,2},{1,3},{2,0},{3,1},{4,6},{5,7},{6,4},{7,5},{8,10},{9,11},{10,... | collective-permute-start | bytes 49160 | tf_op jit(solution)/shard_map/ppermute | solution.py:61
  72.2 3.7 %collective-permute-done.20.refs_1_ = bf16[4,64,128]{2,1,0:T(8,128)(2,1)S(1)} collective-permute-done((bf16[4,64,128]{2,1,0:T(8,128)(2,1)S(1)}, bf16[4,64,128]{2,1,0:T(8,128)(2,1)S(1)}, u32[]{:S(2)}, u32[]{:S(2)}) %collective-permute-start.20) | collective-permute-done | bytes 65568 | tf_op jit(solution)/shard_map/ppermute | solution.py:61
  79.5 3.4 %collective-permute-done.22.got_ref = f32[64,128]{1,0:T(8,128)S(1)} collective-permute-done((f32[64,128]{1,0:T(8,128)S(1)}, f32[64,128]{1,0:T(8,128)S(1)}, u32[]{:S(2)}, u32[]{:S(2)}) %collective-permute-start.22) | collective-permute-done | bytes 32800 | tf_op jit(solution)/shard_map/ppermute | solution.py:61
  82.9 5.4 %mode.1 = (f32[4,64,128]{2,1,0:T(8,128)S(1)}, bf16[4,64,128]{2,1,0:T(8,128)(2,1)S(1)}) custom-call(s32[1]{0:T(128)} %bitcast.me_ref, f32[64,128]{1,0:T(8,128)S(1)} %add.17.mine_ref, f32[64,128]{1,0:T(8,128)S(1)} %collective-permute-done.22.got_ref, f32[64,64]{1,0:T(8,128)S(1)} %get-tuple-element.42.refs_1_.gram_frames_ref, ...), custom_call_target="tpu_custom_call" | custom-call | bytes 15000000 | tf_op jit(solution)/shard_map/mode/pallas_call | solution.py:37
  88.8 3.7 %collective-permute-done.23.got_in = bf16[4,64,128]{2,1,0:T(8,128)(2,1)S(1)} collective-permute-done((bf16[4,64,128]{2,1,0:T(8,128)(2,1)S(1)}, bf16[4,64,128]{2,1,0:T(8,128)(2,1)S(1)}, u32[]{:S(2)}, u32[]{:S(2)}) %collective-permute-start.23) | collective-permute-done | bytes 65568 | tf_op jit(solution)/shard_map/ppermute | solution.py:61
  95.0 2.1 %collective-permute-start.26 = (bf16[64,128]{1,0:T(8,128)(2,1)S(1)}, bf16[64,128]{1,0:T(8,128)(2,1)S(1)}, u32[]{:S(2)}, u32[]{:S(2)}) collective-permute-start(bf16[64,128]{1,0:T(8,128)(2,1)S(1)} %get-tuple-element.55), channel_id=1, source_target_pairs={{0,6},{1,7},{2,4},{3,5},{4,2},{5,3},{6,0},{7,1},{8,14},{9,15},{10,... | collective-permute-start | bytes 49160 | tf_op jit(solution)/shard_map/ppermute | solution.py:61
  98.7 1.9 %collective-permute-done.26 = bf16[64,128]{1,0:T(8,128)(2,1)S(1)} collective-permute-done((bf16[64,128]{1,0:T(8,128)(2,1)S(1)}, bf16[64,128]{1,0:T(8,128)(2,1)S(1)}, u32[]{:S(2)}, u32[]{:S(2)}) %collective-permute-start.26) | collective-permute-done | bytes 16416 | tf_op jit(solution)/shard_map/ppermute | solution.py:61
  (60 shorter events, 28.5 us)
Async XLA Ops:
  1.5 8.5 %collective-permute-start = (bf16[1,96,128]{2,1,0:T(8,128)(2,1)S(1)}, bf16[1,96,128]{2,1,0:T(8,128)(2,1)S(1)}, u32[]{:S(2)}, u32[]{:S(2)}) collective-permute-start(bf16[1,96,128]{2,1,0:T(8,128)(2,1)S(1)} %get-tuple-element.29.after_ref.refs_0_), channel_id=1, source_target_pairs={{0,1},{1,0},{2,3},{3,2},{4,5},{5,4},{6,7},{7,6},{8,9},{9,8},{10,11... | collective-permute-start | bytes 73736 | tf_op jit(solution)/shard_map/ppermute | solution.py:61
  10.0 9.4 %collective-permute-start.3 = (bf16[2,96,128]{2,1,0:T(8,128)(2,1)S(1)}, bf16[2,96,128]{2,1,0:T(8,128)(2,1)S(1)}, u32[]{:S(2)}, u32[]{:S(2)}) collective-permute-start(bf16[2,96,128]{2,1,0:T(8,128)(2,1)S(1)} %stack.2.after_ref.refs_0_), channel_id=1, source_target_pairs={{0,6},{1,7},{2,4},{3,5},{4,2},{5,3},{6,0},{7,1},{8,14},{9,15},{10,... | collective-permute-start | bytes 147464 | tf_op jit(solution)/shard_map/ppermute | solution.py:61
  13.7 5.8 %collective-permute-start.2 = (bf16[2,96,128]{2,1,0:T(8,128)(2,1)S(1)}, bf16[2,96,128]{2,1,0:T(8,128)(2,1)S(1)}, u32[]{:S(2)}, u32[]{:S(2)}) collective-permute-start(bf16[2,96,128]{2,1,0:T(8,128)(2,1)S(1)} %stack.2.after_ref.refs_0_), channel_id=1, source_target_pairs={{0,4},{1,5},{2,6},{3,7},{4,0},{5,1},{6,2},{7,3},{8,12},{9,13},{10,... | collective-permute-start | bytes 147464 | tf_op jit(solution)/shard_map/ppermute | solution.py:61
  13.7 5.8 %collective-permute-start.1 = (bf16[2,96,128]{2,1,0:T(8,128)(2,1)S(1)}, bf16[2,96,128]{2,1,0:T(8,128)(2,1)S(1)}, u32[]{:S(2)}, u32[]{:S(2)}) collective-permute-start(bf16[2,96,128]{2,1,0:T(8,128)(2,1)S(1)} %stack.2.after_ref.refs_0_), channel_id=1, source_target_pairs={{0,2},{1,3},{2,0},{3,1},{4,6},{5,7},{6,4},{7,5},{8,10},{9,11},{10,... | collective-permute-start | bytes 147464 | tf_op jit(solution)/shard_map/ppermute | solution.py:61
  21.4 4.0 %collective-permute-start.5 = (f32[64,64]{1,0:T(8,128)S(1)}, f32[64,64]{1,0:T(8,128)S(1)}, u32[]{:S(2)}, u32[]{:S(2)}) collective-permute-start(f32[64,64]{1,0:T(8,128)S(1)} %add.24.refs_1_.refs_0_), channel_id=1, source_target_pairs={{0,16},{1,17},{2,18},{3,19},{4,20},{5,21},{6,22},{7,23},{8,24},{9,... | collective-permute-start | bytes 49160 | tf_op jit(solution)/shard_map/ppermute | solution.py:61
  28.2 5.4 %collective-permute-start.9 = (f32[64,128]{1,0:T(8,128)S(1)}, f32[64,128]{1,0:T(8,128)S(1)}, u32[]{:S(2)}, u32[]{:S(2)}) collective-permute-start(f32[64,128]{1,0:T(8,128)S(1)} %add.26.refs_2_.refs_0_), channel_id=1, source_target_pairs={{0,17},{1,16},{2,19},{3,18},{4,21},{5,20},{6,23},{7,22},{8,25},{9,... | collective-permute-start | bytes 98312 | tf_op jit(solution)/shard_map/ppermute | solution.py:61
  29.7 3.9 %collective-permute-start.8 = (f32[64,128]{1,0:T(8,128)S(1)}, f32[64,128]{1,0:T(8,128)S(1)}, u32[]{:S(2)}, u32[]{:S(2)}) collective-permute-start(f32[64,128]{1,0:T(8,128)S(1)} %add.26.refs_2_.refs_0_), channel_id=1, source_target_pairs={{0,1},{1,0},{2,3},{3,2},{4,5},{5,4},{6,7},{7,6},{8,9},{9,8},{10,11... | collective-permute-start | bytes 98312 | tf_op jit(solution)/shard_map/ppermute | solution.py:61
  31.1 3.9 %collective-permute-start.7 = (f32[64,128]{1,0:T(8,128)S(1)}, f32[64,128]{1,0:T(8,128)S(1)}, u32[]{:S(2)}, u32[]{:S(2)}) collective-permute-start(f32[64,128]{1,0:T(8,128)S(1)} %add.26.refs_2_.refs_0_), channel_id=1, source_target_pairs={{0,16},{1,17},{2,18},{3,19},{4,20},{5,21},{6,22},{7,23},{8,24},{9,... | collective-permute-start | bytes 98312 | tf_op jit(solution)/shard_map/ppermute | solution.py:61
  35.1 6.4 %collective-permute-start.12 = (f32[64,128]{1,0:T(8,128)S(1)}, f32[64,128]{1,0:T(8,128)S(1)}, u32[]{:S(2)}, u32[]{:S(2)}) collective-permute-start(f32[64,128]{1,0:T(8,128)S(1)} %add.27.refs_1_.refs_0_), channel_id=1, source_target_pairs={{0,6},{1,7},{2,4},{3,5},{4,2},{5,3},{6,0},{7,1},{8,14},{9,15},{10,... | collective-permute-start | bytes 98312 | tf_op jit(solution)/shard_map/ppermute | solution.py:61
  38.7 4.8 %collective-permute-start.11 = (f32[64,128]{1,0:T(8,128)S(1)}, f32[64,128]{1,0:T(8,128)S(1)}, u32[]{:S(2)}, u32[]{:S(2)}) collective-permute-start(f32[64,128]{1,0:T(8,128)S(1)} %add.27.refs_1_.refs_0_), channel_id=1, source_target_pairs={{0,4},{1,5},{2,6},{3,7},{4,0},{5,1},{6,2},{7,3},{8,12},{9,13},{10,... | collective-permute-start | bytes 98312 | tf_op jit(solution)/shard_map/ppermute | solution.py:61
  38.7 4.8 %collective-permute-start.10 = (f32[64,128]{1,0:T(8,128)S(1)}, f32[64,128]{1,0:T(8,128)S(1)}, u32[]{:S(2)}, u32[]{:S(2)}) collective-permute-start(f32[64,128]{1,0:T(8,128)S(1)} %add.27.refs_1_.refs_0_), channel_id=1, source_target_pairs={{0,2},{1,3},{2,0},{3,1},{4,6},{5,7},{6,4},{7,5},{8,10},{9,11},{10,... | collective-permute-start | bytes 98312 | tf_op jit(solution)/shard_map/ppermute | solution.py:61
  51.5 5.0 %collective-permute-start.13 = (f32[4,64,128]{2,1,0:T(8,128)S(1)}, f32[4,64,128]{2,1,0:T(8,128)S(1)}, u32[]{:S(2)}, u32[]{:S(2)}) collective-permute-start(f32[4,64,128]{2,1,0:T(8,128)S(1)} %get-tuple-element.43.refs_2_), channel_id=1, source_target_pairs={{0,1},{1,0},{2,3},{3,2},{4,5},{5,4},{6,7},{7,6},{8,9},{9,8},{10,11... | collective-permute-start | bytes 393224 | tf_op jit(solution)/shard_map/ppermute | solution.py:61
  56.5 6.4 %collective-permute-start.14 = (f32[64,128]{1,0:T(8,128)S(1)}, f32[64,128]{1,0:T(8,128)S(1)}, u32[]{:S(2)}, u32[]{:S(2)}) collective-permute-start(f32[64,128]{1,0:T(8,128)S(1)} %get-tuple-element.46), channel_id=1, source_target_pairs={{0,2},{1,3},{2,0},{3,1},{4,6},{5,7},{6,4},{7,5},{8,10},{9,11},{10,... | collective-permute-start | bytes 98312 | tf_op jit(solution)/shard_map/ppermute | solution.py:61
  56.6 6.3 %collective-permute-start.15 = (f32[64,128]{1,0:T(8,128)S(1)}, f32[64,128]{1,0:T(8,128)S(1)}, u32[]{:S(2)}, u32[]{:S(2)}) collective-permute-start(f32[64,128]{1,0:T(8,128)S(1)} %get-tuple-element.47), channel_id=1, source_target_pairs={{0,4},{1,5},{2,6},{3,7},{4,0},{5,1},{6,2},{7,3},{8,12},{9,13},{10,... | collective-permute-start | bytes 98312 | tf_op jit(solution)/shard_map/ppermute | solution.py:61
  58.7 6.0 %collective-permute-start.16 = (f32[64,128]{1,0:T(8,128)S(1)}, f32[64,128]{1,0:T(8,128)S(1)}, u32[]{:S(2)}, u32[]{:S(2)}) collective-permute-start(f32[64,128]{1,0:T(8,128)S(1)} %get-tuple-element.48), channel_id=1, source_target_pairs={{0,6},{1,7},{2,4},{3,5},{4,2},{5,3},{6,0},{7,1},{8,14},{9,15},{10,... | collective-permute-start | bytes 98312 | tf_op jit(solution)/shard_map/ppermute | solution.py:61
  64.9 5.6 %collective-permute-start.19 = (bf16[1,64,128]{2,1,0:T(8,128)(2,1)S(1)}, bf16[1,64,128]{2,1,0:T(8,128)(2,1)S(1)}, u32[]{:S(2)}, u32[]{:S(2)}) collective-permute-start(bf16[1,64,128]{2,1,0:T(8,128)(2,1)S(1)} %update.1.refs_0_.refs_4_), channel_id=1, source_target_pairs={{0,6},{1,7},{2,4},{3,5},{4,2},{5,3},{6,0},{7,1},{8,14},{9,15},{10,... | collective-permute-start | bytes 49160 | tf_op jit(solution)/shard_map/ppermute | solution.py:61
  67.0 4.6 %collective-permute-start.18 = (bf16[1,64,128]{2,1,0:T(8,128)(2,1)S(1)}, bf16[1,64,128]{2,1,0:T(8,128)(2,1)S(1)}, u32[]{:S(2)}, u32[]{:S(2)}) collective-permute-start(bf16[1,64,128]{2,1,0:T(8,128)(2,1)S(1)} %update.1.refs_0_.refs_4_), channel_id=1, source_target_pairs={{0,4},{1,5},{2,6},{3,7},{4,0},{5,1},{6,2},{7,3},{8,12},{9,13},{10,... | collective-permute-start | bytes 49160 | tf_op jit(solution)/shard_map/ppermute | solution.py:61
  67.0 4.6 %collective-permute-start.17 = (bf16[1,64,128]{2,1,0:T(8,128)(2,1)S(1)}, bf16[1,64,128]{2,1,0:T(8,128)(2,1)S(1)}, u32[]{:S(2)}, u32[]{:S(2)}) collective-permute-start(bf16[1,64,128]{2,1,0:T(8,128)(2,1)S(1)} %update.1.refs_0_.refs_4_), channel_id=1, source_target_pairs={{0,2},{1,3},{2,0},{3,1},{4,6},{5,7},{6,4},{7,5},{8,10},{9,11},{10,... | collective-permute-start | bytes 49160 | tf_op jit(solution)/shard_map/ppermute | solution.py:61
  71.6 4.3 %collective-permute-start.20 = (bf16[4,64,128]{2,1,0:T(8,128)(2,1)S(1)}, bf16[4,64,128]{2,1,0:T(8,128)(2,1)S(1)}, u32[]{:S(2)}, u32[]{:S(2)}) collective-permute-start(bf16[4,64,128]{2,1,0:T(8,128)(2,1)S(1)} %stack.3.refs_0_), channel_id=1, source_target_pairs={{0,1},{1,0},{2,3},{3,2},{4,5},{5,4},{6,7},{7,6},{8,9},{9,8},{10,11... | collective-permute-start | bytes 196616 | tf_op jit(solution)/shard_map/ppermute | solution.py:61
  79.0 3.9 %collective-permute-start.22 = (f32[64,128]{1,0:T(8,128)S(1)}, f32[64,128]{1,0:T(8,128)S(1)}, u32[]{:S(2)}, u32[]{:S(2)}) collective-permute-start(f32[64,128]{1,0:T(8,128)S(1)} %add.17.mine_ref), channel_id=1, source_target_pairs={{0,16},{1,17},{2,18},{3,19},{4,20},{5,21},{6,22},{7,23},{8,24},{9,... | collective-permute-start | bytes 98312 | tf_op jit(solution)/shard_map/ppermute | solution.py:61
  88.2 4.3 %collective-permute-start.23 = (bf16[4,64,128]{2,1,0:T(8,128)(2,1)S(1)}, bf16[4,64,128]{2,1,0:T(8,128)(2,1)S(1)}, u32[]{:S(2)}, u32[]{:S(2)}) collective-permute-start(bf16[4,64,128]{2,1,0:T(8,128)(2,1)S(1)} %get-tuple-element.51), channel_id=1, source_target_pairs={{0,1},{1,0},{2,3},{3,2},{4,5},{5,4},{6,7},{7,6},{8,9},{9,8},{10,11... | collective-permute-start | bytes 196616 | tf_op jit(solution)/shard_map/ppermute | solution.py:61
  92.6 4.5 %collective-permute-start.24 = (bf16[64,128]{1,0:T(8,128)(2,1)S(1)}, bf16[64,128]{1,0:T(8,128)(2,1)S(1)}, u32[]{:S(2)}, u32[]{:S(2)}) collective-permute-start(bf16[64,128]{1,0:T(8,128)(2,1)S(1)} %get-tuple-element.53), channel_id=1, source_target_pairs={{0,2},{1,3},{2,0},{3,1},{4,6},{5,7},{6,4},{7,5},{8,10},{9,11},{10,... | collective-permute-start | bytes 49160 | tf_op jit(solution)/shard_map/ppermute | solution.py:61
  94.0 4.6 %collective-permute-start.25 = (bf16[64,128]{1,0:T(8,128)(2,1)S(1)}, bf16[64,128]{1,0:T(8,128)(2,1)S(1)}, u32[]{:S(2)}, u32[]{:S(2)}) collective-permute-start(bf16[64,128]{1,0:T(8,128)(2,1)S(1)} %get-tuple-element.54), channel_id=1, source_target_pairs={{0,4},{1,5},{2,6},{3,7},{4,0},{5,1},{6,2},{7,3},{8,12},{9,13},{10,... | collective-permute-start | bytes 49160 | tf_op jit(solution)/shard_map/ppermute | solution.py:61
  95.0 5.5 %collective-permute-start.26 = (bf16[64,128]{1,0:T(8,128)(2,1)S(1)}, bf16[64,128]{1,0:T(8,128)(2,1)S(1)}, u32[]{:S(2)}, u32[]{:S(2)}) collective-permute-start(bf16[64,128]{1,0:T(8,128)(2,1)S(1)} %get-tuple-element.55), channel_id=1, source_target_pairs={{0,6},{1,7},{2,4},{3,5},{4,2},{5,3},{6,0},{7,1},{8,14},{9,15},{10,... | collective-permute-start | bytes 49160 | tf_op jit(solution)/shard_map/ppermute | solution.py:61
  (5 other events, 11.5 us)

commit v2 on v1

--- a/solution.py
+++ b/solution.py
@@ -61,7 +61,8 @@
     return lax.ppermute(x, axes, [(n, n ^ offset) for n in range(count)])
 
 
-def join_body(a_hbm, b_hbm, out_ref, turned_ref, second_ref, a_ref, b_ref, sems):
+def join_body(me_ref, a_hbm, b_hbm, out_ref, turned_ref, second_ref, a_ref, b_ref, sems):
+    del me_ref
     moves = [pltpu.make_async_copy(*pair, sems.at[n]) for n, pair in enumerate(((a_hbm, a_ref), (b_hbm, b_ref)))]
     for move in moves:
         move.start()
@@ -79,7 +80,7 @@
     out_ref[0, components:, :] = pair.astype(BF16)
 
 
-def join(first, second_turned):
+def join(me, first, second_turned):
     components, width = first.shape
     cols = second_turned.shape[0]
     height = components + cols // 2 + (-(cols // 2) % 16)
@@ -88,8 +89,8 @@
     return call(
         join_body,
         (shaped((1, height, width), BF16), shaped((cols, components)), shaped((components, 128))),
-        [anywhere()] * 2,
-        (first, second_turned),
+        [smem()] + [anywhere()] * 2,
+        (me, first, second_turned),
         "join",
         [VM(first.shape, BF16), VM(second_turned.shape, BF16), pltpu.SemaphoreType.DMA((2,))],
     )
@@ -125,6 +126,18 @@
 def add(parts, after):
     specs = [vmem()] * len(parts) + [anywhere()]
     return call(add_body, shaped(parts[0].shape), specs, (*parts, after), "add", us=0.2)
+
+
+def split_body(a_ref, b_ref, sum_ref, gram_ref):
+    components = sum_ref.shape[0]
+    sum_ref[...] = a_ref[:components] + b_ref[:components]
+    gram_ref[...] = a_ref[components:, :components] + b_ref[components:, :components]
+
+
+def split_add(a, b):
+    half = a.shape[0] // 2
+    outs = (shaped((half, a.shape[1])), shaped((half, half)))
+    return call(split_body, outs, [vmem()] * 2, (a, b), "split_add", us=0.2)
 
 
 def prepare_body(at, t_ref, b_ref, after_ref, out_ref, wide_ref, token_ref, slab, sems):
@@ -210,36 +223,38 @@
     )
 
 
-def project_body(at, base, cols, last, span, turned_ref, second_ref, t_ref, *refs):
-    *sums, after_ref, out_ref = refs
-    del after_ref
+def project_body(span, turned_ref, second_ref, gram_ref, *refs):
+    *t_refs, out_ref = refs
     components = turned_ref.shape[1]
-    _, frames, rows = t_ref.shape
     weights = turned_ref[...]
-
-    def step(n, total):
-        block = t_ref[pl.ds(base + n * span, span)].reshape(span * frames, rows)
-        product = dot(block, weights, ((1,), (0,))).reshape(span, frames, components)
-        scale = second_ref[pl.ds(pl.multiple_of(at + base + n * span, span), span), :]
-        for s in range(span):
-            total = total + product[s] * scale[s : s + 1, :]
-        return total
-
-    start = sums[0][...] if sums else jnp.zeros((frames, components), F32)
-    total = lax.fori_loop(0, cols // span, step, start)
-    out_ref[...] = total.T if last else total
-
-
-def project(turned, second_turned, t, at, base, cols, sums, after, last):
-    components, frames = turned.shape[1], t.shape[1]
-    shape = (components, frames) if last else (frames, components)
-    return call(
-        functools.partial(project_body, at, base, cols, last, 8),
-        shaped(shape),
-        [vmem()] * (3 + len(sums)) + [anywhere()],
-        (turned, second_turned, t, *sums, after),
+    total, at = 0.0, 0
+    for t_ref in t_refs:
+        cols, frames, rows = t_ref.shape
+
+        def step(n, total, t_ref=t_ref, at=at):
+            block = t_ref[pl.ds(n * span, span)].reshape(span * frames, rows)
+            product = dot(block, weights, ((1,), (0,))).reshape(span, frames, components)
+            scale = second_ref[pl.ds(pl.multiple_of(at + n * span, span), span), :]
+            for s in range(span):
+                total = total + product[s] * scale[s : s + 1, :]
+            return total
+
+        total = lax.fori_loop(0, cols // span, step, total + jnp.zeros((frames, components), F32))
+        at += cols
+    out_ref[:components] = total.T
+    gram = gram_ref[...]
+    out_ref[components:] = jnp.concatenate([gram, gram], axis=1)
+
+
+def project(first_turned, second_turned, gram, turned):
+    components, frames = first_turned.shape[1], turned[0].shape[1]
+    return call(
+        functools.partial(project_body, 8),
+        shaped((2 * components, frames)),
+        [vmem()] * (3 + len(turned)),
+        (first_turned, second_turned, gram, *turned),
         "project",
-        us=cols / 10,
+        us=5,
     )
 
 
@@ -298,6 +313,27 @@
         send_ref[n] = send.astype(send_ref.dtype)
 
 
+def halve_body(shift, me_ref, keep_in, got_in, after_ref, keep_ref, send_ref):
+    del after_ref
+    bit = (me_ref[0] >> shift) & 1
+    for n in range(keep_ref.shape[0]):
+        mine, other = 2 * n + bit, 2 * n + 1 - bit
+        keep_ref[n] = keep_in[mine] + got_in[mine].astype(F32)
+        send_ref[n] = (keep_in[other] + got_in[other].astype(F32)).astype(send_ref.dtype)
+
+
+def halve(me, keep, got, shift, after):
+    shape = (keep.shape[0] // 2,) + keep.shape[1:]
+    return call(
+        functools.partial(halve_body, shift),
+        (shaped(shape), shaped(shape, got.dtype)),
+        [smem(), vmem(), vmem(), anywhere()],
+        (me, keep, got, after),
+        "halve",
+        us=0.2,
+    )
+
+
 def deal_body(me_ref, keep_in, got_in, after_ref, mine_ref, *outs):
     del after_ref
     upper = me_ref[0] >> 1
@@ -335,8 +371,11 @@
     gram_ref[...] = dot(frames, frames, ((1,), (1,)), HIGH)
     high = frames.astype(BF16)
     low = (frames - high.astype(F32)).astype(BF16)
-    both = jnp.concatenate([high, low], axis=0)
-    wide = 256
+    none = jnp.zeros_like(high)
+    both = jnp.concatenate(
+        [jnp.concatenate(pair, axis=1) for pair in ((high, none), (none, high), (low, none), (none, low))], axis=0
+    )
+    frames_count, wide = frames.shape[1], 256
 
     def chunk(c, _):
         lanes = pl.ds(pl.multiple_of(c * wide, wide), wide)
@@ -345,13 +384,16 @@
         for t_ref, wide_ref in zip(t_refs, wide_refs):
 
             def step(n, total, t_ref=t_ref, wide_ref=wide_ref, base=base):
-                for s in range(8):
-                    j = n * 8 + s
-                    product = dot(both, t_ref[j, :, lanes], ((1,), (0,)))
-                    z = product[:components] + product[components:]
-                    z_ref[base + j, :, lanes] = z
-                    scale = wide_ref[j]
-                    total = total + z * jnp.concatenate([scale, scale], axis=1)
+                for s in range(0, 8, 2):
+                    block = t_ref[pl.ds(n * 8 + s, 2), :, lanes].reshape(2 * frames_count, wide)
+                    product = dot(both, block, ((1,), (0,)))
+                    product = product[: 2 * components] + product[2 * components :]
+                    for h in range(2):
+                        j = n * 8 + s + h
+                        z = product[h * components : h * components + components]
+                        z_ref[base + j, :, lanes] = z
+                        scale = wide_ref[j]
+                        total = total + z * jnp.concatenate([scale, scale], axis=1)
                 return total
 
             total = lax.fori_loop(0, t_ref.shape[0] // 8, step, total)
@@ -388,14 +430,15 @@
 
 def update_body(inverse_ref, *refs):
     *parts, out_ref = refs
-    summed = paired([p[...] for p in parts])
-    out_ref[0] = dot(inverse_ref[...], summed, ((1,), (0,)), HIGH).astype(BF16)
+    for n in range(out_ref.shape[0]):
+        summed = paired([p[n] for p in parts])
+        out_ref[n] = dot(inverse_ref[...], summed, ((1,), (0,)), HIGH).astype(BF16)
 
 
 def update(inverse_now, parts):
     return call(
         update_body,
-        shaped((1,) + parts[0].shape, BF16),
+        shaped(parts[0].shape, BF16),
         [vmem()] * (1 + len(parts)),
         (inverse_now, *parts),
         "update",
@@ -406,7 +449,7 @@
     *stacks, z_ref, out_ref, full_ref = refs
     cols, components, rows = z_ref.shape
     blocks = [s[n] for s in stacks for n in range(s.shape[0])]
-    place(me_ref[0], list(zip(offsets, blocks)), blocks[0].shape[1], full_ref)
+    place(me_ref[0] & 3, list(zip(offsets, blocks)), blocks[0].shape[1], full_ref)
     lane = lax.broadcasted_iota(jnp.int32, (8, 128), 1)
 
     def step(n, _):
@@ -488,22 +531,21 @@
     col_bits = [1 << b for b in range(col_size.bit_length() - 1)]
     row_bits = [col_size << b for b in range(row_size.bit_length() - 1)]
     tensor = pltpu.with_memory_space_constraint(tensor, pltpu.HBM)
-    cuts = [(0, GROUP), (GROUP, col_count - GROUP)]
-
-    turned, wides, gathered = [], [], []
+    cuts = [(0, GROUP), (GROUP, GROUP), (2 * GROUP, col_count - 2 * GROUP)]
+
+    turned, wides = [], []
+    order = [0, 4, 2, 6, 1, 5, 3, 7]
     if direct:
-        have, second_turned, second_values = join(first_factor, second_factor.T)
-        token = have
-        for at, cols in cuts:
-            bits = [2, 4] if gathered else [1]
-            gathered = [have] + swaps(have, "col", col_size, bits)
+        have, second_turned, second_values = join(me, first_factor, second_factor.T)
+        for bit, (at, cols) in zip((4, 2, 1), cuts):
+            got = swap(have, "col", col_size, bit)
             t, w, token = prepare(tensor, second_values, at, cols, have)
             turned.append(t)
             wides.append(w)
-            if len(turned) == 1:
-                have = stack(gathered, token)
+            if bit > 1:
+                have = stack([have, got], token)
         first_turned, gram_first, gram_second = assemble_first(
-            me, gathered, token, list(range(col_size)), components, row_count
+            me, [have, got], token, order, components, row_count
         )
     else:
         second_turned = second_factor.T.astype(F32)
@@ -518,46 +560,41 @@
         gram_first = jnp.dot(full, full.T, preferred_element_type=F32)
         gram_second = jnp.dot(others, others.T, preferred_element_type=F32)
 
-    pieces = [(t, at, base) for (at, cols), t in zip(cuts, turned) for base in range(0, cols, GROUP)]
-    sums = []
-    for n, (t, at, base) in enumerate(pieces):
-        got = [swap(gram_first, BOTH, every, bit) for bit in row_bits[n : n + 1]]
-        last = n == len(pieces) - 1
-        sums = [project(first_turned, second_turned, t, at, base, GROUP, sums, gram_first, last)]
-        if got:
-            gram_first = add([gram_first, *got], sums[0])
-    total = sums[0]
-
+    total = project(first_turned, second_turned, gram_first, turned)
+    for bit in row_bits[:-1]:
+        total = add([total, swap(total, BOTH, every, bit)], total)
+    total, gram_first = split_add(total, swap(total, BOTH, every, row_bits[-1]))
     state = (gram_first, gram_second)
-    half = components // 2
-    bits = row_bits[1:] + col_bits
-    stages = [row_bits[:1]] + [bits[n : n + 2] for n in range(0, len(bits), 2)]
-    for n, pair in enumerate(stages):
-        got = swaps(total, BOTH, every, pair)
-        if n in (1, 2):
-            state = (eliminate_part(state, (n - 1) * half, n * half, total),)
-        total = add([total, *got], state[0])
+    marks = [0, 24, 44, components]
+    for n, bit in enumerate(col_bits):
+        got = swap(total, BOTH, every, bit)
+        if n < 3:
+            state = (eliminate_part(state, marks[n], marks[n + 1], total),)
+        total = add([total, got], state[0])
     frames, gram_frames, z, *outs = slab(me, state[0], total, turned, wides, width, direct)
 
     state = (gram_second, gram_frames)
     if direct:
         keep, send = outs
         got = swap(send, "col", col_size, 1)
-        state = (eliminate_part(state, 0, half, send),)
-        mine, *send = deal(me, keep, got, state[0])
-        parts = [mine] + [swap(x, "col", col_size, 2 * n + 2) for n, x in enumerate(send)]
-        state = (eliminate_part(state, half, components, mine),)
-        new = update(state[0], parts)
-        new = stack([new] + swaps(new, "col", col_size, [2, 4]), new)
+        state = (eliminate_part(state, *marks[0:2], send),)
+        keep, send = halve(me, keep, got, 1, state[0])
+        got = swap(send, "col", col_size, 2)
+        state = (eliminate_part(state, *marks[1:3], send),)
+        keep = add([keep, got], state[0])
+        got = swap(keep, "col", col_size, 4)
+        state = (eliminate_part(state, *marks[2:4], keep),)
+        new = update(state[0], [keep, got])
+        new = stack([new, swap(new, "col", col_size, 2)], new)
         stacks = [new, swap(new, "col", col_size, 1)]
     else:
         state = (eliminate_part(state, 0, components, outs[0]),)
         summed = lax.psum_scatter(outs[0], "col", scatter_dimension=1, tiled=True)
-        new = update(state[0], [summed])[0]
+        new = update(state[0], [summed[None]])[0]
         stacks = [lax.all_gather(new, "col", axis=1, tiled=True)[None]]
-    part = second(me, stacks, [0, 2, 4, 6, 1, 3, 5, 7], z)
+    part = second(me, stacks, order, z)
     for bit in row_bits[:-1]:
-        part = part + swap(part, BOTH, every, bit)
+        part = add([part, swap(part, BOTH, every, bit)], part)
     got = swap(part, BOTH, every, row_bits[-1])
     outs = mode(me, part, got, gram_frames, z, width, direct)
     if not direct:

time: 102 us -> 99.2 us (0.973)
  starting transfers between devices: 32.8 us -> 22.8 us
  waiting for transfers between devices: 27.9 us -> 35.2 us
  Pallas kernels: 37 us -> 39.4 us
  local copies, waits for them, and re-layouts: 1.96 us -> 0 us
    ppermute x27 -> x19, starting transfers between devices: 32.8 us -> 22.8 us  [swap(): return lax.ppermute(x, axes, [(n, n ^ offset) for n in range(count)])]
    ppermute x27 -> x19, waiting for transfers between devices: 27.9 us -> 35.2 us  [swap(): return lax.ppermute(x, axes, [(n, n ^ offset) for n in range(count)])]
    pallas_call x24 -> x28, Pallas kernels: 37 us -> 39.4 us  [call(): pl.pallas_call(body, out_shape=outs, in_specs=ins, out_specs=(vmem(),) *...]
    unnamed x4 -> x0, local copies, waits for them, and re-layouts: 1.96 us -> none
  transfers between devices with their start and end apart: 27 -> 19, of which waited for: 14 -> 15; matrix products, arithmetic and copies ran while one was open for 0% -> 0% of each run, Pallas kernels for 19% -> 18%
where the time goes in v2:
time: 99.2 us; the launch traced here: 98.8 us
  Pallas kernels  39.4 us (40%)
  waiting for transfers between devices  35.2 us (35%)
  starting transfers between devices  22.8 us (23%)
    pallas_call x28, Pallas kernels, call(): pl.pallas_call(body, out_shape=outs, in_specs=ins, out_specs=(vmem(),) *...  39.4 us
    ppermute x19, waiting for transfers between devices, swap(): return lax.ppermute(x, axes, [(n, n ^ offset) for n in range(count)])  35.2 us
    ppermute x19, starting transfers between devices, swap(): return lax.ppermute(x, axes, [(n, n ^ offset) for n in range(count)])  22.8 us
  transfers between devices with their start and end apart: 19, of which 15 were waited for; matrix products, arithmetic and copies ran while one was open for 0% of the time, Pallas kernels for 18%

profile of v2, /device:TPU:0, one launch (start us, length us, event | category | flops | bytes accessed | tf_op | source)
XLA Modules:
  0.0 98.8 jit_solution(16293406812212417428)
XLA Ops:
  1.5 4.1 %collective-permute-start = (bf16[1,96,128]{2,1,0:T(8,128)(2,1)S(1)}, bf16[1,96,128]{2,1,0:T(8,128)(2,1)S(1)}, u32[]{:S(2)}, u32[]{:S(2)}) collective-permute-start(bf16[1,96,128]{2,1,0:T(8,128)(2,1)S(1)} %get-tuple-element.32.after_ref.refs_0_), channel_id=1, source_target_pairs={{0,4},{1,5},{2,6},{3,7},{4,0},{5,1},{6,2},{7,3},{8,12},{9,13},{10,... | collective-permute-start | bytes 73736 | tf_op jit(solution)/shard_map/ppermute | solution.py:61
  5.6 3.6 %prepare.3 = (bf16[16,128,1024]{2,1,0:T(8,128)(2,1)S(1)}, f32[16,64,128]{2,1,0:T(8,128)S(1)}, f32[8,128]{1,0:T(8,128)S(1)}) custom-call(bf16[128,48,1024]{2,1,0:T(8,128)(2,1)} %t_ref.5, f32[64,128]{1,0:T(8,128)S(1)} %get-tuple-element.33.b_ref, bf16[1,96,128]{2,1,0:T(8,128)(2,1)S(1)} %get-tuple-element.32.after_ref.refs_0_), custom_call_target="tpu_custom_call" | custom-call | bytes 6000000 | tf_op jit(solution)/shard_map/prepare/pallas_call | solution.py:37
  9.2 1.6 %collective-permute-start.1 = (bf16[2,96,128]{2,1,0:T(8,128)(2,1)S(1)}, bf16[2,96,128]{2,1,0:T(8,128)(2,1)S(1)}, u32[]{:S(2)}, u32[]{:S(2)}) collective-permute-start(bf16[2,96,128]{2,1,0:T(8,128)(2,1)S(1)} %stack.3.after_ref.refs_0_), channel_id=1, source_target_pairs={{0,2},{1,3},{2,0},{3,1},{4,6},{5,7},{6,4},{7,5},{8,10},{9,11},{10,... | collective-permute-start | bytes 147464 | tf_op jit(solution)/shard_map/ppermute | solution.py:61
  10.8 3.6 %prepare.4 = (bf16[16,128,1024]{2,1,0:T(8,128)(2,1)S(1)}, f32[16,64,128]{2,1,0:T(8,128)S(1)}, f32[8,128]{1,0:T(8,128)S(1)}) custom-call(bf16[128,48,1024]{2,1,0:T(8,128)(2,1)} %t_ref.5, f32[64,128]{1,0:T(8,128)S(1)} %get-tuple-element.33.b_ref, bf16[2,96,128]{2,1,0:T(8,128)(2,1)S(1)} %stack.3.after_ref.refs_0_), custom_call_target="tpu_custom_call" | custom-call | bytes 6000000 | tf_op jit(solution)/shard_map/prepare/pallas_call | solution.py:37
  14.4 1.6 %collective-permute-start.2 = (bf16[4,96,128]{2,1,0:T(8,128)(2,1)S(1)}, bf16[4,96,128]{2,1,0:T(8,128)(2,1)S(1)}, u32[]{:S(2)}, u32[]{:S(2)}) collective-permute-start(bf16[4,96,128]{2,1,0:T(8,128)(2,1)S(1)} %stack.4.after_ref.refs_0_), channel_id=1, source_target_pairs={{0,1},{1,0},{2,3},{3,2},{4,5},{5,4},{6,7},{7,6},{8,9},{9,8},{10,11... | collective-permute-start | bytes 294920 | tf_op jit(solution)/shard_map/ppermute | solution.py:61
  15.9 3.6 %prepare.5 = (bf16[16,128,1024]{2,1,0:T(8,128)(2,1)S(1)}, f32[16,64,128]{2,1,0:T(8,128)S(1)}, f32[8,128]{1,0:T(8,128)S(1)}) custom-call(bf16[128,48,1024]{2,1,0:T(8,128)(2,1)} %t_ref.5, f32[64,128]{1,0:T(8,128)S(1)} %get-tuple-element.33.b_ref, bf16[4,96,128]{2,1,0:T(8,128)(2,1)S(1)} %stack.4.after_ref.refs_0_), custom_call_target="tpu_custom_call" | custom-call | bytes 6000000 | tf_op jit(solution)/shard_map/prepare/pallas_call | solution.py:37
  19.9 4.4 %project.1.refs_0_.refs_2_ = f32[128,128]{1,0:T(8,128)S(1)} custom-call(bf16[1024,64]{1,0:T(8,128)(2,1)S(1)} %get-tuple-element.37.turned_ref, f32[48,64]{1,0:T(8,128)S(1)} %get-tuple-element.38.second_ref, f32[64,64]{1,0:T(8,128)S(1)} %get-tuple-element.39.gram_ref, bf16[16,128,1024]{2,1,0:T(8,128)(2,1)S(1)} %get-tuple-element.40.refs_0_, ...), custom_call_target="tpu_custom_call" | custom-call | bytes 15000000 | tf_op jit(solution)/shard_map/project/pallas_call | solution.py:37
  25.6 1.6 %collective-permute-start.4 = (f32[128,128]{1,0:T(8,128)S(1)}, f32[128,128]{1,0:T(8,128)S(1)}, u32[]{:S(2)}, u32[]{:S(2)}) collective-permute-start(f32[128,128]{1,0:T(8,128)S(1)} %add.21.a_ref), channel_id=1, source_target_pairs={{0,16},{1,17},{2,18},{3,19},{4,20},{5,21},{6,22},{7,23},{8,24},{9,... | collective-permute-start | bytes 196616 | tf_op jit(solution)/shard_map/ppermute | solution.py:61
  27.2 2.7 %collective-permute-done.4.b_ref = f32[128,128]{1,0:T(8,128)S(1)} collective-permute-done((f32[128,128]{1,0:T(8,128)S(1)}, f32[128,128]{1,0:T(8,128)S(1)}, u32[]{:S(2)}, u32[]{:S(2)}) %collective-permute-start.4) | collective-permute-done | bytes 65568 | tf_op jit(solution)/shard_map/ppermute | solution.py:61
  35.6 2.3 %collective-permute-done.6.refs_1_ = f32[64,128]{1,0:T(8,128)S(1)} collective-permute-done((f32[64,128]{1,0:T(8,128)S(1)}, f32[64,128]{1,0:T(8,128)S(1)}, u32[]{:S(2)}, u32[]{:S(2)}) %collective-permute-start.6) | collective-permute-done | bytes 32800 | tf_op jit(solution)/shard_map/ppermute | solution.py:61
  40.4 2.6 %collective-permute-done.7.refs_1_ = f32[64,128]{1,0:T(8,128)S(1)} collective-permute-done((f32[64,128]{1,0:T(8,128)S(1)}, f32[64,128]{1,0:T(8,128)S(1)}, u32[]{:S(2)}, u32[]{:S(2)}) %collective-permute-start.7) | collective-permute-done | bytes 32800 | tf_op jit(solution)/shard_map/ppermute | solution.py:61
  43.0 8.5 %slab.1 = (f32[64,128]{1,0:T(8,128)}, f32[64,64]{1,0:T(8,128)S(1)}, f32[48,64,1024]{2,1,0:T(8,128)S(1)}, f32[4,64,128]{2,1,0:T(8,128)S(1)}, f32[4,64,128]{2,1,0:T(8,128)S(1)}) custom-call(s32[1]{0:T(128)} %bitcast.me_ref, f32[64,64]{1,0:T(8,128)S(1)} %eliminate.8.refs_2_.inverse_ref, f32[64,128]{1,0:T(8,128)S(1)} %add.24.summed_ref, ...), custom_call_target="tpu_custom_call" | custom-call | bytes 24000000 | tf_op jit(solution)/shard_map/slab/pallas_call | solution.py:37
  53.9 2.5 %collective-permute-done.8.got_in = f32[4,64,128]{2,1,0:T(8,128)S(1)} collective-permute-done((f32[4,64,128]{2,1,0:T(8,128)S(1)}, f32[4,64,128]{2,1,0:T(8,128)S(1)}, u32[]{:S(2)}, u32[]{:S(2)}) %collective-permute-start.8) | collective-permute-done | bytes 131104 | tf_op jit(solution)/shard_map/ppermute | solution.py:61
  57.9 2.9 %collective-permute-done.9.refs_1_ = f32[2,64,128]{2,1,0:T(8,128)S(1)} collective-permute-done((f32[2,64,128]{2,1,0:T(8,128)S(1)}, f32[2,64,128]{2,1,0:T(8,128)S(1)}, u32[]{:S(2)}, u32[]{:S(2)}) %collective-permute-start.9) | collective-permute-done | bytes 65568 | tf_op jit(solution)/shard_map/ppermute | solution.py:61
  63.1 3.3 %collective-permute-done.10.refs_1_ = f32[2,64,128]{2,1,0:T(8,128)S(1)} collective-permute-done((f32[2,64,128]{2,1,0:T(8,128)S(1)}, f32[2,64,128]{2,1,0:T(8,128)S(1)}, u32[]{:S(2)}, u32[]{:S(2)}) %collective-permute-start.10) | collective-permute-done | bytes 65568 | tf_op jit(solution)/shard_map/ppermute | solution.py:61
  66.7 3.9 %collective-permute-done.11.refs_1_ = bf16[2,64,128]{2,1,0:T(8,128)(2,1)S(1)} collective-permute-done((bf16[2,64,128]{2,1,0:T(8,128)(2,1)S(1)}, bf16[2,64,128]{2,1,0:T(8,128)(2,1)S(1)}, u32[]{:S(2)}, u32[]{:S(2)}) %collective-permute-start.11) | collective-permute-done | bytes 32800 | tf_op jit(solution)/shard_map/ppermute | solution.py:61
  71.7 3.2 %collective-permute-done.12.refs_1_ = bf16[4,64,128]{2,1,0:T(8,128)(2,1)S(1)} collective-permute-done((bf16[4,64,128]{2,1,0:T(8,128)(2,1)S(1)}, bf16[4,64,128]{2,1,0:T(8,128)(2,1)S(1)}, u32[]{:S(2)}, u32[]{:S(2)}) %collective-permute-start.12) | collective-permute-done | bytes 65568 | tf_op jit(solution)/shard_map/ppermute | solution.py:61
  74.9 1.7 %second.1.refs_0_.refs_2_ = f32[64,128]{1,0:T(8,128)S(1)} custom-call(s32[1]{0:T(128)} %bitcast.me_ref, bf16[4,64,128]{2,1,0:T(8,128)(2,1)S(1)} %stack.5.refs_0_, bf16[4,64,128]{2,1,0:T(8,128)(2,1)S(1)} %collective-permute-done.12.refs_1_, f32[48,64,1024]{2,1,0:T(8,128)S(1)} %get-tuple-element.55.refs_2_.z_ref), custom_call_target="tpu_custom_call" | custom-call | bytes 6000000 | tf_op jit(solution)/shard_map/second/pallas_call | solution.py:37
  77.9 1.5 %collective-permute-start.14 = (f32[64,128]{1,0:T(8,128)S(1)}, f32[64,128]{1,0:T(8,128)S(1)}, u32[]{:S(2)}, u32[]{:S(2)}) collective-permute-start(f32[64,128]{1,0:T(8,128)S(1)} %add.26.mine_ref), channel_id=1, source_target_pairs={{0,16},{1,17},{2,18},{3,19},{4,20},{5,21},{6,22},{7,23},{8,24},{9,... | collective-permute-start | bytes 98312 | tf_op jit(solution)/shard_map/ppermute | solution.py:61
  79.4 2.4 %collective-permute-done.14.got_ref = f32[64,128]{1,0:T(8,128)S(1)} collective-permute-done((f32[64,128]{1,0:T(8,128)S(1)}, f32[64,128]{1,0:T(8,128)S(1)}, u32[]{:S(2)}, u32[]{:S(2)}) %collective-permute-start.14) | collective-permute-done | bytes 32800 | tf_op jit(solution)/shard_map/ppermute | solution.py:61
  81.8 5.4 %mode.1 = (f32[4,64,128]{2,1,0:T(8,128)S(1)}, bf16[4,64,128]{2,1,0:T(8,128)(2,1)S(1)}) custom-call(s32[1]{0:T(128)} %bitcast.me_ref, f32[64,128]{1,0:T(8,128)S(1)} %add.26.mine_ref, f32[64,128]{1,0:T(8,128)S(1)} %collective-permute-done.14.got_ref, f32[64,64]{1,0:T(8,128)S(1)} %get-tuple-element.50.refs_1_.gram_frames_ref, ...), custom_call_target="tpu_custom_call" | custom-call | bytes 15000000 | tf_op jit(solution)/shard_map/mode/pallas_call | solution.py:37
  88.3 3.2 %collective-permute-done.15.got_in = bf16[4,64,128]{2,1,0:T(8,128)(2,1)S(1)} collective-permute-done((bf16[4,64,128]{2,1,0:T(8,128)(2,1)S(1)}, bf16[4,64,128]{2,1,0:T(8,128)(2,1)S(1)}, u32[]{:S(2)}, u32[]{:S(2)}) %collective-permute-start.15) | collective-permute-done | bytes 65568 | tf_op jit(solution)/shard_map/ppermute | solution.py:61
  92.6 3.3 %collective-permute-start.18 = (bf16[64,128]{1,0:T(8,128)(2,1)S(1)}, bf16[64,128]{1,0:T(8,128)(2,1)S(1)}, u32[]{:S(2)}, u32[]{:S(2)}) collective-permute-start(bf16[64,128]{1,0:T(8,128)(2,1)S(1)} %get-tuple-element.61), channel_id=1, source_target_pairs={{0,6},{1,7},{2,4},{3,5},{4,2},{5,3},{6,0},{7,1},{8,14},{9,15},{10,... | collective-permute-start | bytes 49160 | tf_op jit(solution)/shard_map/ppermute | solution.py:61
  96.3 1.9 %collective-permute-done.18 = bf16[64,128]{1,0:T(8,128)(2,1)S(1)} collective-permute-done((bf16[64,128]{1,0:T(8,128)(2,1)S(1)}, bf16[64,128]{1,0:T(8,128)(2,1)S(1)}, u32[]{:S(2)}, u32[]{:S(2)}) %collective-permute-start.18) | collective-permute-done | bytes 16416 | tf_op jit(solution)/shard_map/ppermute | solution.py:61
  (43 shorter events, 22.7 us)
Async XLA Ops:
  1.5 7.7 %collective-permute-start = (bf16[1,96,128]{2,1,0:T(8,128)(2,1)S(1)}, bf16[1,96,128]{2,1,0:T(8,128)(2,1)S(1)}, u32[]{:S(2)}, u32[]{:S(2)}) collective-permute-start(bf16[1,96,128]{2,1,0:T(8,128)(2,1)S(1)} %get-tuple-element.32.after_ref.refs_0_), channel_id=1, source_target_pairs={{0,4},{1,5},{2,6},{3,7},{4,0},{5,1},{6,2},{7,3},{8,12},{9,13},{10,... | collective-permute-start | bytes 73736 | tf_op jit(solution)/shard_map/ppermute | solution.py:61
  9.2 5.2 %collective-permute-start.1 = (bf16[2,96,128]{2,1,0:T(8,128)(2,1)S(1)}, bf16[2,96,128]{2,1,0:T(8,128)(2,1)S(1)}, u32[]{:S(2)}, u32[]{:S(2)}) collective-permute-start(bf16[2,96,128]{2,1,0:T(8,128)(2,1)S(1)} %stack.3.after_ref.refs_0_), channel_id=1, source_target_pairs={{0,2},{1,3},{2,0},{3,1},{4,6},{5,7},{6,4},{7,5},{8,10},{9,11},{10,... | collective-permute-start | bytes 147464 | tf_op jit(solution)/shard_map/ppermute | solution.py:61
  14.4 5.1 %collective-permute-start.2 = (bf16[4,96,128]{2,1,0:T(8,128)(2,1)S(1)}, bf16[4,96,128]{2,1,0:T(8,128)(2,1)S(1)}, u32[]{:S(2)}, u32[]{:S(2)}) collective-permute-start(bf16[4,96,128]{2,1,0:T(8,128)(2,1)S(1)} %stack.4.after_ref.refs_0_), channel_id=1, source_target_pairs={{0,1},{1,0},{2,3},{3,2},{4,5},{5,4},{6,7},{7,6},{8,9},{9,8},{10,11... | collective-permute-start | bytes 294920 | tf_op jit(solution)/shard_map/ppermute | solution.py:61
  24.3 1.3 %collective-permute-start.3 = (f32[128,128]{1,0:T(8,128)S(1)}, f32[128,128]{1,0:T(8,128)S(1)}, u32[]{:S(2)}, u32[]{:S(2)}) collective-permute-start(f32[128,128]{1,0:T(8,128)S(1)} %project.1.refs_0_.refs_2_), channel_id=1, source_target_pairs={{0,8},{1,9},{2,10},{3,11},{4,12},{5,13},{6,14},{7,15},{8,0},{9,1},... | collective-permute-start | bytes 196616 | tf_op jit(solution)/shard_map/ppermute | solution.py:61
  25.6 4.3 %collective-permute-start.4 = (f32[128,128]{1,0:T(8,128)S(1)}, f32[128,128]{1,0:T(8,128)S(1)}, u32[]{:S(2)}, u32[]{:S(2)}) collective-permute-start(f32[128,128]{1,0:T(8,128)S(1)} %add.21.a_ref), channel_id=1, source_target_pairs={{0,16},{1,17},{2,18},{3,19},{4,20},{5,21},{6,22},{7,23},{8,24},{9,... | collective-permute-start | bytes 196616 | tf_op jit(solution)/shard_map/ppermute | solution.py:61
  30.0 4.0 %collective-permute-start.5 = (f32[64,128]{1,0:T(8,128)S(1)}, f32[64,128]{1,0:T(8,128)S(1)}, u32[]{:S(2)}, u32[]{:S(2)}) collective-permute-start(f32[64,128]{1,0:T(8,128)S(1)} %get-tuple-element.45.refs_2_.refs_0_), channel_id=1, source_target_pairs={{0,1},{1,0},{2,3},{3,2},{4,5},{5,4},{6,7},{7,6},{8,9},{9,8},{10,11... | collective-permute-start | bytes 98312 | tf_op jit(solution)/shard_map/ppermute | solution.py:61
  34.0 3.9 %collective-permute-start.6 = (f32[64,128]{1,0:T(8,128)S(1)}, f32[64,128]{1,0:T(8,128)S(1)}, u32[]{:S(2)}, u32[]{:S(2)}) collective-permute-start(f32[64,128]{1,0:T(8,128)S(1)} %add.22.refs_1_.refs_0_), channel_id=1, source_target_pairs={{0,2},{1,3},{2,0},{3,1},{4,6},{5,7},{6,4},{7,5},{8,10},{9,11},{10,... | collective-permute-start | bytes 98312 | tf_op jit(solution)/shard_map/ppermute | solution.py:61
  37.9 5.1 %collective-permute-start.7 = (f32[64,128]{1,0:T(8,128)S(1)}, f32[64,128]{1,0:T(8,128)S(1)}, u32[]{:S(2)}, u32[]{:S(2)}) collective-permute-start(f32[64,128]{1,0:T(8,128)S(1)} %add.23.refs_1_.refs_0_), channel_id=1, source_target_pairs={{0,4},{1,5},{2,6},{3,7},{4,0},{5,1},{6,2},{7,3},{8,12},{9,13},{10,... | collective-permute-start | bytes 98312 | tf_op jit(solution)/shard_map/ppermute | solution.py:61
  51.5 5.0 %collective-permute-start.8 = (f32[4,64,128]{2,1,0:T(8,128)S(1)}, f32[4,64,128]{2,1,0:T(8,128)S(1)}, u32[]{:S(2)}, u32[]{:S(2)}) collective-permute-start(f32[4,64,128]{2,1,0:T(8,128)S(1)} %get-tuple-element.51.refs_2_), channel_id=1, source_target_pairs={{0,1},{1,0},{2,3},{3,2},{4,5},{5,4},{6,7},{7,6},{8,9},{9,8},{10,11... | collective-permute-start | bytes 393224 | tf_op jit(solution)/shard_map/ppermute | solution.py:61
  56.5 4.3 %collective-permute-start.9 = (f32[2,64,128]{2,1,0:T(8,128)S(1)}, f32[2,64,128]{2,1,0:T(8,128)S(1)}, u32[]{:S(2)}, u32[]{:S(2)}) collective-permute-start(f32[2,64,128]{2,1,0:T(8,128)S(1)} %get-tuple-element.53.refs_1_), channel_id=1, source_target_pairs={{0,2},{1,3},{2,0},{3,1},{4,6},{5,7},{6,4},{7,5},{8,10},{9,11},{10,... | collective-permute-start | bytes 196616 | tf_op jit(solution)/shard_map/ppermute | solution.py:61
  60.8 5.6 %collective-permute-start.10 = (f32[2,64,128]{2,1,0:T(8,128)S(1)}, f32[2,64,128]{2,1,0:T(8,128)S(1)}, u32[]{:S(2)}, u32[]{:S(2)}) collective-permute-start(f32[2,64,128]{2,1,0:T(8,128)S(1)} %add.25.refs_1_.refs_0_), channel_id=1, source_target_pairs={{0,4},{1,5},{2,6},{3,7},{4,0},{5,1},{6,2},{7,3},{8,12},{9,13},{10,... | collective-permute-start | bytes 196616 | tf_op jit(solution)/shard_map/ppermute | solution.py:61
  66.6 4.0 %collective-permute-start.11 = (bf16[2,64,128]{2,1,0:T(8,128)(2,1)S(1)}, bf16[2,64,128]{2,1,0:T(8,128)(2,1)S(1)}, u32[]{:S(2)}, u32[]{:S(2)}) collective-permute-start(bf16[2,64,128]{2,1,0:T(8,128)(2,1)S(1)} %update.1.refs_0_.refs_2_), channel_id=1, source_target_pairs={{0,2},{1,3},{2,0},{3,1},{4,6},{5,7},{6,4},{7,5},{8,10},{9,11},{10,... | collective-permute-start | bytes 98312 | tf_op jit(solution)/shard_map/ppermute | solution.py:61
  70.6 4.3 %collective-permute-start.12 = (bf16[4,64,128]{2,1,0:T(8,128)(2,1)S(1)}, bf16[4,64,128]{2,1,0:T(8,128)(2,1)S(1)}, u32[]{:S(2)}, u32[]{:S(2)}) collective-permute-start(bf16[4,64,128]{2,1,0:T(8,128)(2,1)S(1)} %stack.5.refs_0_), channel_id=1, source_target_pairs={{0,1},{1,0},{2,3},{3,2},{4,5},{5,4},{6,7},{7,6},{8,9},{9,8},{10,11... | collective-permute-start | bytes 196616 | tf_op jit(solution)/shard_map/ppermute | solution.py:61
  76.6 1.3 %collective-permute-start.13 = (f32[64,128]{1,0:T(8,128)S(1)}, f32[64,128]{1,0:T(8,128)S(1)}, u32[]{:S(2)}, u32[]{:S(2)}) collective-permute-start(f32[64,128]{1,0:T(8,128)S(1)} %second.1.refs_0_.refs_2_), channel_id=1, source_target_pairs={{0,8},{1,9},{2,10},{3,11},{4,12},{5,13},{6,14},{7,15},{8,0},{9,1},... | collective-permute-start | bytes 98312 | tf_op jit(solution)/shard_map/ppermute | solution.py:61
  77.9 3.9 %collective-permute-start.14 = (f32[64,128]{1,0:T(8,128)S(1)}, f32[64,128]{1,0:T(8,128)S(1)}, u32[]{:S(2)}, u32[]{:S(2)}) collective-permute-start(f32[64,128]{1,0:T(8,128)S(1)} %add.26.mine_ref), channel_id=1, source_target_pairs={{0,16},{1,17},{2,18},{3,19},{4,20},{5,21},{6,22},{7,23},{8,24},{9,... | collective-permute-start | bytes 98312 | tf_op jit(solution)/shard_map/ppermute | solution.py:61
  87.2 4.3 %collective-permute-start.15 = (bf16[4,64,128]{2,1,0:T(8,128)(2,1)S(1)}, bf16[4,64,128]{2,1,0:T(8,128)(2,1)S(1)}, u32[]{:S(2)}, u32[]{:S(2)}) collective-permute-start(bf16[4,64,128]{2,1,0:T(8,128)(2,1)S(1)} %get-tuple-element.57), channel_id=1, source_target_pairs={{0,1},{1,0},{2,3},{3,2},{4,5},{5,4},{6,7},{7,6},{8,9},{9,8},{10,11... | collective-permute-start | bytes 196616 | tf_op jit(solution)/shard_map/ppermute | solution.py:61
  91.5 4.5 %collective-permute-start.16 = (bf16[64,128]{1,0:T(8,128)(2,1)S(1)}, bf16[64,128]{1,0:T(8,128)(2,1)S(1)}, u32[]{:S(2)}, u32[]{:S(2)}) collective-permute-start(bf16[64,128]{1,0:T(8,128)(2,1)S(1)} %get-tuple-element.59), channel_id=1, source_target_pairs={{0,2},{1,3},{2,0},{3,1},{4,6},{5,7},{6,4},{7,5},{8,10},{9,11},{10,... | collective-permute-start | bytes 49160 | tf_op jit(solution)/shard_map/ppermute | solution.py:61
  91.6 4.7 %collective-permute-start.17 = (bf16[64,128]{1,0:T(8,128)(2,1)S(1)}, bf16[64,128]{1,0:T(8,128)(2,1)S(1)}, u32[]{:S(2)}, u32[]{:S(2)}) collective-permute-start(bf16[64,128]{1,0:T(8,128)(2,1)S(1)} %get-tuple-element.60), channel_id=1, source_target_pairs={{0,4},{1,5},{2,6},{3,7},{4,0},{5,1},{6,2},{7,3},{8,12},{9,13},{10,... | collective-permute-start | bytes 49160 | tf_op jit(solution)/shard_map/ppermute | solution.py:61
  92.6 5.5 %collective-permute-start.18 = (bf16[64,128]{1,0:T(8,128)(2,1)S(1)}, bf16[64,128]{1,0:T(8,128)(2,1)S(1)}, u32[]{:S(2)}, u32[]{:S(2)}) collective-permute-start(bf16[64,128]{1,0:T(8,128)(2,1)S(1)} %get-tuple-element.61), channel_id=1, source_target_pairs={{0,6},{1,7},{2,4},{3,5},{4,2},{5,3},{6,0},{7,1},{8,14},{9,15},{10,... | collective-permute-start | bytes 49160 | tf_op jit(solution)/shard_map/ppermute | solution.py:61

commit v3 on v2

--- a/solution.py
+++ b/solution.py
@@ -57,8 +57,8 @@
     return [swap(x, axes, count, o) for o in offsets[1:]]
 
 
-def swap(x, axes, count, offset):
-    return lax.ppermute(x, axes, [(n, n ^ offset) for n in range(count)])
+def swap(x, axes, count, offset, only=0):
+    return lax.ppermute(x, axes, [(n, n ^ offset) for n in range(count) if n & only == only])
 
 
 def join_body(me_ref, a_hbm, b_hbm, out_ref, turned_ref, second_ref, a_ref, b_ref, sems):
@@ -128,6 +128,33 @@
     return call(add_body, shaped(parts[0].shape), specs, (*parts, after), "add", us=0.2)
 
 
+def close_body(a_ref, b_ref, inverse_ref, out_ref):
+    components = a_ref.shape[0]
+    out_ref[:components] = a_ref[...] + b_ref[...]
+    inverse = inverse_ref[...]
+    out_ref[components:] = jnp.concatenate([inverse, inverse], axis=1)
+
+
+def close(a, b, inverse):
+    shape = (2 * a.shape[0], a.shape[1])
+    return call(close_body, shaped(shape), [vmem()] * 3, (a, b, inverse), "close", us=0.2)
+
+
+def choose_body(bit, me_ref, mine_ref, got_ref, sum_ref, inverse_ref):
+    components = sum_ref.shape[0]
+    mine = jnp.full(mine_ref.shape, me_ref[0] & bit) == bit
+    chosen = jnp.where(mine, mine_ref[...], got_ref[...])
+    sum_ref[...] = chosen[:components]
+    inverse_ref[...] = chosen[components:, :components]
+
+
+def choose(me, bit, mine, got):
+    half = mine.shape[0] // 2
+    outs = (shaped((half, mine.shape[1])), shaped((half, half)))
+    specs = [smem(), vmem(), vmem()]
+    return call(functools.partial(choose_body, bit), outs, specs, (me, mine, got), "choose", us=0.2)
+
+
 def split_body(a_ref, b_ref, sum_ref, gram_ref):
     components = sum_ref.shape[0]
     sum_ref[...] = a_ref[:components] + b_ref[:components]
@@ -140,17 +167,27 @@
     return call(split_body, outs, [vmem()] * 2, (a, b), "split_add", us=0.2)
 
 
-def prepare_body(at, t_ref, b_ref, after_ref, out_ref, wide_ref, token_ref, slab, sems):
+def prepare_body(at, cols, here, ahead, t_ref, b_ref, after_ref, *refs):
     del after_ref
-    blocks, _, cols, _ = slab.shape
-
-    def fetch(n):
+    slab_ref = refs[0] if here else None
+    refs = list(refs[1:] if here else refs)
+    out_ref, wide_ref, token_ref = refs[:3]
+    next_ref = refs.pop(3) if ahead else None
+    sems = refs[-1]
+    slab_ref = slab_ref if here else refs[3]
+    blocks = slab_ref.shape[0]
+
+    def fetch(n, to_ref, start, sem):
         return pltpu.make_async_copy(
-            t_ref.at[pl.ds(n * GROUP, GROUP), pl.ds(at, cols)], slab.at[n], sems.at[n]
+            t_ref.at[pl.ds(n * GROUP, GROUP), pl.ds(start, to_ref.shape[2])], to_ref.at[n], sems.at[sem, n]
         )
 
-    for n in range(blocks):
-        fetch(n).start()
+    if not here:
+        for n in range(blocks):
+            fetch(n, slab_ref, at, 0).start()
+    if ahead:
+        for n in range(blocks):
+            fetch(n, next_ref, at + cols, 1).start()
     token_ref[...] = jnp.zeros_like(token_ref)
     for j in range(cols):
         wide_ref[j] = jnp.broadcast_to(b_ref[:, at + j : at + j + 1], wide_ref.shape[1:])
@@ -159,29 +196,38 @@
     turn = jnp.where((to // GROUP) + (to % GROUP) * GROUP == of, 1.0, 0.0).astype(BF16)
 
     def step(n, _):
-        fetch(n).wait()
+        if not here:
+            fetch(n, slab_ref, at, 0).wait()
         for g in range(0, cols, GROUP):
-            block = slab[n, :, g : g + GROUP, :].reshape(GROUP * GROUP, -1)
+            block = slab_ref[n, :, g : g + GROUP, :].reshape(GROUP * GROUP, -1)
             turned = dot(turn, block, ((1,), (0,))).astype(BF16).reshape(GROUP, GROUP, -1)
             out_ref[g : g + GROUP, pl.ds(pl.multiple_of(n * GROUP, GROUP), GROUP), :] = turned
         return 0
 
     lax.fori_loop(0, blocks, step, 0)
-
-
-def prepare(tensor, second, at, cols, after):
+    if ahead:
+        for n in range(blocks):
+            fetch(n, next_ref, at + cols, 1).wait()
+
+
+def prepare(tensor, second, at, cols, fetched, next_cols, after):
     frames, _, rows = tensor.shape
     components = second.shape[0]
     blocks = frames // GROUP
-    return call(
-        functools.partial(prepare_body, at),
-        (VM((cols, frames, rows), BF16), VM((cols, components, 128), F32), shaped((8, 128))),
-        [anywhere(), vmem(), anywhere()],
-        (tensor, second, after),
+    outs = (VM((cols, frames, rows), BF16), VM((cols, components, 128), F32), shaped((8, 128)))
+    if next_cols:
+        outs += (VM((blocks, GROUP, next_cols, rows), BF16),)
+    scratch = [] if fetched else [VM((blocks, GROUP, cols, rows), BF16)]
+    got = call(
+        functools.partial(prepare_body, at, cols, bool(fetched), bool(next_cols)),
+        outs,
+        [anywhere(), vmem(), anywhere()] + [vmem()] * len(fetched),
+        (tensor, second, after, *fetched),
         "prepare",
-        [VM((blocks, GROUP, cols, rows), BF16), pltpu.SemaphoreType.DMA((blocks,))],
+        scratch + [pltpu.SemaphoreType.DMA((2, blocks))],
         us=cols / 8,
     )
+    return got[:3], list(got[3:])
 
 
 def place(at, blocks, width, full_ref):
@@ -198,13 +244,13 @@
     components = full_ref.shape[0]
     blocks = [s[n] for s in stacks for n in range(s.shape[0])]
     width = blocks[0].shape[1]
-    place(me_ref[0], [(o, b[:components]) for o, b in zip(offsets, blocks)], width, full_ref)
+    place(me_ref[0] & 7, [(o, b[:components]) for o, b in zip(offsets, blocks)], width, full_ref)
     full = full_ref[...]
     gram_ref[...] = dot(full.astype(BF16), full.astype(BF16), ((1,), (1,)))
     turned_ref[...] = full.T.astype(BF16)
     height = blocks[0].shape[0] - components
     for o, b in zip(offsets, blocks):
-        every_ref[pl.ds(pl.multiple_of((me_ref[0] ^ o) * height, height), height), :] = b[components:].astype(F32)
+        every_ref[pl.ds(pl.multiple_of(((me_ref[0] & 7) ^ o) * height, height), height), :] = b[components:].astype(F32)
     every = every_ref[...].T.astype(BF16)
     both = dot(every, every, ((1,), (1,)))
     other_ref[...] = both[:components, :components] + both[components:, components:]
@@ -336,7 +382,7 @@
 
 def deal_body(me_ref, keep_in, got_in, after_ref, mine_ref, *outs):
     del after_ref
-    upper = me_ref[0] >> 1
+    upper = (me_ref[0] & 7) >> 1
     mine_ref[...] = keep_in[upper] + got_in[upper].astype(F32)
     for n, out in enumerate(outs):
         at = upper ^ (n + 1)
@@ -371,11 +417,8 @@
     gram_ref[...] = dot(frames, frames, ((1,), (1,)), HIGH)
     high = frames.astype(BF16)
     low = (frames - high.astype(F32)).astype(BF16)
-    none = jnp.zeros_like(high)
-    both = jnp.concatenate(
-        [jnp.concatenate(pair, axis=1) for pair in ((high, none), (none, high), (low, none), (none, low))], axis=0
-    )
-    frames_count, wide = frames.shape[1], 256
+    both = jnp.concatenate([high, low], axis=1)
+    wide = 256
 
     def chunk(c, _):
         lanes = pl.ds(pl.multiple_of(c * wide, wide), wide)
@@ -384,16 +427,13 @@
         for t_ref, wide_ref in zip(t_refs, wide_refs):
 
             def step(n, total, t_ref=t_ref, wide_ref=wide_ref, base=base):
-                for s in range(0, 8, 2):
-                    block = t_ref[pl.ds(n * 8 + s, 2), :, lanes].reshape(2 * frames_count, wide)
-                    product = dot(both, block, ((1,), (0,)))
-                    product = product[: 2 * components] + product[2 * components :]
-                    for h in range(2):
-                        j = n * 8 + s + h
-                        z = product[h * components : h * components + components]
-                        z_ref[base + j, :, lanes] = z
-                        scale = wide_ref[j]
-                        total = total + z * jnp.concatenate([scale, scale], axis=1)
+                for s in range(8):
+                    j = n * 8 + s
+                    block = t_ref[j, :, lanes]
+                    z = dot(both, jnp.concatenate([block, block], axis=0), ((1,), (0,)))
+                    z_ref[base + j, :, lanes] = z
+                    scale = wide_ref[j]
+                    total = total + z * jnp.concatenate([scale, scale], axis=1)
                 return total
 
             total = lax.fori_loop(0, t_ref.shape[0] // 8, step, total)
@@ -527,7 +567,7 @@
     every = row_size * col_size
     width = row_count // col_size
     direct = width % 128 == 0 and col_size == 8
-    me = lax.axis_index("col").astype(jnp.int32).reshape(1)
+    me = lax.axis_index(BOTH).astype(jnp.int32).reshape(1)
     col_bits = [1 << b for b in range(col_size.bit_length() - 1)]
     row_bits = [col_size << b for b in range(row_size.bit_length() - 1)]
     tensor = pltpu.with_memory_space_constraint(tensor, pltpu.HBM)
@@ -535,25 +575,26 @@
 
     turned, wides = [], []
     order = [0, 4, 2, 6, 1, 5, 3, 7]
+    ends = [cols for _, cols in cuts[1:]] + [0]
+    fetched = []
     if direct:
         have, second_turned, second_values = join(me, first_factor, second_factor.T)
-        for bit, (at, cols) in zip((4, 2, 1), cuts):
+    else:
+        have = second_values = second_factor.astype(F32)
+        second_turned = second_values.T
+    for (at, cols), following, bit in zip(cuts, ends, (4, 2, 1)):
+        if direct:
             got = swap(have, "col", col_size, bit)
-            t, w, token = prepare(tensor, second_values, at, cols, have)
-            turned.append(t)
-            wides.append(w)
-            if bit > 1:
-                have = stack([have, got], token)
+        (t, w, token), fetched = prepare(tensor, second_values, at, cols, fetched, following, have)
+        turned.append(t)
+        wides.append(w)
+        if direct and bit > 1:
+            have = stack([have, got], token)
+    if direct:
         first_turned, gram_first, gram_second = assemble_first(
             me, [have, got], token, order, components, row_count
         )
     else:
-        second_turned = second_factor.T.astype(F32)
-        second_values = second_factor.astype(F32)
-        for at, cols in cuts:
-            t, w, token = prepare(tensor, second_values, at, cols, second_values)
-            turned.append(t)
-            wides.append(w)
         full = lax.all_gather(first_factor, "col", axis=1, tiled=True)
         others = lax.all_gather(second_factor, "col", axis=1, tiled=True)
         first_turned = full.T
@@ -561,17 +602,20 @@
         gram_second = jnp.dot(others, others.T, preferred_element_type=F32)
 
     total = project(first_turned, second_turned, gram_first, turned)
-    for bit in row_bits[:-1]:
-        total = add([total, swap(total, BOTH, every, bit)], total)
-    total, gram_first = split_add(total, swap(total, BOTH, every, row_bits[-1]))
+    core, upper = row_bits[0], row_bits[1:]
+    total = add([total, swap(total, BOTH, every, core)], total)
+    total, gram_first = split_add(total, swap(total, BOTH, every, upper[0], core))
     state = (gram_first, gram_second)
     marks = [0, 24, 44, components]
-    for n, bit in enumerate(col_bits):
-        got = swap(total, BOTH, every, bit)
+    bits = upper[1:] + col_bits
+    for n, bit in enumerate(bits):
+        got = swap(total, BOTH, every, bit, core)
         if n < 3:
             state = (eliminate_part(state, marks[n], marks[n + 1], total),)
-        total = add([total, got], state[0])
-    frames, gram_frames, z, *outs = slab(me, state[0], total, turned, wides, width, direct)
+        total = add([total, got], state[0]) if n < len(bits) - 1 else close(total, got, state[0])
+    handed = lax.ppermute(total, BOTH, [(n, n ^ core) for n in range(every) if n & core])
+    total, inverse_first = choose(me, core, total, handed)
+    frames, gram_frames, z, *outs = slab(me, inverse_first, total, turned, wides, width, direct)
 
     state = (gram_second, gram_frames)
     if direct:

time: 99.2 us -> 105 us (1.058)
  waiting for transfers between devices: 35.2 us -> 39.6 us
  starting transfers between devices: 22.8 us -> 25.8 us
  Pallas kernels: 39.4 us -> 37.9 us
    ppermute x19 -> x20, waiting for transfers between devices: 35.2 us -> 39.6 us  [the longest x19 25.3 us: swap(): lax.ppermute(x, axes, [(n, n ^ offset) for n in range(count) if n & only...]
    ppermute x19 -> x20, starting transfers between devices: 22.8 us -> 25.8 us  [the longest x19 24.5 us: swap(): lax.ppermute(x, axes, [(n, n ^ offset) for n in range(count) if n & only...]
    pallas_call x28 -> x29, Pallas kernels: 39.4 us -> 37.9 us  [call(): pl.pallas_call(body, out_shape=outs, in_specs=ins, out_specs=(vmem(),) *...]
  transfers between devices with their start and end apart: 19 -> 20, of which waited for: 15 -> 13; matrix products, arithmetic and copies ran while one was open for 0% -> 0% of each run, Pallas kernels for 18% -> 16%
where the time goes in v3:
time: 105 us
  waiting for transfers between devices  39.6 us (38%)
  Pallas kernels  37.9 us (36%)
  starting transfers between devices  25.8 us (25%)
    pallas_call x29, Pallas kernels, call(): pl.pallas_call(body, out_shape=outs, in_specs=ins, out_specs=(vmem(),) *...  37.9 us
    ppermute x19, waiting for transfers between devices, swap(): lax.ppermute(x, axes, [(n, n ^ offset) for n in range(count) if n & only...  25.3 us
    ppermute x19, starting transfers between devices, swap(): lax.ppermute(x, axes, [(n, n ^ offset) for n in range(count) if n & only...  24.5 us
    ppermute x1, waiting for transfers between devices, local(): lax.ppermute(total, BOTH, [(n, n ^ core) for n in range(every) if n & core])  14.3 us
  transfers between devices with their start and end apart: 20, of which 13 were waited for; matrix products, arithmetic and copies ran while one was open for 0% of the time, Pallas kernels for 16%

profile of v3, /device:TPU:0, one launch (start us, length us, event | category | flops | bytes accessed | tf_op | source)
XLA Modules:
  0.0 104.9 jit_solution(1287913889388842586)
XLA Ops:
  1.5 4.1 %collective-permute-start = (bf16[1,96,128]{2,1,0:T(8,128)(2,1)S(1)}, bf16[1,96,128]{2,1,0:T(8,128)(2,1)S(1)}, u32[]{:S(2)}, u32[]{:S(2)}) collective-permute-start(bf16[1,96,128]{2,1,0:T(8,128)(2,1)S(1)} %get-tuple-element.36.after_ref.refs_0_), channel_id=1, source_target_pairs={{0,4},{1,5},{2,6},{3,7},{4,0},{5,1},{6,2},{7,3},{8,12},{9,13},{10,... | collective-permute-start | bytes 73736 | tf_op jit(solution)/shard_map/ppermute | solution.py:61
  5.6 3.6 %prepare.3 = (bf16[16,128,1024]{2,1,0:T(8,128)(2,1)S(1)}, f32[16,64,128]{2,1,0:T(8,128)S(1)}, f32[8,128]{1,0:T(8,128)S(1)}, bf16[8,16,16,1024]{3,2,1,0:T(8,128)(2,1)S(1)}) custom-call(bf16[128,48,1024]{2,1,0:T(8,128)(2,1)} %t_ref.5, f32[64,128]{1,0:T(8,128)S(1)} %get-tuple-element.37.b_ref, bf16[1,96,128]{2,1,0:T(8,128)(2,1)S(1)} %get-tuple-element.36.after_ref.refs_0_), custom_call_target="tpu_custom_call" | custom-call | bytes 6000000 | tf_op jit(solution)/shard_map/prepare/pallas_call | solution.py:37
  9.2 1.6 %collective-permute-start.1 = (bf16[2,96,128]{2,1,0:T(8,128)(2,1)S(1)}, bf16[2,96,128]{2,1,0:T(8,128)(2,1)S(1)}, u32[]{:S(2)}, u32[]{:S(2)}) collective-permute-start(bf16[2,96,128]{2,1,0:T(8,128)(2,1)S(1)} %stack.3.after_ref.refs_0_), channel_id=1, source_target_pairs={{0,2},{1,3},{2,0},{3,1},{4,6},{5,7},{6,4},{7,5},{8,10},{9,11},{10,... | collective-permute-start | bytes 147464 | tf_op jit(solution)/shard_map/ppermute | solution.py:61
  10.9 2.8 %prepare.4 = (bf16[16,128,1024]{2,1,0:T(8,128)(2,1)S(1)}, f32[16,64,128]{2,1,0:T(8,128)S(1)}, f32[8,128]{1,0:T(8,128)S(1)}, bf16[8,16,16,1024]{3,2,1,0:T(8,128)(2,1)S(1)}) custom-call(bf16[128,48,1024]{2,1,0:T(8,128)(2,1)} %t_ref.5, f32[64,128]{1,0:T(8,128)S(1)} %get-tuple-element.37.b_ref, bf16[2,96,128]{2,1,0:T(8,128)(2,1)S(1)} %stack.3.after_ref.refs_0_, ...), custom_call_target="tpu_custom_call" | custom-call | bytes 6000000 | tf_op jit(solution)/shard_map/prepare/pallas_call | solution.py:37
  13.8 1.6 %collective-permute-start.2 = (bf16[4,96,128]{2,1,0:T(8,128)(2,1)S(1)}, bf16[4,96,128]{2,1,0:T(8,128)(2,1)S(1)}, u32[]{:S(2)}, u32[]{:S(2)}) collective-permute-start(bf16[4,96,128]{2,1,0:T(8,128)(2,1)S(1)} %stack.4.after_ref.refs_0_), channel_id=1, source_target_pairs={{0,1},{1,0},{2,3},{3,2},{4,5},{5,4},{6,7},{7,6},{8,9},{9,8},{10,11... | collective-permute-start | bytes 294920 | tf_op jit(solution)/shard_map/ppermute | solution.py:61
  15.3 2.8 %prepare.5 = (bf16[16,128,1024]{2,1,0:T(8,128)(2,1)S(1)}, f32[16,64,128]{2,1,0:T(8,128)S(1)}, f32[8,128]{1,0:T(8,128)S(1)}) custom-call(bf16[128,48,1024]{2,1,0:T(8,128)(2,1)} %t_ref.5, f32[64,128]{1,0:T(8,128)S(1)} %get-tuple-element.37.b_ref, bf16[4,96,128]{2,1,0:T(8,128)(2,1)S(1)} %stack.4.after_ref.refs_0_, ...), custom_call_target="tpu_custom_call" | custom-call | bytes 6000000 | tf_op jit(solution)/shard_map/prepare/pallas_call | solution.py:37
  18.8 4.4 %project.1.refs_0_.refs_2_ = f32[128,128]{1,0:T(8,128)S(1)} custom-call(bf16[1024,64]{1,0:T(8,128)(2,1)S(1)} %get-tuple-element.43.turned_ref, f32[48,64]{1,0:T(8,128)S(1)} %get-tuple-element.44.second_ref, f32[64,64]{1,0:T(8,128)S(1)} %get-tuple-element.45.gram_ref, bf16[16,128,1024]{2,1,0:T(8,128)(2,1)S(1)} %get-tuple-element.46.refs_0_, ...), custom_call_target="tpu_custom_call" | custom-call | bytes 15000000 | tf_op jit(solution)/shard_map/project/pallas_call | solution.py:37
  32.4 14.3 %collective-permute-done.8.got_ref = f32[128,128]{1,0:T(8,128)S(1)} collective-permute-done((f32[128,128]{1,0:T(8,128)S(1)}, f32[128,128]{1,0:T(8,128)S(1)}, u32[]{:S(2)}, u32[]{:S(2)}) %collective-permute-start.8) | collective-permute-done | bytes 65568 | tf_op jit(solution)/shard_map/ppermute | solution.py:616
  46.7 8.3 %slab.1 = (f32[64,128]{1,0:T(8,128)}, f32[64,64]{1,0:T(8,128)S(1)}, f32[48,64,1024]{2,1,0:T(8,128)S(1)}, f32[4,64,128]{2,1,0:T(8,128)S(1)}, f32[4,64,128]{2,1,0:T(8,128)S(1)}) custom-call(s32[1]{0:T(128)} %bitcast.me_ref, f32[64,64]{1,0:T(8,128)S(1)} %get-tuple-element.52.inverse_ref, f32[64,128]{1,0:T(8,128)S(1)} %get-tuple-element.53.summed_ref, ...), custom_call_target="tpu_custom_call" | custom-call | bytes 24000000 | tf_op jit(solution)/shard_map/slab/pallas_call | solution.py:37
  57.9 2.7 %collective-permute-done.9.got_in = f32[4,64,128]{2,1,0:T(8,128)S(1)} collective-permute-done((f32[4,64,128]{2,1,0:T(8,128)S(1)}, f32[4,64,128]{2,1,0:T(8,128)S(1)}, u32[]{:S(2)}, u32[]{:S(2)}) %collective-permute-start.9) | collective-permute-done | bytes 131104 | tf_op jit(solution)/shard_map/ppermute | solution.py:61
  63.0 1.9 %collective-permute-done.10.refs_1_ = f32[2,64,128]{2,1,0:T(8,128)S(1)} collective-permute-done((f32[2,64,128]{2,1,0:T(8,128)S(1)}, f32[2,64,128]{2,1,0:T(8,128)S(1)}, u32[]{:S(2)}, u32[]{:S(2)}) %collective-permute-start.10) | collective-permute-done | bytes 65568 | tf_op jit(solution)/shard_map/ppermute | solution.py:61
  67.4 2.8 %collective-permute-done.11.refs_1_ = f32[2,64,128]{2,1,0:T(8,128)S(1)} collective-permute-done((f32[2,64,128]{2,1,0:T(8,128)S(1)}, f32[2,64,128]{2,1,0:T(8,128)S(1)}, u32[]{:S(2)}, u32[]{:S(2)}) %collective-permute-start.11) | collective-permute-done | bytes 65568 | tf_op jit(solution)/shard_map/ppermute | solution.py:61
  71.7 2.7 %collective-permute-done.12.refs_1_ = bf16[2,64,128]{2,1,0:T(8,128)(2,1)S(1)} collective-permute-done((bf16[2,64,128]{2,1,0:T(8,128)(2,1)S(1)}, bf16[2,64,128]{2,1,0:T(8,128)(2,1)S(1)}, u32[]{:S(2)}, u32[]{:S(2)}) %collective-permute-start.12) | collective-permute-done | bytes 32800 | tf_op jit(solution)/shard_map/ppermute | solution.py:61
  74.4 1.5 %collective-permute-start.13 = (bf16[4,64,128]{2,1,0:T(8,128)(2,1)S(1)}, bf16[4,64,128]{2,1,0:T(8,128)(2,1)S(1)}, u32[]{:S(2)}, u32[]{:S(2)}) collective-permute-start(bf16[4,64,128]{2,1,0:T(8,128)(2,1)S(1)} %stack.5.refs_0_), channel_id=1, source_target_pairs={{0,1},{1,0},{2,3},{3,2},{4,5},{5,4},{6,7},{7,6},{8,9},{9,8},{10,11... | collective-permute-start | bytes 196616 | tf_op jit(solution)/shard_map/ppermute | solution.py:61
  75.9 2.8 %collective-permute-done.13.refs_1_ = bf16[4,64,128]{2,1,0:T(8,128)(2,1)S(1)} collective-permute-done((bf16[4,64,128]{2,1,0:T(8,128)(2,1)S(1)}, bf16[4,64,128]{2,1,0:T(8,128)(2,1)S(1)}, u32[]{:S(2)}, u32[]{:S(2)}) %collective-permute-start.13) | collective-permute-done | bytes 65568 | tf_op jit(solution)/shard_map/ppermute | solution.py:61
  78.6 1.7 %second.1.refs_0_.refs_2_ = f32[64,128]{1,0:T(8,128)S(1)} custom-call(s32[1]{0:T(128)} %bitcast.me_ref, bf16[4,64,128]{2,1,0:T(8,128)(2,1)S(1)} %stack.5.refs_0_, bf16[4,64,128]{2,1,0:T(8,128)(2,1)S(1)} %collective-permute-done.13.refs_1_, f32[48,64,1024]{2,1,0:T(8,128)S(1)} %get-tuple-element.63.refs_2_.z_ref), custom_call_target="tpu_custom_call" | custom-call | bytes 6000000 | tf_op jit(solution)/shard_map/second/pallas_call | solution.py:37
  81.6 1.5 %collective-permute-start.15 = (f32[64,128]{1,0:T(8,128)S(1)}, f32[64,128]{1,0:T(8,128)S(1)}, u32[]{:S(2)}, u32[]{:S(2)}) collective-permute-start(f32[64,128]{1,0:T(8,128)S(1)} %add.28.mine_ref), channel_id=1, source_target_pairs={{0,16},{1,17},{2,18},{3,19},{4,20},{5,21},{6,22},{7,23},{8,24},{9,... | collective-permute-start | bytes 98312 | tf_op jit(solution)/shard_map/ppermute | solution.py:61
  83.1 2.4 %collective-permute-done.15.got_ref = f32[64,128]{1,0:T(8,128)S(1)} collective-permute-done((f32[64,128]{1,0:T(8,128)S(1)}, f32[64,128]{1,0:T(8,128)S(1)}, u32[]{:S(2)}, u32[]{:S(2)}) %collective-permute-start.15) | collective-permute-done | bytes 32800 | tf_op jit(solution)/shard_map/ppermute | solution.py:61
  85.5 5.4 %mode.1 = (f32[4,64,128]{2,1,0:T(8,128)S(1)}, bf16[4,64,128]{2,1,0:T(8,128)(2,1)S(1)}) custom-call(s32[1]{0:T(128)} %bitcast.me_ref, f32[64,128]{1,0:T(8,128)S(1)} %add.28.mine_ref, f32[64,128]{1,0:T(8,128)S(1)} %collective-permute-done.15.got_ref, f32[64,64]{1,0:T(8,128)S(1)} %get-tuple-element.58.refs_1_.gram_frames_ref, ...), custom_call_target="tpu_custom_call" | custom-call | bytes 15000000 | tf_op jit(solution)/shard_map/mode/pallas_call | solution.py:37
  90.9 1.6 %collective-permute-start.16 = (bf16[4,64,128]{2,1,0:T(8,128)(2,1)S(1)}, bf16[4,64,128]{2,1,0:T(8,128)(2,1)S(1)}, u32[]{:S(2)}, u32[]{:S(2)}) collective-permute-start(bf16[4,64,128]{2,1,0:T(8,128)(2,1)S(1)} %get-tuple-element.65), channel_id=1, source_target_pairs={{0,1},{1,0},{2,3},{3,2},{4,5},{5,4},{6,7},{7,6},{8,9},{9,8},{10,11... | collective-permute-start | bytes 196616 | tf_op jit(solution)/shard_map/ppermute | solution.py:61
  92.5 2.8 %collective-permute-done.16.got_in = bf16[4,64,128]{2,1,0:T(8,128)(2,1)S(1)} collective-permute-done((bf16[4,64,128]{2,1,0:T(8,128)(2,1)S(1)}, bf16[4,64,128]{2,1,0:T(8,128)(2,1)S(1)}, u32[]{:S(2)}, u32[]{:S(2)}) %collective-permute-start.16) | collective-permute-done | bytes 65568 | tf_op jit(solution)/shard_map/ppermute | solution.py:61
  96.6 2.2 %collective-permute-start.18 = (bf16[64,128]{1,0:T(8,128)(2,1)S(1)}, bf16[64,128]{1,0:T(8,128)(2,1)S(1)}, u32[]{:S(2)}, u32[]{:S(2)}) collective-permute-start(bf16[64,128]{1,0:T(8,128)(2,1)S(1)} %get-tuple-element.68), channel_id=1, source_target_pairs={{0,4},{1,5},{2,6},{3,7},{4,0},{5,1},{6,2},{7,3},{8,12},{9,13},{10,... | collective-permute-start | bytes 49160 | tf_op jit(solution)/shard_map/ppermute | solution.py:61
  99.7 1.5 %collective-permute-done.18 = bf16[64,128]{1,0:T(8,128)(2,1)S(1)} collective-permute-done((bf16[64,128]{1,0:T(8,128)(2,1)S(1)}, bf16[64,128]{1,0:T(8,128)(2,1)S(1)}, u32[]{:S(2)}, u32[]{:S(2)}) %collective-permute-start.18) | collective-permute-done | bytes 16416 | tf_op jit(solution)/shard_map/ppermute | solution.py:61
  101.2 3.1 %collective-permute-done.19 = bf16[64,128]{1,0:T(8,128)(2,1)S(1)} collective-permute-done((bf16[64,128]{1,0:T(8,128)(2,1)S(1)}, bf16[64,128]{1,0:T(8,128)(2,1)S(1)}, u32[]{:S(2)}, u32[]{:S(2)}) %collective-permute-start.19) | collective-permute-done | bytes 16416 | tf_op jit(solution)/shard_map/ppermute | solution.py:61
  (46 shorter events, 24.0 us)
Async XLA Ops:
  1.5 7.8 %collective-permute-start = (bf16[1,96,128]{2,1,0:T(8,128)(2,1)S(1)}, bf16[1,96,128]{2,1,0:T(8,128)(2,1)S(1)}, u32[]{:S(2)}, u32[]{:S(2)}) collective-permute-start(bf16[1,96,128]{2,1,0:T(8,128)(2,1)S(1)} %get-tuple-element.36.after_ref.refs_0_), channel_id=1, source_target_pairs={{0,4},{1,5},{2,6},{3,7},{4,0},{5,1},{6,2},{7,3},{8,12},{9,13},{10,... | collective-permute-start | bytes 73736 | tf_op jit(solution)/shard_map/ppermute | solution.py:61
  9.2 4.5 %collective-permute-start.1 = (bf16[2,96,128]{2,1,0:T(8,128)(2,1)S(1)}, bf16[2,96,128]{2,1,0:T(8,128)(2,1)S(1)}, u32[]{:S(2)}, u32[]{:S(2)}) collective-permute-start(bf16[2,96,128]{2,1,0:T(8,128)(2,1)S(1)} %stack.3.after_ref.refs_0_), channel_id=1, source_target_pairs={{0,2},{1,3},{2,0},{3,1},{4,6},{5,7},{6,4},{7,5},{8,10},{9,11},{10,... | collective-permute-start | bytes 147464 | tf_op jit(solution)/shard_map/ppermute | solution.py:61
  13.8 4.7 %collective-permute-start.2 = (bf16[4,96,128]{2,1,0:T(8,128)(2,1)S(1)}, bf16[4,96,128]{2,1,0:T(8,128)(2,1)S(1)}, u32[]{:S(2)}, u32[]{:S(2)}) collective-permute-start(bf16[4,96,128]{2,1,0:T(8,128)(2,1)S(1)} %stack.4.after_ref.refs_0_), channel_id=1, source_target_pairs={{0,1},{1,0},{2,3},{3,2},{4,5},{5,4},{6,7},{7,6},{8,9},{9,8},{10,11... | collective-permute-start | bytes 294920 | tf_op jit(solution)/shard_map/ppermute | solution.py:61
  23.2 1.3 %collective-permute-start.3 = (f32[128,128]{1,0:T(8,128)S(1)}, f32[128,128]{1,0:T(8,128)S(1)}, u32[]{:S(2)}, u32[]{:S(2)}) collective-permute-start(f32[128,128]{1,0:T(8,128)S(1)} %project.1.refs_0_.refs_2_), channel_id=1, source_target_pairs={{0,8},{1,9},{2,10},{3,11},{4,12},{5,13},{6,14},{7,15},{8,0},{9,1},... | collective-permute-start | bytes 196616 | tf_op jit(solution)/shard_map/ppermute | solution.py:61
  24.6 0.7 collective-permute-start.4
  25.3 2.1 %collective-permute-start.5 = (f32[64,128]{1,0:T(8,128)S(1)}, f32[64,128]{1,0:T(8,128)S(1)}, u32[]{:S(2)}, u32[]{:S(2)}) collective-permute-start(f32[64,128]{1,0:T(8,128)S(1)} %get-tuple-element.49.refs_2_.refs_0_), channel_id=1, source_target_pairs={{8,9},{9,8},{10,11},{11,10},{12,13},{13,12},{14,15},{15,14},{24,25... | collective-permute-start | bytes 98312 | tf_op jit(solution)/shard_map/ppermute | solution.py:61
  27.3 1.8 %collective-permute-start.6 = (f32[64,128]{1,0:T(8,128)S(1)}, f32[64,128]{1,0:T(8,128)S(1)}, u32[]{:S(2)}, u32[]{:S(2)}) collective-permute-start(f32[64,128]{1,0:T(8,128)S(1)} %add.25.refs_1_.refs_0_), channel_id=1, source_target_pairs={{8,10},{9,11},{10,8},{11,9},{12,14},{13,15},{14,12},{15,13},{24,26... | collective-permute-start | bytes 98312 | tf_op jit(solution)/shard_map/ppermute | solution.py:61
  29.2 1.8 %collective-permute-start.7 = (f32[64,128]{1,0:T(8,128)S(1)}, f32[64,128]{1,0:T(8,128)S(1)}, u32[]{:S(2)}, u32[]{:S(2)}) collective-permute-start(f32[64,128]{1,0:T(8,128)S(1)} %add.26.refs_1_.a_ref), channel_id=1, source_target_pairs={{8,12},{9,13},{10,14},{11,15},{12,8},{13,9},{14,10},{15,11},{24,28... | collective-permute-start | bytes 98312 | tf_op jit(solution)/shard_map/ppermute | solution.py:61
  31.1 15.6 %collective-permute-start.8 = (f32[128,128]{1,0:T(8,128)S(1)}, f32[128,128]{1,0:T(8,128)S(1)}, u32[]{:S(2)}, u32[]{:S(2)}) collective-permute-start(f32[128,128]{1,0:T(8,128)S(1)} %close.1.mine_ref), channel_id=1, source_target_pairs={{8,0},{9,1},{10,2},{11,3},{12,4},{13,5},{14,6},{15,7},{24,16},{25,... | collective-permute-start | bytes 196616 | tf_op jit(solution)/shard_map/ppermute | solution.py:616
  55.0 5.6 %collective-permute-start.9 = (f32[4,64,128]{2,1,0:T(8,128)S(1)}, f32[4,64,128]{2,1,0:T(8,128)S(1)}, u32[]{:S(2)}, u32[]{:S(2)}) collective-permute-start(f32[4,64,128]{2,1,0:T(8,128)S(1)} %get-tuple-element.59.refs_2_), channel_id=1, source_target_pairs={{0,1},{1,0},{2,3},{3,2},{4,5},{5,4},{6,7},{7,6},{8,9},{9,8},{10,11... | collective-permute-start | bytes 393224 | tf_op jit(solution)/shard_map/ppermute | solution.py:61
  60.6 4.3 %collective-permute-start.10 = (f32[2,64,128]{2,1,0:T(8,128)S(1)}, f32[2,64,128]{2,1,0:T(8,128)S(1)}, u32[]{:S(2)}, u32[]{:S(2)}) collective-permute-start(f32[2,64,128]{2,1,0:T(8,128)S(1)} %get-tuple-element.61.refs_1_), channel_id=1, source_target_pairs={{0,2},{1,3},{2,0},{3,1},{4,6},{5,7},{6,4},{7,5},{8,10},{9,11},{10,... | collective-permute-start | bytes 196616 | tf_op jit(solution)/shard_map/ppermute | solution.py:61
  64.9 5.2 %collective-permute-start.11 = (f32[2,64,128]{2,1,0:T(8,128)S(1)}, f32[2,64,128]{2,1,0:T(8,128)S(1)}, u32[]{:S(2)}, u32[]{:S(2)}) collective-permute-start(f32[2,64,128]{2,1,0:T(8,128)S(1)} %add.27.refs_1_.refs_0_), channel_id=1, source_target_pairs={{0,4},{1,5},{2,6},{3,7},{4,0},{5,1},{6,2},{7,3},{8,12},{9,13},{10,... | collective-permute-start | bytes 196616 | tf_op jit(solution)/shard_map/ppermute | solution.py:61
  70.4 4.0 %collective-permute-start.12 = (bf16[2,64,128]{2,1,0:T(8,128)(2,1)S(1)}, bf16[2,64,128]{2,1,0:T(8,128)(2,1)S(1)}, u32[]{:S(2)}, u32[]{:S(2)}) collective-permute-start(bf16[2,64,128]{2,1,0:T(8,128)(2,1)S(1)} %update.1.refs_0_.refs_2_), channel_id=1, source_target_pairs={{0,2},{1,3},{2,0},{3,1},{4,6},{5,7},{6,4},{7,5},{8,10},{9,11},{10,... | collective-permute-start | bytes 98312 | tf_op jit(solution)/shard_map/ppermute | solution.py:61
  74.4 4.3 %collective-permute-start.13 = (bf16[4,64,128]{2,1,0:T(8,128)(2,1)S(1)}, bf16[4,64,128]{2,1,0:T(8,128)(2,1)S(1)}, u32[]{:S(2)}, u32[]{:S(2)}) collective-permute-start(bf16[4,64,128]{2,1,0:T(8,128)(2,1)S(1)} %stack.5.refs_0_), channel_id=1, source_target_pairs={{0,1},{1,0},{2,3},{3,2},{4,5},{5,4},{6,7},{7,6},{8,9},{9,8},{10,11... | collective-permute-start | bytes 196616 | tf_op jit(solution)/shard_map/ppermute | solution.py:61
  80.3 1.3 %collective-permute-start.14 = (f32[64,128]{1,0:T(8,128)S(1)}, f32[64,128]{1,0:T(8,128)S(1)}, u32[]{:S(2)}, u32[]{:S(2)}) collective-permute-start(f32[64,128]{1,0:T(8,128)S(1)} %second.1.refs_0_.refs_2_), channel_id=1, source_target_pairs={{0,8},{1,9},{2,10},{3,11},{4,12},{5,13},{6,14},{7,15},{8,0},{9,1},... | collective-permute-start | bytes 98312 | tf_op jit(solution)/shard_map/ppermute | solution.py:61
  81.6 3.9 %collective-permute-start.15 = (f32[64,128]{1,0:T(8,128)S(1)}, f32[64,128]{1,0:T(8,128)S(1)}, u32[]{:S(2)}, u32[]{:S(2)}) collective-permute-start(f32[64,128]{1,0:T(8,128)S(1)} %add.28.mine_ref), channel_id=1, source_target_pairs={{0,16},{1,17},{2,18},{3,19},{4,20},{5,21},{6,22},{7,23},{8,24},{9,... | collective-permute-start | bytes 98312 | tf_op jit(solution)/shard_map/ppermute | solution.py:61
  90.9 4.3 %collective-permute-start.16 = (bf16[4,64,128]{2,1,0:T(8,128)(2,1)S(1)}, bf16[4,64,128]{2,1,0:T(8,128)(2,1)S(1)}, u32[]{:S(2)}, u32[]{:S(2)}) collective-permute-start(bf16[4,64,128]{2,1,0:T(8,128)(2,1)S(1)} %get-tuple-element.65), channel_id=1, source_target_pairs={{0,1},{1,0},{2,3},{3,2},{4,5},{5,4},{6,7},{7,6},{8,9},{9,8},{10,11... | collective-permute-start | bytes 196616 | tf_op jit(solution)/shard_map/ppermute | solution.py:61
  95.3 4.5 %collective-permute-start.17 = (bf16[64,128]{1,0:T(8,128)(2,1)S(1)}, bf16[64,128]{1,0:T(8,128)(2,1)S(1)}, u32[]{:S(2)}, u32[]{:S(2)}) collective-permute-start(bf16[64,128]{1,0:T(8,128)(2,1)S(1)} %get-tuple-element.67), channel_id=1, source_target_pairs={{0,2},{1,3},{2,0},{3,1},{4,6},{5,7},{6,4},{7,5},{8,10},{9,11},{10,... | collective-permute-start | bytes 49160 | tf_op jit(solution)/shard_map/ppermute | solution.py:61
  96.6 4.6 %collective-permute-start.18 = (bf16[64,128]{1,0:T(8,128)(2,1)S(1)}, bf16[64,128]{1,0:T(8,128)(2,1)S(1)}, u32[]{:S(2)}, u32[]{:S(2)}) collective-permute-start(bf16[64,128]{1,0:T(8,128)(2,1)S(1)} %get-tuple-element.68), channel_id=1, source_target_pairs={{0,4},{1,5},{2,6},{3,7},{4,0},{5,1},{6,2},{7,3},{8,12},{9,13},{10,... | collective-permute-start | bytes 49160 | tf_op jit(solution)/shard_map/ppermute | solution.py:61
  98.7 5.5 %collective-permute-start.19 = (bf16[64,128]{1,0:T(8,128)(2,1)S(1)}, bf16[64,128]{1,0:T(8,128)(2,1)S(1)}, u32[]{:S(2)}, u32[]{:S(2)}) collective-permute-start(bf16[64,128]{1,0:T(8,128)(2,1)S(1)} %get-tuple-element.69), channel_id=1, source_target_pairs={{0,6},{1,7},{2,4},{3,5},{4,2},{5,3},{6,0},{7,1},{8,14},{9,15},{10,... | collective-permute-start | bytes 49160 | tf_op jit(solution)/shard_map/ppermute | solution.py:61

commit v4 on v3

--- a/solution.py
+++ b/solution.py
@@ -57,8 +57,8 @@
     return [swap(x, axes, count, o) for o in offsets[1:]]
 
 
-def swap(x, axes, count, offset, only=0):
-    return lax.ppermute(x, axes, [(n, n ^ offset) for n in range(count) if n & only == only])
+def swap(x, axes, count, offset):
+    return lax.ppermute(x, axes, [(n, n ^ offset) for n in range(count)])
 
 
 def join_body(me_ref, a_hbm, b_hbm, out_ref, turned_ref, second_ref, a_ref, b_ref, sems):
@@ -128,33 +128,6 @@
     return call(add_body, shaped(parts[0].shape), specs, (*parts, after), "add", us=0.2)
 
 
-def close_body(a_ref, b_ref, inverse_ref, out_ref):
-    components = a_ref.shape[0]
-    out_ref[:components] = a_ref[...] + b_ref[...]
-    inverse = inverse_ref[...]
-    out_ref[components:] = jnp.concatenate([inverse, inverse], axis=1)
-
-
-def close(a, b, inverse):
-    shape = (2 * a.shape[0], a.shape[1])
-    return call(close_body, shaped(shape), [vmem()] * 3, (a, b, inverse), "close", us=0.2)
-
-
-def choose_body(bit, me_ref, mine_ref, got_ref, sum_ref, inverse_ref):
-    components = sum_ref.shape[0]
-    mine = jnp.full(mine_ref.shape, me_ref[0] & bit) == bit
-    chosen = jnp.where(mine, mine_ref[...], got_ref[...])
-    sum_ref[...] = chosen[:components]
-    inverse_ref[...] = chosen[components:, :components]
-
-
-def choose(me, bit, mine, got):
-    half = mine.shape[0] // 2
-    outs = (shaped((half, mine.shape[1])), shaped((half, half)))
-    specs = [smem(), vmem(), vmem()]
-    return call(functools.partial(choose_body, bit), outs, specs, (me, mine, got), "choose", us=0.2)
-
-
 def split_body(a_ref, b_ref, sum_ref, gram_ref):
     components = sum_ref.shape[0]
     sum_ref[...] = a_ref[:components] + b_ref[:components]
@@ -304,24 +277,37 @@
     )
 
 
-def eliminate(matrix, start, stop):
+def eliminate(matrix, start, stop, span=4):
     size = matrix.shape[0]
     row_at = lax.broadcasted_iota(jnp.int32, (size, size), 0)
     col_at = lax.broadcasted_iota(jnp.int32, (size, size), 1)
     lane = col_at[:1]
-    for k in range(start, stop, 2):
-        a = jnp.broadcast_to(matrix[:, k : k + 1], matrix.shape)
-        b = jnp.broadcast_to(matrix[:, k + 1 : k + 2], matrix.shape)
-        inverse_a = 1.0 / a[k : k + 1]
-        low = a[k + 1 : k + 2] * inverse_a
-        inverse_b = 1.0 / (b[k + 1 : k + 2] - b[k : k + 1] * low)
-        mine = (lane == k) | (lane == k + 1)
-        p = jnp.where(mine, jnp.where(lane == k, 1.0, 0.0), matrix[k : k + 1])
-        q = jnp.where(mine, jnp.where(lane == k, 0.0, 1.0), matrix[k + 1 : k + 2])
-        q = (q - low * p) * inverse_b
-        p = p * inverse_a - (b[k : k + 1] * inverse_a) * q
-        rest = jnp.where((col_at == k) | (col_at == k + 1), 0.0, matrix) - a * p - b * q
-        matrix = jnp.where(row_at == k, p, jnp.where(row_at == k + 1, q, rest))
+    for k in range(start, stop, span):
+        among = range(span)
+        cols = [jnp.broadcast_to(matrix[:, k + n : k + n + 1], matrix.shape) for n in among]
+        mine = (lane >= k) & (lane < k + span)
+        rows = [
+            jnp.where(mine, jnp.where(lane == k + m, 1.0, 0.0), matrix[k + m : k + m + 1]) for m in among
+        ]
+        block = [[cols[n][k + m : k + m + 1] for n in among] for m in among]
+        for m in among:
+            pivot = 1.0 / block[m][m]
+            rows[m] = rows[m] * pivot
+            for n in range(m + 1, span):
+                block[m][n] = block[m][n] * pivot
+            for other in among:
+                if other != m:
+                    factor = block[other][m]
+                    rows[other] = rows[other] - factor * rows[m]
+                    for n in range(m + 1, span):
+                        block[other][n] = block[other][n] - factor * block[m][n]
+        rest = jnp.where((col_at >= k) & (col_at < k + span), 0.0, matrix)
+        taken = cols[0] * rows[0]
+        for n in range(1, span):
+            taken = taken + cols[n] * rows[n]
+        matrix = rest - taken
+        for m in among:
+            matrix = jnp.where(row_at == k + m, rows[m], matrix)
     return matrix
 
 
@@ -380,27 +366,6 @@
     )
 
 
-def deal_body(me_ref, keep_in, got_in, after_ref, mine_ref, *outs):
-    del after_ref
-    upper = (me_ref[0] & 7) >> 1
-    mine_ref[...] = keep_in[upper] + got_in[upper].astype(F32)
-    for n, out in enumerate(outs):
-        at = upper ^ (n + 1)
-        out[...] = (keep_in[at] + got_in[at].astype(F32)).astype(out.dtype)
-
-
-def deal(me, keep, got, after):
-    count, shape = keep.shape[0], keep.shape[1:]
-    return call(
-        deal_body,
-        (shaped(shape),) + (shaped(shape, got.dtype),) * (count - 1),
-        [smem(), vmem(), vmem(), anywhere()],
-        (me, keep, got, after),
-        "deal",
-        us=0.2,
-    )
-
-
 def shares_out(direct, components, rows, width, send_type):
     if not direct:
         return (shaped((components, rows)),)
@@ -416,8 +381,9 @@
     frames_ref[...] = frames
     gram_ref[...] = dot(frames, frames, ((1,), (1,)), HIGH)
     high = frames.astype(BF16)
-    low = (frames - high.astype(F32)).astype(BF16)
-    both = jnp.concatenate([high, low], axis=1)
+    none = jnp.zeros_like(high)
+    both = jnp.concatenate([jnp.concatenate(pair, axis=1) for pair in ((high, none), (none, high))], axis=0)
+    depth = frames.shape[1]
     wide = 256
 
     def chunk(c, _):
@@ -427,13 +393,15 @@
         for t_ref, wide_ref in zip(t_refs, wide_refs):
 
             def step(n, total, t_ref=t_ref, wide_ref=wide_ref, base=base):
-                for s in range(8):
-                    j = n * 8 + s
-                    block = t_ref[j, :, lanes]
-                    z = dot(both, jnp.concatenate([block, block], axis=0), ((1,), (0,)))
-                    z_ref[base + j, :, lanes] = z
-                    scale = wide_ref[j]
-                    total = total + z * jnp.concatenate([scale, scale], axis=1)
+                for s in range(0, 8, 2):
+                    block = t_ref[pl.ds(n * 8 + s, 2), :, lanes].reshape(2 * depth, wide)
+                    product = dot(both, block, ((1,), (0,)))
+                    for h in range(2):
+                        j = n * 8 + s + h
+                        z = product[h * components : h * components + components]
+                        z_ref[base + j, :, lanes] = z
+                        scale = wide_ref[j]
+                        total = total + z * jnp.concatenate([scale, scale], axis=1)
                 return total
 
             total = lax.fori_loop(0, t_ref.shape[0] // 8, step, total)
@@ -524,7 +492,7 @@
     )
 
 
-def mode_body(me_ref, mine_ref, got_ref, gram_frames_ref, z_ref, *refs):
+def mode_body(mine_ref, got_ref, gram_frames_ref, z_ref, *refs):
     *outs, sum_ref, new_ref = refs
     cols, components, rows = z_ref.shape
     summed = mine_ref[...] + got_ref[...]
@@ -541,19 +509,23 @@
         return 0
 
     lax.fori_loop(0, components // 8, step, 0)
-    if len(outs) == 1:
-        outs[0][...] = sum_ref[...]
+    out_ref = outs[0]
+    if out_ref.shape == sum_ref.shape:
+        out_ref[...] = sum_ref[...]
     else:
-        halve_first(me_ref, sum_ref, *outs)
-
-
-def mode(me, mine, got, gram_frames, z, width, direct):
+        width = out_ref.shape[2]
+        for n in range(out_ref.shape[0]):
+            out_ref[n] = sum_ref[:, n * width : n * width + width].astype(out_ref.dtype)
+
+
+def mode(mine, got, gram_frames, z, width, direct):
     cols, components, rows = z.shape
+    out = shaped((rows // width, components, width), BF16) if direct else shaped((components, rows))
     return call(
         mode_body,
-        shares_out(direct, components, rows, width, BF16),
-        [smem()] + [vmem()] * 4,
-        (me, mine, got, gram_frames, z),
+        out,
+        [vmem()] * 4,
+        (mine, got, gram_frames, z),
         "mode",
         [VM((components, rows), F32), VM((components, 2 * components), F32)],
         us=5,
@@ -604,18 +576,15 @@
     total = project(first_turned, second_turned, gram_first, turned)
     core, upper = row_bits[0], row_bits[1:]
     total = add([total, swap(total, BOTH, every, core)], total)
-    total, gram_first = split_add(total, swap(total, BOTH, every, upper[0], core))
+    total, gram_first = split_add(total, swap(total, BOTH, every, upper[0] | core))
     state = (gram_first, gram_second)
     marks = [0, 24, 44, components]
-    bits = upper[1:] + col_bits
-    for n, bit in enumerate(bits):
-        got = swap(total, BOTH, every, bit, core)
+    for n, bit in enumerate(upper[1:] + col_bits):
+        got = swap(total, BOTH, every, bit | core)
         if n < 3:
             state = (eliminate_part(state, marks[n], marks[n + 1], total),)
-        total = add([total, got], state[0]) if n < len(bits) - 1 else close(total, got, state[0])
-    handed = lax.ppermute(total, BOTH, [(n, n ^ core) for n in range(every) if n & core])
-    total, inverse_first = choose(me, core, total, handed)
-    frames, gram_frames, z, *outs = slab(me, inverse_first, total, turned, wides, width, direct)
+        total = add([total, got], state[0])
+    frames, gram_frames, z, *outs = slab(me, state[0], total, turned, wides, width, direct)
 
     state = (gram_second, gram_frames)
     if direct:
@@ -637,16 +606,13 @@
         new = update(state[0], [summed[None]])[0]
         stacks = [lax.all_gather(new, "col", axis=1, tiled=True)[None]]
     part = second(me, stacks, order, z)
-    for bit in row_bits[:-1]:
-        part = add([part, swap(part, BOTH, every, bit)], part)
-    got = swap(part, BOTH, every, row_bits[-1])
-    outs = mode(me, part, got, gram_frames, z, width, direct)
+    part = add([part, swap(part, BOTH, every, core)], part)
+    got = swap(part, BOTH, every, upper[0] | core)
+    out = mode(part, got, gram_frames, z, width, direct)
     if not direct:
-        return (frames, lax.psum_scatter(outs[0], "col", scatter_dimension=1, tiled=True))
-    keep, send = outs
-    mine, *send = deal(me, keep, swap(send, "col", col_size, 1), keep)
-    parts = [swap(x, "col", col_size, 2 * n + 2) for n, x in enumerate(send)]
-    return (frames, paired([mine] + [x.astype(F32) for x in parts]))
+        return (frames, lax.psum_scatter(out, "col", scatter_dimension=1, tiled=True))
+    shares = lax.all_to_all(out, "col", 0, 0)
+    return (frames, paired([shares[n].astype(F32) for n in range(col_size)]))
 
 
 def solution(mesh):

time: 105 us -> 94 us (0.90)
  waiting for transfers between devices: 39.6 us -> 27 us
  blocking collectives: 0 us -> 12.2 us
  starting transfers between devices: 25.8 us -> 20.3 us
  Pallas kernels: 37.9 us -> 32.7 us
    ppermute x20 -> x15, waiting for transfers between devices: 39.6 us -> 27 us  [swap(): return lax.ppermute(x, axes, [(n, n ^ offset) for n in range(count)])]
    all_to_all x0 -> x1, blocking collectives: none -> 12.2 us  [local(): shares = lax.all_to_all(out, 'col', 0, 0)]
    ppermute x20 -> x15, starting transfers between devices: 25.8 us -> 20.3 us  [swap(): return lax.ppermute(x, axes, [(n, n ^ offset) for n in range(count)])]
    pallas_call x29 -> x27, Pallas kernels: 37.9 us -> 32.7 us  [call(): pl.pallas_call(body, out_shape=outs, in_specs=ins, out_specs=(vmem(),) *...]
  transfers between devices with their start and end apart: 20 -> 15, of which waited for: 13 -> 13; matrix products, arithmetic and copies ran while one was open for 0% -> 0% of each run, Pallas kernels for 16% -> 15%
where the time goes in v4:
time: 94 us; the launch traced here: 93.6 us
  Pallas kernels  32.7 us (35%)
  waiting for transfers between devices  27 us (29%)
  starting transfers between devices  20.3 us (22%)
  blocking collectives  12.2 us (13%)
    pallas_call x27, Pallas kernels, call(): pl.pallas_call(body, out_shape=outs, in_specs=ins, out_specs=(vmem(),) *...  32.7 us
    ppermute x15, waiting for transfers between devices, swap(): return lax.ppermute(x, axes, [(n, n ^ offset) for n in range(count)])  27 us
    ppermute x15, starting transfers between devices, swap(): return lax.ppermute(x, axes, [(n, n ^ offset) for n in range(count)])  20.3 us
    all_to_all x1, blocking collectives, local(): shares = lax.all_to_all(out, 'col', 0, 0)  12.2 us
  transfers between devices with their start and end apart: 15, of which 13 were waited for; matrix products, arithmetic and copies ran while one was open for 0% of the time, Pallas kernels for 15%

profile of v4, /device:TPU:0, one launch (start us, length us, event | category | flops | bytes accessed | tf_op | source)
XLA Modules:
  0.0 93.6 jit_solution(10062168526660786236)
XLA Ops:
  1.5 4.1 %collective-permute-start = (bf16[1,96,128]{2,1,0:T(8,128)(2,1)S(1)}, bf16[1,96,128]{2,1,0:T(8,128)(2,1)S(1)}, u32[]{:S(2)}, u32[]{:S(2)}) collective-permute-start(bf16[1,96,128]{2,1,0:T(8,128)(2,1)S(1)} %get-tuple-element.28.after_ref.refs_0_), channel_id=1, source_target_pairs={{0,4},{1,5},{2,6},{3,7},{4,0},{5,1},{6,2},{7,3},{8,12},{9,13},{10,... | collective-permute-start | bytes 73736 | tf_op jit(solution)/shard_map/ppermute | solution.py:61
  5.6 3.6 %prepare.3 = (bf16[16,128,1024]{2,1,0:T(8,128)(2,1)S(1)}, f32[16,64,128]{2,1,0:T(8,128)S(1)}, f32[8,128]{1,0:T(8,128)S(1)}, bf16[8,16,16,1024]{3,2,1,0:T(8,128)(2,1)S(1)}) custom-call(bf16[128,48,1024]{2,1,0:T(8,128)(2,1)} %t_ref.5, f32[64,128]{1,0:T(8,128)S(1)} %get-tuple-element.29.b_ref, bf16[1,96,128]{2,1,0:T(8,128)(2,1)S(1)} %get-tuple-element.28.after_ref.refs_0_), custom_call_target="tpu_custom_call" | custom-call | bytes 6000000 | tf_op jit(solution)/shard_map/prepare/pallas_call | solution.py:37
  9.2 1.6 %collective-permute-start.1 = (bf16[2,96,128]{2,1,0:T(8,128)(2,1)S(1)}, bf16[2,96,128]{2,1,0:T(8,128)(2,1)S(1)}, u32[]{:S(2)}, u32[]{:S(2)}) collective-permute-start(bf16[2,96,128]{2,1,0:T(8,128)(2,1)S(1)} %stack.3.after_ref.refs_0_), channel_id=1, source_target_pairs={{0,2},{1,3},{2,0},{3,1},{4,6},{5,7},{6,4},{7,5},{8,10},{9,11},{10,... | collective-permute-start | bytes 147464 | tf_op jit(solution)/shard_map/ppermute | solution.py:61
  10.9 2.8 %prepare.4 = (bf16[16,128,1024]{2,1,0:T(8,128)(2,1)S(1)}, f32[16,64,128]{2,1,0:T(8,128)S(1)}, f32[8,128]{1,0:T(8,128)S(1)}, bf16[8,16,16,1024]{3,2,1,0:T(8,128)(2,1)S(1)}) custom-call(bf16[128,48,1024]{2,1,0:T(8,128)(2,1)} %t_ref.5, f32[64,128]{1,0:T(8,128)S(1)} %get-tuple-element.29.b_ref, bf16[2,96,128]{2,1,0:T(8,128)(2,1)S(1)} %stack.3.after_ref.refs_0_, ...), custom_call_target="tpu_custom_call" | custom-call | bytes 6000000 | tf_op jit(solution)/shard_map/prepare/pallas_call | solution.py:37
  13.8 1.6 %collective-permute-start.2 = (bf16[4,96,128]{2,1,0:T(8,128)(2,1)S(1)}, bf16[4,96,128]{2,1,0:T(8,128)(2,1)S(1)}, u32[]{:S(2)}, u32[]{:S(2)}) collective-permute-start(bf16[4,96,128]{2,1,0:T(8,128)(2,1)S(1)} %stack.4.after_ref.refs_0_), channel_id=1, source_target_pairs={{0,1},{1,0},{2,3},{3,2},{4,5},{5,4},{6,7},{7,6},{8,9},{9,8},{10,11... | collective-permute-start | bytes 294920 | tf_op jit(solution)/shard_map/ppermute | solution.py:61
  15.3 2.8 %prepare.5 = (bf16[16,128,1024]{2,1,0:T(8,128)(2,1)S(1)}, f32[16,64,128]{2,1,0:T(8,128)S(1)}, f32[8,128]{1,0:T(8,128)S(1)}) custom-call(bf16[128,48,1024]{2,1,0:T(8,128)(2,1)} %t_ref.5, f32[64,128]{1,0:T(8,128)S(1)} %get-tuple-element.29.b_ref, bf16[4,96,128]{2,1,0:T(8,128)(2,1)S(1)} %stack.4.after_ref.refs_0_, ...), custom_call_target="tpu_custom_call" | custom-call | bytes 6000000 | tf_op jit(solution)/shard_map/prepare/pallas_call | solution.py:37
  18.8 4.4 %project.1.refs_0_.refs_2_ = f32[128,128]{1,0:T(8,128)S(1)} custom-call(bf16[1024,64]{1,0:T(8,128)(2,1)S(1)} %get-tuple-element.35.turned_ref, f32[48,64]{1,0:T(8,128)S(1)} %get-tuple-element.36.second_ref, f32[64,64]{1,0:T(8,128)S(1)} %get-tuple-element.37.gram_ref, bf16[16,128,1024]{2,1,0:T(8,128)(2,1)S(1)} %get-tuple-element.38.refs_0_, ...), custom_call_target="tpu_custom_call" | custom-call | bytes 15000000 | tf_op jit(solution)/shard_map/project/pallas_call | solution.py:37
  24.6 1.3 %collective-permute-start.4 = (f32[128,128]{1,0:T(8,128)S(1)}, f32[128,128]{1,0:T(8,128)S(1)}, u32[]{:S(2)}, u32[]{:S(2)}) collective-permute-start(f32[128,128]{1,0:T(8,128)S(1)} %add.55.a_ref), channel_id=1, source_target_pairs={{0,24},{1,25},{2,26},{3,27},{4,28},{5,29},{6,30},{7,31},{8,16},{9,... | collective-permute-start | bytes 196616 | tf_op jit(solution)/shard_map/ppermute | solution.py:61
  25.9 2.8 %collective-permute-done.4.b_ref = f32[128,128]{1,0:T(8,128)S(1)} collective-permute-done((f32[128,128]{1,0:T(8,128)S(1)}, f32[128,128]{1,0:T(8,128)S(1)}, u32[]{:S(2)}, u32[]{:S(2)}) %collective-permute-start.4) | collective-permute-done | bytes 65568 | tf_op jit(solution)/shard_map/ppermute | solution.py:61
  28.7 1.3 %collective-permute-start.5 = (f32[64,128]{1,0:T(8,128)S(1)}, f32[64,128]{1,0:T(8,128)S(1)}, u32[]{:S(2)}, u32[]{:S(2)}) collective-permute-start(f32[64,128]{1,0:T(8,128)S(1)} %get-tuple-element.43.refs_2_.refs_0_), channel_id=1, source_target_pairs={{0,9},{1,8},{2,11},{3,10},{4,13},{5,12},{6,15},{7,14},{8,1},{9,0},... | collective-permute-start | bytes 98312 | tf_op jit(solution)/shard_map/ppermute | solution.py:61
  33.8 1.6 %collective-permute-done.6.refs_1_ = f32[64,128]{1,0:T(8,128)S(1)} collective-permute-done((f32[64,128]{1,0:T(8,128)S(1)}, f32[64,128]{1,0:T(8,128)S(1)}, u32[]{:S(2)}, u32[]{:S(2)}) %collective-permute-start.6) | collective-permute-done | bytes 32800 | tf_op jit(solution)/shard_map/ppermute | solution.py:61
  37.1 2.6 %collective-permute-done.7.refs_1_ = f32[64,128]{1,0:T(8,128)S(1)} collective-permute-done((f32[64,128]{1,0:T(8,128)S(1)}, f32[64,128]{1,0:T(8,128)S(1)}, u32[]{:S(2)}, u32[]{:S(2)}) %collective-permute-start.7) | collective-permute-done | bytes 32800 | tf_op jit(solution)/shard_map/ppermute | solution.py:61
  39.7 6.8 %slab.1 = (f32[64,128]{1,0:T(8,128)}, f32[64,64]{1,0:T(8,128)S(1)}, f32[48,64,1024]{2,1,0:T(8,128)S(1)}, f32[4,64,128]{2,1,0:T(8,128)S(1)}, f32[4,64,128]{2,1,0:T(8,128)S(1)}) custom-call(s32[1]{0:T(128)} %bitcast.me_ref, f32[64,64]{1,0:T(8,128)S(1)} %eliminate.8.refs_2_.inverse_ref, f32[64,128]{1,0:T(8,128)S(1)} %add.58.summed_ref, ...), custom_call_target="tpu_custom_call" | custom-call | bytes 24000000 | tf_op jit(solution)/shard_map/slab/pallas_call | solution.py:37
  46.6 1.5 %collective-permute-start.8 = (f32[4,64,128]{2,1,0:T(8,128)S(1)}, f32[4,64,128]{2,1,0:T(8,128)S(1)}, u32[]{:S(2)}, u32[]{:S(2)}) collective-permute-start(f32[4,64,128]{2,1,0:T(8,128)S(1)} %get-tuple-element.49.refs_2_), channel_id=1, source_target_pairs={{0,1},{1,0},{2,3},{3,2},{4,5},{5,4},{6,7},{7,6},{8,9},{9,8},{10,11... | collective-permute-start | bytes 393224 | tf_op jit(solution)/shard_map/ppermute | solution.py:61
  49.0 3.1 %collective-permute-done.8.got_in = f32[4,64,128]{2,1,0:T(8,128)S(1)} collective-permute-done((f32[4,64,128]{2,1,0:T(8,128)S(1)}, f32[4,64,128]{2,1,0:T(8,128)S(1)}, u32[]{:S(2)}, u32[]{:S(2)}) %collective-permute-start.8) | collective-permute-done | bytes 131104 | tf_op jit(solution)/shard_map/ppermute | solution.py:61
  54.2 2.3 %collective-permute-done.9.refs_1_ = f32[2,64,128]{2,1,0:T(8,128)S(1)} collective-permute-done((f32[2,64,128]{2,1,0:T(8,128)S(1)}, f32[2,64,128]{2,1,0:T(8,128)S(1)}, u32[]{:S(2)}, u32[]{:S(2)}) %collective-permute-start.9) | collective-permute-done | bytes 65568 | tf_op jit(solution)/shard_map/ppermute | solution.py:61
  58.5 3.2 %collective-permute-done.10.refs_1_ = f32[2,64,128]{2,1,0:T(8,128)S(1)} collective-permute-done((f32[2,64,128]{2,1,0:T(8,128)S(1)}, f32[2,64,128]{2,1,0:T(8,128)S(1)}, u32[]{:S(2)}, u32[]{:S(2)}) %collective-permute-start.10) | collective-permute-done | bytes 65568 | tf_op jit(solution)/shard_map/ppermute | solution.py:61
  63.2 2.7 %collective-permute-done.11.refs_1_ = bf16[2,64,128]{2,1,0:T(8,128)(2,1)S(1)} collective-permute-done((bf16[2,64,128]{2,1,0:T(8,128)(2,1)S(1)}, bf16[2,64,128]{2,1,0:T(8,128)(2,1)S(1)}, u32[]{:S(2)}, u32[]{:S(2)}) %collective-permute-start.11) | collective-permute-done | bytes 32800 | tf_op jit(solution)/shard_map/ppermute | solution.py:61
  65.9 1.5 %collective-permute-start.12 = (bf16[4,64,128]{2,1,0:T(8,128)(2,1)S(1)}, bf16[4,64,128]{2,1,0:T(8,128)(2,1)S(1)}, u32[]{:S(2)}, u32[]{:S(2)}) collective-permute-start(bf16[4,64,128]{2,1,0:T(8,128)(2,1)S(1)} %stack.5.refs_0_), channel_id=1, source_target_pairs={{0,1},{1,0},{2,3},{3,2},{4,5},{5,4},{6,7},{7,6},{8,9},{9,8},{10,11... | collective-permute-start | bytes 196616 | tf_op jit(solution)/shard_map/ppermute | solution.py:61
  67.4 2.7 %collective-permute-done.12.refs_1_ = bf16[4,64,128]{2,1,0:T(8,128)(2,1)S(1)} collective-permute-done((bf16[4,64,128]{2,1,0:T(8,128)(2,1)S(1)}, bf16[4,64,128]{2,1,0:T(8,128)(2,1)S(1)}, u32[]{:S(2)}, u32[]{:S(2)}) %collective-permute-start.12) | collective-permute-done | bytes 65568 | tf_op jit(solution)/shard_map/ppermute | solution.py:61
  70.2 1.7 %second.1.refs_0_.refs_2_ = f32[64,128]{1,0:T(8,128)S(1)} custom-call(s32[1]{0:T(128)} %bitcast.me_ref, bf16[4,64,128]{2,1,0:T(8,128)(2,1)S(1)} %stack.5.refs_0_, bf16[4,64,128]{2,1,0:T(8,128)(2,1)S(1)} %collective-permute-done.12.refs_1_, f32[48,64,1024]{2,1,0:T(8,128)S(1)} %get-tuple-element.53.refs_2_.z_ref), custom_call_target="tpu_custom_call" | custom-call | bytes 6000000 | tf_op jit(solution)/shard_map/second/pallas_call | solution.py:37
  74.4 2.1 %collective-permute-done.14.got_ref = f32[64,128]{1,0:T(8,128)S(1)} collective-permute-done((f32[64,128]{1,0:T(8,128)S(1)}, f32[64,128]{1,0:T(8,128)S(1)}, u32[]{:S(2)}, u32[]{:S(2)}) %collective-permute-start.14) | collective-permute-done | bytes 32800 | tf_op jit(solution)/shard_map/ppermute | solution.py:61
  76.5 4.3 %mode.1 = bf16[8,64,128]{2,1,0:T(8,128)(2,1)S(1)} custom-call(f32[64,128]{1,0:T(8,128)S(1)} %add.60.mine_ref, f32[64,128]{1,0:T(8,128)S(1)} %collective-permute-done.14.got_ref, f32[64,64]{1,0:T(8,128)S(1)} %get-tuple-element.48.refs_1_.gram_frames_ref, f32[48,64,1024]{2,1,0:T(8,128)S(1)} %get-tuple-element.53.refs_2_.z_ref), custom_call_target="tpu_custom_call" | custom-call | bytes 15000000 | tf_op jit(solution)/shard_map/mode/pallas_call | solution.py:37
  80.8 12.2 %all_to_all.5 = bf16[8,64,128]{2,1,0:T(8,128)(2,1)S(1)} all-to-all(bf16[8,64,128]{2,1,0:T(8,128)(2,1)S(1)} %mode.1), channel_id=1, replica_groups=mesh['row'=4,'col'=8] {'col'}, dimensions={0} | all-to-all | bytes 262144 | tf_op jit(solution)/shard_map/all_to_all | solution.py:614
  (35 shorter events, 17.9 us)
Async XLA Ops:
  1.5 7.8 %collective-permute-start = (bf16[1,96,128]{2,1,0:T(8,128)(2,1)S(1)}, bf16[1,96,128]{2,1,0:T(8,128)(2,1)S(1)}, u32[]{:S(2)}, u32[]{:S(2)}) collective-permute-start(bf16[1,96,128]{2,1,0:T(8,128)(2,1)S(1)} %get-tuple-element.28.after_ref.refs_0_), channel_id=1, source_target_pairs={{0,4},{1,5},{2,6},{3,7},{4,0},{5,1},{6,2},{7,3},{8,12},{9,13},{10,... | collective-permute-start | bytes 73736 | tf_op jit(solution)/shard_map/ppermute | solution.py:61
  9.2 4.5 %collective-permute-start.1 = (bf16[2,96,128]{2,1,0:T(8,128)(2,1)S(1)}, bf16[2,96,128]{2,1,0:T(8,128)(2,1)S(1)}, u32[]{:S(2)}, u32[]{:S(2)}) collective-permute-start(bf16[2,96,128]{2,1,0:T(8,128)(2,1)S(1)} %stack.3.after_ref.refs_0_), channel_id=1, source_target_pairs={{0,2},{1,3},{2,0},{3,1},{4,6},{5,7},{6,4},{7,5},{8,10},{9,11},{10,... | collective-permute-start | bytes 147464 | tf_op jit(solution)/shard_map/ppermute | solution.py:61
  13.8 4.7 %collective-permute-start.2 = (bf16[4,96,128]{2,1,0:T(8,128)(2,1)S(1)}, bf16[4,96,128]{2,1,0:T(8,128)(2,1)S(1)}, u32[]{:S(2)}, u32[]{:S(2)}) collective-permute-start(bf16[4,96,128]{2,1,0:T(8,128)(2,1)S(1)} %stack.4.after_ref.refs_0_), channel_id=1, source_target_pairs={{0,1},{1,0},{2,3},{3,2},{4,5},{5,4},{6,7},{7,6},{8,9},{9,8},{10,11... | collective-permute-start | bytes 294920 | tf_op jit(solution)/shard_map/ppermute | solution.py:61
  23.2 1.3 %collective-permute-start.3 = (f32[128,128]{1,0:T(8,128)S(1)}, f32[128,128]{1,0:T(8,128)S(1)}, u32[]{:S(2)}, u32[]{:S(2)}) collective-permute-start(f32[128,128]{1,0:T(8,128)S(1)} %project.1.refs_0_.refs_2_), channel_id=1, source_target_pairs={{0,8},{1,9},{2,10},{3,11},{4,12},{5,13},{6,14},{7,15},{8,0},{9,1},... | collective-permute-start | bytes 196616 | tf_op jit(solution)/shard_map/ppermute | solution.py:61
  24.6 4.1 %collective-permute-start.4 = (f32[128,128]{1,0:T(8,128)S(1)}, f32[128,128]{1,0:T(8,128)S(1)}, u32[]{:S(2)}, u32[]{:S(2)}) collective-permute-start(f32[128,128]{1,0:T(8,128)S(1)} %add.55.a_ref), channel_id=1, source_target_pairs={{0,24},{1,25},{2,26},{3,27},{4,28},{5,29},{6,30},{7,31},{8,16},{9,... | collective-permute-start | bytes 196616 | tf_op jit(solution)/shard_map/ppermute | solution.py:61
  28.7 3.4 %collective-permute-start.5 = (f32[64,128]{1,0:T(8,128)S(1)}, f32[64,128]{1,0:T(8,128)S(1)}, u32[]{:S(2)}, u32[]{:S(2)}) collective-permute-start(f32[64,128]{1,0:T(8,128)S(1)} %get-tuple-element.43.refs_2_.refs_0_), channel_id=1, source_target_pairs={{0,9},{1,8},{2,11},{3,10},{4,13},{5,12},{6,15},{7,14},{8,1},{9,0},... | collective-permute-start | bytes 98312 | tf_op jit(solution)/shard_map/ppermute | solution.py:61
  32.1 3.3 %collective-permute-start.6 = (f32[64,128]{1,0:T(8,128)S(1)}, f32[64,128]{1,0:T(8,128)S(1)}, u32[]{:S(2)}, u32[]{:S(2)}) collective-permute-start(f32[64,128]{1,0:T(8,128)S(1)} %add.56.refs_1_.refs_0_), channel_id=1, source_target_pairs={{0,10},{1,11},{2,8},{3,9},{4,14},{5,15},{6,12},{7,13},{8,2},{9,3},... | collective-permute-start | bytes 98312 | tf_op jit(solution)/shard_map/ppermute | solution.py:61
  35.5 4.2 %collective-permute-start.7 = (f32[64,128]{1,0:T(8,128)S(1)}, f32[64,128]{1,0:T(8,128)S(1)}, u32[]{:S(2)}, u32[]{:S(2)}) collective-permute-start(f32[64,128]{1,0:T(8,128)S(1)} %add.57.refs_1_.refs_0_), channel_id=1, source_target_pairs={{0,12},{1,13},{2,14},{3,15},{4,8},{5,9},{6,10},{7,11},{8,4},{9,5},... | collective-permute-start | bytes 98312 | tf_op jit(solution)/shard_map/ppermute | solution.py:61
  46.6 5.6 %collective-permute-start.8 = (f32[4,64,128]{2,1,0:T(8,128)S(1)}, f32[4,64,128]{2,1,0:T(8,128)S(1)}, u32[]{:S(2)}, u32[]{:S(2)}) collective-permute-start(f32[4,64,128]{2,1,0:T(8,128)S(1)} %get-tuple-element.49.refs_2_), channel_id=1, source_target_pairs={{0,1},{1,0},{2,3},{3,2},{4,5},{5,4},{6,7},{7,6},{8,9},{9,8},{10,11... | collective-permute-start | bytes 393224 | tf_op jit(solution)/shard_map/ppermute | solution.py:61
  52.1 4.3 %collective-permute-start.9 = (f32[2,64,128]{2,1,0:T(8,128)S(1)}, f32[2,64,128]{2,1,0:T(8,128)S(1)}, u32[]{:S(2)}, u32[]{:S(2)}) collective-permute-start(f32[2,64,128]{2,1,0:T(8,128)S(1)} %get-tuple-element.51.refs_1_), channel_id=1, source_target_pairs={{0,2},{1,3},{2,0},{3,1},{4,6},{5,7},{6,4},{7,5},{8,10},{9,11},{10,... | collective-permute-start | bytes 196616 | tf_op jit(solution)/shard_map/ppermute | solution.py:61
  56.5 5.2 %collective-permute-start.10 = (f32[2,64,128]{2,1,0:T(8,128)S(1)}, f32[2,64,128]{2,1,0:T(8,128)S(1)}, u32[]{:S(2)}, u32[]{:S(2)}) collective-permute-start(f32[2,64,128]{2,1,0:T(8,128)S(1)} %add.59.refs_1_.refs_0_), channel_id=1, source_target_pairs={{0,4},{1,5},{2,6},{3,7},{4,0},{5,1},{6,2},{7,3},{8,12},{9,13},{10,... | collective-permute-start | bytes 196616 | tf_op jit(solution)/shard_map/ppermute | solution.py:61
  61.9 4.0 %collective-permute-start.11 = (bf16[2,64,128]{2,1,0:T(8,128)(2,1)S(1)}, bf16[2,64,128]{2,1,0:T(8,128)(2,1)S(1)}, u32[]{:S(2)}, u32[]{:S(2)}) collective-permute-start(bf16[2,64,128]{2,1,0:T(8,128)(2,1)S(1)} %update.1.refs_0_.refs_2_), channel_id=1, source_target_pairs={{0,2},{1,3},{2,0},{3,1},{4,6},{5,7},{6,4},{7,5},{8,10},{9,11},{10,... | collective-permute-start | bytes 98312 | tf_op jit(solution)/shard_map/ppermute | solution.py:61
  65.9 4.3 %collective-permute-start.12 = (bf16[4,64,128]{2,1,0:T(8,128)(2,1)S(1)}, bf16[4,64,128]{2,1,0:T(8,128)(2,1)S(1)}, u32[]{:S(2)}, u32[]{:S(2)}) collective-permute-start(bf16[4,64,128]{2,1,0:T(8,128)(2,1)S(1)} %stack.5.refs_0_), channel_id=1, source_target_pairs={{0,1},{1,0},{2,3},{3,2},{4,5},{5,4},{6,7},{7,6},{8,9},{9,8},{10,11... | collective-permute-start | bytes 196616 | tf_op jit(solution)/shard_map/ppermute | solution.py:61
  71.9 1.3 %collective-permute-start.13 = (f32[64,128]{1,0:T(8,128)S(1)}, f32[64,128]{1,0:T(8,128)S(1)}, u32[]{:S(2)}, u32[]{:S(2)}) collective-permute-start(f32[64,128]{1,0:T(8,128)S(1)} %second.1.refs_0_.refs_2_), channel_id=1, source_target_pairs={{0,8},{1,9},{2,10},{3,11},{4,12},{5,13},{6,14},{7,15},{8,0},{9,1},... | collective-permute-start | bytes 98312 | tf_op jit(solution)/shard_map/ppermute | solution.py:61
  73.2 3.3 %collective-permute-start.14 = (f32[64,128]{1,0:T(8,128)S(1)}, f32[64,128]{1,0:T(8,128)S(1)}, u32[]{:S(2)}, u32[]{:S(2)}) collective-permute-start(f32[64,128]{1,0:T(8,128)S(1)} %add.60.mine_ref), channel_id=1, source_target_pairs={{0,24},{1,25},{2,26},{3,27},{4,28},{5,29},{6,30},{7,31},{8,16},{9,... | collective-permute-start | bytes 98312 | tf_op jit(solution)/shard_map/ppermute | solution.py:61

commit v5 on v4

--- a/solution.py
+++ b/solution.py
@@ -334,105 +334,88 @@
     )
 
 
-def halve_first(me_ref, sum_ref, keep_ref, send_ref):
-    if keep_ref.shape[0] == 0:
-        return
-    count, _, width = keep_ref.shape
-    bit = me_ref[0] & 1
-    for n in range(count):
-        keep_ref[n] = sum_ref[:, pl.ds(pl.multiple_of((2 * n + bit) * width, width), width)]
-        send = sum_ref[:, pl.ds(pl.multiple_of((2 * n + 1 - bit) * width, width), width)]
-        send_ref[n] = send.astype(send_ref.dtype)
-
-
-def halve_body(shift, me_ref, keep_in, got_in, after_ref, keep_ref, send_ref):
-    del after_ref
-    bit = (me_ref[0] >> shift) & 1
-    for n in range(keep_ref.shape[0]):
-        mine, other = 2 * n + bit, 2 * n + 1 - bit
-        keep_ref[n] = keep_in[mine] + got_in[mine].astype(F32)
-        send_ref[n] = (keep_in[other] + got_in[other].astype(F32)).astype(send_ref.dtype)
-
-
-def halve(me, keep, got, shift, after):
-    shape = (keep.shape[0] // 2,) + keep.shape[1:]
-    return call(
-        functools.partial(halve_body, shift),
-        (shaped(shape), shaped(shape, got.dtype)),
-        [smem(), vmem(), vmem(), anywhere()],
-        (me, keep, got, after),
-        "halve",
-        us=0.2,
-    )
-
-
-def shares_out(direct, components, rows, width, send_type):
-    if not direct:
-        return (shaped((components, rows)),)
-    shape = (rows // width // 2, components, width)
-    return (shaped(shape), shaped(shape, send_type))
-
-
-def slab_body(groups, me_ref, inverse_ref, summed_ref, *refs):
-    t_refs, wide_refs = refs[:groups], refs[groups : 2 * groups]
-    frames_ref, gram_ref, z_ref, *outs, sum_ref = refs[2 * groups :]
-    components, rows = sum_ref.shape
-    frames = dot(inverse_ref[...], summed_ref[...], ((1,), (0,)), HIGH)
-    frames_ref[...] = frames
-    gram_ref[...] = dot(frames, frames, ((1,), (1,)), HIGH)
+def block_lanes(me_ref, offset, upper):
+    at = pl.multiple_of((((me_ref[0] & 3) ^ offset) + 4 * upper) * 128, 128)
+    return pl.ds(at, 128)
+
+
+def slab_body(groups, offsets, first, me_ref, *refs):
+    heads, refs = refs[: 2 if first else 1], refs[2 if first else 1 :]
+    t_refs, wide_refs, refs = refs[:groups], refs[groups : 2 * groups], refs[2 * groups :]
+    if first:
+        frames_ref, copy_ref, *refs = refs
+        frames = dot(heads[0][...], heads[1][...], ((1,), (0,)), HIGH)
+        frames_ref[...] = frames
+        copy_ref[...] = frames
+    else:
+        frames = heads[0][...]
+    z_ref, *outs = refs
+    components, depth = frames.shape
     high = frames.astype(BF16)
     none = jnp.zeros_like(high)
     both = jnp.concatenate([jnp.concatenate(pair, axis=1) for pair in ((high, none), (none, high))], axis=0)
-    depth = frames.shape[1]
     wide = 256
-
-    def chunk(c, _):
-        lanes = pl.ds(pl.multiple_of(c * wide, wide), wide)
+    for place_at, (offset, out_ref) in enumerate(zip(offsets, outs)):
+        lanes = [block_lanes(me_ref, offset, n) for n in range(2)]
+        store = pl.ds(place_at * wide, wide)
         total = jnp.zeros((components, wide), F32)
         base = 0
         for t_ref, wide_ref in zip(t_refs, wide_refs):
 
             def step(n, total, t_ref=t_ref, wide_ref=wide_ref, base=base):
                 for s in range(0, 8, 2):
-                    block = t_ref[pl.ds(n * 8 + s, 2), :, lanes].reshape(2 * depth, wide)
+                    rows = pl.ds(n * 8 + s, 2)
+                    block = jnp.concatenate([t_ref[rows, :, at].reshape(2 * depth, 128) for at in lanes], axis=1)
                     product = dot(both, block, ((1,), (0,)))
                     for h in range(2):
                         j = n * 8 + s + h
                         z = product[h * components : h * components + components]
-                        z_ref[base + j, :, lanes] = z
+                        z_ref[base + j, :, store] = z
                         scale = wide_ref[j]
                         total = total + z * jnp.concatenate([scale, scale], axis=1)
                 return total
 
             total = lax.fori_loop(0, t_ref.shape[0] // 8, step, total)
             base += t_ref.shape[0]
-        sum_ref[:, lanes] = total
-        return 0
-
-    lax.fori_loop(0, rows // wide, chunk, 0)
-    if len(outs) == 1:
-        outs[0][...] = sum_ref[...]
-    else:
-        halve_first(me_ref, sum_ref, *outs)
-
-
-def slab(me, inverse_first, frame_sum, turned, wides, width, direct):
-    _, frames, rows = turned[0].shape
-    components = inverse_first.shape[0]
-    groups = len(turned)
-    return call(
-        functools.partial(slab_body, groups),
-        (
-            shaped((components, frames)),
-            shaped((components, components)),
-            VM((sum(t.shape[0] for t in turned), components, rows), F32),
-        )
-        + shares_out(direct, components, rows, width, F32),
-        [smem()] + [vmem()] * (2 + 2 * groups),
-        (me, inverse_first, frame_sum, *turned, *wides),
+        for n in range(2):
+            out_ref[n] = total[:, n * 128 : n * 128 + 128]
+
+
+def slab(me, heads, turned, wides, offsets):
+    _, frames, _ = turned[0].shape
+    components = wides[0].shape[1]
+    first = len(heads) == 2
+    cols = sum(t.shape[0] for t in turned)
+    outs = (VM((cols, components, 256 * len(offsets)), F32),) + (shaped((2, components, 128)),) * len(offsets)
+    if first:
+        outs = (shaped((components, frames)),) * 2 + outs
+    return call(
+        functools.partial(slab_body, len(turned), offsets, first),
+        outs,
+        [smem()] + [vmem()] * (len(heads) + 2 * len(turned)),
+        (me, *heads, *turned, *wides),
         "slab",
-        [VM((components, rows), F32)],
-        us=8,
+        us=2 * len(offsets),
+    )
+
+
+def frames_gram_body(stop, frames_ref, other_ref, after_ref, gram_ref, out_ref):
+    del after_ref
+    frames = frames_ref[...]
+    gram = dot(frames, frames, ((1,), (1,)), HIGH)
+    gram_ref[...] = gram
+    out_ref[...] = eliminate(ridged(gram * other_ref[...]), 0, stop)
+
+
+def frames_gram(frames, other, stop, after):
+    square = shaped(other.shape)
+    return call(
+        functools.partial(frames_gram_body, stop),
+        (square, square),
+        [vmem(), vmem(), anywhere()],
+        (frames, other, after),
+        "frames_gram",
+        us=2,
     )
 
 
@@ -453,11 +436,12 @@
     )
 
 
-def second_body(offsets, me_ref, *refs):
-    *stacks, z_ref, out_ref, full_ref = refs
-    cols, components, rows = z_ref.shape
+def second_body(*refs):
+    *stacks, kept_ref, sent_ref, out_ref, full_ref = refs
+    cols, components, near = kept_ref.shape
     blocks = [s[n] for s in stacks for n in range(s.shape[0])]
-    place(me_ref[0] & 3, list(zip(offsets, blocks)), blocks[0].shape[1], full_ref)
+    for n, block in enumerate(blocks):
+        full_ref[:, n * 128 : n * 128 + 128] = block.astype(F32)
     lane = lax.broadcasted_iota(jnp.int32, (8, 128), 1)
 
     def step(n, _):
@@ -465,10 +449,9 @@
         mine = full_ref[at, :]
         total = jnp.zeros((8, 128), F32)
         for j in range(cols):
-            product = z_ref[j, at, :] * mine
-            folded = product[:, :128]
-            for c in range(1, rows // 128):
-                folded = folded + product[:, c * 128 : c * 128 + 128]
+            products = kept_ref[j, at, :] * mine[:, :near], sent_ref[j, at, :] * mine[:, near:]
+            folds = [p[:, c : c + 128] for p in products for c in range(0, p.shape[1], 128)]
+            folded = paired(folds)
             total = jnp.where(lane == j, jnp.sum(folded, axis=1, keepdims=True), total)
         out_ref[at, :] = total
         return 0
@@ -479,56 +462,93 @@
     out_ref[...] = jnp.concatenate([out_ref[:, :components], gram], axis=1)
 
 
-def second(me, stacks, offsets, z):
-    cols, components, rows = z.shape
-    return call(
-        functools.partial(second_body, offsets),
+def second(stacks, kept, sent):
+    components = kept.shape[1]
+    return call(
+        second_body,
         shaped((components, 2 * components)),
-        [smem()] + [vmem()] * (1 + len(stacks)),
-        (me, *stacks, z),
+        [vmem()] * (2 + len(stacks)),
+        (*stacks, kept, sent),
         "second",
-        [VM((components, rows), F32)],
+        [VM((components, kept.shape[2] + sent.shape[2]), F32)],
         us=2,
     )
 
 
-def mode_body(mine_ref, got_ref, gram_frames_ref, z_ref, *refs):
-    *outs, sum_ref, new_ref = refs
-    cols, components, rows = z_ref.shape
+def mode_sums(new_ref, parts, out_ref):
+    components = new_ref.shape[0]
+
+    def step(n, _):
+        at = pl.ds(pl.multiple_of(n * 8, 8), 8)
+        scale = new_ref[at, :]
+        totals = [jnp.zeros((8, 256), F32) for _ in parts]
+        for j in range(parts[0][0].shape[0]):
+            factor = scale[:, j : j + 1]
+            totals = [t + z[j, at, lane : lane + 256] * factor for t, (z, lane) in zip(totals, parts)]
+        for p, total in enumerate(totals):
+            for h in range(2):
+                out_ref[2 * p + h, at, :] = total[:, h * 128 : h * 128 + 128]
+        return 0
+
+    lax.fori_loop(0, components // 8, step, 0)
+
+
+def mode_send_body(mine_ref, got_ref, gram_frames_ref, sent_ref, new_ref, out_ref, sums_ref):
+    components = new_ref.shape[0]
     summed = mine_ref[...] + got_ref[...]
     solver = eliminate(ridged(summed[:, components:] * gram_frames_ref[...]), 0, components)
     new_ref[...] = dot(solver, summed, ((1,), (0,)), HIGH)
-
-    def step(n, _):
-        at = pl.ds(pl.multiple_of(n * 8, 8), 8)
-        scale = new_ref[at, :]
-        total = jnp.zeros((8, rows), F32)
-        for j in range(cols):
-            total = total + z_ref[j, at, :] * scale[:, j : j + 1]
-        sum_ref[at, :] = total
-        return 0
-
-    lax.fori_loop(0, components // 8, step, 0)
-    out_ref = outs[0]
-    if out_ref.shape == sum_ref.shape:
-        out_ref[...] = sum_ref[...]
-    else:
-        width = out_ref.shape[2]
-        for n in range(out_ref.shape[0]):
-            out_ref[n] = sum_ref[:, n * width : n * width + width].astype(out_ref.dtype)
-
-
-def mode(mine, got, gram_frames, z, width, direct):
-    cols, components, rows = z.shape
-    out = shaped((rows // width, components, width), BF16) if direct else shaped((components, rows))
-    return call(
-        mode_body,
-        out,
+    mode_sums(new_ref, [(sent_ref, 0), (sent_ref, 512)], sums_ref)
+    out_ref[...] = sums_ref[...].astype(out_ref.dtype)
+
+
+def mode_send(mine, got, gram_frames, sent, kind):
+    components = sent.shape[1]
+    shape = (4, components, 128)
+    return call(
+        mode_send_body,
+        (shaped((components, 2 * components)), shaped(shape, kind)),
         [vmem()] * 4,
-        (mine, got, gram_frames, z),
-        "mode",
-        [VM((components, rows), F32), VM((components, 2 * components), F32)],
-        us=5,
+        (mine, got, gram_frames, sent),
+        "mode_send",
+        [VM(shape, F32)],
+        us=4,
+    )
+
+
+def mode_keep_body(new_ref, kept_ref, sent_ref, after_ref, out_ref):
+    del after_ref
+    mode_sums(new_ref, [(kept_ref, 0), (sent_ref, 256)], out_ref)
+
+
+def mode_keep(new, kept, sent, after):
+    return call(
+        mode_keep_body,
+        shaped((4, kept.shape[1], 128)),
+        [vmem()] * 3 + [anywhere()],
+        (new, kept, sent, after),
+        "mode_keep",
+    )
+
+
+def deal_body(me_ref, keep_ref, got_ref, mine_ref, *outs):
+    upper = (me_ref[0] >> 2) & 1
+    places = [upper, 2 + upper, 1 - upper, 3 - upper]
+    values = [keep_ref[at] + got_ref[at].astype(F32) for at in places]
+    mine_ref[...] = values[0]
+    for out, value in zip(outs, values[1:]):
+        out[...] = value.astype(out.dtype)
+
+
+def deal(me, keep, got):
+    shape = keep.shape[1:]
+    return call(
+        deal_body,
+        (shaped(shape),) + (shaped(shape, got.dtype),) * 3,
+        [smem(), vmem(), vmem()],
+        (me, keep, got),
+        "deal",
+        us=0.2,
     )
 
 
@@ -584,35 +604,42 @@
         if n < 3:
             state = (eliminate_part(state, marks[n], marks[n + 1], total),)
         total = add([total, got], state[0])
-    frames, gram_frames, z, *outs = slab(me, state[0], total, turned, wides, width, direct)
-
-    state = (gram_second, gram_frames)
+    at = me if direct else jnp.zeros((1,), jnp.int32)
+    near, far = (0,), (1, 2, 3)
+    frames, frames_again, sent, *sends = slab(at, (state[0], total), turned, wides, far)
     if direct:
-        keep, send = outs
-        got = swap(send, "col", col_size, 1)
-        state = (eliminate_part(state, *marks[0:2], send),)
-        keep, send = halve(me, keep, got, 1, state[0])
-        got = swap(send, "col", col_size, 2)
-        state = (eliminate_part(state, *marks[1:3], send),)
-        keep = add([keep, got], state[0])
+        got = [swap(x, "col", col_size, o) for o, x in zip(far, sends)]
+    kept, keep = slab(at, (frames_again,), turned, wides, near)
+
+    gram_frames, state = frames_gram(frames_again, gram_second, 44, keep)
+    if direct:
+        keep = add([keep, *got], state)
         got = swap(keep, "col", col_size, 4)
-        state = (eliminate_part(state, *marks[2:4], keep),)
-        new = update(state[0], [keep, got])
-        new = stack([new, swap(new, "col", col_size, 2)], new)
-        stacks = [new, swap(new, "col", col_size, 1)]
+        state = eliminate_part((state,), 44, components, keep)
+        new = update(state, [keep, got])
+        stacks = [new] + [swap(new, "col", col_size, o) for o in far]
     else:
-        state = (eliminate_part(state, 0, components, outs[0]),)
-        summed = lax.psum_scatter(outs[0], "col", scatter_dimension=1, tiled=True)
-        new = update(state[0], [summed[None]])[0]
-        stacks = [lax.all_gather(new, "col", axis=1, tiled=True)[None]]
-    part = second(me, stacks, order, z)
+        state = eliminate_part((state,), 44, components, keep)
+        blocks = jnp.stack([keep, *sends]).transpose(2, 1, 0, 3).reshape(components, row_count)
+        summed = lax.psum_scatter(blocks, "col", scatter_dimension=1, tiled=True)
+        new = update(state, [summed[None]])[0]
+        new = lax.all_gather(new, "col", axis=1, tiled=True).reshape(components, 2, 4, 128)
+        stacks = list(new.transpose(2, 1, 0, 3))
+    part = second(stacks, kept, sent)
     part = add([part, swap(part, BOTH, every, core)], part)
     got = swap(part, BOTH, every, upper[0] | core)
-    out = mode(part, got, gram_frames, z, width, direct)
+
+    new_second, send = mode_send(part, got, gram_frames, sent, BF16 if direct else F32)
     if not direct:
-        return (frames, lax.psum_scatter(out, "col", scatter_dimension=1, tiled=True))
-    shares = lax.all_to_all(out, "col", 0, 0)
-    return (frames, paired([shares[n].astype(F32) for n in range(col_size)]))
+        keep = mode_keep(new_second, kept, sent, new_second)
+        odd, even = send.reshape(2, 2, components, 128), keep.reshape(2, 2, components, 128)
+        blocks = jnp.stack([even[0], odd[0], even[1], odd[1]]).transpose(2, 1, 0, 3).reshape(components, row_count)
+        return (frames, lax.psum_scatter(blocks, "col", scatter_dimension=1, tiled=True))
+    got = swap(send, "col", col_size, 1)
+    keep = mode_keep(new_second, kept, sent, send)
+    mine, *send = deal(me, keep, got)
+    got = [swap(x, "col", col_size, 2 * n + 2).astype(F32) for n, x in enumerate(send)]
+    return (frames, paired([mine, *got]))
 
 
 def solution(mesh):

time: 94 us -> 90.7 us (0.965)
  blocking collectives: 12.2 us -> 0 us
  starting transfers between devices: 20.3 us -> 28.5 us
  Pallas kernels: 32.7 us -> 35.3 us
  waiting for transfers between devices: 27 us -> 25.1 us
    all_to_all x1 -> x0, blocking collectives: 12.2 us -> none  [local(): shares = lax.all_to_all(out, 'col', 0, 0)]
    ppermute x15 -> x21, starting transfers between devices: 20.3 us -> 28.5 us  [swap(): return lax.ppermute(x, axes, [(n, n ^ offset) for n in range(count)])]
    pallas_call x27, Pallas kernels: 32.7 us -> 35.3 us  [call(): pl.pallas_call(body, out_shape=outs, in_specs=ins, out_specs=(vmem(),) *...]
    ppermute x15 -> x21, waiting for transfers between devices: 27 us -> 25.1 us  [swap(): return lax.ppermute(x, axes, [(n, n ^ offset) for n in range(count)])]
  transfers between devices with their start and end apart: 15 -> 21, of which waited for: 13 -> 15; matrix products, arithmetic and copies ran while one was open for 0% -> 0% of each run, Pallas kernels for 15% -> 19%
where the time goes in v5:
time: 90.7 us; the launch traced here: 90.3 us
  Pallas kernels  35.3 us (39%)
  starting transfers between devices  28.5 us (31%)
  waiting for transfers between devices  25.1 us (28%)
    pallas_call x27, Pallas kernels, call(): pl.pallas_call(body, out_shape=outs, in_specs=ins, out_specs=(vmem(),) *...  35.3 us
    ppermute x21, starting transfers between devices, swap(): return lax.ppermute(x, axes, [(n, n ^ offset) for n in range(count)])  28.5 us
    ppermute x21, waiting for transfers between devices, swap(): return lax.ppermute(x, axes, [(n, n ^ offset) for n in range(count)])  25.1 us
  transfers between devices with their start and end apart: 21, of which 15 were waited for; matrix products, arithmetic and copies ran while one was open for 0% of the time, Pallas kernels for 19%

profile of v5, /device:TPU:0, one launch (start us, length us, event | category | flops | bytes accessed | tf_op | source)
XLA Modules:
  0.0 90.3 jit_solution(4970347812869791745)
XLA Ops:
  1.5 4.1 %collective-permute-start = (bf16[1,96,128]{2,1,0:T(8,128)(2,1)S(1)}, bf16[1,96,128]{2,1,0:T(8,128)(2,1)S(1)}, u32[]{:S(2)}, u32[]{:S(2)}) collective-permute-start(bf16[1,96,128]{2,1,0:T(8,128)(2,1)S(1)} %get-tuple-element.37.after_ref.refs_0_), channel_id=1, source_target_pairs={{0,4},{1,5},{2,6},{3,7},{4,0},{5,1},{6,2},{7,3},{8,12},{9,13},{10,... | collective-permute-start | bytes 73736 | tf_op jit(solution)/shard_map/ppermute | solution.py:61
  5.6 3.6 %prepare.3 = (bf16[16,128,1024]{2,1,0:T(8,128)(2,1)S(1)}, f32[16,64,128]{2,1,0:T(8,128)S(1)}, f32[8,128]{1,0:T(8,128)S(1)}, bf16[8,16,16,1024]{3,2,1,0:T(8,128)(2,1)S(1)}) custom-call(bf16[128,48,1024]{2,1,0:T(8,128)(2,1)} %t_ref.5, f32[64,128]{1,0:T(8,128)S(1)} %get-tuple-element.38.b_ref, bf16[1,96,128]{2,1,0:T(8,128)(2,1)S(1)} %get-tuple-element.37.after_ref.refs_0_), custom_call_target="tpu_custom_call" | custom-call | bytes 6000000 | tf_op jit(solution)/shard_map/prepare/pallas_call | solution.py:37
  9.2 1.6 %collective-permute-start.1 = (bf16[2,96,128]{2,1,0:T(8,128)(2,1)S(1)}, bf16[2,96,128]{2,1,0:T(8,128)(2,1)S(1)}, u32[]{:S(2)}, u32[]{:S(2)}) collective-permute-start(bf16[2,96,128]{2,1,0:T(8,128)(2,1)S(1)} %stack.2.after_ref.refs_0_), channel_id=1, source_target_pairs={{0,2},{1,3},{2,0},{3,1},{4,6},{5,7},{6,4},{7,5},{8,10},{9,11},{10,... | collective-permute-start | bytes 147464 | tf_op jit(solution)/shard_map/ppermute | solution.py:61
  10.9 2.8 %prepare.4 = (bf16[16,128,1024]{2,1,0:T(8,128)(2,1)S(1)}, f32[16,64,128]{2,1,0:T(8,128)S(1)}, f32[8,128]{1,0:T(8,128)S(1)}, bf16[8,16,16,1024]{3,2,1,0:T(8,128)(2,1)S(1)}) custom-call(bf16[128,48,1024]{2,1,0:T(8,128)(2,1)} %t_ref.5, f32[64,128]{1,0:T(8,128)S(1)} %get-tuple-element.38.b_ref, bf16[2,96,128]{2,1,0:T(8,128)(2,1)S(1)} %stack.2.after_ref.refs_0_, ...), custom_call_target="tpu_custom_call" | custom-call | bytes 6000000 | tf_op jit(solution)/shard_map/prepare/pallas_call | solution.py:37
  13.8 1.6 %collective-permute-start.2 = (bf16[4,96,128]{2,1,0:T(8,128)(2,1)S(1)}, bf16[4,96,128]{2,1,0:T(8,128)(2,1)S(1)}, u32[]{:S(2)}, u32[]{:S(2)}) collective-permute-start(bf16[4,96,128]{2,1,0:T(8,128)(2,1)S(1)} %stack.3.after_ref.refs_0_), channel_id=1, source_target_pairs={{0,1},{1,0},{2,3},{3,2},{4,5},{5,4},{6,7},{7,6},{8,9},{9,8},{10,11... | collective-permute-start | bytes 294920 | tf_op jit(solution)/shard_map/ppermute | solution.py:61
  15.3 2.8 %prepare.5 = (bf16[16,128,1024]{2,1,0:T(8,128)(2,1)S(1)}, f32[16,64,128]{2,1,0:T(8,128)S(1)}, f32[8,128]{1,0:T(8,128)S(1)}) custom-call(bf16[128,48,1024]{2,1,0:T(8,128)(2,1)} %t_ref.5, f32[64,128]{1,0:T(8,128)S(1)} %get-tuple-element.38.b_ref, bf16[4,96,128]{2,1,0:T(8,128)(2,1)S(1)} %stack.3.after_ref.refs_0_, ...), custom_call_target="tpu_custom_call" | custom-call | bytes 6000000 | tf_op jit(solution)/shard_map/prepare/pallas_call | solution.py:37
  18.8 4.4 %project.1.refs_0_.refs_2_ = f32[128,128]{1,0:T(8,128)S(1)} custom-call(bf16[1024,64]{1,0:T(8,128)(2,1)S(1)} %get-tuple-element.44.turned_ref, f32[48,64]{1,0:T(8,128)S(1)} %get-tuple-element.45.second_ref, f32[64,64]{1,0:T(8,128)S(1)} %get-tuple-element.46.gram_ref, bf16[16,128,1024]{2,1,0:T(8,128)(2,1)S(1)} %get-tuple-element.47.refs_0_.refs_2_.refs_1_, ...), custom_call_target="tpu_custom_call" | custom-call | bytes 15000000 | tf_op jit(solution)/shard_map/project/pallas_call | solution.py:37
  25.9 2.8 %collective-permute-done.4.b_ref = f32[128,128]{1,0:T(8,128)S(1)} collective-permute-done((f32[128,128]{1,0:T(8,128)S(1)}, f32[128,128]{1,0:T(8,128)S(1)}, u32[]{:S(2)}, u32[]{:S(2)}) %collective-permute-start.4) | collective-permute-done | bytes 65568 | tf_op jit(solution)/shard_map/ppermute | solution.py:61
  33.8 1.6 %collective-permute-done.6.refs_1_ = f32[64,128]{1,0:T(8,128)S(1)} collective-permute-done((f32[64,128]{1,0:T(8,128)S(1)}, f32[64,128]{1,0:T(8,128)S(1)}, u32[]{:S(2)}, u32[]{:S(2)}) %collective-permute-start.6) | collective-permute-done | bytes 32800 | tf_op jit(solution)/shard_map/ppermute | solution.py:61
  37.1 2.6 %collective-permute-done.7.refs_1_ = f32[64,128]{1,0:T(8,128)S(1)} collective-permute-done((f32[64,128]{1,0:T(8,128)S(1)}, f32[64,128]{1,0:T(8,128)S(1)}, u32[]{:S(2)}, u32[]{:S(2)}) %collective-permute-start.7) | collective-permute-done | bytes 32800 | tf_op jit(solution)/shard_map/ppermute | solution.py:61
  39.7 6.3 %slab.2 = (f32[64,128]{1,0:T(8,128)}, f32[64,128]{1,0:T(8,128)S(1)}, f32[48,64,768]{2,1,0:T(8,128)S(1)}, f32[2,64,128]{2,1,0:T(8,128)S(1)}, f32[2,64,128]{2,1,0:T(8,128)S(1)}, /*index=5*/f32[2,64,128]{2,1,0:T(8,128)S(1)}) custom-call(s32[1]{0:T(128)} %bitcast.me_ref, f32[64,64]{1,0:T(8,128)S(1)} %eliminate.6.refs_2_.refs_0_, f32[64,128]{1,0:T(8,128)S(1)} %add.28.refs_1_, ...), custom_call_target="tpu_custom_call" | custom-call | bytes 18000000 | tf_op jit(solution)/shard_map/slab/pallas_call | solution.py:37
  46.0 1.5 %collective-permute-start.8 = (f32[2,64,128]{2,1,0:T(8,128)S(1)}, f32[2,64,128]{2,1,0:T(8,128)S(1)}, u32[]{:S(2)}, u32[]{:S(2)}) collective-permute-start(f32[2,64,128]{2,1,0:T(8,128)S(1)} %get-tuple-element.60), channel_id=1, source_target_pairs={{0,1},{1,0},{2,3},{3,2},{4,5},{5,4},{6,7},{7,6},{8,9},{9,8},{10,11... | collective-permute-start | bytes 196616 | tf_op jit(solution)/shard_map/ppermute | solution.py:61
  49.5 1.9 %slab.3 = (f32[48,64,256]{2,1,0:T(8,128)S(1)}, f32[2,64,128]{2,1,0:T(8,128)S(1)}) custom-call(s32[1]{0:T(128)} %bitcast.me_ref, f32[64,128]{1,0:T(8,128)S(1)} %get-tuple-element.57.refs_0_.frames_ref, bf16[16,128,1024]{2,1,0:T(8,128)(2,1)S(1)} %get-tuple-element.47.refs_0_.refs_2_.refs_1_, ...), custom_call_target="tpu_custom_call" | custom-call | bytes 6000000 | tf_op jit(solution)/shard_map/slab/pallas_call | solution.py:37
  51.4 1.9 %frames_gram.1 = (f32[64,64]{1,0:T(8,128)S(1)}, f32[64,64]{1,0:T(8,128)S(1)}) custom-call(f32[64,128]{1,0:T(8,128)S(1)} %get-tuple-element.57.refs_0_.frames_ref, f32[64,64]{1,0:T(8,128)S(1)} %get-tuple-element.51.refs_1_.other_ref, f32[2,64,128]{2,1,0:T(8,128)S(1)} %get-tuple-element.58.after_ref.refs_0_), custom_call_target="tpu_custom_call" | custom-call | bytes 6000000 | tf_op jit(solution)/shard_map/frames_gram/pallas_call | solution.py:37
  53.9 1.9 %collective-permute-start.11 = (f32[2,64,128]{2,1,0:T(8,128)S(1)}, f32[2,64,128]{2,1,0:T(8,128)S(1)}, u32[]{:S(2)}, u32[]{:S(2)}) collective-permute-start(f32[2,64,128]{2,1,0:T(8,128)S(1)} %add.29.refs_1_.refs_0_), channel_id=1, source_target_pairs={{0,4},{1,5},{2,6},{3,7},{4,0},{5,1},{6,2},{7,3},{8,12},{9,13},{10,... | collective-permute-start | bytes 196616 | tf_op jit(solution)/shard_map/ppermute | solution.py:61
  56.5 3.4 %collective-permute-done.11.refs_1_ = f32[2,64,128]{2,1,0:T(8,128)S(1)} collective-permute-done((f32[2,64,128]{2,1,0:T(8,128)S(1)}, f32[2,64,128]{2,1,0:T(8,128)S(1)}, u32[]{:S(2)}, u32[]{:S(2)}) %collective-permute-start.11) | collective-permute-done | bytes 65568 | tf_op jit(solution)/shard_map/ppermute | solution.py:61
  61.8 1.8 %collective-permute-start.12 = (bf16[2,64,128]{2,1,0:T(8,128)(2,1)S(1)}, bf16[2,64,128]{2,1,0:T(8,128)(2,1)S(1)}, u32[]{:S(2)}, u32[]{:S(2)}) collective-permute-start(bf16[2,64,128]{2,1,0:T(8,128)(2,1)S(1)} %update.1.refs_0_), channel_id=1, source_target_pairs={{0,1},{1,0},{2,3},{3,2},{4,5},{5,4},{6,7},{7,6},{8,9},{9,8},{10,11... | collective-permute-start | bytes 98312 | tf_op jit(solution)/shard_map/ppermute | solution.py:61
  65.7 1.7 %second.1.refs_0_.refs_2_ = f32[64,128]{1,0:T(8,128)S(1)} custom-call(bf16[2,64,128]{2,1,0:T(8,128)(2,1)S(1)} %update.1.refs_0_, bf16[2,64,128]{2,1,0:T(8,128)(2,1)S(1)} %collective-permute-done.12.refs_1_, bf16[2,64,128]{2,1,0:T(8,128)(2,1)S(1)} %collective-permute-done.13.refs_2_, bf16[2,64,128]{2,1,0:T(8,128)(2,1)S(1)} %collective-permute-done.14.refs_3_, ...), custom_call_target="tpu_custom_call" | custom-call | bytes 6000000 | tf_op jit(solution)/shard_map/second/pallas_call | solution.py:37
  70.0 2.1 %collective-permute-done.16.got_ref = f32[64,128]{1,0:T(8,128)S(1)} collective-permute-done((f32[64,128]{1,0:T(8,128)S(1)}, f32[64,128]{1,0:T(8,128)S(1)}, u32[]{:S(2)}, u32[]{:S(2)}) %collective-permute-start.16) | collective-permute-done | bytes 32800 | tf_op jit(solution)/shard_map/ppermute | solution.py:61
  72.1 4.1 %mode_send.1 = (f32[64,128]{1,0:T(8,128)S(1)}, bf16[4,64,128]{2,1,0:T(8,128)(2,1)S(1)}) custom-call(f32[64,128]{1,0:T(8,128)S(1)} %add.30.mine_ref, f32[64,128]{1,0:T(8,128)S(1)} %collective-permute-done.16.got_ref, f32[64,64]{1,0:T(8,128)S(1)} %get-tuple-element.65.gram_frames_ref, f32[48,64,768]{2,1,0:T(8,128)S(1)} %get-tuple-element.64.refs_5_.sent_ref), custom_call_target="tpu_custom_call" | custom-call | bytes 12000000 | tf_op jit(solution)/shard_map/mode_send/pallas_call | solution.py:37
  76.2 1.9 %collective-permute-start.17 = (bf16[4,64,128]{2,1,0:T(8,128)(2,1)S(1)}, bf16[4,64,128]{2,1,0:T(8,128)(2,1)S(1)}, u32[]{:S(2)}, u32[]{:S(2)}) collective-permute-start(bf16[4,64,128]{2,1,0:T(8,128)(2,1)S(1)} %get-tuple-element.67.after_ref), channel_id=1, source_target_pairs={{0,1},{1,0},{2,3},{3,2},{4,5},{5,4},{6,7},{7,6},{8,9},{9,8},{10,11... | collective-permute-start | bytes 196616 | tf_op jit(solution)/shard_map/ppermute | solution.py:61
  81.9 2.3 %collective-permute-start.19 = (bf16[64,128]{1,0:T(8,128)(2,1)S(1)}, bf16[64,128]{1,0:T(8,128)(2,1)S(1)}, u32[]{:S(2)}, u32[]{:S(2)}) collective-permute-start(bf16[64,128]{1,0:T(8,128)(2,1)S(1)} %get-tuple-element.70), channel_id=1, source_target_pairs={{0,4},{1,5},{2,6},{3,7},{4,0},{5,1},{6,2},{7,3},{8,12},{9,13},{10,... | collective-permute-start | bytes 49160 | tf_op jit(solution)/shard_map/ppermute | solution.py:61
  85.0 1.5 %collective-permute-done.19 = bf16[64,128]{1,0:T(8,128)(2,1)S(1)} collective-permute-done((bf16[64,128]{1,0:T(8,128)(2,1)S(1)}, bf16[64,128]{1,0:T(8,128)(2,1)S(1)}, u32[]{:S(2)}, u32[]{:S(2)}) %collective-permute-start.19) | collective-permute-done | bytes 16416 | tf_op jit(solution)/shard_map/ppermute | solution.py:61
  86.5 3.2 %collective-permute-done.20 = bf16[64,128]{1,0:T(8,128)(2,1)S(1)} collective-permute-done((bf16[64,128]{1,0:T(8,128)(2,1)S(1)}, bf16[64,128]{1,0:T(8,128)(2,1)S(1)}, u32[]{:S(2)}, u32[]{:S(2)}) %collective-permute-start.20) | collective-permute-done | bytes 16416 | tf_op jit(solution)/shard_map/ppermute | solution.py:61
  (46 shorter events, 26.1 us)
Async XLA Ops:
  1.5 7.8 %collective-permute-start = (bf16[1,96,128]{2,1,0:T(8,128)(2,1)S(1)}, bf16[1,96,128]{2,1,0:T(8,128)(2,1)S(1)}, u32[]{:S(2)}, u32[]{:S(2)}) collective-permute-start(bf16[1,96,128]{2,1,0:T(8,128)(2,1)S(1)} %get-tuple-element.37.after_ref.refs_0_), channel_id=1, source_target_pairs={{0,4},{1,5},{2,6},{3,7},{4,0},{5,1},{6,2},{7,3},{8,12},{9,13},{10,... | collective-permute-start | bytes 73736 | tf_op jit(solution)/shard_map/ppermute | solution.py:61
  9.2 4.5 %collective-permute-start.1 = (bf16[2,96,128]{2,1,0:T(8,128)(2,1)S(1)}, bf16[2,96,128]{2,1,0:T(8,128)(2,1)S(1)}, u32[]{:S(2)}, u32[]{:S(2)}) collective-permute-start(bf16[2,96,128]{2,1,0:T(8,128)(2,1)S(1)} %stack.2.after_ref.refs_0_), channel_id=1, source_target_pairs={{0,2},{1,3},{2,0},{3,1},{4,6},{5,7},{6,4},{7,5},{8,10},{9,11},{10,... | collective-permute-start | bytes 147464 | tf_op jit(solution)/shard_map/ppermute | solution.py:61
  13.8 4.7 %collective-permute-start.2 = (bf16[4,96,128]{2,1,0:T(8,128)(2,1)S(1)}, bf16[4,96,128]{2,1,0:T(8,128)(2,1)S(1)}, u32[]{:S(2)}, u32[]{:S(2)}) collective-permute-start(bf16[4,96,128]{2,1,0:T(8,128)(2,1)S(1)} %stack.3.after_ref.refs_0_), channel_id=1, source_target_pairs={{0,1},{1,0},{2,3},{3,2},{4,5},{5,4},{6,7},{7,6},{8,9},{9,8},{10,11... | collective-permute-start | bytes 294920 | tf_op jit(solution)/shard_map/ppermute | solution.py:61
  23.2 1.3 %collective-permute-start.3 = (f32[128,128]{1,0:T(8,128)S(1)}, f32[128,128]{1,0:T(8,128)S(1)}, u32[]{:S(2)}, u32[]{:S(2)}) collective-permute-start(f32[128,128]{1,0:T(8,128)S(1)} %project.1.refs_0_.refs_2_), channel_id=1, source_target_pairs={{0,8},{1,9},{2,10},{3,11},{4,12},{5,13},{6,14},{7,15},{8,0},{9,1},... | collective-permute-start | bytes 196616 | tf_op jit(solution)/shard_map/ppermute | solution.py:61
  24.6 4.1 %collective-permute-start.4 = (f32[128,128]{1,0:T(8,128)S(1)}, f32[128,128]{1,0:T(8,128)S(1)}, u32[]{:S(2)}, u32[]{:S(2)}) collective-permute-start(f32[128,128]{1,0:T(8,128)S(1)} %add.25.a_ref), channel_id=1, source_target_pairs={{0,24},{1,25},{2,26},{3,27},{4,28},{5,29},{6,30},{7,31},{8,16},{9,... | collective-permute-start | bytes 196616 | tf_op jit(solution)/shard_map/ppermute | solution.py:61
  28.7 3.4 %collective-permute-start.5 = (f32[64,128]{1,0:T(8,128)S(1)}, f32[64,128]{1,0:T(8,128)S(1)}, u32[]{:S(2)}, u32[]{:S(2)}) collective-permute-start(f32[64,128]{1,0:T(8,128)S(1)} %get-tuple-element.52.refs_2_.refs_0_), channel_id=1, source_target_pairs={{0,9},{1,8},{2,11},{3,10},{4,13},{5,12},{6,15},{7,14},{8,1},{9,0},... | collective-permute-start | bytes 98312 | tf_op jit(solution)/shard_map/ppermute | solution.py:61
  32.1 3.3 %collective-permute-start.6 = (f32[64,128]{1,0:T(8,128)S(1)}, f32[64,128]{1,0:T(8,128)S(1)}, u32[]{:S(2)}, u32[]{:S(2)}) collective-permute-start(f32[64,128]{1,0:T(8,128)S(1)} %add.26.refs_1_.refs_0_), channel_id=1, source_target_pairs={{0,10},{1,11},{2,8},{3,9},{4,14},{5,15},{6,12},{7,13},{8,2},{9,3},... | collective-permute-start | bytes 98312 | tf_op jit(solution)/shard_map/ppermute | solution.py:61
  35.5 4.2 %collective-permute-start.7 = (f32[64,128]{1,0:T(8,128)S(1)}, f32[64,128]{1,0:T(8,128)S(1)}, u32[]{:S(2)}, u32[]{:S(2)}) collective-permute-start(f32[64,128]{1,0:T(8,128)S(1)} %add.27.refs_1_.refs_0_), channel_id=1, source_target_pairs={{0,12},{1,13},{2,14},{3,15},{4,8},{5,9},{6,10},{7,11},{8,4},{9,5},... | collective-permute-start | bytes 98312 | tf_op jit(solution)/shard_map/ppermute | solution.py:61
  46.0 7.3 %collective-permute-start.8 = (f32[2,64,128]{2,1,0:T(8,128)S(1)}, f32[2,64,128]{2,1,0:T(8,128)S(1)}, u32[]{:S(2)}, u32[]{:S(2)}) collective-permute-start(f32[2,64,128]{2,1,0:T(8,128)S(1)} %get-tuple-element.60), channel_id=1, source_target_pairs={{0,1},{1,0},{2,3},{3,2},{4,5},{5,4},{6,7},{7,6},{8,9},{9,8},{10,11... | collective-permute-start | bytes 196616 | tf_op jit(solution)/shard_map/ppermute | solution.py:61
  47.5 5.8 %collective-permute-start.9 = (f32[2,64,128]{2,1,0:T(8,128)S(1)}, f32[2,64,128]{2,1,0:T(8,128)S(1)}, u32[]{:S(2)}, u32[]{:S(2)}) collective-permute-start(f32[2,64,128]{2,1,0:T(8,128)S(1)} %get-tuple-element.61), channel_id=1, source_target_pairs={{0,2},{1,3},{2,0},{3,1},{4,6},{5,7},{6,4},{7,5},{8,10},{9,11},{10,... | collective-permute-start | bytes 196616 | tf_op jit(solution)/shard_map/ppermute | solution.py:61
  48.8 5.2 %collective-permute-start.10 = (f32[2,64,128]{2,1,0:T(8,128)S(1)}, f32[2,64,128]{2,1,0:T(8,128)S(1)}, u32[]{:S(2)}, u32[]{:S(2)}) collective-permute-start(f32[2,64,128]{2,1,0:T(8,128)S(1)} %get-tuple-element.62), channel_id=1, source_target_pairs={{0,3},{1,2},{2,1},{3,0},{4,7},{5,6},{6,5},{7,4},{8,11},{9,10},{10,... | collective-permute-start | bytes 196616 | tf_op jit(solution)/shard_map/ppermute | solution.py:61
  53.9 5.9 %collective-permute-start.11 = (f32[2,64,128]{2,1,0:T(8,128)S(1)}, f32[2,64,128]{2,1,0:T(8,128)S(1)}, u32[]{:S(2)}, u32[]{:S(2)}) collective-permute-start(f32[2,64,128]{2,1,0:T(8,128)S(1)} %add.29.refs_1_.refs_0_), channel_id=1, source_target_pairs={{0,4},{1,5},{2,6},{3,7},{4,0},{5,1},{6,2},{7,3},{8,12},{9,13},{10,... | collective-permute-start | bytes 196616 | tf_op jit(solution)/shard_map/ppermute | solution.py:61
  60.1 4.9 %collective-permute-start.14 = (bf16[2,64,128]{2,1,0:T(8,128)(2,1)S(1)}, bf16[2,64,128]{2,1,0:T(8,128)(2,1)S(1)}, u32[]{:S(2)}, u32[]{:S(2)}) collective-permute-start(bf16[2,64,128]{2,1,0:T(8,128)(2,1)S(1)} %update.1.refs_0_), channel_id=1, source_target_pairs={{0,3},{1,2},{2,1},{3,0},{4,7},{5,6},{6,5},{7,4},{8,11},{9,10},{10,... | collective-permute-start | bytes 98312 | tf_op jit(solution)/shard_map/ppermute | solution.py:61
  61.1 3.9 %collective-permute-start.13 = (bf16[2,64,128]{2,1,0:T(8,128)(2,1)S(1)}, bf16[2,64,128]{2,1,0:T(8,128)(2,1)S(1)}, u32[]{:S(2)}, u32[]{:S(2)}) collective-permute-start(bf16[2,64,128]{2,1,0:T(8,128)(2,1)S(1)} %update.1.refs_0_), channel_id=1, source_target_pairs={{0,2},{1,3},{2,0},{3,1},{4,6},{5,7},{6,4},{7,5},{8,10},{9,11},{10,... | collective-permute-start | bytes 98312 | tf_op jit(solution)/shard_map/ppermute | solution.py:61
  61.8 3.9 %collective-permute-start.12 = (bf16[2,64,128]{2,1,0:T(8,128)(2,1)S(1)}, bf16[2,64,128]{2,1,0:T(8,128)(2,1)S(1)}, u32[]{:S(2)}, u32[]{:S(2)}) collective-permute-start(bf16[2,64,128]{2,1,0:T(8,128)(2,1)S(1)} %update.1.refs_0_), channel_id=1, source_target_pairs={{0,1},{1,0},{2,3},{3,2},{4,5},{5,4},{6,7},{7,6},{8,9},{9,8},{10,11... | collective-permute-start | bytes 98312 | tf_op jit(solution)/shard_map/ppermute | solution.py:61
  67.4 1.3 %collective-permute-start.15 = (f32[64,128]{1,0:T(8,128)S(1)}, f32[64,128]{1,0:T(8,128)S(1)}, u32[]{:S(2)}, u32[]{:S(2)}) collective-permute-start(f32[64,128]{1,0:T(8,128)S(1)} %second.1.refs_0_.refs_2_), channel_id=1, source_target_pairs={{0,8},{1,9},{2,10},{3,11},{4,12},{5,13},{6,14},{7,15},{8,0},{9,1},... | collective-permute-start | bytes 98312 | tf_op jit(solution)/shard_map/ppermute | solution.py:61
  68.7 3.3 %collective-permute-start.16 = (f32[64,128]{1,0:T(8,128)S(1)}, f32[64,128]{1,0:T(8,128)S(1)}, u32[]{:S(2)}, u32[]{:S(2)}) collective-permute-start(f32[64,128]{1,0:T(8,128)S(1)} %add.30.mine_ref), channel_id=1, source_target_pairs={{0,24},{1,25},{2,26},{3,27},{4,28},{5,29},{6,30},{7,31},{8,16},{9,... | collective-permute-start | bytes 98312 | tf_op jit(solution)/shard_map/ppermute | solution.py:61
  76.2 4.3 %collective-permute-start.17 = (bf16[4,64,128]{2,1,0:T(8,128)(2,1)S(1)}, bf16[4,64,128]{2,1,0:T(8,128)(2,1)S(1)}, u32[]{:S(2)}, u32[]{:S(2)}) collective-permute-start(bf16[4,64,128]{2,1,0:T(8,128)(2,1)S(1)} %get-tuple-element.67.after_ref), channel_id=1, source_target_pairs={{0,1},{1,0},{2,3},{3,2},{4,5},{5,4},{6,7},{7,6},{8,9},{9,8},{10,11... | collective-permute-start | bytes 196616 | tf_op jit(solution)/shard_map/ppermute | solution.py:61
  80.5 4.5 %collective-permute-start.18 = (bf16[64,128]{1,0:T(8,128)(2,1)S(1)}, bf16[64,128]{1,0:T(8,128)(2,1)S(1)}, u32[]{:S(2)}, u32[]{:S(2)}) collective-permute-start(bf16[64,128]{1,0:T(8,128)(2,1)S(1)} %get-tuple-element.69), channel_id=1, source_target_pairs={{0,2},{1,3},{2,0},{3,1},{4,6},{5,7},{6,4},{7,5},{8,10},{9,11},{10,... | collective-permute-start | bytes 49160 | tf_op jit(solution)/shard_map/ppermute | solution.py:61
  81.9 4.6 %collective-permute-start.19 = (bf16[64,128]{1,0:T(8,128)(2,1)S(1)}, bf16[64,128]{1,0:T(8,128)(2,1)S(1)}, u32[]{:S(2)}, u32[]{:S(2)}) collective-permute-start(bf16[64,128]{1,0:T(8,128)(2,1)S(1)} %get-tuple-element.70), channel_id=1, source_target_pairs={{0,4},{1,5},{2,6},{3,7},{4,0},{5,1},{6,2},{7,3},{8,12},{9,13},{10,... | collective-permute-start | bytes 49160 | tf_op jit(solution)/shard_map/ppermute | solution.py:61
  84.2 5.5 %collective-permute-start.20 = (bf16[64,128]{1,0:T(8,128)(2,1)S(1)}, bf16[64,128]{1,0:T(8,128)(2,1)S(1)}, u32[]{:S(2)}, u32[]{:S(2)}) collective-permute-start(bf16[64,128]{1,0:T(8,128)(2,1)S(1)} %get-tuple-element.71), channel_id=1, source_target_pairs={{0,6},{1,7},{2,4},{3,5},{4,2},{5,3},{6,0},{7,1},{8,14},{9,15},{10,... | collective-permute-start | bytes 49160 | tf_op jit(solution)/shard_map/ppermute | solution.py:61

commit v6 on v5

--- a/solution.py
+++ b/solution.py
@@ -128,16 +128,28 @@
     return call(add_body, shaped(parts[0].shape), specs, (*parts, after), "add", us=0.2)
 
 
-def split_body(a_ref, b_ref, sum_ref, gram_ref):
+def split_body(*refs):
+    *parts, sum_ref, gram_ref = refs
     components = sum_ref.shape[0]
-    sum_ref[...] = a_ref[:components] + b_ref[:components]
-    gram_ref[...] = a_ref[components:, :components] + b_ref[components:, :components]
-
-
-def split_add(a, b):
-    half = a.shape[0] // 2
-    outs = (shaped((half, a.shape[1])), shaped((half, half)))
-    return call(split_body, outs, [vmem()] * 2, (a, b), "split_add", us=0.2)
+    sum_ref[...] = paired([p[:components] for p in parts])
+    gram_ref[...] = parts[0][components:, :components] + parts[1][components:, :components]
+
+
+def split_add(parts):
+    half = parts[0].shape[0] // 2
+    outs = (shaped((half, parts[0].shape[1])), shaped((half, half)))
+    return call(split_body, outs, [vmem()] * len(parts), parts, "split_add", us=0.2)
+
+
+def core_add_body(a_ref, b_ref, out_ref, sum_ref):
+    total = a_ref[...] + b_ref[...]
+    out_ref[...] = total
+    sum_ref[...] = total[: sum_ref.shape[0]]
+
+
+def core_add(a, b):
+    outs = (shaped(a.shape), shaped((a.shape[0] // 2, a.shape[1])))
+    return call(core_add_body, outs, [vmem()] * 2, (a, b), "core_add", us=0.2)
 
 
 def prepare_body(at, cols, here, ahead, t_ref, b_ref, after_ref, *refs):
@@ -475,78 +487,80 @@
     )
 
 
-def mode_sums(new_ref, parts, out_ref):
+def mode_sums(new_ref, z_ref, out_refs):
     components = new_ref.shape[0]
 
     def step(n, _):
         at = pl.ds(pl.multiple_of(n * 8, 8), 8)
         scale = new_ref[at, :]
-        totals = [jnp.zeros((8, 256), F32) for _ in parts]
-        for j in range(parts[0][0].shape[0]):
-            factor = scale[:, j : j + 1]
-            totals = [t + z[j, at, lane : lane + 256] * factor for t, (z, lane) in zip(totals, parts)]
-        for p, total in enumerate(totals):
+        total = jnp.zeros((8, z_ref.shape[2]), F32)
+        for j in range(z_ref.shape[0]):
+            total = total + z_ref[j, at, :] * scale[:, j : j + 1]
+        for p, out_ref in enumerate(out_refs):
             for h in range(2):
-                out_ref[2 * p + h, at, :] = total[:, h * 128 : h * 128 + 128]
+                lane = 256 * p + 128 * h
+                out_ref[h, at, :] = total[:, lane : lane + 128]
         return 0
 
     lax.fori_loop(0, components // 8, step, 0)
 
 
-def mode_send_body(mine_ref, got_ref, gram_frames_ref, sent_ref, new_ref, out_ref, sums_ref):
+def mode_send_body(mine_ref, got_ref, gram_frames_ref, sent_ref, new_ref, *refs):
+    outs, sums = refs[:3], refs[3:]
     components = new_ref.shape[0]
     summed = mine_ref[...] + got_ref[...]
     solver = eliminate(ridged(summed[:, components:] * gram_frames_ref[...]), 0, components)
     new_ref[...] = dot(solver, summed, ((1,), (0,)), HIGH)
-    mode_sums(new_ref, [(sent_ref, 0), (sent_ref, 512)], sums_ref)
-    out_ref[...] = sums_ref[...].astype(out_ref.dtype)
+    mode_sums(new_ref, sent_ref, sums)
+    for out_ref, sum_ref in zip(outs, sums):
+        out_ref[...] = sum_ref[...].astype(out_ref.dtype)
 
 
 def mode_send(mine, got, gram_frames, sent, kind):
     components = sent.shape[1]
-    shape = (4, components, 128)
+    shape = (2, components, 128)
     return call(
         mode_send_body,
-        (shaped((components, 2 * components)), shaped(shape, kind)),
+        (shaped((components, 2 * components)),) + (shaped(shape, kind),) * 3,
         [vmem()] * 4,
         (mine, got, gram_frames, sent),
         "mode_send",
-        [VM(shape, F32)],
+        [VM(shape, F32)] * 3,
         us=4,
     )
 
 
-def mode_keep_body(new_ref, kept_ref, sent_ref, after_ref, out_ref):
+def mode_keep_body(new_ref, kept_ref, after_ref, out_ref):
     del after_ref
-    mode_sums(new_ref, [(kept_ref, 0), (sent_ref, 256)], out_ref)
-
-
-def mode_keep(new, kept, sent, after):
+    mode_sums(new_ref, kept_ref, [out_ref])
+
+
+def mode_keep(new, kept, after):
     return call(
         mode_keep_body,
-        shaped((4, kept.shape[1], 128)),
-        [vmem()] * 3 + [anywhere()],
-        (new, kept, sent, after),
+        shaped((2, kept.shape[1], 128)),
+        [vmem()] * 2 + [anywhere()],
+        (new, kept, after),
         "mode_keep",
-    )
-
-
-def deal_body(me_ref, keep_ref, got_ref, mine_ref, *outs):
+        us=0.5,
+    )
+
+
+def deal_body(me_ref, *refs):
+    *parts, mine_ref, out_ref = refs
     upper = (me_ref[0] >> 2) & 1
-    places = [upper, 2 + upper, 1 - upper, 3 - upper]
-    values = [keep_ref[at] + got_ref[at].astype(F32) for at in places]
-    mine_ref[...] = values[0]
-    for out, value in zip(outs, values[1:]):
-        out[...] = value.astype(out.dtype)
-
-
-def deal(me, keep, got):
-    shape = keep.shape[1:]
+    own, other = (paired([p[at].astype(F32) for p in parts]) for at in (upper, 1 - upper))
+    mine_ref[...] = own
+    out_ref[...] = other.astype(out_ref.dtype)
+
+
+def deal(me, parts, kind):
+    shape = parts[0].shape[1:]
     return call(
         deal_body,
-        (shaped(shape),) + (shaped(shape, got.dtype),) * 3,
-        [smem(), vmem(), vmem()],
-        (me, keep, got),
+        (shaped(shape), shaped(shape, kind)),
+        [smem()] + [vmem()] * len(parts),
+        (me, *parts),
         "deal",
         us=0.2,
     )
@@ -595,15 +609,18 @@
 
     total = project(first_turned, second_turned, gram_first, turned)
     core, upper = row_bits[0], row_bits[1:]
-    total = add([total, swap(total, BOTH, every, core)], total)
-    total, gram_first = split_add(total, swap(total, BOTH, every, upper[0] | core))
+    total, alone = core_add(total, swap(total, BOTH, every, core))
+    row, col = upper[0] | core, col_bits[0]
+    got = [swap(total, BOTH, every, row)] + [swap(alone, BOTH, every, o) for o in (col | core, row | col)]
+    total, gram_first = split_add([total, *got])
     state = (gram_first, gram_second)
-    marks = [0, 24, 44, components]
-    for n, bit in enumerate(upper[1:] + col_bits):
+    marks = [0, 44, components]
+    for n, bit in enumerate(col_bits[1:]):
         got = swap(total, BOTH, every, bit | core)
-        if n < 3:
+        if n < 2:
             state = (eliminate_part(state, marks[n], marks[n + 1], total),)
         total = add([total, got], state[0])
+
     at = me if direct else jnp.zeros((1,), jnp.int32)
     near, far = (0,), (1, 2, 3)
     frames, frames_again, sent, *sends = slab(at, (state[0], total), turned, wides, far)
@@ -629,17 +646,15 @@
     part = add([part, swap(part, BOTH, every, core)], part)
     got = swap(part, BOTH, every, upper[0] | core)
 
-    new_second, send = mode_send(part, got, gram_frames, sent, BF16 if direct else F32)
+    new_second, *sends = mode_send(part, got, gram_frames, sent, BF16 if direct else F32)
     if not direct:
-        keep = mode_keep(new_second, kept, sent, new_second)
-        odd, even = send.reshape(2, 2, components, 128), keep.reshape(2, 2, components, 128)
-        blocks = jnp.stack([even[0], odd[0], even[1], odd[1]]).transpose(2, 1, 0, 3).reshape(components, row_count)
+        keep = mode_keep(new_second, kept, new_second)
+        blocks = jnp.stack([keep, *sends]).transpose(2, 1, 0, 3).reshape(components, row_count)
         return (frames, lax.psum_scatter(blocks, "col", scatter_dimension=1, tiled=True))
-    got = swap(send, "col", col_size, 1)
-    keep = mode_keep(new_second, kept, sent, send)
-    mine, *send = deal(me, keep, got)
-    got = [swap(x, "col", col_size, 2 * n + 2).astype(F32) for n, x in enumerate(send)]
-    return (frames, paired([mine, *got]))
+    got = [swap(x, "col", col_size, o) for o, x in zip(far, sends)]
+    keep = mode_keep(new_second, kept, sends[0])
+    mine, send = deal(me, [keep, *got], BF16)
+    return (frames, mine + swap(send, "col", col_size, 4).astype(F32))
 
 
 def solution(mesh):

time: 90.7 us -> 86.6 us (0.955)
  waiting for transfers between devices: 25.1 us -> 21.7 us
    ppermute x21 -> x22, waiting for transfers between devices: 25.1 us -> 21.7 us  [swap(): return lax.ppermute(x, axes, [(n, n ^ offset) for n in range(count)])]
    ppermute x21 -> x22, starting transfers between devices: 28.5 us -> 27.7 us  [swap(): return lax.ppermute(x, axes, [(n, n ^ offset) for n in range(count)])]
    pallas_call x27 -> x25, Pallas kernels: 35.3 us -> 35.4 us  [call(): pl.pallas_call(body, out_shape=outs, in_specs=ins, out_specs=(vmem(),) *...]
  transfers between devices with their start and end apart: 21 -> 22, of which waited for: 15 -> 16; matrix products, arithmetic and copies ran while one was open for 0% -> 0% of each run, Pallas kernels for 19% -> 20%
where the time goes in v6:
time: 86.6 us; the launch traced here: 86.2 us
  Pallas kernels  35.4 us (41%)
  starting transfers between devices  27.7 us (32%)
  waiting for transfers between devices  21.7 us (25%)
    pallas_call x25, Pallas kernels, call(): pl.pallas_call(body, out_shape=outs, in_specs=ins, out_specs=(vmem(),) *...  35.4 us
    ppermute x22, starting transfers between devices, swap(): return lax.ppermute(x, axes, [(n, n ^ offset) for n in range(count)])  27.7 us
    ppermute x22, waiting for transfers between devices, swap(): return lax.ppermute(x, axes, [(n, n ^ offset) for n in range(count)])  21.7 us
  transfers between devices with their start and end apart: 22, of which 16 were waited for; matrix products, arithmetic and copies ran while one was open for 0% of the time, Pallas kernels for 20%

profile of v6, /device:TPU:0, one launch (start us, length us, event | category | flops | bytes accessed | tf_op | source)
XLA Modules:
  0.0 86.2 jit_solution(6635267522559477857)
XLA Ops:
  1.5 4.1 %collective-permute-start = (bf16[1,96,128]{2,1,0:T(8,128)(2,1)S(1)}, bf16[1,96,128]{2,1,0:T(8,128)(2,1)S(1)}, u32[]{:S(2)}, u32[]{:S(2)}) collective-permute-start(bf16[1,96,128]{2,1,0:T(8,128)(2,1)S(1)} %get-tuple-element.39.after_ref.refs_0_), channel_id=1, source_target_pairs={{0,4},{1,5},{2,6},{3,7},{4,0},{5,1},{6,2},{7,3},{8,12},{9,13},{10,... | collective-permute-start | bytes 73736 | tf_op jit(solution)/shard_map/ppermute | solution.py:61
  5.6 3.6 %prepare.3 = (bf16[16,128,1024]{2,1,0:T(8,128)(2,1)S(1)}, f32[16,64,128]{2,1,0:T(8,128)S(1)}, f32[8,128]{1,0:T(8,128)S(1)}, bf16[8,16,16,1024]{3,2,1,0:T(8,128)(2,1)S(1)}) custom-call(bf16[128,48,1024]{2,1,0:T(8,128)(2,1)} %t_ref.5, f32[64,128]{1,0:T(8,128)S(1)} %get-tuple-element.40.b_ref, bf16[1,96,128]{2,1,0:T(8,128)(2,1)S(1)} %get-tuple-element.39.after_ref.refs_0_), custom_call_target="tpu_custom_call" | custom-call | bytes 6000000 | tf_op jit(solution)/shard_map/prepare/pallas_call | solution.py:37
  9.2 1.6 %collective-permute-start.1 = (bf16[2,96,128]{2,1,0:T(8,128)(2,1)S(1)}, bf16[2,96,128]{2,1,0:T(8,128)(2,1)S(1)}, u32[]{:S(2)}, u32[]{:S(2)}) collective-permute-start(bf16[2,96,128]{2,1,0:T(8,128)(2,1)S(1)} %stack.2.after_ref.refs_0_), channel_id=1, source_target_pairs={{0,2},{1,3},{2,0},{3,1},{4,6},{5,7},{6,4},{7,5},{8,10},{9,11},{10,... | collective-permute-start | bytes 147464 | tf_op jit(solution)/shard_map/ppermute | solution.py:61
  10.9 2.8 %prepare.4 = (bf16[16,128,1024]{2,1,0:T(8,128)(2,1)S(1)}, f32[16,64,128]{2,1,0:T(8,128)S(1)}, f32[8,128]{1,0:T(8,128)S(1)}, bf16[8,16,16,1024]{3,2,1,0:T(8,128)(2,1)S(1)}) custom-call(bf16[128,48,1024]{2,1,0:T(8,128)(2,1)} %t_ref.5, f32[64,128]{1,0:T(8,128)S(1)} %get-tuple-element.40.b_ref, bf16[2,96,128]{2,1,0:T(8,128)(2,1)S(1)} %stack.2.after_ref.refs_0_, ...), custom_call_target="tpu_custom_call" | custom-call | bytes 6000000 | tf_op jit(solution)/shard_map/prepare/pallas_call | solution.py:37
  13.8 1.6 %collective-permute-start.2 = (bf16[4,96,128]{2,1,0:T(8,128)(2,1)S(1)}, bf16[4,96,128]{2,1,0:T(8,128)(2,1)S(1)}, u32[]{:S(2)}, u32[]{:S(2)}) collective-permute-start(bf16[4,96,128]{2,1,0:T(8,128)(2,1)S(1)} %stack.3.after_ref.refs_0_), channel_id=1, source_target_pairs={{0,1},{1,0},{2,3},{3,2},{4,5},{5,4},{6,7},{7,6},{8,9},{9,8},{10,11... | collective-permute-start | bytes 294920 | tf_op jit(solution)/shard_map/ppermute | solution.py:61
  15.3 2.8 %prepare.5 = (bf16[16,128,1024]{2,1,0:T(8,128)(2,1)S(1)}, f32[16,64,128]{2,1,0:T(8,128)S(1)}, f32[8,128]{1,0:T(8,128)S(1)}) custom-call(bf16[128,48,1024]{2,1,0:T(8,128)(2,1)} %t_ref.5, f32[64,128]{1,0:T(8,128)S(1)} %get-tuple-element.40.b_ref, bf16[4,96,128]{2,1,0:T(8,128)(2,1)S(1)} %stack.3.after_ref.refs_0_, ...), custom_call_target="tpu_custom_call" | custom-call | bytes 6000000 | tf_op jit(solution)/shard_map/prepare/pallas_call | solution.py:37
  18.8 4.4 %project.1.a_ref = f32[128,128]{1,0:T(8,128)S(1)} custom-call(bf16[1024,64]{1,0:T(8,128)(2,1)S(1)} %get-tuple-element.46.turned_ref, f32[48,64]{1,0:T(8,128)S(1)} %get-tuple-element.47.second_ref, f32[64,64]{1,0:T(8,128)S(1)} %get-tuple-element.48.gram_ref, bf16[16,128,1024]{2,1,0:T(8,128)(2,1)S(1)} %get-tuple-element.49.refs_0_.refs_2_.refs_1_, ...), custom_call_target="tpu_custom_call" | custom-call | bytes 15000000 | tf_op jit(solution)/shard_map/project/pallas_call | solution.py:37
  27.6 2.5 %collective-permute-done.6.refs_3_ = f32[64,128]{1,0:T(8,128)S(1)} collective-permute-done((f32[64,128]{1,0:T(8,128)S(1)}, f32[64,128]{1,0:T(8,128)S(1)}, u32[]{:S(2)}, u32[]{:S(2)}) %collective-permute-start.6) | collective-permute-done | bytes 32800 | tf_op jit(solution)/shard_map/ppermute | solution.py:61
  31.7 1.7 %eliminate.3.refs_2_.refs_0_ = f32[64,64]{1,0:T(8,128)S(1)} custom-call(f32[64,64]{1,0:T(8,128)S(1)} %get-tuple-element.54.refs_0_, f32[64,64]{1,0:T(8,128)S(1)} %get-tuple-element.55.refs_1_.other_ref, f32[64,128]{1,0:T(8,128)S(1)} %get-tuple-element.56.refs_2_.refs_0_), custom_call_target="tpu_custom_call" | custom-call | bytes 3000000 | tf_op jit(solution)/shard_map/eliminate/pallas_call | solution.py:37
  35.7 2.6 %collective-permute-done.8.refs_1_ = f32[64,128]{1,0:T(8,128)S(1)} collective-permute-done((f32[64,128]{1,0:T(8,128)S(1)}, f32[64,128]{1,0:T(8,128)S(1)}, u32[]{:S(2)}, u32[]{:S(2)}) %collective-permute-start.8) | collective-permute-done | bytes 32800 | tf_op jit(solution)/shard_map/ppermute | solution.py:61
  38.3 6.3 %slab.2 = (f32[64,128]{1,0:T(8,128)}, f32[64,128]{1,0:T(8,128)S(1)}, f32[48,64,768]{2,1,0:T(8,128)S(1)}, f32[2,64,128]{2,1,0:T(8,128)S(1)}, f32[2,64,128]{2,1,0:T(8,128)S(1)}, /*index=5*/f32[2,64,128]{2,1,0:T(8,128)S(1)}) custom-call(s32[1]{0:T(128)} %bitcast.me_ref, f32[64,64]{1,0:T(8,128)S(1)} %eliminate.4.refs_2_.refs_0_, f32[64,128]{1,0:T(8,128)S(1)} %add.14.refs_1_, ...), custom_call_target="tpu_custom_call" | custom-call | bytes 18000000 | tf_op jit(solution)/shard_map/slab/pallas_call | solution.py:37
  48.1 1.9 %slab.3 = (f32[48,64,256]{2,1,0:T(8,128)S(1)}, f32[2,64,128]{2,1,0:T(8,128)S(1)}) custom-call(s32[1]{0:T(128)} %bitcast.me_ref, f32[64,128]{1,0:T(8,128)S(1)} %get-tuple-element.61.refs_0_.frames_ref, bf16[16,128,1024]{2,1,0:T(8,128)(2,1)S(1)} %get-tuple-element.49.refs_0_.refs_2_.refs_1_, ...), custom_call_target="tpu_custom_call" | custom-call | bytes 6000000 | tf_op jit(solution)/shard_map/slab/pallas_call | solution.py:37
  50.0 1.9 %frames_gram.1 = (f32[64,64]{1,0:T(8,128)S(1)}, f32[64,64]{1,0:T(8,128)S(1)}) custom-call(f32[64,128]{1,0:T(8,128)S(1)} %get-tuple-element.61.refs_0_.frames_ref, f32[64,64]{1,0:T(8,128)S(1)} %get-tuple-element.55.refs_1_.other_ref, f32[2,64,128]{2,1,0:T(8,128)S(1)} %get-tuple-element.62.after_ref.refs_0_), custom_call_target="tpu_custom_call" | custom-call | bytes 6000000 | tf_op jit(solution)/shard_map/frames_gram/pallas_call | solution.py:37
  52.0 1.5 %collective-permute-start.12 = (f32[2,64,128]{2,1,0:T(8,128)S(1)}, f32[2,64,128]{2,1,0:T(8,128)S(1)}, u32[]{:S(2)}, u32[]{:S(2)}) collective-permute-start(f32[2,64,128]{2,1,0:T(8,128)S(1)} %add.15.refs_1_.refs_0_), channel_id=1, source_target_pairs={{0,4},{1,5},{2,6},{3,7},{4,0},{5,1},{6,2},{7,3},{8,12},{9,13},{10,... | collective-permute-start | bytes 196616 | tf_op jit(solution)/shard_map/ppermute | solution.py:61
  54.3 3.0 %collective-permute-done.12.refs_1_ = f32[2,64,128]{2,1,0:T(8,128)S(1)} collective-permute-done((f32[2,64,128]{2,1,0:T(8,128)S(1)}, f32[2,64,128]{2,1,0:T(8,128)S(1)}, u32[]{:S(2)}, u32[]{:S(2)}) %collective-permute-start.12) | collective-permute-done | bytes 65568 | tf_op jit(solution)/shard_map/ppermute | solution.py:61
  57.5 1.7 %collective-permute-start.15 = (bf16[2,64,128]{2,1,0:T(8,128)(2,1)S(1)}, bf16[2,64,128]{2,1,0:T(8,128)(2,1)S(1)}, u32[]{:S(2)}, u32[]{:S(2)}) collective-permute-start(bf16[2,64,128]{2,1,0:T(8,128)(2,1)S(1)} %update.1.refs_0_), channel_id=1, source_target_pairs={{0,3},{1,2},{2,1},{3,0},{4,7},{5,6},{6,5},{7,4},{8,11},{9,10},{10,... | collective-permute-start | bytes 98312 | tf_op jit(solution)/shard_map/ppermute | solution.py:61
  59.2 1.9 %collective-permute-start.14 = (bf16[2,64,128]{2,1,0:T(8,128)(2,1)S(1)}, bf16[2,64,128]{2,1,0:T(8,128)(2,1)S(1)}, u32[]{:S(2)}, u32[]{:S(2)}) collective-permute-start(bf16[2,64,128]{2,1,0:T(8,128)(2,1)S(1)} %update.1.refs_0_), channel_id=1, source_target_pairs={{0,2},{1,3},{2,0},{3,1},{4,6},{5,7},{6,4},{7,5},{8,10},{9,11},{10,... | collective-permute-start | bytes 98312 | tf_op jit(solution)/shard_map/ppermute | solution.py:61
  63.3 1.7 %collective-permute-done.13.refs_1_ = bf16[2,64,128]{2,1,0:T(8,128)(2,1)S(1)} collective-permute-done((bf16[2,64,128]{2,1,0:T(8,128)(2,1)S(1)}, bf16[2,64,128]{2,1,0:T(8,128)(2,1)S(1)}, u32[]{:S(2)}, u32[]{:S(2)}) %collective-permute-start.13) | collective-permute-done | bytes 32800 | tf_op jit(solution)/shard_map/ppermute | solution.py:61
  65.0 1.7 %second.1.refs_0_.refs_2_ = f32[64,128]{1,0:T(8,128)S(1)} custom-call(bf16[2,64,128]{2,1,0:T(8,128)(2,1)S(1)} %update.1.refs_0_, bf16[2,64,128]{2,1,0:T(8,128)(2,1)S(1)} %collective-permute-done.13.refs_1_, bf16[2,64,128]{2,1,0:T(8,128)(2,1)S(1)} %collective-permute-done.14.refs_2_, bf16[2,64,128]{2,1,0:T(8,128)(2,1)S(1)} %collective-permute-done.15.refs_3_, ...), custom_call_target="tpu_custom_call" | custom-call | bytes 6000000 | tf_op jit(solution)/shard_map/second/pallas_call | solution.py:37
  68.9 2.4 %collective-permute-done.17.got_ref = f32[64,128]{1,0:T(8,128)S(1)} collective-permute-done((f32[64,128]{1,0:T(8,128)S(1)}, f32[64,128]{1,0:T(8,128)S(1)}, u32[]{:S(2)}, u32[]{:S(2)}) %collective-permute-start.17) | collective-permute-done | bytes 32800 | tf_op jit(solution)/shard_map/ppermute | solution.py:61
  71.3 4.1 %mode_send.1 = (f32[64,128]{1,0:T(8,128)S(1)}, bf16[2,64,128]{2,1,0:T(8,128)(2,1)S(1)}, bf16[2,64,128]{2,1,0:T(8,128)(2,1)S(1)}, bf16[2,64,128]{2,1,0:T(8,128)(2,1)S(1)}) custom-call(f32[64,128]{1,0:T(8,128)S(1)} %add.16.mine_ref, f32[64,128]{1,0:T(8,128)S(1)} %collective-permute-done.17.got_ref, f32[64,64]{1,0:T(8,128)S(1)} %get-tuple-element.69.gram_frames_ref, ...), custom_call_target="tpu_custom_call" | custom-call | bytes 12000000 | tf_op jit(solution)/shard_map/mode_send/pallas_call | solution.py:37
  77.0 2.0 %collective-permute-start.18 = (bf16[2,64,128]{2,1,0:T(8,128)(2,1)S(1)}, bf16[2,64,128]{2,1,0:T(8,128)(2,1)S(1)}, u32[]{:S(2)}, u32[]{:S(2)}) collective-permute-start(bf16[2,64,128]{2,1,0:T(8,128)(2,1)S(1)} %get-tuple-element.71.after_ref), channel_id=1, source_target_pairs={{0,1},{1,0},{2,3},{3,2},{4,5},{5,4},{6,7},{7,6},{8,9},{9,8},{10,11... | collective-permute-start | bytes 98312 | tf_op jit(solution)/shard_map/ppermute | solution.py:61
  80.9 2.1 %collective-permute-start.21 = (bf16[64,128]{1,0:T(8,128)(2,1)S(1)}, bf16[64,128]{1,0:T(8,128)(2,1)S(1)}, u32[]{:S(2)}, u32[]{:S(2)}) collective-permute-start(bf16[64,128]{1,0:T(8,128)(2,1)S(1)} %get-tuple-element.75), channel_id=1, source_target_pairs={{0,4},{1,5},{2,6},{3,7},{4,0},{5,1},{6,2},{7,3},{8,12},{9,13},{10,... | collective-permute-start | bytes 49160 | tf_op jit(solution)/shard_map/ppermute | solution.py:61
  83.0 2.6 %collective-permute-done.21 = bf16[64,128]{1,0:T(8,128)(2,1)S(1)} collective-permute-done((bf16[64,128]{1,0:T(8,128)(2,1)S(1)}, bf16[64,128]{1,0:T(8,128)(2,1)S(1)}, u32[]{:S(2)}, u32[]{:S(2)}) %collective-permute-start.21) | collective-permute-done | bytes 16416 | tf_op jit(solution)/shard_map/ppermute | solution.py:61
  (46 shorter events, 22.6 us)
Async XLA Ops:
  1.5 7.8 %collective-permute-start = (bf16[1,96,128]{2,1,0:T(8,128)(2,1)S(1)}, bf16[1,96,128]{2,1,0:T(8,128)(2,1)S(1)}, u32[]{:S(2)}, u32[]{:S(2)}) collective-permute-start(bf16[1,96,128]{2,1,0:T(8,128)(2,1)S(1)} %get-tuple-element.39.after_ref.refs_0_), channel_id=1, source_target_pairs={{0,4},{1,5},{2,6},{3,7},{4,0},{5,1},{6,2},{7,3},{8,12},{9,13},{10,... | collective-permute-start | bytes 73736 | tf_op jit(solution)/shard_map/ppermute | solution.py:61
  9.2 4.5 %collective-permute-start.1 = (bf16[2,96,128]{2,1,0:T(8,128)(2,1)S(1)}, bf16[2,96,128]{2,1,0:T(8,128)(2,1)S(1)}, u32[]{:S(2)}, u32[]{:S(2)}) collective-permute-start(bf16[2,96,128]{2,1,0:T(8,128)(2,1)S(1)} %stack.2.after_ref.refs_0_), channel_id=1, source_target_pairs={{0,2},{1,3},{2,0},{3,1},{4,6},{5,7},{6,4},{7,5},{8,10},{9,11},{10,... | collective-permute-start | bytes 147464 | tf_op jit(solution)/shard_map/ppermute | solution.py:61
  13.8 4.7 %collective-permute-start.2 = (bf16[4,96,128]{2,1,0:T(8,128)(2,1)S(1)}, bf16[4,96,128]{2,1,0:T(8,128)(2,1)S(1)}, u32[]{:S(2)}, u32[]{:S(2)}) collective-permute-start(bf16[4,96,128]{2,1,0:T(8,128)(2,1)S(1)} %stack.3.after_ref.refs_0_), channel_id=1, source_target_pairs={{0,1},{1,0},{2,3},{3,2},{4,5},{5,4},{6,7},{7,6},{8,9},{9,8},{10,11... | collective-permute-start | bytes 294920 | tf_op jit(solution)/shard_map/ppermute | solution.py:61
  23.2 1.3 %collective-permute-start.3 = (f32[128,128]{1,0:T(8,128)S(1)}, f32[128,128]{1,0:T(8,128)S(1)}, u32[]{:S(2)}, u32[]{:S(2)}) collective-permute-start(f32[128,128]{1,0:T(8,128)S(1)} %project.1.a_ref), channel_id=1, source_target_pairs={{0,8},{1,9},{2,10},{3,11},{4,12},{5,13},{6,14},{7,15},{8,0},{9,1},... | collective-permute-start | bytes 196616 | tf_op jit(solution)/shard_map/ppermute | solution.py:61
  24.6 6.1 %collective-permute-start.4 = (f32[128,128]{1,0:T(8,128)S(1)}, f32[128,128]{1,0:T(8,128)S(1)}, u32[]{:S(2)}, u32[]{:S(2)}) collective-permute-start(f32[128,128]{1,0:T(8,128)S(1)} %get-tuple-element.52.refs_0_), channel_id=1, source_target_pairs={{0,24},{1,25},{2,26},{3,27},{4,28},{5,29},{6,30},{7,31},{8,16},{9,... | collective-permute-start | bytes 196616 | tf_op jit(solution)/shard_map/ppermute | solution.py:61
  25.9 4.2 %collective-permute-start.6 = (f32[64,128]{1,0:T(8,128)S(1)}, f32[64,128]{1,0:T(8,128)S(1)}, u32[]{:S(2)}, u32[]{:S(2)}) collective-permute-start(f32[64,128]{1,0:T(8,128)S(1)} %get-tuple-element.53), channel_id=1, source_target_pairs={{0,25},{1,24},{2,27},{3,26},{4,29},{5,28},{6,31},{7,30},{8,17},{9,... | collective-permute-start | bytes 98312 | tf_op jit(solution)/shard_map/ppermute | solution.py:61
  27.3 3.4 %collective-permute-start.5 = (f32[64,128]{1,0:T(8,128)S(1)}, f32[64,128]{1,0:T(8,128)S(1)}, u32[]{:S(2)}, u32[]{:S(2)}) collective-permute-start(f32[64,128]{1,0:T(8,128)S(1)} %get-tuple-element.53), channel_id=1, source_target_pairs={{0,9},{1,8},{2,11},{3,10},{4,13},{5,12},{6,15},{7,14},{8,1},{9,0},... | collective-permute-start | bytes 98312 | tf_op jit(solution)/shard_map/ppermute | solution.py:61
  30.7 3.4 %collective-permute-start.7 = (f32[64,128]{1,0:T(8,128)S(1)}, f32[64,128]{1,0:T(8,128)S(1)}, u32[]{:S(2)}, u32[]{:S(2)}) collective-permute-start(f32[64,128]{1,0:T(8,128)S(1)} %get-tuple-element.56.refs_2_.refs_0_), channel_id=1, source_target_pairs={{0,10},{1,11},{2,8},{3,9},{4,14},{5,15},{6,12},{7,13},{8,2},{9,3},... | collective-permute-start | bytes 98312 | tf_op jit(solution)/shard_map/ppermute | solution.py:61
  34.1 4.2 %collective-permute-start.8 = (f32[64,128]{1,0:T(8,128)S(1)}, f32[64,128]{1,0:T(8,128)S(1)}, u32[]{:S(2)}, u32[]{:S(2)}) collective-permute-start(f32[64,128]{1,0:T(8,128)S(1)} %add.13.refs_1_.refs_0_), channel_id=1, source_target_pairs={{0,12},{1,13},{2,14},{3,15},{4,8},{5,9},{6,10},{7,11},{8,4},{9,5},... | collective-permute-start | bytes 98312 | tf_op jit(solution)/shard_map/ppermute | solution.py:61
  44.6 7.3 %collective-permute-start.9 = (f32[2,64,128]{2,1,0:T(8,128)S(1)}, f32[2,64,128]{2,1,0:T(8,128)S(1)}, u32[]{:S(2)}, u32[]{:S(2)}) collective-permute-start(f32[2,64,128]{2,1,0:T(8,128)S(1)} %get-tuple-element.64), channel_id=1, source_target_pairs={{0,1},{1,0},{2,3},{3,2},{4,5},{5,4},{6,7},{7,6},{8,9},{9,8},{10,11... | collective-permute-start | bytes 196616 | tf_op jit(solution)/shard_map/ppermute | solution.py:61
  45.6 6.3 %collective-permute-start.10 = (f32[2,64,128]{2,1,0:T(8,128)S(1)}, f32[2,64,128]{2,1,0:T(8,128)S(1)}, u32[]{:S(2)}, u32[]{:S(2)}) collective-permute-start(f32[2,64,128]{2,1,0:T(8,128)S(1)} %get-tuple-element.65), channel_id=1, source_target_pairs={{0,2},{1,3},{2,0},{3,1},{4,6},{5,7},{6,4},{7,5},{8,10},{9,11},{10,... | collective-permute-start | bytes 196616 | tf_op jit(solution)/shard_map/ppermute | solution.py:61
  46.9 5.2 %collective-permute-start.11 = (f32[2,64,128]{2,1,0:T(8,128)S(1)}, f32[2,64,128]{2,1,0:T(8,128)S(1)}, u32[]{:S(2)}, u32[]{:S(2)}) collective-permute-start(f32[2,64,128]{2,1,0:T(8,128)S(1)} %get-tuple-element.66), channel_id=1, source_target_pairs={{0,3},{1,2},{2,1},{3,0},{4,7},{5,6},{6,5},{7,4},{8,11},{9,10},{10,... | collective-permute-start | bytes 196616 | tf_op jit(solution)/shard_map/ppermute | solution.py:61
  52.0 5.2 %collective-permute-start.12 = (f32[2,64,128]{2,1,0:T(8,128)S(1)}, f32[2,64,128]{2,1,0:T(8,128)S(1)}, u32[]{:S(2)}, u32[]{:S(2)}) collective-permute-start(f32[2,64,128]{2,1,0:T(8,128)S(1)} %add.15.refs_1_.refs_0_), channel_id=1, source_target_pairs={{0,4},{1,5},{2,6},{3,7},{4,0},{5,1},{6,2},{7,3},{8,12},{9,13},{10,... | collective-permute-start | bytes 196616 | tf_op jit(solution)/shard_map/ppermute | solution.py:61
  57.5 5.0 %collective-permute-start.15 = (bf16[2,64,128]{2,1,0:T(8,128)(2,1)S(1)}, bf16[2,64,128]{2,1,0:T(8,128)(2,1)S(1)}, u32[]{:S(2)}, u32[]{:S(2)}) collective-permute-start(bf16[2,64,128]{2,1,0:T(8,128)(2,1)S(1)} %update.1.refs_0_), channel_id=1, source_target_pairs={{0,3},{1,2},{2,1},{3,0},{4,7},{5,6},{6,5},{7,4},{8,11},{9,10},{10,... | collective-permute-start | bytes 98312 | tf_op jit(solution)/shard_map/ppermute | solution.py:61
  59.2 4.1 %collective-permute-start.14 = (bf16[2,64,128]{2,1,0:T(8,128)(2,1)S(1)}, bf16[2,64,128]{2,1,0:T(8,128)(2,1)S(1)}, u32[]{:S(2)}, u32[]{:S(2)}) collective-permute-start(bf16[2,64,128]{2,1,0:T(8,128)(2,1)S(1)} %update.1.refs_0_), channel_id=1, source_target_pairs={{0,2},{1,3},{2,0},{3,1},{4,6},{5,7},{6,4},{7,5},{8,10},{9,11},{10,... | collective-permute-start | bytes 98312 | tf_op jit(solution)/shard_map/ppermute | solution.py:61
  61.1 3.9 %collective-permute-start.13 = (bf16[2,64,128]{2,1,0:T(8,128)(2,1)S(1)}, bf16[2,64,128]{2,1,0:T(8,128)(2,1)S(1)}, u32[]{:S(2)}, u32[]{:S(2)}) collective-permute-start(bf16[2,64,128]{2,1,0:T(8,128)(2,1)S(1)} %update.1.refs_0_), channel_id=1, source_target_pairs={{0,1},{1,0},{2,3},{3,2},{4,5},{5,4},{6,7},{7,6},{8,9},{9,8},{10,11... | collective-permute-start | bytes 98312 | tf_op jit(solution)/shard_map/ppermute | solution.py:61
  66.7 1.3 %collective-permute-start.16 = (f32[64,128]{1,0:T(8,128)S(1)}, f32[64,128]{1,0:T(8,128)S(1)}, u32[]{:S(2)}, u32[]{:S(2)}) collective-permute-start(f32[64,128]{1,0:T(8,128)S(1)} %second.1.refs_0_.refs_2_), channel_id=1, source_target_pairs={{0,8},{1,9},{2,10},{3,11},{4,12},{5,13},{6,14},{7,15},{8,0},{9,1},... | collective-permute-start | bytes 98312 | tf_op jit(solution)/shard_map/ppermute | solution.py:61
  67.9 3.3 %collective-permute-start.17 = (f32[64,128]{1,0:T(8,128)S(1)}, f32[64,128]{1,0:T(8,128)S(1)}, u32[]{:S(2)}, u32[]{:S(2)}) collective-permute-start(f32[64,128]{1,0:T(8,128)S(1)} %add.16.mine_ref), channel_id=1, source_target_pairs={{0,24},{1,25},{2,26},{3,27},{4,28},{5,29},{6,30},{7,31},{8,16},{9,... | collective-permute-start | bytes 98312 | tf_op jit(solution)/shard_map/ppermute | solution.py:61
  75.4 4.8 %collective-permute-start.19 = (bf16[2,64,128]{2,1,0:T(8,128)(2,1)S(1)}, bf16[2,64,128]{2,1,0:T(8,128)(2,1)S(1)}, u32[]{:S(2)}, u32[]{:S(2)}) collective-permute-start(bf16[2,64,128]{2,1,0:T(8,128)(2,1)S(1)} %get-tuple-element.72), channel_id=1, source_target_pairs={{0,2},{1,3},{2,0},{3,1},{4,6},{5,7},{6,4},{7,5},{8,10},{9,11},{10,... | collective-permute-start | bytes 98312 | tf_op jit(solution)/shard_map/ppermute | solution.py:61
  75.6 4.8 %collective-permute-start.20 = (bf16[2,64,128]{2,1,0:T(8,128)(2,1)S(1)}, bf16[2,64,128]{2,1,0:T(8,128)(2,1)S(1)}, u32[]{:S(2)}, u32[]{:S(2)}) collective-permute-start(bf16[2,64,128]{2,1,0:T(8,128)(2,1)S(1)} %get-tuple-element.73), channel_id=1, source_target_pairs={{0,3},{1,2},{2,1},{3,0},{4,7},{5,6},{6,5},{7,4},{8,11},{9,10},{10,... | collective-permute-start | bytes 98312 | tf_op jit(solution)/shard_map/ppermute | solution.py:61
  77.0 3.9 %collective-permute-start.18 = (bf16[2,64,128]{2,1,0:T(8,128)(2,1)S(1)}, bf16[2,64,128]{2,1,0:T(8,128)(2,1)S(1)}, u32[]{:S(2)}, u32[]{:S(2)}) collective-permute-start(bf16[2,64,128]{2,1,0:T(8,128)(2,1)S(1)} %get-tuple-element.71.after_ref), channel_id=1, source_target_pairs={{0,1},{1,0},{2,3},{3,2},{4,5},{5,4},{6,7},{7,6},{8,9},{9,8},{10,11... | collective-permute-start | bytes 98312 | tf_op jit(solution)/shard_map/ppermute | solution.py:61
  80.9 4.7 %collective-permute-start.21 = (bf16[64,128]{1,0:T(8,128)(2,1)S(1)}, bf16[64,128]{1,0:T(8,128)(2,1)S(1)}, u32[]{:S(2)}, u32[]{:S(2)}) collective-permute-start(bf16[64,128]{1,0:T(8,128)(2,1)S(1)} %get-tuple-element.75), channel_id=1, source_target_pairs={{0,4},{1,5},{2,6},{3,7},{4,0},{5,1},{6,2},{7,3},{8,12},{9,13},{10,... | collective-permute-start | bytes 49160 | tf_op jit(solution)/shard_map/ppermute | solution.py:61

commit v7 on v6

--- a/solution.py
+++ b/solution.py
@@ -129,16 +129,18 @@
 
 
 def split_body(*refs):
-    *parts, sum_ref, gram_ref = refs
+    *parts, after_ref, sum_ref, gram_ref = refs
+    del after_ref
     components = sum_ref.shape[0]
     sum_ref[...] = paired([p[:components] for p in parts])
     gram_ref[...] = parts[0][components:, :components] + parts[1][components:, :components]
 
 
-def split_add(parts):
+def split_add(parts, after):
     half = parts[0].shape[0] // 2
     outs = (shaped((half, parts[0].shape[1])), shaped((half, half)))
-    return call(split_body, outs, [vmem()] * len(parts), parts, "split_add", us=0.2)
+    specs = [vmem()] * len(parts) + [anywhere()]
+    return call(split_body, outs, specs, (*parts, after), "split_add", us=0.2)
 
 
 def core_add_body(a_ref, b_ref, out_ref, sum_ref):
@@ -152,14 +154,14 @@
     return call(core_add_body, outs, [vmem()] * 2, (a, b), "core_add", us=0.2)
 
 
-def prepare_body(at, cols, here, ahead, t_ref, b_ref, after_ref, *refs):
+def prepare_body(at, cols, here, ahead, t_ref, after_ref, *refs):
     del after_ref
     slab_ref = refs[0] if here else None
     refs = list(refs[1:] if here else refs)
-    out_ref, wide_ref, token_ref = refs[:3]
-    next_ref = refs.pop(3) if ahead else None
+    out_ref, token_ref = refs[:2]
+    next_ref = refs.pop(2) if ahead else None
     sems = refs[-1]
-    slab_ref = slab_ref if here else refs[3]
+    slab_ref = slab_ref if here else refs[2]
     blocks = slab_ref.shape[0]
 
     def fetch(n, to_ref, start, sem):
@@ -174,8 +176,6 @@
         for n in range(blocks):
             fetch(n, next_ref, at + cols, 1).start()
     token_ref[...] = jnp.zeros_like(token_ref)
-    for j in range(cols):
-        wide_ref[j] = jnp.broadcast_to(b_ref[:, at + j : at + j + 1], wide_ref.shape[1:])
     to = lax.broadcasted_iota(jnp.int32, (256, 256), 0)
     of = lax.broadcasted_iota(jnp.int32, (256, 256), 1)
     turn = jnp.where((to // GROUP) + (to % GROUP) * GROUP == of, 1.0, 0.0).astype(BF16)
@@ -195,24 +195,36 @@
             fetch(n, next_ref, at + cols, 1).wait()
 
 
-def prepare(tensor, second, at, cols, fetched, next_cols, after):
+def prepare(tensor, at, cols, fetched, next_cols, after):
     frames, _, rows = tensor.shape
-    components = second.shape[0]
     blocks = frames // GROUP
-    outs = (VM((cols, frames, rows), BF16), VM((cols, components, 128), F32), shaped((8, 128)))
+    outs = (VM((cols, frames, rows), BF16), shaped((8, 128)))
     if next_cols:
         outs += (VM((blocks, GROUP, next_cols, rows), BF16),)
     scratch = [] if fetched else [VM((blocks, GROUP, cols, rows), BF16)]
     got = call(
         functools.partial(prepare_body, at, cols, bool(fetched), bool(next_cols)),
         outs,
-        [anywhere(), vmem(), anywhere()] + [vmem()] * len(fetched),
-        (tensor, second, after, *fetched),
+        [anywhere(), anywhere()] + [vmem()] * len(fetched),
+        (tensor, after, *fetched),
         "prepare",
         scratch + [pltpu.SemaphoreType.DMA((2, blocks))],
         us=cols / 8,
     )
-    return got[:3], list(got[3:])
+    return got[:2], list(got[2:])
+
+
+def widen_body(b_ref, after_ref, out_ref, token_ref):
+    del after_ref
+    token_ref[...] = jnp.zeros_like(token_ref)
+    for j in range(out_ref.shape[0]):
+        out_ref[j] = jnp.broadcast_to(b_ref[:, j : j + 1], out_ref.shape[1:])
+
+
+def widen(second, cols, after):
+    specs = [vmem(), anywhere()]
+    outs = (VM((cols, second.shape[0], 128), F32), shaped((8, 128)))
+    return call(widen_body, outs, specs, (second, after), "widen")
 
 
 def place(at, blocks, width, full_ref):
@@ -351,12 +363,11 @@
     return pl.ds(at, 128)
 
 
-def slab_body(groups, offsets, first, me_ref, *refs):
-    heads, refs = refs[: 2 if first else 1], refs[2 if first else 1 :]
-    t_refs, wide_refs, refs = refs[:groups], refs[groups : 2 * groups], refs[2 * groups :]
-    if first:
+def slab_body(groups, offsets, head_count, me_ref, wide_ref, *refs):
+    heads, t_refs, refs = refs[:head_count], refs[head_count : head_count + groups], refs[head_count + groups :]
+    if head_count > 1:
         frames_ref, copy_ref, *refs = refs
-        frames = dot(heads[0][...], heads[1][...], ((1,), (0,)), HIGH)
+        frames = dot(heads[0][...], paired([h[...] for h in heads[1:]]), ((1,), (0,)), HIGH)
         frames_ref[...] = frames
         copy_ref[...] = frames
     else:
@@ -372,9 +383,9 @@
         store = pl.ds(place_at * wide, wide)
         total = jnp.zeros((components, wide), F32)
         base = 0
-        for t_ref, wide_ref in zip(t_refs, wide_refs):
-
-            def step(n, total, t_ref=t_ref, wide_ref=wide_ref, base=base):
+        for t_ref in t_refs:
+
+            def step(n, total, t_ref=t_ref, base=base):
                 for s in range(0, 8, 2):
                     rows = pl.ds(n * 8 + s, 2)
                     block = jnp.concatenate([t_ref[rows, :, at].reshape(2 * depth, 128) for at in lanes], axis=1)
@@ -383,7 +394,7 @@
                         j = n * 8 + s + h
                         z = product[h * components : h * components + components]
                         z_ref[base + j, :, store] = z
-                        scale = wide_ref[j]
+                        scale = wide_ref[base + j]
                         total = total + z * jnp.concatenate([scale, scale], axis=1)
                 return total
 
@@ -393,19 +404,17 @@
             out_ref[n] = total[:, n * 128 : n * 128 + 128]
 
 
-def slab(me, heads, turned, wides, offsets):
+def slab(me, wide, heads, turned, offsets):
     _, frames, _ = turned[0].shape
-    components = wides[0].shape[1]
-    first = len(heads) == 2
-    cols = sum(t.shape[0] for t in turned)
+    cols, components, _ = wide.shape
     outs = (VM((cols, components, 256 * len(offsets)), F32),) + (shaped((2, components, 128)),) * len(offsets)
-    if first:
+    if len(heads) > 1:
         outs = (shaped((components, frames)),) * 2 + outs
     return call(
-        functools.partial(slab_body, len(turned), offsets, first),
+        functools.partial(slab_body, len(turned), offsets, len(heads)),
         outs,
-        [smem()] + [vmem()] * (len(heads) + 2 * len(turned)),
-        (me, *heads, *turned, *wides),
+        [smem()] + [vmem()] * (1 + len(heads) + len(turned)),
+        (me, wide, *heads, *turned),
         "slab",
         us=2 * len(offsets),
     )
@@ -449,22 +458,30 @@
 
 
 def second_body(*refs):
-    *stacks, kept_ref, sent_ref, out_ref, full_ref = refs
+    *stacks, kept_ref, sent_ref, out_ref, full_ref, fold_ref = refs
     cols, components, near = kept_ref.shape
     blocks = [s[n] for s in stacks for n in range(s.shape[0])]
     for n, block in enumerate(blocks):
         full_ref[:, n * 128 : n * 128 + 128] = block.astype(F32)
     lane = lax.broadcasted_iota(jnp.int32, (8, 128), 1)
+    ones = jnp.ones((256, 128), BF16)
+
+    def folded(j, at, mine):
+        products = kept_ref[j, at, :] * mine[:, :near], sent_ref[j, at, :] * mine[:, near:]
+        return paired([p[:, c : c + 128] for p in products for c in range(0, p.shape[1], 128)])
 
     def step(n, _):
         at = pl.ds(pl.multiple_of(n * 8, 8), 8)
         mine = full_ref[at, :]
+        for j in range(0, cols, 2):
+            pair = jnp.concatenate([folded(j, at, mine), folded(j + 1, at, mine)], axis=0)
+            high = pair.astype(BF16)
+            fold_ref[8 * j : 8 * j + 16, :128] = high
+            fold_ref[8 * j : 8 * j + 16, 128:] = (pair - high.astype(F32)).astype(BF16)
+        sums = dot(fold_ref[...], ones, ((1,), (0,)))
         total = jnp.zeros((8, 128), F32)
         for j in range(cols):
-            products = kept_ref[j, at, :] * mine[:, :near], sent_ref[j, at, :] * mine[:, near:]
-            folds = [p[:, c : c + 128] for p in products for c in range(0, p.shape[1], 128)]
-            folded = paired(folds)
-            total = jnp.where(lane == j, jnp.sum(folded, axis=1, keepdims=True), total)
+            total = jnp.where(lane == j, sums[8 * j : 8 * j + 8], total)
         out_ref[at, :] = total
         return 0
 
@@ -482,7 +499,7 @@
         [vmem()] * (2 + len(stacks)),
         (*stacks, kept, sent),
         "second",
-        [VM((components, kept.shape[2] + sent.shape[2]), F32)],
+        [VM((components, kept.shape[2] + sent.shape[2]), F32), VM((8 * kept.shape[0], 256), BF16)],
         us=2,
     )
 
@@ -579,7 +596,7 @@
     tensor = pltpu.with_memory_space_constraint(tensor, pltpu.HBM)
     cuts = [(0, GROUP), (GROUP, GROUP), (2 * GROUP, col_count - 2 * GROUP)]
 
-    turned, wides = [], []
+    turned = []
     order = [0, 4, 2, 6, 1, 5, 3, 7]
     ends = [cols for _, cols in cuts[1:]] + [0]
     fetched = []
@@ -591,9 +608,8 @@
     for (at, cols), following, bit in zip(cuts, ends, (4, 2, 1)):
         if direct:
             got = swap(have, "col", col_size, bit)
-        (t, w, token), fetched = prepare(tensor, second_values, at, cols, fetched, following, have)
+        (t, token), fetched = prepare(tensor, at, cols, fetched, following, have)
         turned.append(t)
-        wides.append(w)
         if direct and bit > 1:
             have = stack([have, got], token)
     if direct:
@@ -612,31 +628,34 @@
     total, alone = core_add(total, swap(total, BOTH, every, core))
     row, col = upper[0] | core, col_bits[0]
     got = [swap(total, BOTH, every, row)] + [swap(alone, BOTH, every, o) for o in (col | core, row | col)]
-    total, gram_first = split_add([total, *got])
+    wide, token = widen(second_values, col_count, total)
+    total, gram_first = split_add([total, *got], token)
     state = (gram_first, gram_second)
     marks = [0, 44, components]
+    sums = [total]
     for n, bit in enumerate(col_bits[1:]):
-        got = swap(total, BOTH, every, bit | core)
+        if n:
+            total = add(sums, state[0])
+        sums = [total, swap(total, BOTH, every, bit | core)]
         if n < 2:
             state = (eliminate_part(state, marks[n], marks[n + 1], total),)
-        total = add([total, got], state[0])
 
     at = me if direct else jnp.zeros((1,), jnp.int32)
     near, far = (0,), (1, 2, 3)
-    frames, frames_again, sent, *sends = slab(at, (state[0], total), turned, wides, far)
+    frames, frames_again, sent, *sends = slab(at, wide, (state[0], *sums), turned, far)
     if direct:
         got = [swap(x, "col", col_size, o) for o, x in zip(far, sends)]
-    kept, keep = slab(at, (frames_again,), turned, wides, near)
-
-    gram_frames, state = frames_gram(frames_again, gram_second, 44, keep)
+    kept, keep = slab(at, wide, (frames_again,), turned, near)
+
+    gram_frames, state = frames_gram(frames_again, gram_second, 20, keep)
     if direct:
         keep = add([keep, *got], state)
         got = swap(keep, "col", col_size, 4)
-        state = eliminate_part((state,), 44, components, keep)
+        state = eliminate_part((state,), 20, components, keep)
         new = update(state, [keep, got])
         stacks = [new] + [swap(new, "col", col_size, o) for o in far]
     else:
-        state = eliminate_part((state,), 44, components, keep)
+        state = eliminate_part((state,), 20, components, keep)
         blocks = jnp.stack([keep, *sends]).transpose(2, 1, 0, 3).reshape(components, row_count)
         summed = lax.psum_scatter(blocks, "col", scatter_dimension=1, tiled=True)
         new = update(state, [summed[None]])[0]

time: 86.6 us -> 88.5 us (1.022)
  waiting for transfers between devices: 21.7 us -> 23.2 us
  Pallas kernels: 35.4 us -> 36.6 us
    ppermute x22, waiting for transfers between devices: 21.7 us -> 23.2 us  [swap(): return lax.ppermute(x, axes, [(n, n ^ offset) for n in range(count)])]
    pallas_call x25, Pallas kernels: 35.4 us -> 36.6 us  [call(): pl.pallas_call(body, out_shape=outs, in_specs=ins, out_specs=(vmem(),) *...]
  transfers between devices with their start and end apart: 22 -> 22, of which waited for: 16 -> 15; matrix products, arithmetic and copies ran while one was open for 0% -> 0% of each run, Pallas kernels for 20% -> 20%
where the time goes in v7:
time: 88.5 us; the launch traced here: 88.1 us
  Pallas kernels  36.6 us (41%)
  starting transfers between devices  26.9 us (30%)
  waiting for transfers between devices  23.2 us (26%)
    pallas_call x25, Pallas kernels, call(): pl.pallas_call(body, out_shape=outs, in_specs=ins, out_specs=(vmem(),) *...  36.6 us
    ppermute x22, starting transfers between devices, swap(): return lax.ppermute(x, axes, [(n, n ^ offset) for n in range(count)])  26.9 us
    ppermute x22, waiting for transfers between devices, swap(): return lax.ppermute(x, axes, [(n, n ^ offset) for n in range(count)])  23.2 us
  transfers between devices with their start and end apart: 22, of which 15 were waited for; matrix products, arithmetic and copies ran while one was open for 0% of the time, Pallas kernels for 20%

profile of v7, /device:TPU:0, one launch (start us, length us, event | category | flops | bytes accessed | tf_op | source)
XLA Modules:
  0.0 88.1 jit_solution(13674362995801324778)
XLA Ops:
  1.5 4.1 %collective-permute-start = (bf16[1,96,128]{2,1,0:T(8,128)(2,1)S(1)}, bf16[1,96,128]{2,1,0:T(8,128)(2,1)S(1)}, u32[]{:S(2)}, u32[]{:S(2)}) collective-permute-start(bf16[1,96,128]{2,1,0:T(8,128)(2,1)S(1)} %get-tuple-element.39.after_ref.refs_0_), channel_id=1, source_target_pairs={{0,4},{1,5},{2,6},{3,7},{4,0},{5,1},{6,2},{7,3},{8,12},{9,13},{10,... | collective-permute-start | bytes 73736 | tf_op jit(solution)/shard_map/ppermute | solution.py:61
  5.6 3.6 %prepare.3 = (bf16[16,128,1024]{2,1,0:T(8,128)(2,1)S(1)}, f32[8,128]{1,0:T(8,128)S(1)}, bf16[8,16,16,1024]{3,2,1,0:T(8,128)(2,1)S(1)}) custom-call(bf16[128,48,1024]{2,1,0:T(8,128)(2,1)} %t_ref.5, bf16[1,96,128]{2,1,0:T(8,128)(2,1)S(1)} %get-tuple-element.39.after_ref.refs_0_), custom_call_target="tpu_custom_call" | custom-call | bytes 6000000 | tf_op jit(solution)/shard_map/prepare/pallas_call | solution.py:37
  9.2 1.6 %collective-permute-start.1 = (bf16[2,96,128]{2,1,0:T(8,128)(2,1)S(1)}, bf16[2,96,128]{2,1,0:T(8,128)(2,1)S(1)}, u32[]{:S(2)}, u32[]{:S(2)}) collective-permute-start(bf16[2,96,128]{2,1,0:T(8,128)(2,1)S(1)} %stack.2.after_ref.refs_0_), channel_id=1, source_target_pairs={{0,2},{1,3},{2,0},{3,1},{4,6},{5,7},{6,4},{7,5},{8,10},{9,11},{10,... | collective-permute-start | bytes 147464 | tf_op jit(solution)/shard_map/ppermute | solution.py:61
  10.9 2.7 %prepare.4 = (bf16[16,128,1024]{2,1,0:T(8,128)(2,1)S(1)}, f32[8,128]{1,0:T(8,128)S(1)}, bf16[8,16,16,1024]{3,2,1,0:T(8,128)(2,1)S(1)}) custom-call(bf16[128,48,1024]{2,1,0:T(8,128)(2,1)} %t_ref.5, bf16[2,96,128]{2,1,0:T(8,128)(2,1)S(1)} %stack.2.after_ref.refs_0_, bf16[8,16,16,1024]{3,2,1,0:T(8,128)(2,1)S(1)} %get-tuple-element.41.refs_0_), custom_call_target="tpu_custom_call" | custom-call | bytes 6000000 | tf_op jit(solution)/shard_map/prepare/pallas_call | solution.py:37
  13.6 1.6 %collective-permute-start.2 = (bf16[4,96,128]{2,1,0:T(8,128)(2,1)S(1)}, bf16[4,96,128]{2,1,0:T(8,128)(2,1)S(1)}, u32[]{:S(2)}, u32[]{:S(2)}) collective-permute-start(bf16[4,96,128]{2,1,0:T(8,128)(2,1)S(1)} %stack.3.after_ref.refs_0_), channel_id=1, source_target_pairs={{0,1},{1,0},{2,3},{3,2},{4,5},{5,4},{6,7},{7,6},{8,9},{9,8},{10,11... | collective-permute-start | bytes 294920 | tf_op jit(solution)/shard_map/ppermute | solution.py:61
  15.1 2.7 %prepare.5 = (bf16[16,128,1024]{2,1,0:T(8,128)(2,1)S(1)}, f32[8,128]{1,0:T(8,128)S(1)}) custom-call(bf16[128,48,1024]{2,1,0:T(8,128)(2,1)} %t_ref.5, bf16[4,96,128]{2,1,0:T(8,128)(2,1)S(1)} %stack.3.after_ref.refs_0_, bf16[8,16,16,1024]{3,2,1,0:T(8,128)(2,1)S(1)} %get-tuple-element.43.refs_0_), custom_call_target="tpu_custom_call" | custom-call | bytes 6000000 | tf_op jit(solution)/shard_map/prepare/pallas_call | solution.py:37
  18.6 4.4 %project.1.a_ref = f32[128,128]{1,0:T(8,128)S(1)} custom-call(bf16[1024,64]{1,0:T(8,128)(2,1)S(1)} %get-tuple-element.45.turned_ref, f32[48,64]{1,0:T(8,128)S(1)} %get-tuple-element.46.second_ref, f32[64,64]{1,0:T(8,128)S(1)} %get-tuple-element.47.gram_ref, bf16[16,128,1024]{2,1,0:T(8,128)(2,1)S(1)} %get-tuple-element.48.refs_0_.refs_3_.refs_1_, ...), custom_call_target="tpu_custom_call" | custom-call | bytes 15000000 | tf_op jit(solution)/shard_map/project/pallas_call | solution.py:37
  25.7 1.4 %collective-permute-start.6 = (f32[64,128]{1,0:T(8,128)S(1)}, f32[64,128]{1,0:T(8,128)S(1)}, u32[]{:S(2)}, u32[]{:S(2)}) collective-permute-start(f32[64,128]{1,0:T(8,128)S(1)} %get-tuple-element.53), channel_id=1, source_target_pairs={{0,25},{1,24},{2,27},{3,26},{4,29},{5,28},{6,31},{7,30},{8,17},{9,... | collective-permute-start | bytes 98312 | tf_op jit(solution)/shard_map/ppermute | solution.py:61
  28.0 2.0 %collective-permute-done.6.refs_3_ = f32[64,128]{1,0:T(8,128)S(1)} collective-permute-done((f32[64,128]{1,0:T(8,128)S(1)}, f32[64,128]{1,0:T(8,128)S(1)}, u32[]{:S(2)}, u32[]{:S(2)}) %collective-permute-start.6) | collective-permute-done | bytes 32800 | tf_op jit(solution)/shard_map/ppermute | solution.py:61
  31.7 1.7 %eliminate.3.refs_2_.refs_0_ = f32[64,64]{1,0:T(8,128)S(1)} custom-call(f32[64,64]{1,0:T(8,128)S(1)} %get-tuple-element.55.refs_0_, f32[64,64]{1,0:T(8,128)S(1)} %get-tuple-element.56.refs_1_.other_ref, f32[64,128]{1,0:T(8,128)S(1)} %get-tuple-element.57.refs_2_.refs_0_), custom_call_target="tpu_custom_call" | custom-call | bytes 3000000 | tf_op jit(solution)/shard_map/eliminate/pallas_call | solution.py:37
  35.5 2.6 %collective-permute-done.8.refs_2_ = f32[64,128]{1,0:T(8,128)S(1)} collective-permute-done((f32[64,128]{1,0:T(8,128)S(1)}, f32[64,128]{1,0:T(8,128)S(1)}, u32[]{:S(2)}, u32[]{:S(2)}) %collective-permute-start.8) | collective-permute-done | bytes 32800 | tf_op jit(solution)/shard_map/ppermute | solution.py:61
  38.1 6.3 %slab.2 = (f32[64,128]{1,0:T(8,128)}, f32[64,128]{1,0:T(8,128)S(1)}, f32[48,64,768]{2,1,0:T(8,128)S(1)}, f32[2,64,128]{2,1,0:T(8,128)S(1)}, f32[2,64,128]{2,1,0:T(8,128)S(1)}, /*index=5*/f32[2,64,128]{2,1,0:T(8,128)S(1)}) custom-call(s32[1]{0:T(128)} %bitcast.me_ref, f32[48,64,128]{2,1,0:T(8,128)S(1)} %get-tuple-element.52.wide_ref, ...), custom_call_target="tpu_custom_call" | custom-call | bytes 18000000 | tf_op jit(solution)/shard_map/slab/pallas_call | solution.py:37
  45.6 1.4 %collective-permute-start.10 = (f32[2,64,128]{2,1,0:T(8,128)S(1)}, f32[2,64,128]{2,1,0:T(8,128)S(1)}, u32[]{:S(2)}, u32[]{:S(2)}) collective-permute-start(f32[2,64,128]{2,1,0:T(8,128)S(1)} %get-tuple-element.63), channel_id=1, source_target_pairs={{0,2},{1,3},{2,0},{3,1},{4,6},{5,7},{6,4},{7,5},{8,10},{9,11},{10,... | collective-permute-start | bytes 196616 | tf_op jit(solution)/shard_map/ppermute | solution.py:61
  47.9 1.9 %slab.3 = (f32[48,64,256]{2,1,0:T(8,128)S(1)}, f32[2,64,128]{2,1,0:T(8,128)S(1)}) custom-call(s32[1]{0:T(128)} %bitcast.me_ref, f32[48,64,128]{2,1,0:T(8,128)S(1)} %get-tuple-element.52.wide_ref, f32[64,128]{1,0:T(8,128)S(1)} %get-tuple-element.59.refs_0_.frames_ref, bf16[16,128,1024]{2,1,0:T(8,128)(2,1)S(1)} %get-tuple-element.48.refs_0_.refs_3_.refs_1_, ...), custom_call_target="tpu_custom_call" | custom-call | bytes 6000000 | tf_op jit(solution)/shard_map/slab/pallas_call | solution.py:37
  52.1 1.5 %collective-permute-start.12 = (f32[2,64,128]{2,1,0:T(8,128)S(1)}, f32[2,64,128]{2,1,0:T(8,128)S(1)}, u32[]{:S(2)}, u32[]{:S(2)}) collective-permute-start(f32[2,64,128]{2,1,0:T(8,128)S(1)} %add.13.refs_1_.refs_0_), channel_id=1, source_target_pairs={{0,4},{1,5},{2,6},{3,7},{4,0},{5,1},{6,2},{7,3},{8,12},{9,13},{10,... | collective-permute-start | bytes 196616 | tf_op jit(solution)/shard_map/ppermute | solution.py:61
  53.6 1.7 %eliminate.5.inverse_ref = f32[64,64]{1,0:T(8,128)S(1)} custom-call(f32[64,64]{1,0:T(8,128)S(1)} %get-tuple-element.61.refs_4_.refs_0_, f32[2,64,128]{2,1,0:T(8,128)S(1)} %add.13.refs_1_.refs_0_), custom_call_target="tpu_custom_call" | custom-call | bytes 3000000 | tf_op jit(solution)/shard_map/eliminate/pallas_call | solution.py:37
  55.3 2.8 %collective-permute-done.12.refs_1_ = f32[2,64,128]{2,1,0:T(8,128)S(1)} collective-permute-done((f32[2,64,128]{2,1,0:T(8,128)S(1)}, f32[2,64,128]{2,1,0:T(8,128)S(1)}, u32[]{:S(2)}, u32[]{:S(2)}) %collective-permute-start.12) | collective-permute-done | bytes 65568 | tf_op jit(solution)/shard_map/ppermute | solution.py:61
  59.1 1.6 %collective-permute-start.14 = (bf16[2,64,128]{2,1,0:T(8,128)(2,1)S(1)}, bf16[2,64,128]{2,1,0:T(8,128)(2,1)S(1)}, u32[]{:S(2)}, u32[]{:S(2)}) collective-permute-start(bf16[2,64,128]{2,1,0:T(8,128)(2,1)S(1)} %update.1.refs_0_), channel_id=1, source_target_pairs={{0,2},{1,3},{2,0},{3,1},{4,6},{5,7},{6,4},{7,5},{8,10},{9,11},{10,... | collective-permute-start | bytes 98312 | tf_op jit(solution)/shard_map/ppermute | solution.py:61
  63.1 1.5 %collective-permute-done.13.refs_1_ = bf16[2,64,128]{2,1,0:T(8,128)(2,1)S(1)} collective-permute-done((bf16[2,64,128]{2,1,0:T(8,128)(2,1)S(1)}, bf16[2,64,128]{2,1,0:T(8,128)(2,1)S(1)}, u32[]{:S(2)}, u32[]{:S(2)}) %collective-permute-start.13) | collective-permute-done | bytes 32800 | tf_op jit(solution)/shard_map/ppermute | solution.py:61
  64.6 2.7 %second.1.refs_0_.refs_2_ = f32[64,128]{1,0:T(8,128)S(1)} custom-call(bf16[2,64,128]{2,1,0:T(8,128)(2,1)S(1)} %update.1.refs_0_, bf16[2,64,128]{2,1,0:T(8,128)(2,1)S(1)} %collective-permute-done.13.refs_1_, bf16[2,64,128]{2,1,0:T(8,128)(2,1)S(1)} %collective-permute-done.14.refs_2_, bf16[2,64,128]{2,1,0:T(8,128)(2,1)S(1)} %collective-permute-done.15.refs_3_, ...), custom_call_target="tpu_custom_call" | custom-call | bytes 6000000 | tf_op jit(solution)/shard_map/second/pallas_call | solution.py:37
  69.9 2.0 %collective-permute-done.17.got_ref = f32[64,128]{1,0:T(8,128)S(1)} collective-permute-done((f32[64,128]{1,0:T(8,128)S(1)}, f32[64,128]{1,0:T(8,128)S(1)}, u32[]{:S(2)}, u32[]{:S(2)}) %collective-permute-start.17) | collective-permute-done | bytes 32800 | tf_op jit(solution)/shard_map/ppermute | solution.py:61
  71.9 4.1 %mode_send.1 = (f32[64,128]{1,0:T(8,128)S(1)}, bf16[2,64,128]{2,1,0:T(8,128)(2,1)S(1)}, bf16[2,64,128]{2,1,0:T(8,128)(2,1)S(1)}, bf16[2,64,128]{2,1,0:T(8,128)(2,1)S(1)}) custom-call(f32[64,128]{1,0:T(8,128)S(1)} %add.14.mine_ref, f32[64,128]{1,0:T(8,128)S(1)} %collective-permute-done.17.got_ref, f32[64,64]{1,0:T(8,128)S(1)} %get-tuple-element.67.gram_frames_ref, ...), custom_call_target="tpu_custom_call" | custom-call | bytes 12000000 | tf_op jit(solution)/shard_map/mode_send/pallas_call | solution.py:37
  76.6 2.1 %collective-permute-start.20 = (bf16[2,64,128]{2,1,0:T(8,128)(2,1)S(1)}, bf16[2,64,128]{2,1,0:T(8,128)(2,1)S(1)}, u32[]{:S(2)}, u32[]{:S(2)}) collective-permute-start(bf16[2,64,128]{2,1,0:T(8,128)(2,1)S(1)} %get-tuple-element.71), channel_id=1, source_target_pairs={{0,3},{1,2},{2,1},{3,0},{4,7},{5,6},{6,5},{7,4},{8,11},{9,10},{10,... | collective-permute-start | bytes 98312 | tf_op jit(solution)/shard_map/ppermute | solution.py:61
  83.5 4.0 %collective-permute-done.21 = bf16[64,128]{1,0:T(8,128)(2,1)S(1)} collective-permute-done((bf16[64,128]{1,0:T(8,128)(2,1)S(1)}, bf16[64,128]{1,0:T(8,128)(2,1)S(1)}, u32[]{:S(2)}, u32[]{:S(2)}) %collective-permute-start.21) | collective-permute-done | bytes 16416 | tf_op jit(solution)/shard_map/ppermute | solution.py:61
  (46 shorter events, 25.3 us)
Async XLA Ops:
  1.5 7.7 %collective-permute-start = (bf16[1,96,128]{2,1,0:T(8,128)(2,1)S(1)}, bf16[1,96,128]{2,1,0:T(8,128)(2,1)S(1)}, u32[]{:S(2)}, u32[]{:S(2)}) collective-permute-start(bf16[1,96,128]{2,1,0:T(8,128)(2,1)S(1)} %get-tuple-element.39.after_ref.refs_0_), channel_id=1, source_target_pairs={{0,4},{1,5},{2,6},{3,7},{4,0},{5,1},{6,2},{7,3},{8,12},{9,13},{10,... | collective-permute-start | bytes 73736 | tf_op jit(solution)/shard_map/ppermute | solution.py:61
  9.2 4.3 %collective-permute-start.1 = (bf16[2,96,128]{2,1,0:T(8,128)(2,1)S(1)}, bf16[2,96,128]{2,1,0:T(8,128)(2,1)S(1)}, u32[]{:S(2)}, u32[]{:S(2)}) collective-permute-start(bf16[2,96,128]{2,1,0:T(8,128)(2,1)S(1)} %stack.2.after_ref.refs_0_), channel_id=1, source_target_pairs={{0,2},{1,3},{2,0},{3,1},{4,6},{5,7},{6,4},{7,5},{8,10},{9,11},{10,... | collective-permute-start | bytes 147464 | tf_op jit(solution)/shard_map/ppermute | solution.py:61
  13.6 4.7 %collective-permute-start.2 = (bf16[4,96,128]{2,1,0:T(8,128)(2,1)S(1)}, bf16[4,96,128]{2,1,0:T(8,128)(2,1)S(1)}, u32[]{:S(2)}, u32[]{:S(2)}) collective-permute-start(bf16[4,96,128]{2,1,0:T(8,128)(2,1)S(1)} %stack.3.after_ref.refs_0_), channel_id=1, source_target_pairs={{0,1},{1,0},{2,3},{3,2},{4,5},{5,4},{6,7},{7,6},{8,9},{9,8},{10,11... | collective-permute-start | bytes 294920 | tf_op jit(solution)/shard_map/ppermute | solution.py:61
  23.0 1.3 %collective-permute-start.3 = (f32[128,128]{1,0:T(8,128)S(1)}, f32[128,128]{1,0:T(8,128)S(1)}, u32[]{:S(2)}, u32[]{:S(2)}) collective-permute-start(f32[128,128]{1,0:T(8,128)S(1)} %project.1.a_ref), channel_id=1, source_target_pairs={{0,8},{1,9},{2,10},{3,11},{4,12},{5,13},{6,14},{7,15},{8,0},{9,1},... | collective-permute-start | bytes 196616 | tf_op jit(solution)/shard_map/ppermute | solution.py:61
  24.4 6.1 %collective-permute-start.4 = (f32[128,128]{1,0:T(8,128)S(1)}, f32[128,128]{1,0:T(8,128)S(1)}, u32[]{:S(2)}, u32[]{:S(2)}) collective-permute-start(f32[128,128]{1,0:T(8,128)S(1)} %get-tuple-element.51.after_ref.refs_0_), channel_id=1, source_target_pairs={{0,24},{1,25},{2,26},{3,27},{4,28},{5,29},{6,30},{7,31},{8,16},{9,... | collective-permute-start | bytes 196616 | tf_op jit(solution)/shard_map/ppermute | solution.py:61
  25.7 4.2 %collective-permute-start.6 = (f32[64,128]{1,0:T(8,128)S(1)}, f32[64,128]{1,0:T(8,128)S(1)}, u32[]{:S(2)}, u32[]{:S(2)}) collective-permute-start(f32[64,128]{1,0:T(8,128)S(1)} %get-tuple-element.53), channel_id=1, source_target_pairs={{0,25},{1,24},{2,27},{3,26},{4,29},{5,28},{6,31},{7,30},{8,17},{9,... | collective-permute-start | bytes 98312 | tf_op jit(solution)/shard_map/ppermute | solution.py:61
  27.1 3.4 %collective-permute-start.5 = (f32[64,128]{1,0:T(8,128)S(1)}, f32[64,128]{1,0:T(8,128)S(1)}, u32[]{:S(2)}, u32[]{:S(2)}) collective-permute-start(f32[64,128]{1,0:T(8,128)S(1)} %get-tuple-element.53), channel_id=1, source_target_pairs={{0,9},{1,8},{2,11},{3,10},{4,13},{5,12},{6,15},{7,14},{8,1},{9,0},... | collective-permute-start | bytes 98312 | tf_op jit(solution)/shard_map/ppermute | solution.py:61
  30.5 3.4 %collective-permute-start.7 = (f32[64,128]{1,0:T(8,128)S(1)}, f32[64,128]{1,0:T(8,128)S(1)}, u32[]{:S(2)}, u32[]{:S(2)}) collective-permute-start(f32[64,128]{1,0:T(8,128)S(1)} %get-tuple-element.57.refs_2_.refs_0_), channel_id=1, source_target_pairs={{0,10},{1,11},{2,8},{3,9},{4,14},{5,15},{6,12},{7,13},{8,2},{9,3},... | collective-permute-start | bytes 98312 | tf_op jit(solution)/shard_map/ppermute | solution.py:61
  33.9 4.2 %collective-permute-start.8 = (f32[64,128]{1,0:T(8,128)S(1)}, f32[64,128]{1,0:T(8,128)S(1)}, u32[]{:S(2)}, u32[]{:S(2)}) collective-permute-start(f32[64,128]{1,0:T(8,128)S(1)} %add.12.refs_1_), channel_id=1, source_target_pairs={{0,12},{1,13},{2,14},{3,15},{4,8},{5,9},{6,10},{7,11},{8,4},{9,5},... | collective-permute-start | bytes 98312 | tf_op jit(solution)/shard_map/ppermute | solution.py:61
  44.4 6.3 %collective-permute-start.9 = (f32[2,64,128]{2,1,0:T(8,128)S(1)}, f32[2,64,128]{2,1,0:T(8,128)S(1)}, u32[]{:S(2)}, u32[]{:S(2)}) collective-permute-start(f32[2,64,128]{2,1,0:T(8,128)S(1)} %get-tuple-element.62), channel_id=1, source_target_pairs={{0,1},{1,0},{2,3},{3,2},{4,5},{5,4},{6,7},{7,6},{8,9},{9,8},{10,11... | collective-permute-start | bytes 196616 | tf_op jit(solution)/shard_map/ppermute | solution.py:61
  45.6 5.2 %collective-permute-start.10 = (f32[2,64,128]{2,1,0:T(8,128)S(1)}, f32[2,64,128]{2,1,0:T(8,128)S(1)}, u32[]{:S(2)}, u32[]{:S(2)}) collective-permute-start(f32[2,64,128]{2,1,0:T(8,128)S(1)} %get-tuple-element.63), channel_id=1, source_target_pairs={{0,2},{1,3},{2,0},{3,1},{4,6},{5,7},{6,4},{7,5},{8,10},{9,11},{10,... | collective-permute-start | bytes 196616 | tf_op jit(solution)/shard_map/ppermute | solution.py:61
  46.9 5.2 %collective-permute-start.11 = (f32[2,64,128]{2,1,0:T(8,128)S(1)}, f32[2,64,128]{2,1,0:T(8,128)S(1)}, u32[]{:S(2)}, u32[]{:S(2)}) collective-permute-start(f32[2,64,128]{2,1,0:T(8,128)S(1)} %get-tuple-element.64), channel_id=1, source_target_pairs={{0,3},{1,2},{2,1},{3,0},{4,7},{5,6},{6,5},{7,4},{8,11},{9,10},{10,... | collective-permute-start | bytes 196616 | tf_op jit(solution)/shard_map/ppermute | solution.py:61
  52.1 5.9 %collective-permute-start.12 = (f32[2,64,128]{2,1,0:T(8,128)S(1)}, f32[2,64,128]{2,1,0:T(8,128)S(1)}, u32[]{:S(2)}, u32[]{:S(2)}) collective-permute-start(f32[2,64,128]{2,1,0:T(8,128)S(1)} %add.13.refs_1_.refs_0_), channel_id=1, source_target_pairs={{0,4},{1,5},{2,6},{3,7},{4,0},{5,1},{6,2},{7,3},{8,12},{9,13},{10,... | collective-permute-start | bytes 196616 | tf_op jit(solution)/shard_map/ppermute | solution.py:61
  58.2 4.9 %collective-permute-start.15 = (bf16[2,64,128]{2,1,0:T(8,128)(2,1)S(1)}, bf16[2,64,128]{2,1,0:T(8,128)(2,1)S(1)}, u32[]{:S(2)}, u32[]{:S(2)}) collective-permute-start(bf16[2,64,128]{2,1,0:T(8,128)(2,1)S(1)} %update.1.refs_0_), channel_id=1, source_target_pairs={{0,3},{1,2},{2,1},{3,0},{4,7},{5,6},{6,5},{7,4},{8,11},{9,10},{10,... | collective-permute-start | bytes 98312 | tf_op jit(solution)/shard_map/ppermute | solution.py:61
  59.1 4.0 %collective-permute-start.14 = (bf16[2,64,128]{2,1,0:T(8,128)(2,1)S(1)}, bf16[2,64,128]{2,1,0:T(8,128)(2,1)S(1)}, u32[]{:S(2)}, u32[]{:S(2)}) collective-permute-start(bf16[2,64,128]{2,1,0:T(8,128)(2,1)S(1)} %update.1.refs_0_), channel_id=1, source_target_pairs={{0,2},{1,3},{2,0},{3,1},{4,6},{5,7},{6,4},{7,5},{8,10},{9,11},{10,... | collective-permute-start | bytes 98312 | tf_op jit(solution)/shard_map/ppermute | solution.py:61
  60.7 3.9 %collective-permute-start.13 = (bf16[2,64,128]{2,1,0:T(8,128)(2,1)S(1)}, bf16[2,64,128]{2,1,0:T(8,128)(2,1)S(1)}, u32[]{:S(2)}, u32[]{:S(2)}) collective-permute-start(bf16[2,64,128]{2,1,0:T(8,128)(2,1)S(1)} %update.1.refs_0_), channel_id=1, source_target_pairs={{0,1},{1,0},{2,3},{3,2},{4,5},{5,4},{6,7},{7,6},{8,9},{9,8},{10,11... | collective-permute-start | bytes 98312 | tf_op jit(solution)/shard_map/ppermute | solution.py:61
  67.3 1.3 %collective-permute-start.16 = (f32[64,128]{1,0:T(8,128)S(1)}, f32[64,128]{1,0:T(8,128)S(1)}, u32[]{:S(2)}, u32[]{:S(2)}) collective-permute-start(f32[64,128]{1,0:T(8,128)S(1)} %second.1.refs_0_.refs_2_), channel_id=1, source_target_pairs={{0,8},{1,9},{2,10},{3,11},{4,12},{5,13},{6,14},{7,15},{8,0},{9,1},... | collective-permute-start | bytes 98312 | tf_op jit(solution)/shard_map/ppermute | solution.py:61
  68.6 3.3 %collective-permute-start.17 = (f32[64,128]{1,0:T(8,128)S(1)}, f32[64,128]{1,0:T(8,128)S(1)}, u32[]{:S(2)}, u32[]{:S(2)}) collective-permute-start(f32[64,128]{1,0:T(8,128)S(1)} %add.14.mine_ref), channel_id=1, source_target_pairs={{0,24},{1,25},{2,26},{3,27},{4,28},{5,29},{6,30},{7,31},{8,16},{9,... | collective-permute-start | bytes 98312 | tf_op jit(solution)/shard_map/ppermute | solution.py:61
  76.1 4.8 %collective-permute-start.19 = (bf16[2,64,128]{2,1,0:T(8,128)(2,1)S(1)}, bf16[2,64,128]{2,1,0:T(8,128)(2,1)S(1)}, u32[]{:S(2)}, u32[]{:S(2)}) collective-permute-start(bf16[2,64,128]{2,1,0:T(8,128)(2,1)S(1)} %get-tuple-element.70), channel_id=1, source_target_pairs={{0,2},{1,3},{2,0},{3,1},{4,6},{5,7},{6,4},{7,5},{8,10},{9,11},{10,... | collective-permute-start | bytes 98312 | tf_op jit(solution)/shard_map/ppermute | solution.py:61
  76.6 4.9 %collective-permute-start.20 = (bf16[2,64,128]{2,1,0:T(8,128)(2,1)S(1)}, bf16[2,64,128]{2,1,0:T(8,128)(2,1)S(1)}, u32[]{:S(2)}, u32[]{:S(2)}) collective-permute-start(bf16[2,64,128]{2,1,0:T(8,128)(2,1)S(1)} %get-tuple-element.71), channel_id=1, source_target_pairs={{0,3},{1,2},{2,1},{3,0},{4,7},{5,6},{6,5},{7,4},{8,11},{9,10},{10,... | collective-permute-start | bytes 98312 | tf_op jit(solution)/shard_map/ppermute | solution.py:61
  78.7 3.9 %collective-permute-start.18 = (bf16[2,64,128]{2,1,0:T(8,128)(2,1)S(1)}, bf16[2,64,128]{2,1,0:T(8,128)(2,1)S(1)}, u32[]{:S(2)}, u32[]{:S(2)}) collective-permute-start(bf16[2,64,128]{2,1,0:T(8,128)(2,1)S(1)} %get-tuple-element.69.after_ref), channel_id=1, source_target_pairs={{0,1},{1,0},{2,3},{3,2},{4,5},{5,4},{6,7},{7,6},{8,9},{9,8},{10,11... | collective-permute-start | bytes 98312 | tf_op jit(solution)/shard_map/ppermute | solution.py:61
  82.6 4.9 %collective-permute-start.21 = (bf16[64,128]{1,0:T(8,128)(2,1)S(1)}, bf16[64,128]{1,0:T(8,128)(2,1)S(1)}, u32[]{:S(2)}, u32[]{:S(2)}) collective-permute-start(bf16[64,128]{1,0:T(8,128)(2,1)S(1)} %get-tuple-element.73), channel_id=1, source_target_pairs={{0,4},{1,5},{2,6},{3,7},{4,0},{5,1},{6,2},{7,3},{8,12},{9,13},{10,... | collective-permute-start | bytes 49160 | tf_op jit(solution)/shard_map/ppermute | solution.py:61

commit v8 on v7

--- a/solution.py
+++ b/solution.py
@@ -457,51 +457,54 @@
     )
 
 
-def second_body(*refs):
-    *stacks, kept_ref, sent_ref, out_ref, full_ref, fold_ref = refs
-    cols, components, near = kept_ref.shape
+def gather_gram_body(*refs):
+    *stacks, full_ref, gram_ref = refs
     blocks = [s[n] for s in stacks for n in range(s.shape[0])]
     for n, block in enumerate(blocks):
         full_ref[:, n * 128 : n * 128 + 128] = block.astype(F32)
+    full = full_ref[...].astype(BF16)
+    gram_ref[...] = dot(full, full, ((1,), (1,)))
+
+
+def gather_gram(stacks):
+    components = stacks[0].shape[1]
+    total = sum(s.shape[0] * s.shape[2] for s in stacks)
+    outs = (shaped((components, total)), shaped((components, components)))
+    return call(gather_gram_body, outs, [vmem()] * len(stacks), stacks, "gather_gram", us=0.3)
+
+
+def second_body(full_ref, kept_ref, sent_ref, out_ref):
+    cols, components, near = kept_ref.shape
     lane = lax.broadcasted_iota(jnp.int32, (8, 128), 1)
-    ones = jnp.ones((256, 128), BF16)
-
-    def folded(j, at, mine):
-        products = kept_ref[j, at, :] * mine[:, :near], sent_ref[j, at, :] * mine[:, near:]
-        return paired([p[:, c : c + 128] for p in products for c in range(0, p.shape[1], 128)])
 
     def step(n, _):
         at = pl.ds(pl.multiple_of(n * 8, 8), 8)
         mine = full_ref[at, :]
-        for j in range(0, cols, 2):
-            pair = jnp.concatenate([folded(j, at, mine), folded(j + 1, at, mine)], axis=0)
-            high = pair.astype(BF16)
-            fold_ref[8 * j : 8 * j + 16, :128] = high
-            fold_ref[8 * j : 8 * j + 16, 128:] = (pair - high.astype(F32)).astype(BF16)
-        sums = dot(fold_ref[...], ones, ((1,), (0,)))
         total = jnp.zeros((8, 128), F32)
         for j in range(cols):
-            total = jnp.where(lane == j, sums[8 * j : 8 * j + 8], total)
+            products = kept_ref[j, at, :] * mine[:, :near], sent_ref[j, at, :] * mine[:, near:]
+            folded = paired([p[:, c : c + 128] for p in products for c in range(0, p.shape[1], 128)])
+            total = jnp.where(lane == j, jnp.sum(folded, axis=1, keepdims=True), total)
         out_ref[at, :] = total
         return 0
 
     lax.fori_loop(0, components // 8, step, 0)
-    full = full_ref[...].astype(BF16)
-    gram = dot(full, full, ((1,), (1,)))
-    out_ref[...] = jnp.concatenate([out_ref[:, :components], gram], axis=1)
-
-
-def second(stacks, kept, sent):
+
+
+def second(full, kept, sent):
     components = kept.shape[1]
-    return call(
-        second_body,
-        shaped((components, 2 * components)),
-        [vmem()] * (2 + len(stacks)),
-        (*stacks, kept, sent),
-        "second",
-        [VM((components, kept.shape[2] + sent.shape[2]), F32), VM((8 * kept.shape[0], 256), BF16)],
-        us=2,
-    )
+    return call(second_body, shaped((components, 128)), [vmem()] * 3, (full, kept, sent), "second", us=2)
+
+
+def third_inverse_body(mine_ref, got_ref, other_ref, after_ref, out_ref):
+    del after_ref
+    gram = (mine_ref[...] + got_ref[...]) * other_ref[...]
+    out_ref[...] = eliminate(ridged(gram), 0, gram.shape[0], 8)
+
+
+def third_inverse(mine, got, other, after):
+    specs = [vmem()] * 3 + [anywhere()]
+    return call(third_inverse_body, shaped(other.shape), specs, (mine, got, other, after), "third_inverse", us=3)
 
 
 def mode_sums(new_ref, z_ref, out_refs):
@@ -522,28 +525,25 @@
     lax.fori_loop(0, components // 8, step, 0)
 
 
-def mode_send_body(mine_ref, got_ref, gram_frames_ref, sent_ref, new_ref, *refs):
+def mode_send_body(mine_ref, got_ref, inverse_ref, sent_ref, new_ref, *refs):
     outs, sums = refs[:3], refs[3:]
-    components = new_ref.shape[0]
-    summed = mine_ref[...] + got_ref[...]
-    solver = eliminate(ridged(summed[:, components:] * gram_frames_ref[...]), 0, components)
-    new_ref[...] = dot(solver, summed, ((1,), (0,)), HIGH)
+    new_ref[...] = dot(inverse_ref[...], mine_ref[...] + got_ref[...], ((1,), (0,)), HIGH)
     mode_sums(new_ref, sent_ref, sums)
     for out_ref, sum_ref in zip(outs, sums):
         out_ref[...] = sum_ref[...].astype(out_ref.dtype)
 
 
-def mode_send(mine, got, gram_frames, sent, kind):
+def mode_send(mine, got, inverse_now, sent, kind):
     components = sent.shape[1]
     shape = (2, components, 128)
     return call(
         mode_send_body,
-        (shaped((components, 2 * components)),) + (shaped(shape, kind),) * 3,
+        (shaped(mine.shape),) + (shaped(shape, kind),) * 3,
         [vmem()] * 4,
-        (mine, got, gram_frames, sent),
+        (mine, got, inverse_now, sent),
         "mode_send",
         [VM(shape, F32)] * 3,
-        us=4,
+        us=1.5,
     )
 
 
@@ -661,11 +661,16 @@
         new = update(state, [summed[None]])[0]
         new = lax.all_gather(new, "col", axis=1, tiled=True).reshape(components, 2, 4, 128)
         stacks = list(new.transpose(2, 1, 0, 3))
-    part = second(stacks, kept, sent)
-    part = add([part, swap(part, BOTH, every, core)], part)
+    full, gram_new = gather_gram(stacks)
+    got = swap(gram_new, BOTH, every, core)
+    part = second(full, kept, sent)
+    gram_new = add([gram_new, got], part)
+    gram_got = swap(gram_new, BOTH, every, upper[0] | core)
+    part = add([part, swap(part, BOTH, every, core)], gram_new)
     got = swap(part, BOTH, every, upper[0] | core)
-
-    new_second, *sends = mode_send(part, got, gram_frames, sent, BF16 if direct else F32)
+    inverse_third = third_inverse(gram_new, gram_got, gram_frames, part)
+
+    new_second, *sends = mode_send(part, got, inverse_third, sent, BF16 if direct else F32)
     if not direct:
         keep = mode_keep(new_second, kept, new_second)
         blocks = jnp.stack([keep, *sends]).transpose(2, 1, 0, 3).reshape(components, row_count)

time: 88.5 us -> 87.8 us (level)
  Pallas kernels: 36.6 us -> 34.6 us
  starting transfers between devices: 26.9 us -> 28.5 us
    pallas_call x25 -> x28, Pallas kernels: 36.6 us -> 34.6 us  [call(): pl.pallas_call(body, out_shape=outs, in_specs=ins, out_specs=(vmem(),) *...]
    ppermute x22 -> x24, starting transfers between devices: 26.9 us -> 28.5 us  [swap(): return lax.ppermute(x, axes, [(n, n ^ offset) for n in range(count)])]
    ppermute x22 -> x24, waiting for transfers between devices: 23.2 us -> 22.9 us  [swap(): return lax.ppermute(x, axes, [(n, n ^ offset) for n in range(count)])]
  transfers between devices with their start and end apart: 22 -> 24, of which waited for: 15 -> 15; matrix products, arithmetic and copies ran while one was open for 0% -> 0% of each run, Pallas kernels for 20% -> 22%
where the time goes in v8:
time: 87.8 us; the launch traced here: 87.4 us
  Pallas kernels  34.6 us (39%)
  starting transfers between devices  28.5 us (32%)
  waiting for transfers between devices  22.9 us (26%)
    pallas_call x28, Pallas kernels, call(): pl.pallas_call(body, out_shape=outs, in_specs=ins, out_specs=(vmem(),) *...  34.6 us
    ppermute x24, starting transfers between devices, swap(): return lax.ppermute(x, axes, [(n, n ^ offset) for n in range(count)])  28.5 us
    ppermute x24, waiting for transfers between devices, swap(): return lax.ppermute(x, axes, [(n, n ^ offset) for n in range(count)])  22.9 us
  transfers between devices with their start and end apart: 24, of which 15 were waited for; matrix products, arithmetic and copies ran while one was open for 0% of the time, Pallas kernels for 22%

profile of v8, /device:TPU:0, one launch (start us, length us, event | category | flops | bytes accessed | tf_op | source)
XLA Modules:
  0.0 87.4 jit_solution(13026504477471645759)
XLA Ops:
  1.5 4.1 %collective-permute-start = (bf16[1,96,128]{2,1,0:T(8,128)(2,1)S(1)}, bf16[1,96,128]{2,1,0:T(8,128)(2,1)S(1)}, u32[]{:S(2)}, u32[]{:S(2)}) collective-permute-start(bf16[1,96,128]{2,1,0:T(8,128)(2,1)S(1)} %get-tuple-element.41.after_ref.refs_0_), channel_id=1, source_target_pairs={{0,4},{1,5},{2,6},{3,7},{4,0},{5,1},{6,2},{7,3},{8,12},{9,13},{10,... | collective-permute-start | bytes 73736 | tf_op jit(solution)/shard_map/ppermute | solution.py:61
  5.6 3.6 %prepare.3 = (bf16[16,128,1024]{2,1,0:T(8,128)(2,1)S(1)}, f32[8,128]{1,0:T(8,128)S(1)}, bf16[8,16,16,1024]{3,2,1,0:T(8,128)(2,1)S(1)}) custom-call(bf16[128,48,1024]{2,1,0:T(8,128)(2,1)} %t_ref.5, bf16[1,96,128]{2,1,0:T(8,128)(2,1)S(1)} %get-tuple-element.41.after_ref.refs_0_), custom_call_target="tpu_custom_call" | custom-call | bytes 6000000 | tf_op jit(solution)/shard_map/prepare/pallas_call | solution.py:37
  9.2 1.6 %collective-permute-start.1 = (bf16[2,96,128]{2,1,0:T(8,128)(2,1)S(1)}, bf16[2,96,128]{2,1,0:T(8,128)(2,1)S(1)}, u32[]{:S(2)}, u32[]{:S(2)}) collective-permute-start(bf16[2,96,128]{2,1,0:T(8,128)(2,1)S(1)} %stack.2.after_ref.refs_0_), channel_id=1, source_target_pairs={{0,2},{1,3},{2,0},{3,1},{4,6},{5,7},{6,4},{7,5},{8,10},{9,11},{10,... | collective-permute-start | bytes 147464 | tf_op jit(solution)/shard_map/ppermute | solution.py:61
  10.9 2.7 %prepare.4 = (bf16[16,128,1024]{2,1,0:T(8,128)(2,1)S(1)}, f32[8,128]{1,0:T(8,128)S(1)}, bf16[8,16,16,1024]{3,2,1,0:T(8,128)(2,1)S(1)}) custom-call(bf16[128,48,1024]{2,1,0:T(8,128)(2,1)} %t_ref.5, bf16[2,96,128]{2,1,0:T(8,128)(2,1)S(1)} %stack.2.after_ref.refs_0_, bf16[8,16,16,1024]{3,2,1,0:T(8,128)(2,1)S(1)} %get-tuple-element.43.refs_0_), custom_call_target="tpu_custom_call" | custom-call | bytes 6000000 | tf_op jit(solution)/shard_map/prepare/pallas_call | solution.py:37
  13.6 1.6 %collective-permute-start.2 = (bf16[4,96,128]{2,1,0:T(8,128)(2,1)S(1)}, bf16[4,96,128]{2,1,0:T(8,128)(2,1)S(1)}, u32[]{:S(2)}, u32[]{:S(2)}) collective-permute-start(bf16[4,96,128]{2,1,0:T(8,128)(2,1)S(1)} %stack.3.after_ref.refs_0_), channel_id=1, source_target_pairs={{0,1},{1,0},{2,3},{3,2},{4,5},{5,4},{6,7},{7,6},{8,9},{9,8},{10,11... | collective-permute-start | bytes 294920 | tf_op jit(solution)/shard_map/ppermute | solution.py:61
  15.1 2.7 %prepare.5 = (bf16[16,128,1024]{2,1,0:T(8,128)(2,1)S(1)}, f32[8,128]{1,0:T(8,128)S(1)}) custom-call(bf16[128,48,1024]{2,1,0:T(8,128)(2,1)} %t_ref.5, bf16[4,96,128]{2,1,0:T(8,128)(2,1)S(1)} %stack.3.after_ref.refs_0_, bf16[8,16,16,1024]{3,2,1,0:T(8,128)(2,1)S(1)} %get-tuple-element.45.refs_0_), custom_call_target="tpu_custom_call" | custom-call | bytes 6000000 | tf_op jit(solution)/shard_map/prepare/pallas_call | solution.py:37
  18.6 4.4 %project.1.a_ref = f32[128,128]{1,0:T(8,128)S(1)} custom-call(bf16[1024,64]{1,0:T(8,128)(2,1)S(1)} %get-tuple-element.47.turned_ref, f32[48,64]{1,0:T(8,128)S(1)} %get-tuple-element.48.second_ref, f32[64,64]{1,0:T(8,128)S(1)} %get-tuple-element.49.gram_ref, bf16[16,128,1024]{2,1,0:T(8,128)(2,1)S(1)} %get-tuple-element.50.refs_0_.refs_3_.refs_1_, ...), custom_call_target="tpu_custom_call" | custom-call | bytes 15000000 | tf_op jit(solution)/shard_map/project/pallas_call | solution.py:37
  28.0 2.0 %collective-permute-done.6.refs_3_ = f32[64,128]{1,0:T(8,128)S(1)} collective-permute-done((f32[64,128]{1,0:T(8,128)S(1)}, f32[64,128]{1,0:T(8,128)S(1)}, u32[]{:S(2)}, u32[]{:S(2)}) %collective-permute-start.6) | collective-permute-done | bytes 32800 | tf_op jit(solution)/shard_map/ppermute | solution.py:61
  31.7 1.7 %eliminate.3.refs_2_.refs_0_ = f32[64,64]{1,0:T(8,128)S(1)} custom-call(f32[64,64]{1,0:T(8,128)S(1)} %get-tuple-element.57.refs_0_, f32[64,64]{1,0:T(8,128)S(1)} %get-tuple-element.58.refs_1_.other_ref, f32[64,128]{1,0:T(8,128)S(1)} %get-tuple-element.59.refs_2_.refs_0_), custom_call_target="tpu_custom_call" | custom-call | bytes 3000000 | tf_op jit(solution)/shard_map/eliminate/pallas_call | solution.py:37
  35.5 2.6 %collective-permute-done.8.refs_2_ = f32[64,128]{1,0:T(8,128)S(1)} collective-permute-done((f32[64,128]{1,0:T(8,128)S(1)}, f32[64,128]{1,0:T(8,128)S(1)}, u32[]{:S(2)}, u32[]{:S(2)}) %collective-permute-start.8) | collective-permute-done | bytes 32800 | tf_op jit(solution)/shard_map/ppermute | solution.py:61
  38.1 6.3 %slab.2 = (f32[64,128]{1,0:T(8,128)}, f32[64,128]{1,0:T(8,128)S(1)}, f32[48,64,768]{2,1,0:T(8,128)S(1)}, f32[2,64,128]{2,1,0:T(8,128)S(1)}, f32[2,64,128]{2,1,0:T(8,128)S(1)}, /*index=5*/f32[2,64,128]{2,1,0:T(8,128)S(1)}) custom-call(s32[1]{0:T(128)} %bitcast.me_ref, f32[48,64,128]{2,1,0:T(8,128)S(1)} %get-tuple-element.54.wide_ref, ...), custom_call_target="tpu_custom_call" | custom-call | bytes 18000000 | tf_op jit(solution)/shard_map/slab/pallas_call | solution.py:37
  47.9 1.9 %slab.3 = (f32[48,64,256]{2,1,0:T(8,128)S(1)}, f32[2,64,128]{2,1,0:T(8,128)S(1)}) custom-call(s32[1]{0:T(128)} %bitcast.me_ref, f32[48,64,128]{2,1,0:T(8,128)S(1)} %get-tuple-element.54.wide_ref, f32[64,128]{1,0:T(8,128)S(1)} %get-tuple-element.61.refs_0_.frames_ref, bf16[16,128,1024]{2,1,0:T(8,128)(2,1)S(1)} %get-tuple-element.50.refs_0_.refs_3_.refs_1_, ...), custom_call_target="tpu_custom_call" | custom-call | bytes 6000000 | tf_op jit(solution)/shard_map/slab/pallas_call | solution.py:37
  52.1 1.5 %collective-permute-start.12 = (f32[2,64,128]{2,1,0:T(8,128)S(1)}, f32[2,64,128]{2,1,0:T(8,128)S(1)}, u32[]{:S(2)}, u32[]{:S(2)}) collective-permute-start(f32[2,64,128]{2,1,0:T(8,128)S(1)} %add.14.refs_1_.refs_0_), channel_id=1, source_target_pairs={{0,4},{1,5},{2,6},{3,7},{4,0},{5,1},{6,2},{7,3},{8,12},{9,13},{10,... | collective-permute-start | bytes 196616 | tf_op jit(solution)/shard_map/ppermute | solution.py:61
  53.6 1.7 %eliminate.5.inverse_ref = f32[64,64]{1,0:T(8,128)S(1)} custom-call(f32[64,64]{1,0:T(8,128)S(1)} %get-tuple-element.63.refs_4_.refs_0_, f32[2,64,128]{2,1,0:T(8,128)S(1)} %add.14.refs_1_.refs_0_), custom_call_target="tpu_custom_call" | custom-call | bytes 3000000 | tf_op jit(solution)/shard_map/eliminate/pallas_call | solution.py:37
  55.3 2.8 %collective-permute-done.12.refs_1_ = f32[2,64,128]{2,1,0:T(8,128)S(1)} collective-permute-done((f32[2,64,128]{2,1,0:T(8,128)S(1)}, f32[2,64,128]{2,1,0:T(8,128)S(1)}, u32[]{:S(2)}, u32[]{:S(2)}) %collective-permute-start.12) | collective-permute-done | bytes 65568 | tf_op jit(solution)/shard_map/ppermute | solution.py:61
  59.1 1.6 %collective-permute-start.14 = (bf16[2,64,128]{2,1,0:T(8,128)(2,1)S(1)}, bf16[2,64,128]{2,1,0:T(8,128)(2,1)S(1)}, u32[]{:S(2)}, u32[]{:S(2)}) collective-permute-start(bf16[2,64,128]{2,1,0:T(8,128)(2,1)S(1)} %update.1.refs_0_), channel_id=1, source_target_pairs={{0,2},{1,3},{2,0},{3,1},{4,6},{5,7},{6,4},{7,5},{8,10},{9,11},{10,... | collective-permute-start | bytes 98312 | tf_op jit(solution)/shard_map/ppermute | solution.py:61
  63.1 1.5 %collective-permute-done.13.refs_1_ = bf16[2,64,128]{2,1,0:T(8,128)(2,1)S(1)} collective-permute-done((bf16[2,64,128]{2,1,0:T(8,128)(2,1)S(1)}, bf16[2,64,128]{2,1,0:T(8,128)(2,1)S(1)}, u32[]{:S(2)}, u32[]{:S(2)}) %collective-permute-start.13) | collective-permute-done | bytes 32800 | tf_op jit(solution)/shard_map/ppermute | solution.py:61
  64.8 1.4 %second.1.refs_2_.refs_0_ = f32[64,128]{1,0:T(8,128)S(1)} custom-call(f32[64,1024]{1,0:T(8,128)S(1)} %get-tuple-element.67.full_ref, f32[48,64,256]{2,1,0:T(8,128)S(1)} %get-tuple-element.68.kept_ref, f32[48,64,768]{2,1,0:T(8,128)S(1)} %get-tuple-element.69.sent_ref), custom_call_target="tpu_custom_call" | custom-call | bytes 6000000 | tf_op jit(solution)/shard_map/second/pallas_call | solution.py:37
  67.7 1.6 %collective-permute-start.18 = (f32[64,128]{1,0:T(8,128)S(1)}, f32[64,128]{1,0:T(8,128)S(1)}, u32[]{:S(2)}, u32[]{:S(2)}) collective-permute-start(f32[64,128]{1,0:T(8,128)S(1)} %add.16.after_ref.mine_ref), channel_id=1, source_target_pairs={{0,24},{1,25},{2,26},{3,27},{4,28},{5,29},{6,30},{7,31},{8,16},{9,... | collective-permute-start | bytes 98312 | tf_op jit(solution)/shard_map/ppermute | solution.py:61
  69.5 3.1 %collective-permute-done.19.got_ref = f32[64,64]{1,0:T(8,128)S(1)} collective-permute-done((f32[64,64]{1,0:T(8,128)S(1)}, f32[64,64]{1,0:T(8,128)S(1)}, u32[]{:S(2)}, u32[]{:S(2)}) %collective-permute-start.19) | collective-permute-done | bytes 16416 | tf_op jit(solution)/shard_map/ppermute | solution.py:61
  72.6 1.8 %third_inverse.1.inverse_ref = f32[64,64]{1,0:T(8,128)S(1)} custom-call(f32[64,64]{1,0:T(8,128)S(1)} %add.15.refs_2_.mine_ref, f32[64,64]{1,0:T(8,128)S(1)} %collective-permute-done.19.got_ref, f32[64,64]{1,0:T(8,128)S(1)} %get-tuple-element.71.other_ref, f32[64,128]{1,0:T(8,128)S(1)} %add.16.after_ref.mine_ref), custom_call_target="tpu_custom_call" | custom-call | bytes 9000000 | tf_op jit(solution)/shard_map/third_inverse/pallas_call | solution.py:37
  75.9 2.2 %collective-permute-start.22 = (bf16[2,64,128]{2,1,0:T(8,128)(2,1)S(1)}, bf16[2,64,128]{2,1,0:T(8,128)(2,1)S(1)}, u32[]{:S(2)}, u32[]{:S(2)}) collective-permute-start(bf16[2,64,128]{2,1,0:T(8,128)(2,1)S(1)} %get-tuple-element.75), channel_id=1, source_target_pairs={{0,3},{1,2},{2,1},{3,0},{4,7},{5,6},{6,5},{7,4},{8,11},{9,10},{10,... | collective-permute-start | bytes 98312 | tf_op jit(solution)/shard_map/ppermute | solution.py:61
  82.1 1.4 %collective-permute-start.23 = (bf16[64,128]{1,0:T(8,128)(2,1)S(1)}, bf16[64,128]{1,0:T(8,128)(2,1)S(1)}, u32[]{:S(2)}, u32[]{:S(2)}) collective-permute-start(bf16[64,128]{1,0:T(8,128)(2,1)S(1)} %get-tuple-element.77), channel_id=1, source_target_pairs={{0,4},{1,5},{2,6},{3,7},{4,0},{5,1},{6,2},{7,3},{8,12},{9,13},{10,... | collective-permute-start | bytes 49160 | tf_op jit(solution)/shard_map/ppermute | solution.py:61
  83.5 3.3 %collective-permute-done.23 = bf16[64,128]{1,0:T(8,128)(2,1)S(1)} collective-permute-done((bf16[64,128]{1,0:T(8,128)(2,1)S(1)}, bf16[64,128]{1,0:T(8,128)(2,1)S(1)}, u32[]{:S(2)}, u32[]{:S(2)}) %collective-permute-start.23) | collective-permute-done | bytes 16416 | tf_op jit(solution)/shard_map/ppermute | solution.py:61
  (53 shorter events, 27.6 us)
Async XLA Ops:
  1.5 7.7 %collective-permute-start = (bf16[1,96,128]{2,1,0:T(8,128)(2,1)S(1)}, bf16[1,96,128]{2,1,0:T(8,128)(2,1)S(1)}, u32[]{:S(2)}, u32[]{:S(2)}) collective-permute-start(bf16[1,96,128]{2,1,0:T(8,128)(2,1)S(1)} %get-tuple-element.41.after_ref.refs_0_), channel_id=1, source_target_pairs={{0,4},{1,5},{2,6},{3,7},{4,0},{5,1},{6,2},{7,3},{8,12},{9,13},{10,... | collective-permute-start | bytes 73736 | tf_op jit(solution)/shard_map/ppermute | solution.py:61
  9.2 4.3 %collective-permute-start.1 = (bf16[2,96,128]{2,1,0:T(8,128)(2,1)S(1)}, bf16[2,96,128]{2,1,0:T(8,128)(2,1)S(1)}, u32[]{:S(2)}, u32[]{:S(2)}) collective-permute-start(bf16[2,96,128]{2,1,0:T(8,128)(2,1)S(1)} %stack.2.after_ref.refs_0_), channel_id=1, source_target_pairs={{0,2},{1,3},{2,0},{3,1},{4,6},{5,7},{6,4},{7,5},{8,10},{9,11},{10,... | collective-permute-start | bytes 147464 | tf_op jit(solution)/shard_map/ppermute | solution.py:61
  13.6 4.7 %collective-permute-start.2 = (bf16[4,96,128]{2,1,0:T(8,128)(2,1)S(1)}, bf16[4,96,128]{2,1,0:T(8,128)(2,1)S(1)}, u32[]{:S(2)}, u32[]{:S(2)}) collective-permute-start(bf16[4,96,128]{2,1,0:T(8,128)(2,1)S(1)} %stack.3.after_ref.refs_0_), channel_id=1, source_target_pairs={{0,1},{1,0},{2,3},{3,2},{4,5},{5,4},{6,7},{7,6},{8,9},{9,8},{10,11... | collective-permute-start | bytes 294920 | tf_op jit(solution)/shard_map/ppermute | solution.py:61
  23.0 1.3 %collective-permute-start.3 = (f32[128,128]{1,0:T(8,128)S(1)}, f32[128,128]{1,0:T(8,128)S(1)}, u32[]{:S(2)}, u32[]{:S(2)}) collective-permute-start(f32[128,128]{1,0:T(8,128)S(1)} %project.1.a_ref), channel_id=1, source_target_pairs={{0,8},{1,9},{2,10},{3,11},{4,12},{5,13},{6,14},{7,15},{8,0},{9,1},... | collective-permute-start | bytes 196616 | tf_op jit(solution)/shard_map/ppermute | solution.py:61
  24.4 6.1 %collective-permute-start.4 = (f32[128,128]{1,0:T(8,128)S(1)}, f32[128,128]{1,0:T(8,128)S(1)}, u32[]{:S(2)}, u32[]{:S(2)}) collective-permute-start(f32[128,128]{1,0:T(8,128)S(1)} %get-tuple-element.53.after_ref.refs_0_), channel_id=1, source_target_pairs={{0,24},{1,25},{2,26},{3,27},{4,28},{5,29},{6,30},{7,31},{8,16},{9,... | collective-permute-start | bytes 196616 | tf_op jit(solution)/shard_map/ppermute | solution.py:61
  25.7 4.2 %collective-permute-start.6 = (f32[64,128]{1,0:T(8,128)S(1)}, f32[64,128]{1,0:T(8,128)S(1)}, u32[]{:S(2)}, u32[]{:S(2)}) collective-permute-start(f32[64,128]{1,0:T(8,128)S(1)} %get-tuple-element.55), channel_id=1, source_target_pairs={{0,25},{1,24},{2,27},{3,26},{4,29},{5,28},{6,31},{7,30},{8,17},{9,... | collective-permute-start | bytes 98312 | tf_op jit(solution)/shard_map/ppermute | solution.py:61
  27.1 3.4 %collective-permute-start.5 = (f32[64,128]{1,0:T(8,128)S(1)}, f32[64,128]{1,0:T(8,128)S(1)}, u32[]{:S(2)}, u32[]{:S(2)}) collective-permute-start(f32[64,128]{1,0:T(8,128)S(1)} %get-tuple-element.55), channel_id=1, source_target_pairs={{0,9},{1,8},{2,11},{3,10},{4,13},{5,12},{6,15},{7,14},{8,1},{9,0},... | collective-permute-start | bytes 98312 | tf_op jit(solution)/shard_map/ppermute | solution.py:61
  30.5 3.4 %collective-permute-start.7 = (f32[64,128]{1,0:T(8,128)S(1)}, f32[64,128]{1,0:T(8,128)S(1)}, u32[]{:S(2)}, u32[]{:S(2)}) collective-permute-start(f32[64,128]{1,0:T(8,128)S(1)} %get-tuple-element.59.refs_2_.refs_0_), channel_id=1, source_target_pairs={{0,10},{1,11},{2,8},{3,9},{4,14},{5,15},{6,12},{7,13},{8,2},{9,3},... | collective-permute-start | bytes 98312 | tf_op jit(solution)/shard_map/ppermute | solution.py:61
  33.9 4.2 %collective-permute-start.8 = (f32[64,128]{1,0:T(8,128)S(1)}, f32[64,128]{1,0:T(8,128)S(1)}, u32[]{:S(2)}, u32[]{:S(2)}) collective-permute-start(f32[64,128]{1,0:T(8,128)S(1)} %add.13.refs_1_), channel_id=1, source_target_pairs={{0,12},{1,13},{2,14},{3,15},{4,8},{5,9},{6,10},{7,11},{8,4},{9,5},... | collective-permute-start | bytes 98312 | tf_op jit(solution)/shard_map/ppermute | solution.py:61
  44.4 6.3 %collective-permute-start.9 = (f32[2,64,128]{2,1,0:T(8,128)S(1)}, f32[2,64,128]{2,1,0:T(8,128)S(1)}, u32[]{:S(2)}, u32[]{:S(2)}) collective-permute-start(f32[2,64,128]{2,1,0:T(8,128)S(1)} %get-tuple-element.64), channel_id=1, source_target_pairs={{0,1},{1,0},{2,3},{3,2},{4,5},{5,4},{6,7},{7,6},{8,9},{9,8},{10,11... | collective-permute-start | bytes 196616 | tf_op jit(solution)/shard_map/ppermute | solution.py:61
  45.6 5.2 %collective-permute-start.10 = (f32[2,64,128]{2,1,0:T(8,128)S(1)}, f32[2,64,128]{2,1,0:T(8,128)S(1)}, u32[]{:S(2)}, u32[]{:S(2)}) collective-permute-start(f32[2,64,128]{2,1,0:T(8,128)S(1)} %get-tuple-element.65), channel_id=1, source_target_pairs={{0,2},{1,3},{2,0},{3,1},{4,6},{5,7},{6,4},{7,5},{8,10},{9,11},{10,... | collective-permute-start | bytes 196616 | tf_op jit(solution)/shard_map/ppermute | solution.py:61
  46.9 5.2 %collective-permute-start.11 = (f32[2,64,128]{2,1,0:T(8,128)S(1)}, f32[2,64,128]{2,1,0:T(8,128)S(1)}, u32[]{:S(2)}, u32[]{:S(2)}) collective-permute-start(f32[2,64,128]{2,1,0:T(8,128)S(1)} %get-tuple-element.66), channel_id=1, source_target_pairs={{0,3},{1,2},{2,1},{3,0},{4,7},{5,6},{6,5},{7,4},{8,11},{9,10},{10,... | collective-permute-start | bytes 196616 | tf_op jit(solution)/shard_map/ppermute | solution.py:61
  52.1 5.9 %collective-permute-start.12 = (f32[2,64,128]{2,1,0:T(8,128)S(1)}, f32[2,64,128]{2,1,0:T(8,128)S(1)}, u32[]{:S(2)}, u32[]{:S(2)}) collective-permute-start(f32[2,64,128]{2,1,0:T(8,128)S(1)} %add.14.refs_1_.refs_0_), channel_id=1, source_target_pairs={{0,4},{1,5},{2,6},{3,7},{4,0},{5,1},{6,2},{7,3},{8,12},{9,13},{10,... | collective-permute-start | bytes 196616 | tf_op jit(solution)/shard_map/ppermute | solution.py:61
  58.2 4.9 %collective-permute-start.15 = (bf16[2,64,128]{2,1,0:T(8,128)(2,1)S(1)}, bf16[2,64,128]{2,1,0:T(8,128)(2,1)S(1)}, u32[]{:S(2)}, u32[]{:S(2)}) collective-permute-start(bf16[2,64,128]{2,1,0:T(8,128)(2,1)S(1)} %update.1.refs_0_), channel_id=1, source_target_pairs={{0,3},{1,2},{2,1},{3,0},{4,7},{5,6},{6,5},{7,4},{8,11},{9,10},{10,... | collective-permute-start | bytes 98312 | tf_op jit(solution)/shard_map/ppermute | solution.py:61
  59.1 4.0 %collective-permute-start.14 = (bf16[2,64,128]{2,1,0:T(8,128)(2,1)S(1)}, bf16[2,64,128]{2,1,0:T(8,128)(2,1)S(1)}, u32[]{:S(2)}, u32[]{:S(2)}) collective-permute-start(bf16[2,64,128]{2,1,0:T(8,128)(2,1)S(1)} %update.1.refs_0_), channel_id=1, source_target_pairs={{0,2},{1,3},{2,0},{3,1},{4,6},{5,7},{6,4},{7,5},{8,10},{9,11},{10,... | collective-permute-start | bytes 98312 | tf_op jit(solution)/shard_map/ppermute | solution.py:61
  60.7 3.9 %collective-permute-start.13 = (bf16[2,64,128]{2,1,0:T(8,128)(2,1)S(1)}, bf16[2,64,128]{2,1,0:T(8,128)(2,1)S(1)}, u32[]{:S(2)}, u32[]{:S(2)}) collective-permute-start(bf16[2,64,128]{2,1,0:T(8,128)(2,1)S(1)} %update.1.refs_0_), channel_id=1, source_target_pairs={{0,1},{1,0},{2,3},{3,2},{4,5},{5,4},{6,7},{7,6},{8,9},{9,8},{10,11... | collective-permute-start | bytes 98312 | tf_op jit(solution)/shard_map/ppermute | solution.py:61
  66.2 1.4 %collective-permute-start.16 = (f32[64,128]{1,0:T(8,128)S(1)}, f32[64,128]{1,0:T(8,128)S(1)}, u32[]{:S(2)}, u32[]{:S(2)}) collective-permute-start(f32[64,128]{1,0:T(8,128)S(1)} %second.1.refs_2_.refs_0_), channel_id=1, source_target_pairs={{0,8},{1,9},{2,10},{3,11},{4,12},{5,13},{6,14},{7,15},{8,0},{9,1},... | collective-permute-start | bytes 98312 | tf_op jit(solution)/shard_map/ppermute | solution.py:61
  66.3 1.4 %collective-permute-start.17 = (f32[64,64]{1,0:T(8,128)S(1)}, f32[64,64]{1,0:T(8,128)S(1)}, u32[]{:S(2)}, u32[]{:S(2)}) collective-permute-start(f32[64,64]{1,0:T(8,128)S(1)} %get-tuple-element.70.refs_0_), channel_id=1, source_target_pairs={{0,8},{1,9},{2,10},{3,11},{4,12},{5,13},{6,14},{7,15},{8,0},{9,1},... | collective-permute-start | bytes 49160 | tf_op jit(solution)/shard_map/ppermute | solution.py:61
  67.7 6.7 %collective-permute-start.18 = (f32[64,128]{1,0:T(8,128)S(1)}, f32[64,128]{1,0:T(8,128)S(1)}, u32[]{:S(2)}, u32[]{:S(2)}) collective-permute-start(f32[64,128]{1,0:T(8,128)S(1)} %add.16.after_ref.mine_ref), channel_id=1, source_target_pairs={{0,24},{1,25},{2,26},{3,27},{4,28},{5,29},{6,30},{7,31},{8,16},{9,... | collective-permute-start | bytes 98312 | tf_op jit(solution)/shard_map/ppermute | solution.py:61
  69.3 3.3 %collective-permute-start.19 = (f32[64,64]{1,0:T(8,128)S(1)}, f32[64,64]{1,0:T(8,128)S(1)}, u32[]{:S(2)}, u32[]{:S(2)}) collective-permute-start(f32[64,64]{1,0:T(8,128)S(1)} %add.15.refs_2_.mine_ref), channel_id=1, source_target_pairs={{0,24},{1,25},{2,26},{3,27},{4,28},{5,29},{6,30},{7,31},{8,16},{9,... | collective-permute-start | bytes 49160 | tf_op jit(solution)/shard_map/ppermute | solution.py:61
  75.8 4.8 %collective-permute-start.21 = (bf16[2,64,128]{2,1,0:T(8,128)(2,1)S(1)}, bf16[2,64,128]{2,1,0:T(8,128)(2,1)S(1)}, u32[]{:S(2)}, u32[]{:S(2)}) collective-permute-start(bf16[2,64,128]{2,1,0:T(8,128)(2,1)S(1)} %get-tuple-element.74), channel_id=1, source_target_pairs={{0,2},{1,3},{2,0},{3,1},{4,6},{5,7},{6,4},{7,5},{8,10},{9,11},{10,... | collective-permute-start | bytes 98312 | tf_op jit(solution)/shard_map/ppermute | solution.py:61
  75.9 4.9 %collective-permute-start.22 = (bf16[2,64,128]{2,1,0:T(8,128)(2,1)S(1)}, bf16[2,64,128]{2,1,0:T(8,128)(2,1)S(1)}, u32[]{:S(2)}, u32[]{:S(2)}) collective-permute-start(bf16[2,64,128]{2,1,0:T(8,128)(2,1)S(1)} %get-tuple-element.75), channel_id=1, source_target_pairs={{0,3},{1,2},{2,1},{3,0},{4,7},{5,6},{6,5},{7,4},{8,11},{9,10},{10,... | collective-permute-start | bytes 98312 | tf_op jit(solution)/shard_map/ppermute | solution.py:61
  78.2 3.9 %collective-permute-start.20 = (bf16[2,64,128]{2,1,0:T(8,128)(2,1)S(1)}, bf16[2,64,128]{2,1,0:T(8,128)(2,1)S(1)}, u32[]{:S(2)}, u32[]{:S(2)}) collective-permute-start(bf16[2,64,128]{2,1,0:T(8,128)(2,1)S(1)} %get-tuple-element.73.after_ref), channel_id=1, source_target_pairs={{0,1},{1,0},{2,3},{3,2},{4,5},{5,4},{6,7},{7,6},{8,9},{9,8},{10,11... | collective-permute-start | bytes 98312 | tf_op jit(solution)/shard_map/ppermute | solution.py:61
  82.1 4.7 %collective-permute-start.23 = (bf16[64,128]{1,0:T(8,128)(2,1)S(1)}, bf16[64,128]{1,0:T(8,128)(2,1)S(1)}, u32[]{:S(2)}, u32[]{:S(2)}) collective-permute-start(bf16[64,128]{1,0:T(8,128)(2,1)S(1)} %get-tuple-element.77), channel_id=1, source_target_pairs={{0,4},{1,5},{2,6},{3,7},{4,0},{5,1},{6,2},{7,3},{8,12},{9,13},{10,... | collective-permute-start | bytes 49160 | tf_op jit(solution)/shard_map/ppermute | solution.py:61

commit v9 on v7

--- a/solution.py
+++ b/solution.py
@@ -301,7 +301,7 @@
     )
 
 
-def eliminate(matrix, start, stop, span=4):
+def eliminate(matrix, start, stop, span=8):
     size = matrix.shape[0]
     row_at = lax.broadcasted_iota(jnp.int32, (size, size), 0)
     col_at = lax.broadcasted_iota(jnp.int32, (size, size), 1)
@@ -363,7 +363,8 @@
     return pl.ds(at, 128)
 
 
-def slab_body(groups, offsets, head_count, me_ref, wide_ref, *refs):
+def slab_body(groups, offset, head_count, me_ref, wide_ref, after_ref, *refs):
+    del after_ref
     heads, t_refs, refs = refs[:head_count], refs[head_count : head_count + groups], refs[head_count + groups :]
     if head_count > 1:
         frames_ref, copy_ref, *refs = refs
@@ -372,51 +373,48 @@
         copy_ref[...] = frames
     else:
         frames = heads[0][...]
-    z_ref, *outs = refs
+    z_ref, out_ref = refs
     components, depth = frames.shape
     high = frames.astype(BF16)
     none = jnp.zeros_like(high)
     both = jnp.concatenate([jnp.concatenate(pair, axis=1) for pair in ((high, none), (none, high))], axis=0)
-    wide = 256
-    for place_at, (offset, out_ref) in enumerate(zip(offsets, outs)):
-        lanes = [block_lanes(me_ref, offset, n) for n in range(2)]
-        store = pl.ds(place_at * wide, wide)
-        total = jnp.zeros((components, wide), F32)
-        base = 0
-        for t_ref in t_refs:
-
-            def step(n, total, t_ref=t_ref, base=base):
-                for s in range(0, 8, 2):
-                    rows = pl.ds(n * 8 + s, 2)
-                    block = jnp.concatenate([t_ref[rows, :, at].reshape(2 * depth, 128) for at in lanes], axis=1)
-                    product = dot(both, block, ((1,), (0,)))
-                    for h in range(2):
-                        j = n * 8 + s + h
-                        z = product[h * components : h * components + components]
-                        z_ref[base + j, :, store] = z
-                        scale = wide_ref[base + j]
-                        total = total + z * jnp.concatenate([scale, scale], axis=1)
-                return total
-
-            total = lax.fori_loop(0, t_ref.shape[0] // 8, step, total)
-            base += t_ref.shape[0]
-        for n in range(2):
-            out_ref[n] = total[:, n * 128 : n * 128 + 128]
-
-
-def slab(me, wide, heads, turned, offsets):
+    lanes = [block_lanes(me_ref, offset, n) for n in range(2)]
+    total = jnp.zeros((components, 256), F32)
+    base = 0
+    for t_ref in t_refs:
+
+        def step(n, total, t_ref=t_ref, base=base):
+            for s in range(0, 8, 2):
+                rows = pl.ds(n * 8 + s, 2)
+                block = jnp.concatenate([t_ref[rows, :, at].reshape(2 * depth, 128) for at in lanes], axis=1)
+                product = dot(both, block, ((1,), (0,)))
+                for h in range(2):
+                    j = base + n * 8 + s + h
+                    z = product[h * components : h * components + components]
+                    z_ref[j] = z
+                    scale = wide_ref[j]
+                    total = total + z * jnp.concatenate([scale, scale], axis=1)
+            return total
+
+        total = lax.fori_loop(0, t_ref.shape[0] // 8, step, total)
+        base += t_ref.shape[0]
+    for n in range(2):
+        out_ref[n] = total[:, n * 128 : n * 128 + 128]
+
+
+def slab(me, wide, heads, turned, offset, after):
     _, frames, _ = turned[0].shape
     cols, components, _ = wide.shape
-    outs = (VM((cols, components, 256 * len(offsets)), F32),) + (shaped((2, components, 128)),) * len(offsets)
+    outs = (VM((cols, components, 256), F32), shaped((2, components, 128)))
     if len(heads) > 1:
         outs = (shaped((components, frames)),) * 2 + outs
     return call(
-        functools.partial(slab_body, len(turned), offsets, len(heads)),
+        functools.partial(slab_body, len(turned), offset, len(heads)),
         outs,
-        [smem()] + [vmem()] * (1 + len(heads) + len(turned)),
-        (me, wide, *heads, *turned),
+        [smem(), vmem(), anywhere()] + [vmem()] * (len(heads) + len(turned)),
+        (me, wide, after, *heads, *turned),
         "slab",
-        us=2 * len(offsets),
+        us=2,
     )
 
 
@@ -457,31 +455,22 @@
     )
 
 
-def second_body(*refs):
-    *stacks, kept_ref, sent_ref, out_ref, full_ref, fold_ref = refs
-    cols, components, near = kept_ref.shape
+def second_body(count, *refs):
+    z_refs, stacks, (out_ref, full_ref) = refs[:count], refs[count:-2], refs[-2:]
+    cols, components, width = z_refs[0].shape
     blocks = [s[n] for s in stacks for n in range(s.shape[0])]
     for n, block in enumerate(blocks):
         full_ref[:, n * 128 : n * 128 + 128] = block.astype(F32)
     lane = lax.broadcasted_iota(jnp.int32, (8, 128), 1)
-    ones = jnp.ones((256, 128), BF16)
-
-    def folded(j, at, mine):
-        products = kept_ref[j, at, :] * mine[:, :near], sent_ref[j, at, :] * mine[:, near:]
-        return paired([p[:, c : c + 128] for p in products for c in range(0, p.shape[1], 128)])
 
     def step(n, _):
         at = pl.ds(pl.multiple_of(n * 8, 8), 8)
         mine = full_ref[at, :]
-        for j in range(0, cols, 2):
-            pair = jnp.concatenate([folded(j, at, mine), folded(j + 1, at, mine)], axis=0)
-            high = pair.astype(BF16)
-            fold_ref[8 * j : 8 * j + 16, :128] = high
-            fold_ref[8 * j : 8 * j + 16, 128:] = (pair - high.astype(F32)).astype(BF16)
-        sums = dot(fold_ref[...], ones, ((1,), (0,)))
         total = jnp.zeros((8, 128), F32)
         for j in range(cols):
-            total = jnp.where(lane == j, sums[8 * j : 8 * j + 8], total)
+            products = [z_refs[p][j, at, :] * mine[:, p * width : p * width + width] for p in range(count)]
+            folded = paired([p[:, c : c + 128] for p in products for c in range(0, width, 128)])
+            total = jnp.where(lane == j, jnp.sum(folded, axis=1, keepdims=True), total)
         out_ref[at, :] = total
         return 0
 
@@ -491,76 +480,70 @@
     out_ref[...] = jnp.concatenate([out_ref[:, :components], gram], axis=1)
 
 
-def second(stacks, kept, sent):
-    components = kept.shape[1]
-    return call(
-        second_body,
+def second(zs, stacks):
+    components = zs[0].shape[1]
+    return call(
+        functools.partial(second_body, len(zs)),
         shaped((components, 2 * components)),
-        [vmem()] * (2 + len(stacks)),
-        (*stacks, kept, sent),
+        [vmem()] * (len(zs) + len(stacks)),
+        (*zs, *stacks),
         "second",
-        [VM((components, kept.shape[2] + sent.shape[2]), F32), VM((8 * kept.shape[0], 256), BF16)],
+        [VM((components, len(zs) * zs[0].shape[2]), F32)],
         us=2,
     )
 
 
-def mode_sums(new_ref, z_ref, out_refs):
+def mode_sums(new_ref, z_refs, out_refs):
     components = new_ref.shape[0]
 
     def step(n, _):
         at = pl.ds(pl.multiple_of(n * 8, 8), 8)
         scale = new_ref[at, :]
-        total = jnp.zeros((8, z_ref.shape[2]), F32)
-        for j in range(z_ref.shape[0]):
-            total = total + z_ref[j, at, :] * scale[:, j : j + 1]
-        for p, out_ref in enumerate(out_refs):
+        totals = [jnp.zeros((8, z.shape[2]), F32) for z in z_refs]
+        for j in range(z_refs[0].shape[0]):
+            factor = jnp.broadcast_to(scale[:, j : j + 1], totals[0].shape)
+            totals = [t + z[j, at, :] * factor for t, z in zip(totals, z_refs)]
+        for total, out_ref in zip(totals, out_refs):
             for h in range(2):
-                lane = 256 * p + 128 * h
-                out_ref[h, at, :] = total[:, lane : lane + 128]
+                out_ref[h, at, :] = total[:, h * 128 : h * 128 + 128]
         return 0
 
     lax.fori_loop(0, components // 8, step, 0)
 
 
-def mode_send_body(mine_ref, got_ref, gram_frames_ref, sent_ref, new_ref, *refs):
-    outs, sums = refs[:3], refs[3:]
+def mode_send_body(mine_ref, got_ref, gram_frames_ref, *refs):
+    z_refs, new_ref, outs, sums = refs[:3], refs[3], refs[4:7], refs[7:]
     components = new_ref.shape[0]
     summed = mine_ref[...] + got_ref[...]
     solver = eliminate(ridged(summed[:, components:] * gram_frames_ref[...]), 0, components)
     new_ref[...] = dot(solver, summed, ((1,), (0,)), HIGH)
-    mode_sums(new_ref, sent_ref, sums)
+    mode_sums(new_ref, z_refs, sums)
     for out_ref, sum_ref in zip(outs, sums):
         out_ref[...] = sum_ref[...].astype(out_ref.dtype)
 
 
-def mode_send(mine, got, gram_frames, sent, kind):
-    components = sent.shape[1]
+def mode_send(mine, got, gram_frames, zs, kind):
+    components = zs[0].shape[1]
     shape = (2, components, 128)
     return call(
         mode_send_body,
-        (shaped((components, 2 * components)),) + (shaped(shape, kind),) * 3,
-        [vmem()] * 4,
-        (mine, got, gram_frames, sent),
+        (shaped(mine.shape),) + (shaped(shape, kind),) * 3,
+        [vmem()] * 6,
+        (mine, got, gram_frames, *zs),
         "mode_send",
         [VM(shape, F32)] * 3,
-        us=4,
-    )
-
-
-def mode_keep_body(new_ref, kept_ref, after_ref, out_ref):
-    del after_ref
-    mode_sums(new_ref, kept_ref, [out_ref])
-
-
-def mode_keep(new, kept, after):
-    return call(
-        mode_keep_body,
-        shaped((2, kept.shape[1], 128)),
-        [vmem()] * 2 + [anywhere()],
-        (new, kept, after),
-        "mode_keep",
-        us=0.5,
-    )
+        us=3.5,
+    )
+
+
+def mode_keep_body(new_ref, z_ref, after_ref, out_ref):
+    del after_ref
+    mode_sums(new_ref, [z_ref], [out_ref])
+
+
+def mode_keep(new, z, after):
+    specs = [vmem()] * 2 + [anywhere()]
+    return call(mode_keep_body, shaped((2, z.shape[1], 128)), specs, (new, z, after), "mode_keep", us=1)
 
 
 def deal_body(me_ref, *refs):
@@ -631,7 +614,7 @@
     wide, token = widen(second_values, col_count, total)
     total, gram_first = split_add([total, *got], token)
     state = (gram_first, gram_second)
-    marks = [0, 44, components]
+    marks = [0, 40, components]
     sums = [total]
     for n, bit in enumerate(col_bits[1:]):
         if n:
@@ -641,37 +624,45 @@
             state = (eliminate_part(state, marks[n], marks[n + 1], total),)
 
     at = me if direct else jnp.zeros((1,), jnp.int32)
-    near, far = (0,), (1, 2, 3)
-    frames, frames_again, sent, *sends = slab(at, wide, (state[0], *sums), turned, far)
-    if direct:
-        got = [swap(x, "col", col_size, o) for o, x in zip(far, sends)]
-    kept, keep = slab(at, wide, (frames_again,), turned, near)
-
-    gram_frames, state = frames_gram(frames_again, gram_second, 20, keep)
+    far = (1, 2, 3)
+    heads, zs, sends, got = (state[0], *sums), [], [], []
+    for o in far:
+        *made, z, send = slab(at, wide, heads, turned, o, sends[-1] if sends else total)
+        if made:
+            frames, frames_again = made
+            heads = (frames_again,)
+        zs.append(z)
+        sends.append(send)
+        if direct:
+            got.append(swap(send, "col", col_size, o))
+    z, keep = slab(at, wide, heads, turned, 0, send)
+    zs = [z] + zs
+
+    gram_frames, state = frames_gram(frames_again, gram_second, 40, keep)
     if direct:
         keep = add([keep, *got], state)
         got = swap(keep, "col", col_size, 4)
-        state = eliminate_part((state,), 20, components, keep)
+        state = eliminate_part((state,), 40, components, keep)
         new = update(state, [keep, got])
         stacks = [new] + [swap(new, "col", col_size, o) for o in far]
     else:
-        state = eliminate_part((state,), 20, components, keep)
+        state = eliminate_part((state,), 40, components, keep)
         blocks = jnp.stack([keep, *sends]).transpose(2, 1, 0, 3).reshape(components, row_count)
         summed = lax.psum_scatter(blocks, "col", scatter_dimension=1, tiled=True)
         new = update(state, [summed[None]])[0]
         new = lax.all_gather(new, "col", axis=1, tiled=True).reshape(components, 2, 4, 128)
         stacks = list(new.transpose(2, 1, 0, 3))
-    part = second(stacks, kept, sent)
+    part = second(zs, stacks)
     part = add([part, swap(part, BOTH, every, core)], part)
     got = swap(part, BOTH, every, upper[0] | core)
 
-    new_second, *sends = mode_send(part, got, gram_frames, sent, BF16 if direct else F32)
+    new_second, *sends = mode_send(part, got, gram_frames, zs[1:], BF16 if direct else F32)
     if not direct:
-        keep = mode_keep(new_second, kept, new_second)
+        keep = mode_keep(new_second, zs[0], new_second)
         blocks = jnp.stack([keep, *sends]).transpose(2, 1, 0, 3).reshape(components, row_count)
         return (frames, lax.psum_scatter(blocks, "col", scatter_dimension=1, tiled=True))
     got = [swap(x, "col", col_size, o) for o, x in zip(far, sends)]
-    keep = mode_keep(new_second, kept, sends[0])
+    keep = mode_keep(new_second, zs[0], sends[0])
     mine, send = deal(me, [keep, *got], BF16)
     return (frames, mine + swap(send, "col", col_size, 4).astype(F32))
 

time: 88.5 us -> 87.1 us (0.984)
  Pallas kernels: 36.6 us -> 33.9 us
  waiting for transfers between devices: 23.2 us -> 24.4 us
    pallas_call x25 -> x27, Pallas kernels: 36.6 us -> 33.9 us  [call(): pl.pallas_call(body, out_shape=outs, in_specs=ins, out_specs=(vmem(),) *...]
    ppermute x22, waiting for transfers between devices: 23.2 us -> 24.4 us  [swap(): return lax.ppermute(x, axes, [(n, n ^ offset) for n in range(count)])]
  transfers between devices with their start and end apart: 22 -> 22, of which waited for: 15 -> 15; matrix products, arithmetic and copies ran while one was open for 0% -> 0% of each run, Pallas kernels for 20% -> 23%
where the time goes in v9:
time: 87.1 us; the launch traced here: 86.8 us
  Pallas kernels  33.9 us (39%)
  starting transfers between devices  27 us (31%)
  waiting for transfers between devices  24.4 us (28%)
    pallas_call x27, Pallas kernels, call(): pl.pallas_call(body, out_shape=outs, in_specs=ins, out_specs=(vmem(),) *...  33.9 us
    ppermute x22, starting transfers between devices, swap(): return lax.ppermute(x, axes, [(n, n ^ offset) for n in range(count)])  27 us
    ppermute x22, waiting for transfers between devices, swap(): return lax.ppermute(x, axes, [(n, n ^ offset) for n in range(count)])  24.4 us
  transfers between devices with their start and end apart: 22, of which 15 were waited for; matrix products, arithmetic and copies ran while one was open for 0% of the time, Pallas kernels for 23%

profile of v9, /device:TPU:0, one launch (start us, length us, event | category | flops | bytes accessed | tf_op | source)
XLA Modules:
  0.0 86.8 jit_solution(14962948199004479847)
XLA Ops:
  1.5 4.1 %collective-permute-start = (bf16[1,96,128]{2,1,0:T(8,128)(2,1)S(1)}, bf16[1,96,128]{2,1,0:T(8,128)(2,1)S(1)}, u32[]{:S(2)}, u32[]{:S(2)}) collective-permute-start(bf16[1,96,128]{2,1,0:T(8,128)(2,1)S(1)} %get-tuple-element.41.after_ref.refs_0_), channel_id=1, source_target_pairs={{0,4},{1,5},{2,6},{3,7},{4,0},{5,1},{6,2},{7,3},{8,12},{9,13},{10,... | collective-permute-start | bytes 73736 | tf_op jit(solution)/shard_map/ppermute | solution.py:61
  5.6 3.6 %prepare.3 = (bf16[16,128,1024]{2,1,0:T(8,128)(2,1)S(1)}, f32[8,128]{1,0:T(8,128)S(1)}, bf16[8,16,16,1024]{3,2,1,0:T(8,128)(2,1)S(1)}) custom-call(bf16[128,48,1024]{2,1,0:T(8,128)(2,1)} %t_ref.5, bf16[1,96,128]{2,1,0:T(8,128)(2,1)S(1)} %get-tuple-element.41.after_ref.refs_0_), custom_call_target="tpu_custom_call" | custom-call | bytes 6000000 | tf_op jit(solution)/shard_map/prepare/pallas_call | solution.py:37
  9.2 1.6 %collective-permute-start.1 = (bf16[2,96,128]{2,1,0:T(8,128)(2,1)S(1)}, bf16[2,96,128]{2,1,0:T(8,128)(2,1)S(1)}, u32[]{:S(2)}, u32[]{:S(2)}) collective-permute-start(bf16[2,96,128]{2,1,0:T(8,128)(2,1)S(1)} %stack.2.after_ref.refs_0_), channel_id=1, source_target_pairs={{0,2},{1,3},{2,0},{3,1},{4,6},{5,7},{6,4},{7,5},{8,10},{9,11},{10,... | collective-permute-start | bytes 147464 | tf_op jit(solution)/shard_map/ppermute | solution.py:61
  10.9 2.7 %prepare.4 = (bf16[16,128,1024]{2,1,0:T(8,128)(2,1)S(1)}, f32[8,128]{1,0:T(8,128)S(1)}, bf16[8,16,16,1024]{3,2,1,0:T(8,128)(2,1)S(1)}) custom-call(bf16[128,48,1024]{2,1,0:T(8,128)(2,1)} %t_ref.5, bf16[2,96,128]{2,1,0:T(8,128)(2,1)S(1)} %stack.2.after_ref.refs_0_, bf16[8,16,16,1024]{3,2,1,0:T(8,128)(2,1)S(1)} %get-tuple-element.43.refs_0_), custom_call_target="tpu_custom_call" | custom-call | bytes 6000000 | tf_op jit(solution)/shard_map/prepare/pallas_call | solution.py:37
  13.6 1.6 %collective-permute-start.2 = (bf16[4,96,128]{2,1,0:T(8,128)(2,1)S(1)}, bf16[4,96,128]{2,1,0:T(8,128)(2,1)S(1)}, u32[]{:S(2)}, u32[]{:S(2)}) collective-permute-start(bf16[4,96,128]{2,1,0:T(8,128)(2,1)S(1)} %stack.3.after_ref.refs_0_), channel_id=1, source_target_pairs={{0,1},{1,0},{2,3},{3,2},{4,5},{5,4},{6,7},{7,6},{8,9},{9,8},{10,11... | collective-permute-start | bytes 294920 | tf_op jit(solution)/shard_map/ppermute | solution.py:61
  15.1 2.7 %prepare.5 = (bf16[16,128,1024]{2,1,0:T(8,128)(2,1)S(1)}, f32[8,128]{1,0:T(8,128)S(1)}) custom-call(bf16[128,48,1024]{2,1,0:T(8,128)(2,1)} %t_ref.5, bf16[4,96,128]{2,1,0:T(8,128)(2,1)S(1)} %stack.3.after_ref.refs_0_, bf16[8,16,16,1024]{3,2,1,0:T(8,128)(2,1)S(1)} %get-tuple-element.45.refs_0_), custom_call_target="tpu_custom_call" | custom-call | bytes 6000000 | tf_op jit(solution)/shard_map/prepare/pallas_call | solution.py:37
  18.6 4.4 %project.1.a_ref = f32[128,128]{1,0:T(8,128)S(1)} custom-call(bf16[1024,64]{1,0:T(8,128)(2,1)S(1)} %get-tuple-element.47.turned_ref, f32[48,64]{1,0:T(8,128)S(1)} %get-tuple-element.48.second_ref, f32[64,64]{1,0:T(8,128)S(1)} %get-tuple-element.49.gram_ref, bf16[16,128,1024]{2,1,0:T(8,128)(2,1)S(1)} %get-tuple-element.50.refs_0_.refs_3_.refs_1_, ...), custom_call_target="tpu_custom_call" | custom-call | bytes 15000000 | tf_op jit(solution)/shard_map/project/pallas_call | solution.py:37
  27.9 2.0 %collective-permute-done.6.refs_3_ = f32[64,128]{1,0:T(8,128)S(1)} collective-permute-done((f32[64,128]{1,0:T(8,128)S(1)}, f32[64,128]{1,0:T(8,128)S(1)}, u32[]{:S(2)}, u32[]{:S(2)}) %collective-permute-start.6) | collective-permute-done | bytes 32800 | tf_op jit(solution)/shard_map/ppermute | solution.py:61
  35.5 2.7 %collective-permute-done.8.refs_2_ = f32[64,128]{1,0:T(8,128)S(1)} collective-permute-done((f32[64,128]{1,0:T(8,128)S(1)}, f32[64,128]{1,0:T(8,128)S(1)}, u32[]{:S(2)}, u32[]{:S(2)}) %collective-permute-start.8) | collective-permute-done | bytes 32800 | tf_op jit(solution)/shard_map/ppermute | solution.py:61
  38.1 2.5 %slab.4 = (f32[64,128]{1,0:T(8,128)}, f32[64,128]{1,0:T(8,128)S(1)}, f32[48,64,256]{2,1,0:T(8,128)S(1)}, f32[2,64,128]{2,1,0:T(8,128)S(1)}) custom-call(s32[1]{0:T(128)} %bitcast.me_ref, f32[48,64,128]{2,1,0:T(8,128)S(1)} %get-tuple-element.54.wide_ref, f32[64,128]{1,0:T(8,128)S(1)} %add.12.refs_1_.after_ref, f32[64,64]{1,0:T(8,128)S(1)} %eliminate.4.refs_0_, ...), custom_call_target="tpu_custom_call" | custom-call | bytes 6000000 | tf_op jit(solution)/shard_map/slab/pallas_call | solution.py:37
  41.6 1.9 %slab.5 = (f32[48,64,256]{2,1,0:T(8,128)S(1)}, f32[2,64,128]{2,1,0:T(8,128)S(1)}) custom-call(s32[1]{0:T(128)} %bitcast.me_ref, f32[48,64,128]{2,1,0:T(8,128)S(1)} %get-tuple-element.54.wide_ref, f32[2,64,128]{2,1,0:T(8,128)S(1)} %get-tuple-element.61.after_ref, f32[64,128]{1,0:T(8,128)S(1)} %get-tuple-element.62.refs_0_.frames_ref, ...), custom_call_target="tpu_custom_call" | custom-call | bytes 6000000 | tf_op jit(solution)/shard_map/slab/pallas_call | solution.py:37
  43.5 1.6 %collective-permute-start.10 = (f32[2,64,128]{2,1,0:T(8,128)S(1)}, f32[2,64,128]{2,1,0:T(8,128)S(1)}, u32[]{:S(2)}, u32[]{:S(2)}) collective-permute-start(f32[2,64,128]{2,1,0:T(8,128)S(1)} %get-tuple-element.63.after_ref), channel_id=1, source_target_pairs={{0,2},{1,3},{2,0},{3,1},{4,6},{5,7},{6,4},{7,5},{8,10},{9,11},{10,... | collective-permute-start | bytes 196616 | tf_op jit(solution)/shard_map/ppermute | solution.py:61
  45.1 1.9 %slab.6 = (f32[48,64,256]{2,1,0:T(8,128)S(1)}, f32[2,64,128]{2,1,0:T(8,128)S(1)}) custom-call(s32[1]{0:T(128)} %bitcast.me_ref, f32[48,64,128]{2,1,0:T(8,128)S(1)} %get-tuple-element.54.wide_ref, f32[2,64,128]{2,1,0:T(8,128)S(1)} %get-tuple-element.63.after_ref, f32[64,128]{1,0:T(8,128)S(1)} %get-tuple-element.62.refs_0_.frames_ref, ...), custom_call_target="tpu_custom_call" | custom-call | bytes 6000000 | tf_op jit(solution)/shard_map/slab/pallas_call | solution.py:37
  48.1 1.9 %slab.7 = (f32[48,64,256]{2,1,0:T(8,128)S(1)}, f32[2,64,128]{2,1,0:T(8,128)S(1)}) custom-call(s32[1]{0:T(128)} %bitcast.me_ref, f32[48,64,128]{2,1,0:T(8,128)S(1)} %get-tuple-element.54.wide_ref, f32[2,64,128]{2,1,0:T(8,128)S(1)} %get-tuple-element.64.after_ref, f32[64,128]{1,0:T(8,128)S(1)} %get-tuple-element.62.refs_0_.frames_ref, ...), custom_call_target="tpu_custom_call" | custom-call | bytes 6000000 | tf_op jit(solution)/shard_map/slab/pallas_call | solution.py:37
  52.3 1.5 %collective-permute-start.12 = (f32[2,64,128]{2,1,0:T(8,128)S(1)}, f32[2,64,128]{2,1,0:T(8,128)S(1)}, u32[]{:S(2)}, u32[]{:S(2)}) collective-permute-start(f32[2,64,128]{2,1,0:T(8,128)S(1)} %add.13.refs_1_.refs_0_), channel_id=1, source_target_pairs={{0,4},{1,5},{2,6},{3,7},{4,0},{5,1},{6,2},{7,3},{8,12},{9,13},{10,... | collective-permute-start | bytes 196616 | tf_op jit(solution)/shard_map/ppermute | solution.py:61
  54.4 3.8 %collective-permute-done.12.refs_1_ = f32[2,64,128]{2,1,0:T(8,128)S(1)} collective-permute-done((f32[2,64,128]{2,1,0:T(8,128)S(1)}, f32[2,64,128]{2,1,0:T(8,128)S(1)}, u32[]{:S(2)}, u32[]{:S(2)}) %collective-permute-start.12) | collective-permute-done | bytes 65568 | tf_op jit(solution)/shard_map/ppermute | solution.py:61
  58.8 2.0 %collective-permute-start.14 = (bf16[2,64,128]{2,1,0:T(8,128)(2,1)S(1)}, bf16[2,64,128]{2,1,0:T(8,128)(2,1)S(1)}, u32[]{:S(2)}, u32[]{:S(2)}) collective-permute-start(bf16[2,64,128]{2,1,0:T(8,128)(2,1)S(1)} %update.1.refs_4_), channel_id=1, source_target_pairs={{0,2},{1,3},{2,0},{3,1},{4,6},{5,7},{6,4},{7,5},{8,10},{9,11},{10,... | collective-permute-start | bytes 98312 | tf_op jit(solution)/shard_map/ppermute | solution.py:61
  63.3 1.5 %collective-permute-done.13.refs_5_ = bf16[2,64,128]{2,1,0:T(8,128)(2,1)S(1)} collective-permute-done((bf16[2,64,128]{2,1,0:T(8,128)(2,1)S(1)}, bf16[2,64,128]{2,1,0:T(8,128)(2,1)S(1)}, u32[]{:S(2)}, u32[]{:S(2)}) %collective-permute-start.13) | collective-permute-done | bytes 32800 | tf_op jit(solution)/shard_map/ppermute | solution.py:61
  64.8 1.9 %second.1.refs_0_.refs_2_ = f32[64,128]{1,0:T(8,128)S(1)} custom-call(f32[48,64,256]{2,1,0:T(8,128)S(1)} %get-tuple-element.65.refs_0_.z_ref, f32[48,64,256]{2,1,0:T(8,128)S(1)} %get-tuple-element.66.refs_1_.refs_0_, f32[48,64,256]{2,1,0:T(8,128)S(1)} %get-tuple-element.67.refs_2_.refs_1_, f32[48,64,256]{2,1,0:T(8,128)S(1)} %get-tuple-element.68.refs_3_.refs_2_, ...), custom_call_target="tpu_custom_call" | custom-call | bytes 6000000 | tf_op jit(solution)/shard_map/second/pallas_call | solution.py:37
  69.3 2.1 %collective-permute-done.17.got_ref = f32[64,128]{1,0:T(8,128)S(1)} collective-permute-done((f32[64,128]{1,0:T(8,128)S(1)}, f32[64,128]{1,0:T(8,128)S(1)}, u32[]{:S(2)}, u32[]{:S(2)}) %collective-permute-start.17) | collective-permute-done | bytes 32800 | tf_op jit(solution)/shard_map/ppermute | solution.py:61
  71.3 3.5 %mode_send.1 = (f32[64,128]{1,0:T(8,128)S(1)}, bf16[2,64,128]{2,1,0:T(8,128)(2,1)S(1)}, bf16[2,64,128]{2,1,0:T(8,128)(2,1)S(1)}, bf16[2,64,128]{2,1,0:T(8,128)(2,1)S(1)}) custom-call(f32[64,128]{1,0:T(8,128)S(1)} %add.14.mine_ref, f32[64,128]{1,0:T(8,128)S(1)} %collective-permute-done.17.got_ref, f32[64,64]{1,0:T(8,128)S(1)} %get-tuple-element.71.gram_frames_ref, ...), custom_call_target="tpu_custom_call" | custom-call | bytes 10500000 | tf_op jit(solution)/shard_map/mode_send/pallas_call | solution.py:37
  74.9 2.5 %collective-permute-start.20 = (bf16[2,64,128]{2,1,0:T(8,128)(2,1)S(1)}, bf16[2,64,128]{2,1,0:T(8,128)(2,1)S(1)}, u32[]{:S(2)}, u32[]{:S(2)}) collective-permute-start(bf16[2,64,128]{2,1,0:T(8,128)(2,1)S(1)} %get-tuple-element.75), channel_id=1, source_target_pairs={{0,3},{1,2},{2,1},{3,0},{4,7},{5,6},{6,5},{7,4},{8,11},{9,10},{10,... | collective-permute-start | bytes 98312 | tf_op jit(solution)/shard_map/ppermute | solution.py:61
  79.8 1.6 %collective-permute-done.18.refs_1_ = bf16[2,64,128]{2,1,0:T(8,128)(2,1)S(1)} collective-permute-done((bf16[2,64,128]{2,1,0:T(8,128)(2,1)S(1)}, bf16[2,64,128]{2,1,0:T(8,128)(2,1)S(1)}, u32[]{:S(2)}, u32[]{:S(2)}) %collective-permute-start.18) | collective-permute-done | bytes 32800 | tf_op jit(solution)/shard_map/ppermute | solution.py:61
  82.3 3.9 %collective-permute-done.21 = bf16[64,128]{1,0:T(8,128)(2,1)S(1)} collective-permute-done((bf16[64,128]{1,0:T(8,128)(2,1)S(1)}, bf16[64,128]{1,0:T(8,128)(2,1)S(1)}, u32[]{:S(2)}, u32[]{:S(2)}) %collective-permute-start.21) | collective-permute-done | bytes 16416 | tf_op jit(solution)/shard_map/ppermute | solution.py:61
  (48 shorter events, 26.6 us)
Async XLA Ops:
  1.5 7.7 %collective-permute-start = (bf16[1,96,128]{2,1,0:T(8,128)(2,1)S(1)}, bf16[1,96,128]{2,1,0:T(8,128)(2,1)S(1)}, u32[]{:S(2)}, u32[]{:S(2)}) collective-permute-start(bf16[1,96,128]{2,1,0:T(8,128)(2,1)S(1)} %get-tuple-element.41.after_ref.refs_0_), channel_id=1, source_target_pairs={{0,4},{1,5},{2,6},{3,7},{4,0},{5,1},{6,2},{7,3},{8,12},{9,13},{10,... | collective-permute-start | bytes 73736 | tf_op jit(solution)/shard_map/ppermute | solution.py:61
  9.2 4.3 %collective-permute-start.1 = (bf16[2,96,128]{2,1,0:T(8,128)(2,1)S(1)}, bf16[2,96,128]{2,1,0:T(8,128)(2,1)S(1)}, u32[]{:S(2)}, u32[]{:S(2)}) collective-permute-start(bf16[2,96,128]{2,1,0:T(8,128)(2,1)S(1)} %stack.2.after_ref.refs_0_), channel_id=1, source_target_pairs={{0,2},{1,3},{2,0},{3,1},{4,6},{5,7},{6,4},{7,5},{8,10},{9,11},{10,... | collective-permute-start | bytes 147464 | tf_op jit(solution)/shard_map/ppermute | solution.py:61
  13.6 4.7 %collective-permute-start.2 = (bf16[4,96,128]{2,1,0:T(8,128)(2,1)S(1)}, bf16[4,96,128]{2,1,0:T(8,128)(2,1)S(1)}, u32[]{:S(2)}, u32[]{:S(2)}) collective-permute-start(bf16[4,96,128]{2,1,0:T(8,128)(2,1)S(1)} %stack.3.after_ref.refs_0_), channel_id=1, source_target_pairs={{0,1},{1,0},{2,3},{3,2},{4,5},{5,4},{6,7},{7,6},{8,9},{9,8},{10,11... | collective-permute-start | bytes 294920 | tf_op jit(solution)/shard_map/ppermute | solution.py:61
  23.0 1.3 %collective-permute-start.3 = (f32[128,128]{1,0:T(8,128)S(1)}, f32[128,128]{1,0:T(8,128)S(1)}, u32[]{:S(2)}, u32[]{:S(2)}) collective-permute-start(f32[128,128]{1,0:T(8,128)S(1)} %project.1.a_ref), channel_id=1, source_target_pairs={{0,8},{1,9},{2,10},{3,11},{4,12},{5,13},{6,14},{7,15},{8,0},{9,1},... | collective-permute-start | bytes 196616 | tf_op jit(solution)/shard_map/ppermute | solution.py:61
  24.4 6.1 %collective-permute-start.4 = (f32[128,128]{1,0:T(8,128)S(1)}, f32[128,128]{1,0:T(8,128)S(1)}, u32[]{:S(2)}, u32[]{:S(2)}) collective-permute-start(f32[128,128]{1,0:T(8,128)S(1)} %get-tuple-element.53.after_ref.refs_0_), channel_id=1, source_target_pairs={{0,24},{1,25},{2,26},{3,27},{4,28},{5,29},{6,30},{7,31},{8,16},{9,... | collective-permute-start | bytes 196616 | tf_op jit(solution)/shard_map/ppermute | solution.py:61
  25.7 4.2 %collective-permute-start.6 = (f32[64,128]{1,0:T(8,128)S(1)}, f32[64,128]{1,0:T(8,128)S(1)}, u32[]{:S(2)}, u32[]{:S(2)}) collective-permute-start(f32[64,128]{1,0:T(8,128)S(1)} %get-tuple-element.55), channel_id=1, source_target_pairs={{0,25},{1,24},{2,27},{3,26},{4,29},{5,28},{6,31},{7,30},{8,17},{9,... | collective-permute-start | bytes 98312 | tf_op jit(solution)/shard_map/ppermute | solution.py:61
  27.1 3.4 %collective-permute-start.5 = (f32[64,128]{1,0:T(8,128)S(1)}, f32[64,128]{1,0:T(8,128)S(1)}, u32[]{:S(2)}, u32[]{:S(2)}) collective-permute-start(f32[64,128]{1,0:T(8,128)S(1)} %get-tuple-element.55), channel_id=1, source_target_pairs={{0,9},{1,8},{2,11},{3,10},{4,13},{5,12},{6,15},{7,14},{8,1},{9,0},... | collective-permute-start | bytes 98312 | tf_op jit(solution)/shard_map/ppermute | solution.py:61
  30.5 3.4 %collective-permute-start.7 = (f32[64,128]{1,0:T(8,128)S(1)}, f32[64,128]{1,0:T(8,128)S(1)}, u32[]{:S(2)}, u32[]{:S(2)}) collective-permute-start(f32[64,128]{1,0:T(8,128)S(1)} %get-tuple-element.57.refs_2_.refs_0_), channel_id=1, source_target_pairs={{0,10},{1,11},{2,8},{3,9},{4,14},{5,15},{6,12},{7,13},{8,2},{9,3},... | collective-permute-start | bytes 98312 | tf_op jit(solution)/shard_map/ppermute | solution.py:61
  33.9 4.2 %collective-permute-start.8 = (f32[64,128]{1,0:T(8,128)S(1)}, f32[64,128]{1,0:T(8,128)S(1)}, u32[]{:S(2)}, u32[]{:S(2)}) collective-permute-start(f32[64,128]{1,0:T(8,128)S(1)} %add.12.refs_1_.after_ref), channel_id=1, source_target_pairs={{0,12},{1,13},{2,14},{3,15},{4,8},{5,9},{6,10},{7,11},{8,4},{9,5},... | collective-permute-start | bytes 98312 | tf_op jit(solution)/shard_map/ppermute | solution.py:61
  40.6 10.7 %collective-permute-start.9 = (f32[2,64,128]{2,1,0:T(8,128)S(1)}, f32[2,64,128]{2,1,0:T(8,128)S(1)}, u32[]{:S(2)}, u32[]{:S(2)}) collective-permute-start(f32[2,64,128]{2,1,0:T(8,128)S(1)} %get-tuple-element.61.after_ref), channel_id=1, source_target_pairs={{0,1},{1,0},{2,3},{3,2},{4,5},{5,4},{6,7},{7,6},{8,9},{9,8},{10,11... | collective-permute-start | bytes 196616 | tf_op jit(solution)/shard_map/ppermute | solution.py:61
  43.5 7.8 %collective-permute-start.10 = (f32[2,64,128]{2,1,0:T(8,128)S(1)}, f32[2,64,128]{2,1,0:T(8,128)S(1)}, u32[]{:S(2)}, u32[]{:S(2)}) collective-permute-start(f32[2,64,128]{2,1,0:T(8,128)S(1)} %get-tuple-element.63.after_ref), channel_id=1, source_target_pairs={{0,2},{1,3},{2,0},{3,1},{4,6},{5,7},{6,4},{7,5},{8,10},{9,11},{10,... | collective-permute-start | bytes 196616 | tf_op jit(solution)/shard_map/ppermute | solution.py:61
  47.0 5.2 %collective-permute-start.11 = (f32[2,64,128]{2,1,0:T(8,128)S(1)}, f32[2,64,128]{2,1,0:T(8,128)S(1)}, u32[]{:S(2)}, u32[]{:S(2)}) collective-permute-start(f32[2,64,128]{2,1,0:T(8,128)S(1)} %get-tuple-element.64.after_ref), channel_id=1, source_target_pairs={{0,3},{1,2},{2,1},{3,0},{4,7},{5,6},{6,5},{7,4},{8,11},{9,10},{10,... | collective-permute-start | bytes 196616 | tf_op jit(solution)/shard_map/ppermute | solution.py:61
  52.3 5.9 %collective-permute-start.12 = (f32[2,64,128]{2,1,0:T(8,128)S(1)}, f32[2,64,128]{2,1,0:T(8,128)S(1)}, u32[]{:S(2)}, u32[]{:S(2)}) collective-permute-start(f32[2,64,128]{2,1,0:T(8,128)S(1)} %add.13.refs_1_.refs_0_), channel_id=1, source_target_pairs={{0,4},{1,5},{2,6},{3,7},{4,0},{5,1},{6,2},{7,3},{8,12},{9,13},{10,... | collective-permute-start | bytes 196616 | tf_op jit(solution)/shard_map/ppermute | solution.py:61
  58.4 4.9 %collective-permute-start.15 = (bf16[2,64,128]{2,1,0:T(8,128)(2,1)S(1)}, bf16[2,64,128]{2,1,0:T(8,128)(2,1)S(1)}, u32[]{:S(2)}, u32[]{:S(2)}) collective-permute-start(bf16[2,64,128]{2,1,0:T(8,128)(2,1)S(1)} %update.1.refs_4_), channel_id=1, source_target_pairs={{0,3},{1,2},{2,1},{3,0},{4,7},{5,6},{6,5},{7,4},{8,11},{9,10},{10,... | collective-permute-start | bytes 98312 | tf_op jit(solution)/shard_map/ppermute | solution.py:61
  58.8 4.4 %collective-permute-start.14 = (bf16[2,64,128]{2,1,0:T(8,128)(2,1)S(1)}, bf16[2,64,128]{2,1,0:T(8,128)(2,1)S(1)}, u32[]{:S(2)}, u32[]{:S(2)}) collective-permute-start(bf16[2,64,128]{2,1,0:T(8,128)(2,1)S(1)} %update.1.refs_4_), channel_id=1, source_target_pairs={{0,2},{1,3},{2,0},{3,1},{4,6},{5,7},{6,4},{7,5},{8,10},{9,11},{10,... | collective-permute-start | bytes 98312 | tf_op jit(solution)/shard_map/ppermute | solution.py:61
  60.8 3.9 %collective-permute-start.13 = (bf16[2,64,128]{2,1,0:T(8,128)(2,1)S(1)}, bf16[2,64,128]{2,1,0:T(8,128)(2,1)S(1)}, u32[]{:S(2)}, u32[]{:S(2)}) collective-permute-start(bf16[2,64,128]{2,1,0:T(8,128)(2,1)S(1)} %update.1.refs_4_), channel_id=1, source_target_pairs={{0,1},{1,0},{2,3},{3,2},{4,5},{5,4},{6,7},{7,6},{8,9},{9,8},{10,11... | collective-permute-start | bytes 98312 | tf_op jit(solution)/shard_map/ppermute | solution.py:61
  66.7 1.3 %collective-permute-start.16 = (f32[64,128]{1,0:T(8,128)S(1)}, f32[64,128]{1,0:T(8,128)S(1)}, u32[]{:S(2)}, u32[]{:S(2)}) collective-permute-start(f32[64,128]{1,0:T(8,128)S(1)} %second.1.refs_0_.refs_2_), channel_id=1, source_target_pairs={{0,8},{1,9},{2,10},{3,11},{4,12},{5,13},{6,14},{7,15},{8,0},{9,1},... | collective-permute-start | bytes 98312 | tf_op jit(solution)/shard_map/ppermute | solution.py:61
  68.0 3.3 %collective-permute-start.17 = (f32[64,128]{1,0:T(8,128)S(1)}, f32[64,128]{1,0:T(8,128)S(1)}, u32[]{:S(2)}, u32[]{:S(2)}) collective-permute-start(f32[64,128]{1,0:T(8,128)S(1)} %add.14.mine_ref), channel_id=1, source_target_pairs={{0,24},{1,25},{2,26},{3,27},{4,28},{5,29},{6,30},{7,31},{8,16},{9,... | collective-permute-start | bytes 98312 | tf_op jit(solution)/shard_map/ppermute | solution.py:61
  74.8 4.8 %collective-permute-start.19 = (bf16[2,64,128]{2,1,0:T(8,128)(2,1)S(1)}, bf16[2,64,128]{2,1,0:T(8,128)(2,1)S(1)}, u32[]{:S(2)}, u32[]{:S(2)}) collective-permute-start(bf16[2,64,128]{2,1,0:T(8,128)(2,1)S(1)} %get-tuple-element.74), channel_id=1, source_target_pairs={{0,2},{1,3},{2,0},{3,1},{4,6},{5,7},{6,4},{7,5},{8,10},{9,11},{10,... | collective-permute-start | bytes 98312 | tf_op jit(solution)/shard_map/ppermute | solution.py:61
  74.9 4.9 %collective-permute-start.20 = (bf16[2,64,128]{2,1,0:T(8,128)(2,1)S(1)}, bf16[2,64,128]{2,1,0:T(8,128)(2,1)S(1)}, u32[]{:S(2)}, u32[]{:S(2)}) collective-permute-start(bf16[2,64,128]{2,1,0:T(8,128)(2,1)S(1)} %get-tuple-element.75), channel_id=1, source_target_pairs={{0,3},{1,2},{2,1},{3,0},{4,7},{5,6},{6,5},{7,4},{8,11},{9,10},{10,... | collective-permute-start | bytes 98312 | tf_op jit(solution)/shard_map/ppermute | solution.py:61
  77.4 3.9 %collective-permute-start.18 = (bf16[2,64,128]{2,1,0:T(8,128)(2,1)S(1)}, bf16[2,64,128]{2,1,0:T(8,128)(2,1)S(1)}, u32[]{:S(2)}, u32[]{:S(2)}) collective-permute-start(bf16[2,64,128]{2,1,0:T(8,128)(2,1)S(1)} %get-tuple-element.73.after_ref), channel_id=1, source_target_pairs={{0,1},{1,0},{2,3},{3,2},{4,5},{5,4},{6,7},{7,6},{8,9},{9,8},{10,11... | collective-permute-start | bytes 98312 | tf_op jit(solution)/shard_map/ppermute | solution.py:61
  81.4 4.8 %collective-permute-start.21 = (bf16[64,128]{1,0:T(8,128)(2,1)S(1)}, bf16[64,128]{1,0:T(8,128)(2,1)S(1)}, u32[]{:S(2)}, u32[]{:S(2)}) collective-permute-start(bf16[64,128]{1,0:T(8,128)(2,1)S(1)} %get-tuple-element.77), channel_id=1, source_target_pairs={{0,4},{1,5},{2,6},{3,7},{4,0},{5,1},{6,2},{7,3},{8,12},{9,13},{10,... | collective-permute-start | bytes 49160 | tf_op jit(solution)/shard_map/ppermute | solution.py:61

commit v10 on v7

--- a/solution.py
+++ b/solution.py
@@ -301,7 +301,7 @@
     )
 
 
-def eliminate(matrix, start, stop, span=4):
+def eliminate(matrix, start, stop, span=8):
     size = matrix.shape[0]
     row_at = lax.broadcasted_iota(jnp.int32, (size, size), 0)
     col_at = lax.broadcasted_iota(jnp.int32, (size, size), 1)
@@ -458,30 +458,22 @@
 
 
 def second_body(*refs):
-    *stacks, kept_ref, sent_ref, out_ref, full_ref, fold_ref = refs
+    *stacks, kept_ref, sent_ref, out_ref, full_ref = refs
     cols, components, near = kept_ref.shape
     blocks = [s[n] for s in stacks for n in range(s.shape[0])]
     for n, block in enumerate(blocks):
         full_ref[:, n * 128 : n * 128 + 128] = block.astype(F32)
     lane = lax.broadcasted_iota(jnp.int32, (8, 128), 1)
-    ones = jnp.ones((256, 128), BF16)
-
-    def folded(j, at, mine):
-        products = kept_ref[j, at, :] * mine[:, :near], sent_ref[j, at, :] * mine[:, near:]
-        return paired([p[:, c : c + 128] for p in products for c in range(0, p.shape[1], 128)])
 
     def step(n, _):
         at = pl.ds(pl.multiple_of(n * 8, 8), 8)
         mine = full_ref[at, :]
-        for j in range(0, cols, 2):
-            pair = jnp.concatenate([folded(j, at, mine), folded(j + 1, at, mine)], axis=0)
-            high = pair.astype(BF16)
-            fold_ref[8 * j : 8 * j + 16, :128] = high
-            fold_ref[8 * j : 8 * j + 16, 128:] = (pair - high.astype(F32)).astype(BF16)
-        sums = dot(fold_ref[...], ones, ((1,), (0,)))
         total = jnp.zeros((8, 128), F32)
         for j in range(cols):
-            total = jnp.where(lane == j, sums[8 * j : 8 * j + 8], total)
+            products = kept_ref[j, at, :] * mine[:, :near], sent_ref[j, at, :] * mine[:, near:]
+            folds = [p[:, c : c + 128] for p in products for c in range(0, p.shape[1], 128)]
+            folded = paired(folds)
+            total = jnp.where(lane == j, jnp.sum(folded, axis=1, keepdims=True), total)
         out_ref[at, :] = total
         return 0
 
@@ -499,7 +491,7 @@
         [vmem()] * (2 + len(stacks)),
         (*stacks, kept, sent),
         "second",
-        [VM((components, kept.shape[2] + sent.shape[2]), F32), VM((8 * kept.shape[0], 256), BF16)],
+        [VM((components, kept.shape[2] + sent.shape[2]), F32)],
         us=2,
     )
 
@@ -631,7 +623,7 @@
     wide, token = widen(second_values, col_count, total)
     total, gram_first = split_add([total, *got], token)
     state = (gram_first, gram_second)
-    marks = [0, 44, components]
+    marks = [0, 40, components]
     sums = [total]
     for n, bit in enumerate(col_bits[1:]):
         if n:
@@ -647,15 +639,15 @@
         got = [swap(x, "col", col_size, o) for o, x in zip(far, sends)]
     kept, keep = slab(at, wide, (frames_again,), turned, near)
 
-    gram_frames, state = frames_gram(frames_again, gram_second, 20, keep)
+    gram_frames, state = frames_gram(frames_again, gram_second, 40, keep)
     if direct:
         keep = add([keep, *got], state)
         got = swap(keep, "col", col_size, 4)
-        state = eliminate_part((state,), 20, components, keep)
+        state = eliminate_part((state,), 40, components, keep)
         new = update(state, [keep, got])
         stacks = [new] + [swap(new, "col", col_size, o) for o in far]
     else:
-        state = eliminate_part((state,), 20, components, keep)
+        state = eliminate_part((state,), 40, components, keep)
         blocks = jnp.stack([keep, *sends]).transpose(2, 1, 0, 3).reshape(components, row_count)
         summed = lax.psum_scatter(blocks, "col", scatter_dimension=1, tiled=True)
         new = update(state, [summed[None]])[0]

time: 88.5 us -> 87 us (0.983)
  Pallas kernels: 36.6 us -> 33.8 us
  waiting for transfers between devices: 23.2 us -> 24.5 us
    pallas_call x25, Pallas kernels: 36.6 us -> 33.8 us  [call(): pl.pallas_call(body, out_shape=outs, in_specs=ins, out_specs=(vmem(),) *...]
    ppermute x22, waiting for transfers between devices: 23.2 us -> 24.5 us  [swap(): return lax.ppermute(x, axes, [(n, n ^ offset) for n in range(count)])]
  transfers between devices with their start and end apart: 22 -> 22, of which waited for: 15 -> 15; matrix products, arithmetic and copies ran while one was open for 0% -> 0% of each run, Pallas kernels for 20% -> 19%
where the time goes in v10:
time: 87 us; the launch traced here: 86.7 us
  Pallas kernels  33.8 us (39%)
  starting transfers between devices  26.9 us (31%)
  waiting for transfers between devices  24.5 us (28%)
    pallas_call x25, Pallas kernels, call(): pl.pallas_call(body, out_shape=outs, in_specs=ins, out_specs=(vmem(),) *...  33.8 us
    ppermute x22, starting transfers between devices, swap(): return lax.ppermute(x, axes, [(n, n ^ offset) for n in range(count)])  26.9 us
    ppermute x22, waiting for transfers between devices, swap(): return lax.ppermute(x, axes, [(n, n ^ offset) for n in range(count)])  24.5 us
  transfers between devices with their start and end apart: 22, of which 15 were waited for; matrix products, arithmetic and copies ran while one was open for 0% of the time, Pallas kernels for 19%

profile of v10, /device:TPU:0, one launch (start us, length us, event | category | flops | bytes accessed | tf_op | source)
XLA Modules:
  0.0 86.7 jit_solution(14310844813946643272)
XLA Ops:
  1.5 4.1 %collective-permute-start = (bf16[1,96,128]{2,1,0:T(8,128)(2,1)S(1)}, bf16[1,96,128]{2,1,0:T(8,128)(2,1)S(1)}, u32[]{:S(2)}, u32[]{:S(2)}) collective-permute-start(bf16[1,96,128]{2,1,0:T(8,128)(2,1)S(1)} %get-tuple-element.39.after_ref.refs_0_), channel_id=1, source_target_pairs={{0,4},{1,5},{2,6},{3,7},{4,0},{5,1},{6,2},{7,3},{8,12},{9,13},{10,... | collective-permute-start | bytes 73736 | tf_op jit(solution)/shard_map/ppermute | solution.py:61
  5.6 3.6 %prepare.3 = (bf16[16,128,1024]{2,1,0:T(8,128)(2,1)S(1)}, f32[8,128]{1,0:T(8,128)S(1)}, bf16[8,16,16,1024]{3,2,1,0:T(8,128)(2,1)S(1)}) custom-call(bf16[128,48,1024]{2,1,0:T(8,128)(2,1)} %t_ref.5, bf16[1,96,128]{2,1,0:T(8,128)(2,1)S(1)} %get-tuple-element.39.after_ref.refs_0_), custom_call_target="tpu_custom_call" | custom-call | bytes 6000000 | tf_op jit(solution)/shard_map/prepare/pallas_call | solution.py:37
  9.2 1.6 %collective-permute-start.1 = (bf16[2,96,128]{2,1,0:T(8,128)(2,1)S(1)}, bf16[2,96,128]{2,1,0:T(8,128)(2,1)S(1)}, u32[]{:S(2)}, u32[]{:S(2)}) collective-permute-start(bf16[2,96,128]{2,1,0:T(8,128)(2,1)S(1)} %stack.2.after_ref.refs_0_), channel_id=1, source_target_pairs={{0,2},{1,3},{2,0},{3,1},{4,6},{5,7},{6,4},{7,5},{8,10},{9,11},{10,... | collective-permute-start | bytes 147464 | tf_op jit(solution)/shard_map/ppermute | solution.py:61
  10.9 2.7 %prepare.4 = (bf16[16,128,1024]{2,1,0:T(8,128)(2,1)S(1)}, f32[8,128]{1,0:T(8,128)S(1)}, bf16[8,16,16,1024]{3,2,1,0:T(8,128)(2,1)S(1)}) custom-call(bf16[128,48,1024]{2,1,0:T(8,128)(2,1)} %t_ref.5, bf16[2,96,128]{2,1,0:T(8,128)(2,1)S(1)} %stack.2.after_ref.refs_0_, bf16[8,16,16,1024]{3,2,1,0:T(8,128)(2,1)S(1)} %get-tuple-element.41.refs_0_), custom_call_target="tpu_custom_call" | custom-call | bytes 6000000 | tf_op jit(solution)/shard_map/prepare/pallas_call | solution.py:37
  13.6 1.6 %collective-permute-start.2 = (bf16[4,96,128]{2,1,0:T(8,128)(2,1)S(1)}, bf16[4,96,128]{2,1,0:T(8,128)(2,1)S(1)}, u32[]{:S(2)}, u32[]{:S(2)}) collective-permute-start(bf16[4,96,128]{2,1,0:T(8,128)(2,1)S(1)} %stack.3.after_ref.refs_0_), channel_id=1, source_target_pairs={{0,1},{1,0},{2,3},{3,2},{4,5},{5,4},{6,7},{7,6},{8,9},{9,8},{10,11... | collective-permute-start | bytes 294920 | tf_op jit(solution)/shard_map/ppermute | solution.py:61
  15.1 2.7 %prepare.5 = (bf16[16,128,1024]{2,1,0:T(8,128)(2,1)S(1)}, f32[8,128]{1,0:T(8,128)S(1)}) custom-call(bf16[128,48,1024]{2,1,0:T(8,128)(2,1)} %t_ref.5, bf16[4,96,128]{2,1,0:T(8,128)(2,1)S(1)} %stack.3.after_ref.refs_0_, bf16[8,16,16,1024]{3,2,1,0:T(8,128)(2,1)S(1)} %get-tuple-element.43.refs_0_), custom_call_target="tpu_custom_call" | custom-call | bytes 6000000 | tf_op jit(solution)/shard_map/prepare/pallas_call | solution.py:37
  18.6 4.4 %project.1.a_ref = f32[128,128]{1,0:T(8,128)S(1)} custom-call(bf16[1024,64]{1,0:T(8,128)(2,1)S(1)} %get-tuple-element.45.turned_ref, f32[48,64]{1,0:T(8,128)S(1)} %get-tuple-element.46.second_ref, f32[64,64]{1,0:T(8,128)S(1)} %get-tuple-element.47.gram_ref, bf16[16,128,1024]{2,1,0:T(8,128)(2,1)S(1)} %get-tuple-element.48.refs_0_.refs_3_.refs_1_, ...), custom_call_target="tpu_custom_call" | custom-call | bytes 15000000 | tf_op jit(solution)/shard_map/project/pallas_call | solution.py:37
  24.4 1.3 %collective-permute-start.4 = (f32[128,128]{1,0:T(8,128)S(1)}, f32[128,128]{1,0:T(8,128)S(1)}, u32[]{:S(2)}, u32[]{:S(2)}) collective-permute-start(f32[128,128]{1,0:T(8,128)S(1)} %get-tuple-element.51.after_ref.refs_0_), channel_id=1, source_target_pairs={{0,24},{1,25},{2,26},{3,27},{4,28},{5,29},{6,30},{7,31},{8,16},{9,... | collective-permute-start | bytes 196616 | tf_op jit(solution)/shard_map/ppermute | solution.py:61
  25.7 1.4 %collective-permute-start.6 = (f32[64,128]{1,0:T(8,128)S(1)}, f32[64,128]{1,0:T(8,128)S(1)}, u32[]{:S(2)}, u32[]{:S(2)}) collective-permute-start(f32[64,128]{1,0:T(8,128)S(1)} %get-tuple-element.53), channel_id=1, source_target_pairs={{0,25},{1,24},{2,27},{3,26},{4,29},{5,28},{6,31},{7,30},{8,17},{9,... | collective-permute-start | bytes 98312 | tf_op jit(solution)/shard_map/ppermute | solution.py:61
  27.9 2.0 %collective-permute-done.6.refs_3_ = f32[64,128]{1,0:T(8,128)S(1)} collective-permute-done((f32[64,128]{1,0:T(8,128)S(1)}, f32[64,128]{1,0:T(8,128)S(1)}, u32[]{:S(2)}, u32[]{:S(2)}) %collective-permute-start.6) | collective-permute-done | bytes 32800 | tf_op jit(solution)/shard_map/ppermute | solution.py:61
  35.5 2.7 %collective-permute-done.8.refs_2_ = f32[64,128]{1,0:T(8,128)S(1)} collective-permute-done((f32[64,128]{1,0:T(8,128)S(1)}, f32[64,128]{1,0:T(8,128)S(1)}, u32[]{:S(2)}, u32[]{:S(2)}) %collective-permute-start.8) | collective-permute-done | bytes 32800 | tf_op jit(solution)/shard_map/ppermute | solution.py:61
  38.1 6.3 %slab.2 = (f32[64,128]{1,0:T(8,128)}, f32[64,128]{1,0:T(8,128)S(1)}, f32[48,64,768]{2,1,0:T(8,128)S(1)}, f32[2,64,128]{2,1,0:T(8,128)S(1)}, f32[2,64,128]{2,1,0:T(8,128)S(1)}, /*index=5*/f32[2,64,128]{2,1,0:T(8,128)S(1)}) custom-call(s32[1]{0:T(128)} %bitcast.me_ref, f32[48,64,128]{2,1,0:T(8,128)S(1)} %get-tuple-element.52.wide_ref, ...), custom_call_target="tpu_custom_call" | custom-call | bytes 18000000 | tf_op jit(solution)/shard_map/slab/pallas_call | solution.py:37
  45.4 1.5 %collective-permute-start.10 = (f32[2,64,128]{2,1,0:T(8,128)S(1)}, f32[2,64,128]{2,1,0:T(8,128)S(1)}, u32[]{:S(2)}, u32[]{:S(2)}) collective-permute-start(f32[2,64,128]{2,1,0:T(8,128)S(1)} %get-tuple-element.63), channel_id=1, source_target_pairs={{0,2},{1,3},{2,0},{3,1},{4,6},{5,7},{6,4},{7,5},{8,10},{9,11},{10,... | collective-permute-start | bytes 196616 | tf_op jit(solution)/shard_map/ppermute | solution.py:61
  47.9 1.9 %slab.3 = (f32[48,64,256]{2,1,0:T(8,128)S(1)}, f32[2,64,128]{2,1,0:T(8,128)S(1)}) custom-call(s32[1]{0:T(128)} %bitcast.me_ref, f32[48,64,128]{2,1,0:T(8,128)S(1)} %get-tuple-element.52.wide_ref, f32[64,128]{1,0:T(8,128)S(1)} %get-tuple-element.59.refs_0_.frames_ref, bf16[16,128,1024]{2,1,0:T(8,128)(2,1)S(1)} %get-tuple-element.48.refs_0_.refs_3_.refs_1_, ...), custom_call_target="tpu_custom_call" | custom-call | bytes 6000000 | tf_op jit(solution)/shard_map/slab/pallas_call | solution.py:37
  52.1 1.5 %collective-permute-start.12 = (f32[2,64,128]{2,1,0:T(8,128)S(1)}, f32[2,64,128]{2,1,0:T(8,128)S(1)}, u32[]{:S(2)}, u32[]{:S(2)}) collective-permute-start(f32[2,64,128]{2,1,0:T(8,128)S(1)} %add.13.refs_1_.refs_0_), channel_id=1, source_target_pairs={{0,4},{1,5},{2,6},{3,7},{4,0},{5,1},{6,2},{7,3},{8,12},{9,13},{10,... | collective-permute-start | bytes 196616 | tf_op jit(solution)/shard_map/ppermute | solution.py:61
  54.3 3.8 %collective-permute-done.12.refs_1_ = f32[2,64,128]{2,1,0:T(8,128)S(1)} collective-permute-done((f32[2,64,128]{2,1,0:T(8,128)S(1)}, f32[2,64,128]{2,1,0:T(8,128)S(1)}, u32[]{:S(2)}, u32[]{:S(2)}) %collective-permute-start.12) | collective-permute-done | bytes 65568 | tf_op jit(solution)/shard_map/ppermute | solution.py:61
  59.1 1.6 %collective-permute-start.14 = (bf16[2,64,128]{2,1,0:T(8,128)(2,1)S(1)}, bf16[2,64,128]{2,1,0:T(8,128)(2,1)S(1)}, u32[]{:S(2)}, u32[]{:S(2)}) collective-permute-start(bf16[2,64,128]{2,1,0:T(8,128)(2,1)S(1)} %update.1.refs_0_), channel_id=1, source_target_pairs={{0,2},{1,3},{2,0},{3,1},{4,6},{5,7},{6,4},{7,5},{8,10},{9,11},{10,... | collective-permute-start | bytes 98312 | tf_op jit(solution)/shard_map/ppermute | solution.py:61
  61.8 1.3 %collective-permute-done.15.refs_3_ = bf16[2,64,128]{2,1,0:T(8,128)(2,1)S(1)} collective-permute-done((bf16[2,64,128]{2,1,0:T(8,128)(2,1)S(1)}, bf16[2,64,128]{2,1,0:T(8,128)(2,1)S(1)}, u32[]{:S(2)}, u32[]{:S(2)}) %collective-permute-start.15) | collective-permute-done | bytes 32800 | tf_op jit(solution)/shard_map/ppermute | solution.py:61
  63.1 1.5 %collective-permute-done.13.refs_1_ = bf16[2,64,128]{2,1,0:T(8,128)(2,1)S(1)} collective-permute-done((bf16[2,64,128]{2,1,0:T(8,128)(2,1)S(1)}, bf16[2,64,128]{2,1,0:T(8,128)(2,1)S(1)}, u32[]{:S(2)}, u32[]{:S(2)}) %collective-permute-start.13) | collective-permute-done | bytes 32800 | tf_op jit(solution)/shard_map/ppermute | solution.py:61
  64.6 1.9 %second.1.refs_0_.refs_2_ = f32[64,128]{1,0:T(8,128)S(1)} custom-call(bf16[2,64,128]{2,1,0:T(8,128)(2,1)S(1)} %update.1.refs_0_, bf16[2,64,128]{2,1,0:T(8,128)(2,1)S(1)} %collective-permute-done.13.refs_1_, bf16[2,64,128]{2,1,0:T(8,128)(2,1)S(1)} %collective-permute-done.14.refs_2_, bf16[2,64,128]{2,1,0:T(8,128)(2,1)S(1)} %collective-permute-done.15.refs_3_, ...), custom_call_target="tpu_custom_call" | custom-call | bytes 6000000 | tf_op jit(solution)/shard_map/second/pallas_call | solution.py:37
  69.0 2.1 %collective-permute-done.17.got_ref = f32[64,128]{1,0:T(8,128)S(1)} collective-permute-done((f32[64,128]{1,0:T(8,128)S(1)}, f32[64,128]{1,0:T(8,128)S(1)}, u32[]{:S(2)}, u32[]{:S(2)}) %collective-permute-start.17) | collective-permute-done | bytes 32800 | tf_op jit(solution)/shard_map/ppermute | solution.py:61
  71.1 3.5 %mode_send.1 = (f32[64,128]{1,0:T(8,128)S(1)}, bf16[2,64,128]{2,1,0:T(8,128)(2,1)S(1)}, bf16[2,64,128]{2,1,0:T(8,128)(2,1)S(1)}, bf16[2,64,128]{2,1,0:T(8,128)(2,1)S(1)}) custom-call(f32[64,128]{1,0:T(8,128)S(1)} %add.14.mine_ref, f32[64,128]{1,0:T(8,128)S(1)} %collective-permute-done.17.got_ref, f32[64,64]{1,0:T(8,128)S(1)} %get-tuple-element.67.gram_frames_ref, ...), custom_call_target="tpu_custom_call" | custom-call | bytes 12000000 | tf_op jit(solution)/shard_map/mode_send/pallas_call | solution.py:37
  75.1 2.1 %collective-permute-start.20 = (bf16[2,64,128]{2,1,0:T(8,128)(2,1)S(1)}, bf16[2,64,128]{2,1,0:T(8,128)(2,1)S(1)}, u32[]{:S(2)}, u32[]{:S(2)}) collective-permute-start(bf16[2,64,128]{2,1,0:T(8,128)(2,1)S(1)} %get-tuple-element.71), channel_id=1, source_target_pairs={{0,3},{1,2},{2,1},{3,0},{4,7},{5,6},{6,5},{7,4},{8,11},{9,10},{10,... | collective-permute-start | bytes 98312 | tf_op jit(solution)/shard_map/ppermute | solution.py:61
  82.1 4.0 %collective-permute-done.21 = bf16[64,128]{1,0:T(8,128)(2,1)S(1)} collective-permute-done((bf16[64,128]{1,0:T(8,128)(2,1)S(1)}, bf16[64,128]{1,0:T(8,128)(2,1)S(1)}, u32[]{:S(2)}, u32[]{:S(2)}) %collective-permute-start.21) | collective-permute-done | bytes 16416 | tf_op jit(solution)/shard_map/ppermute | solution.py:61
  (46 shorter events, 24.9 us)
Async XLA Ops:
  1.5 7.7 %collective-permute-start = (bf16[1,96,128]{2,1,0:T(8,128)(2,1)S(1)}, bf16[1,96,128]{2,1,0:T(8,128)(2,1)S(1)}, u32[]{:S(2)}, u32[]{:S(2)}) collective-permute-start(bf16[1,96,128]{2,1,0:T(8,128)(2,1)S(1)} %get-tuple-element.39.after_ref.refs_0_), channel_id=1, source_target_pairs={{0,4},{1,5},{2,6},{3,7},{4,0},{5,1},{6,2},{7,3},{8,12},{9,13},{10,... | collective-permute-start | bytes 73736 | tf_op jit(solution)/shard_map/ppermute | solution.py:61
  9.2 4.3 %collective-permute-start.1 = (bf16[2,96,128]{2,1,0:T(8,128)(2,1)S(1)}, bf16[2,96,128]{2,1,0:T(8,128)(2,1)S(1)}, u32[]{:S(2)}, u32[]{:S(2)}) collective-permute-start(bf16[2,96,128]{2,1,0:T(8,128)(2,1)S(1)} %stack.2.after_ref.refs_0_), channel_id=1, source_target_pairs={{0,2},{1,3},{2,0},{3,1},{4,6},{5,7},{6,4},{7,5},{8,10},{9,11},{10,... | collective-permute-start | bytes 147464 | tf_op jit(solution)/shard_map/ppermute | solution.py:61
  13.6 4.7 %collective-permute-start.2 = (bf16[4,96,128]{2,1,0:T(8,128)(2,1)S(1)}, bf16[4,96,128]{2,1,0:T(8,128)(2,1)S(1)}, u32[]{:S(2)}, u32[]{:S(2)}) collective-permute-start(bf16[4,96,128]{2,1,0:T(8,128)(2,1)S(1)} %stack.3.after_ref.refs_0_), channel_id=1, source_target_pairs={{0,1},{1,0},{2,3},{3,2},{4,5},{5,4},{6,7},{7,6},{8,9},{9,8},{10,11... | collective-permute-start | bytes 294920 | tf_op jit(solution)/shard_map/ppermute | solution.py:61
  23.0 1.3 %collective-permute-start.3 = (f32[128,128]{1,0:T(8,128)S(1)}, f32[128,128]{1,0:T(8,128)S(1)}, u32[]{:S(2)}, u32[]{:S(2)}) collective-permute-start(f32[128,128]{1,0:T(8,128)S(1)} %project.1.a_ref), channel_id=1, source_target_pairs={{0,8},{1,9},{2,10},{3,11},{4,12},{5,13},{6,14},{7,15},{8,0},{9,1},... | collective-permute-start | bytes 196616 | tf_op jit(solution)/shard_map/ppermute | solution.py:61
  24.4 6.1 %collective-permute-start.4 = (f32[128,128]{1,0:T(8,128)S(1)}, f32[128,128]{1,0:T(8,128)S(1)}, u32[]{:S(2)}, u32[]{:S(2)}) collective-permute-start(f32[128,128]{1,0:T(8,128)S(1)} %get-tuple-element.51.after_ref.refs_0_), channel_id=1, source_target_pairs={{0,24},{1,25},{2,26},{3,27},{4,28},{5,29},{6,30},{7,31},{8,16},{9,... | collective-permute-start | bytes 196616 | tf_op jit(solution)/shard_map/ppermute | solution.py:61
  25.7 4.2 %collective-permute-start.6 = (f32[64,128]{1,0:T(8,128)S(1)}, f32[64,128]{1,0:T(8,128)S(1)}, u32[]{:S(2)}, u32[]{:S(2)}) collective-permute-start(f32[64,128]{1,0:T(8,128)S(1)} %get-tuple-element.53), channel_id=1, source_target_pairs={{0,25},{1,24},{2,27},{3,26},{4,29},{5,28},{6,31},{7,30},{8,17},{9,... | collective-permute-start | bytes 98312 | tf_op jit(solution)/shard_map/ppermute | solution.py:61
  27.1 3.4 %collective-permute-start.5 = (f32[64,128]{1,0:T(8,128)S(1)}, f32[64,128]{1,0:T(8,128)S(1)}, u32[]{:S(2)}, u32[]{:S(2)}) collective-permute-start(f32[64,128]{1,0:T(8,128)S(1)} %get-tuple-element.53), channel_id=1, source_target_pairs={{0,9},{1,8},{2,11},{3,10},{4,13},{5,12},{6,15},{7,14},{8,1},{9,0},... | collective-permute-start | bytes 98312 | tf_op jit(solution)/shard_map/ppermute | solution.py:61
  30.5 3.4 %collective-permute-start.7 = (f32[64,128]{1,0:T(8,128)S(1)}, f32[64,128]{1,0:T(8,128)S(1)}, u32[]{:S(2)}, u32[]{:S(2)}) collective-permute-start(f32[64,128]{1,0:T(8,128)S(1)} %get-tuple-element.57.refs_2_.refs_0_), channel_id=1, source_target_pairs={{0,10},{1,11},{2,8},{3,9},{4,14},{5,15},{6,12},{7,13},{8,2},{9,3},... | collective-permute-start | bytes 98312 | tf_op jit(solution)/shard_map/ppermute | solution.py:61
  33.9 4.2 %collective-permute-start.8 = (f32[64,128]{1,0:T(8,128)S(1)}, f32[64,128]{1,0:T(8,128)S(1)}, u32[]{:S(2)}, u32[]{:S(2)}) collective-permute-start(f32[64,128]{1,0:T(8,128)S(1)} %add.12.refs_1_), channel_id=1, source_target_pairs={{0,12},{1,13},{2,14},{3,15},{4,8},{5,9},{6,10},{7,11},{8,4},{9,5},... | collective-permute-start | bytes 98312 | tf_op jit(solution)/shard_map/ppermute | solution.py:61
  44.4 6.7 %collective-permute-start.9 = (f32[2,64,128]{2,1,0:T(8,128)S(1)}, f32[2,64,128]{2,1,0:T(8,128)S(1)}, u32[]{:S(2)}, u32[]{:S(2)}) collective-permute-start(f32[2,64,128]{2,1,0:T(8,128)S(1)} %get-tuple-element.62), channel_id=1, source_target_pairs={{0,1},{1,0},{2,3},{3,2},{4,5},{5,4},{6,7},{7,6},{8,9},{9,8},{10,11... | collective-permute-start | bytes 196616 | tf_op jit(solution)/shard_map/ppermute | solution.py:61
  45.4 5.7 %collective-permute-start.10 = (f32[2,64,128]{2,1,0:T(8,128)S(1)}, f32[2,64,128]{2,1,0:T(8,128)S(1)}, u32[]{:S(2)}, u32[]{:S(2)}) collective-permute-start(f32[2,64,128]{2,1,0:T(8,128)S(1)} %get-tuple-element.63), channel_id=1, source_target_pairs={{0,2},{1,3},{2,0},{3,1},{4,6},{5,7},{6,4},{7,5},{8,10},{9,11},{10,... | collective-permute-start | bytes 196616 | tf_op jit(solution)/shard_map/ppermute | solution.py:61
  46.9 5.2 %collective-permute-start.11 = (f32[2,64,128]{2,1,0:T(8,128)S(1)}, f32[2,64,128]{2,1,0:T(8,128)S(1)}, u32[]{:S(2)}, u32[]{:S(2)}) collective-permute-start(f32[2,64,128]{2,1,0:T(8,128)S(1)} %get-tuple-element.64), channel_id=1, source_target_pairs={{0,3},{1,2},{2,1},{3,0},{4,7},{5,6},{6,5},{7,4},{8,11},{9,10},{10,... | collective-permute-start | bytes 196616 | tf_op jit(solution)/shard_map/ppermute | solution.py:61
  52.1 5.9 %collective-permute-start.12 = (f32[2,64,128]{2,1,0:T(8,128)S(1)}, f32[2,64,128]{2,1,0:T(8,128)S(1)}, u32[]{:S(2)}, u32[]{:S(2)}) collective-permute-start(f32[2,64,128]{2,1,0:T(8,128)S(1)} %add.13.refs_1_.refs_0_), channel_id=1, source_target_pairs={{0,4},{1,5},{2,6},{3,7},{4,0},{5,1},{6,2},{7,3},{8,12},{9,13},{10,... | collective-permute-start | bytes 196616 | tf_op jit(solution)/shard_map/ppermute | solution.py:61
  58.2 4.9 %collective-permute-start.15 = (bf16[2,64,128]{2,1,0:T(8,128)(2,1)S(1)}, bf16[2,64,128]{2,1,0:T(8,128)(2,1)S(1)}, u32[]{:S(2)}, u32[]{:S(2)}) collective-permute-start(bf16[2,64,128]{2,1,0:T(8,128)(2,1)S(1)} %update.1.refs_0_), channel_id=1, source_target_pairs={{0,3},{1,2},{2,1},{3,0},{4,7},{5,6},{6,5},{7,4},{8,11},{9,10},{10,... | collective-permute-start | bytes 98312 | tf_op jit(solution)/shard_map/ppermute | solution.py:61
  59.1 4.0 %collective-permute-start.14 = (bf16[2,64,128]{2,1,0:T(8,128)(2,1)S(1)}, bf16[2,64,128]{2,1,0:T(8,128)(2,1)S(1)}, u32[]{:S(2)}, u32[]{:S(2)}) collective-permute-start(bf16[2,64,128]{2,1,0:T(8,128)(2,1)S(1)} %update.1.refs_0_), channel_id=1, source_target_pairs={{0,2},{1,3},{2,0},{3,1},{4,6},{5,7},{6,4},{7,5},{8,10},{9,11},{10,... | collective-permute-start | bytes 98312 | tf_op jit(solution)/shard_map/ppermute | solution.py:61
  60.7 3.9 %collective-permute-start.13 = (bf16[2,64,128]{2,1,0:T(8,128)(2,1)S(1)}, bf16[2,64,128]{2,1,0:T(8,128)(2,1)S(1)}, u32[]{:S(2)}, u32[]{:S(2)}) collective-permute-start(bf16[2,64,128]{2,1,0:T(8,128)(2,1)S(1)} %update.1.refs_0_), channel_id=1, source_target_pairs={{0,1},{1,0},{2,3},{3,2},{4,5},{5,4},{6,7},{7,6},{8,9},{9,8},{10,11... | collective-permute-start | bytes 98312 | tf_op jit(solution)/shard_map/ppermute | solution.py:61
  66.5 1.3 %collective-permute-start.16 = (f32[64,128]{1,0:T(8,128)S(1)}, f32[64,128]{1,0:T(8,128)S(1)}, u32[]{:S(2)}, u32[]{:S(2)}) collective-permute-start(f32[64,128]{1,0:T(8,128)S(1)} %second.1.refs_0_.refs_2_), channel_id=1, source_target_pairs={{0,8},{1,9},{2,10},{3,11},{4,12},{5,13},{6,14},{7,15},{8,0},{9,1},... | collective-permute-start | bytes 98312 | tf_op jit(solution)/shard_map/ppermute | solution.py:61
  67.8 3.3 %collective-permute-start.17 = (f32[64,128]{1,0:T(8,128)S(1)}, f32[64,128]{1,0:T(8,128)S(1)}, u32[]{:S(2)}, u32[]{:S(2)}) collective-permute-start(f32[64,128]{1,0:T(8,128)S(1)} %add.14.mine_ref), channel_id=1, source_target_pairs={{0,24},{1,25},{2,26},{3,27},{4,28},{5,29},{6,30},{7,31},{8,16},{9,... | collective-permute-start | bytes 98312 | tf_op jit(solution)/shard_map/ppermute | solution.py:61
  74.6 4.8 %collective-permute-start.19 = (bf16[2,64,128]{2,1,0:T(8,128)(2,1)S(1)}, bf16[2,64,128]{2,1,0:T(8,128)(2,1)S(1)}, u32[]{:S(2)}, u32[]{:S(2)}) collective-permute-start(bf16[2,64,128]{2,1,0:T(8,128)(2,1)S(1)} %get-tuple-element.70), channel_id=1, source_target_pairs={{0,2},{1,3},{2,0},{3,1},{4,6},{5,7},{6,4},{7,5},{8,10},{9,11},{10,... | collective-permute-start | bytes 98312 | tf_op jit(solution)/shard_map/ppermute | solution.py:61
  75.1 4.9 %collective-permute-start.20 = (bf16[2,64,128]{2,1,0:T(8,128)(2,1)S(1)}, bf16[2,64,128]{2,1,0:T(8,128)(2,1)S(1)}, u32[]{:S(2)}, u32[]{:S(2)}) collective-permute-start(bf16[2,64,128]{2,1,0:T(8,128)(2,1)S(1)} %get-tuple-element.71), channel_id=1, source_target_pairs={{0,3},{1,2},{2,1},{3,0},{4,7},{5,6},{6,5},{7,4},{8,11},{9,10},{10,... | collective-permute-start | bytes 98312 | tf_op jit(solution)/shard_map/ppermute | solution.py:61
  77.2 3.9 %collective-permute-start.18 = (bf16[2,64,128]{2,1,0:T(8,128)(2,1)S(1)}, bf16[2,64,128]{2,1,0:T(8,128)(2,1)S(1)}, u32[]{:S(2)}, u32[]{:S(2)}) collective-permute-start(bf16[2,64,128]{2,1,0:T(8,128)(2,1)S(1)} %get-tuple-element.69.after_ref), channel_id=1, source_target_pairs={{0,1},{1,0},{2,3},{3,2},{4,5},{5,4},{6,7},{7,6},{8,9},{9,8},{10,11... | collective-permute-start | bytes 98312 | tf_op jit(solution)/shard_map/ppermute | solution.py:61
  81.2 4.9 %collective-permute-start.21 = (bf16[64,128]{1,0:T(8,128)(2,1)S(1)}, bf16[64,128]{1,0:T(8,128)(2,1)S(1)}, u32[]{:S(2)}, u32[]{:S(2)}) collective-permute-start(bf16[64,128]{1,0:T(8,128)(2,1)S(1)} %get-tuple-element.73), channel_id=1, source_target_pairs={{0,4},{1,5},{2,6},{3,7},{4,0},{5,1},{6,2},{7,3},{8,12},{9,13},{10,... | collective-permute-start | bytes 49160 | tf_op jit(solution)/shard_map/ppermute | solution.py:61

commit v11 on v6

--- a/solution.py
+++ b/solution.py
@@ -509,7 +509,7 @@
     outs, sums = refs[:3], refs[3:]
     components = new_ref.shape[0]
     summed = mine_ref[...] + got_ref[...]
-    solver = eliminate(ridged(summed[:, components:] * gram_frames_ref[...]), 0, components)
+    solver = eliminate(ridged(summed[:, components:] * gram_frames_ref[...]), 0, components, 8)
     new_ref[...] = dot(solver, summed, ((1,), (0,)), HIGH)
     mode_sums(new_ref, sent_ref, sums)
     for out_ref, sum_ref in zip(outs, sums):

time: 86.6 us -> 86 us (level)
  no operation moved by 1% of the time
where the time goes in v11:
time: 86 us; the launch traced here: 85.6 us
  Pallas kernels  34.8 us (40%)
  starting transfers between devices  27.7 us (32%)
  waiting for transfers between devices  21.7 us (25%)
    pallas_call x25, Pallas kernels, call(): pl.pallas_call(body, out_shape=outs, in_specs=ins, out_specs=(vmem(),) *...  34.8 us
    ppermute x22, starting transfers between devices, swap(): return lax.ppermute(x, axes, [(n, n ^ offset) for n in range(count)])  27.7 us
    ppermute x22, waiting for transfers between devices, swap(): return lax.ppermute(x, axes, [(n, n ^ offset) for n in range(count)])  21.7 us
  transfers between devices with their start and end apart: 22, of which 16 were waited for; matrix products, arithmetic and copies ran while one was open for 0% of the time, Pallas kernels for 20%

profile of v11, /device:TPU:0, one launch (start us, length us, event | category | flops | bytes accessed | tf_op | source)
XLA Modules:
  0.0 85.6 jit_solution(14390225209455017310)
XLA Ops:
  1.5 4.1 %collective-permute-start = (bf16[1,96,128]{2,1,0:T(8,128)(2,1)S(1)}, bf16[1,96,128]{2,1,0:T(8,128)(2,1)S(1)}, u32[]{:S(2)}, u32[]{:S(2)}) collective-permute-start(bf16[1,96,128]{2,1,0:T(8,128)(2,1)S(1)} %get-tuple-element.39.after_ref.refs_0_), channel_id=1, source_target_pairs={{0,4},{1,5},{2,6},{3,7},{4,0},{5,1},{6,2},{7,3},{8,12},{9,13},{10,... | collective-permute-start | bytes 73736 | tf_op jit(solution)/shard_map/ppermute | solution.py:61
  5.6 3.6 %prepare.3 = (bf16[16,128,1024]{2,1,0:T(8,128)(2,1)S(1)}, f32[16,64,128]{2,1,0:T(8,128)S(1)}, f32[8,128]{1,0:T(8,128)S(1)}, bf16[8,16,16,1024]{3,2,1,0:T(8,128)(2,1)S(1)}) custom-call(bf16[128,48,1024]{2,1,0:T(8,128)(2,1)} %t_ref.5, f32[64,128]{1,0:T(8,128)S(1)} %get-tuple-element.40.b_ref, bf16[1,96,128]{2,1,0:T(8,128)(2,1)S(1)} %get-tuple-element.39.after_ref.refs_0_), custom_call_target="tpu_custom_call" | custom-call | bytes 6000000 | tf_op jit(solution)/shard_map/prepare/pallas_call | solution.py:37
  9.2 1.6 %collective-permute-start.1 = (bf16[2,96,128]{2,1,0:T(8,128)(2,1)S(1)}, bf16[2,96,128]{2,1,0:T(8,128)(2,1)S(1)}, u32[]{:S(2)}, u32[]{:S(2)}) collective-permute-start(bf16[2,96,128]{2,1,0:T(8,128)(2,1)S(1)} %stack.2.after_ref.refs_0_), channel_id=1, source_target_pairs={{0,2},{1,3},{2,0},{3,1},{4,6},{5,7},{6,4},{7,5},{8,10},{9,11},{10,... | collective-permute-start | bytes 147464 | tf_op jit(solution)/shard_map/ppermute | solution.py:61
  10.9 2.8 %prepare.4 = (bf16[16,128,1024]{2,1,0:T(8,128)(2,1)S(1)}, f32[16,64,128]{2,1,0:T(8,128)S(1)}, f32[8,128]{1,0:T(8,128)S(1)}, bf16[8,16,16,1024]{3,2,1,0:T(8,128)(2,1)S(1)}) custom-call(bf16[128,48,1024]{2,1,0:T(8,128)(2,1)} %t_ref.5, f32[64,128]{1,0:T(8,128)S(1)} %get-tuple-element.40.b_ref, bf16[2,96,128]{2,1,0:T(8,128)(2,1)S(1)} %stack.2.after_ref.refs_0_, ...), custom_call_target="tpu_custom_call" | custom-call | bytes 6000000 | tf_op jit(solution)/shard_map/prepare/pallas_call | solution.py:37
  13.8 1.6 %collective-permute-start.2 = (bf16[4,96,128]{2,1,0:T(8,128)(2,1)S(1)}, bf16[4,96,128]{2,1,0:T(8,128)(2,1)S(1)}, u32[]{:S(2)}, u32[]{:S(2)}) collective-permute-start(bf16[4,96,128]{2,1,0:T(8,128)(2,1)S(1)} %stack.3.after_ref.refs_0_), channel_id=1, source_target_pairs={{0,1},{1,0},{2,3},{3,2},{4,5},{5,4},{6,7},{7,6},{8,9},{9,8},{10,11... | collective-permute-start | bytes 294920 | tf_op jit(solution)/shard_map/ppermute | solution.py:61
  15.3 2.8 %prepare.5 = (bf16[16,128,1024]{2,1,0:T(8,128)(2,1)S(1)}, f32[16,64,128]{2,1,0:T(8,128)S(1)}, f32[8,128]{1,0:T(8,128)S(1)}) custom-call(bf16[128,48,1024]{2,1,0:T(8,128)(2,1)} %t_ref.5, f32[64,128]{1,0:T(8,128)S(1)} %get-tuple-element.40.b_ref, bf16[4,96,128]{2,1,0:T(8,128)(2,1)S(1)} %stack.3.after_ref.refs_0_, ...), custom_call_target="tpu_custom_call" | custom-call | bytes 6000000 | tf_op jit(solution)/shard_map/prepare/pallas_call | solution.py:37
  18.8 4.4 %project.1.a_ref = f32[128,128]{1,0:T(8,128)S(1)} custom-call(bf16[1024,64]{1,0:T(8,128)(2,1)S(1)} %get-tuple-element.46.turned_ref, f32[48,64]{1,0:T(8,128)S(1)} %get-tuple-element.47.second_ref, f32[64,64]{1,0:T(8,128)S(1)} %get-tuple-element.48.gram_ref, bf16[16,128,1024]{2,1,0:T(8,128)(2,1)S(1)} %get-tuple-element.49.refs_0_.refs_2_.refs_1_, ...), custom_call_target="tpu_custom_call" | custom-call | bytes 15000000 | tf_op jit(solution)/shard_map/project/pallas_call | solution.py:37
  27.6 2.5 %collective-permute-done.6.refs_3_ = f32[64,128]{1,0:T(8,128)S(1)} collective-permute-done((f32[64,128]{1,0:T(8,128)S(1)}, f32[64,128]{1,0:T(8,128)S(1)}, u32[]{:S(2)}, u32[]{:S(2)}) %collective-permute-start.6) | collective-permute-done | bytes 32800 | tf_op jit(solution)/shard_map/ppermute | solution.py:61
  31.7 1.7 %eliminate.3.refs_2_.refs_0_ = f32[64,64]{1,0:T(8,128)S(1)} custom-call(f32[64,64]{1,0:T(8,128)S(1)} %get-tuple-element.54.refs_0_, f32[64,64]{1,0:T(8,128)S(1)} %get-tuple-element.55.refs_1_.other_ref, f32[64,128]{1,0:T(8,128)S(1)} %get-tuple-element.56.refs_2_.refs_0_), custom_call_target="tpu_custom_call" | custom-call | bytes 3000000 | tf_op jit(solution)/shard_map/eliminate/pallas_call | solution.py:37
  35.7 2.6 %collective-permute-done.8.refs_1_ = f32[64,128]{1,0:T(8,128)S(1)} collective-permute-done((f32[64,128]{1,0:T(8,128)S(1)}, f32[64,128]{1,0:T(8,128)S(1)}, u32[]{:S(2)}, u32[]{:S(2)}) %collective-permute-start.8) | collective-permute-done | bytes 32800 | tf_op jit(solution)/shard_map/ppermute | solution.py:61
  38.3 6.3 %slab.2 = (f32[64,128]{1,0:T(8,128)}, f32[64,128]{1,0:T(8,128)S(1)}, f32[48,64,768]{2,1,0:T(8,128)S(1)}, f32[2,64,128]{2,1,0:T(8,128)S(1)}, f32[2,64,128]{2,1,0:T(8,128)S(1)}, /*index=5*/f32[2,64,128]{2,1,0:T(8,128)S(1)}) custom-call(s32[1]{0:T(128)} %bitcast.me_ref, f32[64,64]{1,0:T(8,128)S(1)} %eliminate.4.refs_2_.refs_0_, f32[64,128]{1,0:T(8,128)S(1)} %add.14.refs_1_, ...), custom_call_target="tpu_custom_call" | custom-call | bytes 18000000 | tf_op jit(solution)/shard_map/slab/pallas_call | solution.py:37
  48.1 1.9 %slab.3 = (f32[48,64,256]{2,1,0:T(8,128)S(1)}, f32[2,64,128]{2,1,0:T(8,128)S(1)}) custom-call(s32[1]{0:T(128)} %bitcast.me_ref, f32[64,128]{1,0:T(8,128)S(1)} %get-tuple-element.61.refs_0_.frames_ref, bf16[16,128,1024]{2,1,0:T(8,128)(2,1)S(1)} %get-tuple-element.49.refs_0_.refs_2_.refs_1_, ...), custom_call_target="tpu_custom_call" | custom-call | bytes 6000000 | tf_op jit(solution)/shard_map/slab/pallas_call | solution.py:37
  50.0 1.9 %frames_gram.1 = (f32[64,64]{1,0:T(8,128)S(1)}, f32[64,64]{1,0:T(8,128)S(1)}) custom-call(f32[64,128]{1,0:T(8,128)S(1)} %get-tuple-element.61.refs_0_.frames_ref, f32[64,64]{1,0:T(8,128)S(1)} %get-tuple-element.55.refs_1_.other_ref, f32[2,64,128]{2,1,0:T(8,128)S(1)} %get-tuple-element.62.after_ref.refs_0_), custom_call_target="tpu_custom_call" | custom-call | bytes 6000000 | tf_op jit(solution)/shard_map/frames_gram/pallas_call | solution.py:37
  52.0 1.5 %collective-permute-start.12 = (f32[2,64,128]{2,1,0:T(8,128)S(1)}, f32[2,64,128]{2,1,0:T(8,128)S(1)}, u32[]{:S(2)}, u32[]{:S(2)}) collective-permute-start(f32[2,64,128]{2,1,0:T(8,128)S(1)} %add.15.refs_1_.refs_0_), channel_id=1, source_target_pairs={{0,4},{1,5},{2,6},{3,7},{4,0},{5,1},{6,2},{7,3},{8,12},{9,13},{10,... | collective-permute-start | bytes 196616 | tf_op jit(solution)/shard_map/ppermute | solution.py:61
  54.3 3.0 %collective-permute-done.12.refs_1_ = f32[2,64,128]{2,1,0:T(8,128)S(1)} collective-permute-done((f32[2,64,128]{2,1,0:T(8,128)S(1)}, f32[2,64,128]{2,1,0:T(8,128)S(1)}, u32[]{:S(2)}, u32[]{:S(2)}) %collective-permute-start.12) | collective-permute-done | bytes 65568 | tf_op jit(solution)/shard_map/ppermute | solution.py:61
  57.5 1.7 %collective-permute-start.15 = (bf16[2,64,128]{2,1,0:T(8,128)(2,1)S(1)}, bf16[2,64,128]{2,1,0:T(8,128)(2,1)S(1)}, u32[]{:S(2)}, u32[]{:S(2)}) collective-permute-start(bf16[2,64,128]{2,1,0:T(8,128)(2,1)S(1)} %update.1.refs_0_), channel_id=1, source_target_pairs={{0,3},{1,2},{2,1},{3,0},{4,7},{5,6},{6,5},{7,4},{8,11},{9,10},{10,... | collective-permute-start | bytes 98312 | tf_op jit(solution)/shard_map/ppermute | solution.py:61
  59.2 1.9 %collective-permute-start.14 = (bf16[2,64,128]{2,1,0:T(8,128)(2,1)S(1)}, bf16[2,64,128]{2,1,0:T(8,128)(2,1)S(1)}, u32[]{:S(2)}, u32[]{:S(2)}) collective-permute-start(bf16[2,64,128]{2,1,0:T(8,128)(2,1)S(1)} %update.1.refs_0_), channel_id=1, source_target_pairs={{0,2},{1,3},{2,0},{3,1},{4,6},{5,7},{6,4},{7,5},{8,10},{9,11},{10,... | collective-permute-start | bytes 98312 | tf_op jit(solution)/shard_map/ppermute | solution.py:61
  63.3 1.7 %collective-permute-done.13.refs_1_ = bf16[2,64,128]{2,1,0:T(8,128)(2,1)S(1)} collective-permute-done((bf16[2,64,128]{2,1,0:T(8,128)(2,1)S(1)}, bf16[2,64,128]{2,1,0:T(8,128)(2,1)S(1)}, u32[]{:S(2)}, u32[]{:S(2)}) %collective-permute-start.13) | collective-permute-done | bytes 32800 | tf_op jit(solution)/shard_map/ppermute | solution.py:61
  65.0 1.7 %second.1.refs_0_.refs_2_ = f32[64,128]{1,0:T(8,128)S(1)} custom-call(bf16[2,64,128]{2,1,0:T(8,128)(2,1)S(1)} %update.1.refs_0_, bf16[2,64,128]{2,1,0:T(8,128)(2,1)S(1)} %collective-permute-done.13.refs_1_, bf16[2,64,128]{2,1,0:T(8,128)(2,1)S(1)} %collective-permute-done.14.refs_2_, bf16[2,64,128]{2,1,0:T(8,128)(2,1)S(1)} %collective-permute-done.15.refs_3_, ...), custom_call_target="tpu_custom_call" | custom-call | bytes 6000000 | tf_op jit(solution)/shard_map/second/pallas_call | solution.py:37
  68.9 2.4 %collective-permute-done.17.got_ref = f32[64,128]{1,0:T(8,128)S(1)} collective-permute-done((f32[64,128]{1,0:T(8,128)S(1)}, f32[64,128]{1,0:T(8,128)S(1)}, u32[]{:S(2)}, u32[]{:S(2)}) %collective-permute-start.17) | collective-permute-done | bytes 32800 | tf_op jit(solution)/shard_map/ppermute | solution.py:61
  71.3 3.5 %mode_send.1 = (f32[64,128]{1,0:T(8,128)S(1)}, bf16[2,64,128]{2,1,0:T(8,128)(2,1)S(1)}, bf16[2,64,128]{2,1,0:T(8,128)(2,1)S(1)}, bf16[2,64,128]{2,1,0:T(8,128)(2,1)S(1)}) custom-call(f32[64,128]{1,0:T(8,128)S(1)} %add.16.mine_ref, f32[64,128]{1,0:T(8,128)S(1)} %collective-permute-done.17.got_ref, f32[64,64]{1,0:T(8,128)S(1)} %get-tuple-element.69.gram_frames_ref, ...), custom_call_target="tpu_custom_call" | custom-call | bytes 12000000 | tf_op jit(solution)/shard_map/mode_send/pallas_call | solution.py:37
  76.3 2.0 %collective-permute-start.18 = (bf16[2,64,128]{2,1,0:T(8,128)(2,1)S(1)}, bf16[2,64,128]{2,1,0:T(8,128)(2,1)S(1)}, u32[]{:S(2)}, u32[]{:S(2)}) collective-permute-start(bf16[2,64,128]{2,1,0:T(8,128)(2,1)S(1)} %get-tuple-element.71.after_ref), channel_id=1, source_target_pairs={{0,1},{1,0},{2,3},{3,2},{4,5},{5,4},{6,7},{7,6},{8,9},{9,8},{10,11... | collective-permute-start | bytes 98312 | tf_op jit(solution)/shard_map/ppermute | solution.py:61
  80.3 2.1 %collective-permute-start.21 = (bf16[64,128]{1,0:T(8,128)(2,1)S(1)}, bf16[64,128]{1,0:T(8,128)(2,1)S(1)}, u32[]{:S(2)}, u32[]{:S(2)}) collective-permute-start(bf16[64,128]{1,0:T(8,128)(2,1)S(1)} %get-tuple-element.75), channel_id=1, source_target_pairs={{0,4},{1,5},{2,6},{3,7},{4,0},{5,1},{6,2},{7,3},{8,12},{9,13},{10,... | collective-permute-start | bytes 49160 | tf_op jit(solution)/shard_map/ppermute | solution.py:61
  82.3 2.6 %collective-permute-done.21 = bf16[64,128]{1,0:T(8,128)(2,1)S(1)} collective-permute-done((bf16[64,128]{1,0:T(8,128)(2,1)S(1)}, bf16[64,128]{1,0:T(8,128)(2,1)S(1)}, u32[]{:S(2)}, u32[]{:S(2)}) %collective-permute-start.21) | collective-permute-done | bytes 16416 | tf_op jit(solution)/shard_map/ppermute | solution.py:61
  (46 shorter events, 22.6 us)
Async XLA Ops:
  1.5 7.8 %collective-permute-start = (bf16[1,96,128]{2,1,0:T(8,128)(2,1)S(1)}, bf16[1,96,128]{2,1,0:T(8,128)(2,1)S(1)}, u32[]{:S(2)}, u32[]{:S(2)}) collective-permute-start(bf16[1,96,128]{2,1,0:T(8,128)(2,1)S(1)} %get-tuple-element.39.after_ref.refs_0_), channel_id=1, source_target_pairs={{0,4},{1,5},{2,6},{3,7},{4,0},{5,1},{6,2},{7,3},{8,12},{9,13},{10,... | collective-permute-start | bytes 73736 | tf_op jit(solution)/shard_map/ppermute | solution.py:61
  9.2 4.5 %collective-permute-start.1 = (bf16[2,96,128]{2,1,0:T(8,128)(2,1)S(1)}, bf16[2,96,128]{2,1,0:T(8,128)(2,1)S(1)}, u32[]{:S(2)}, u32[]{:S(2)}) collective-permute-start(bf16[2,96,128]{2,1,0:T(8,128)(2,1)S(1)} %stack.2.after_ref.refs_0_), channel_id=1, source_target_pairs={{0,2},{1,3},{2,0},{3,1},{4,6},{5,7},{6,4},{7,5},{8,10},{9,11},{10,... | collective-permute-start | bytes 147464 | tf_op jit(solution)/shard_map/ppermute | solution.py:61
  13.8 4.7 %collective-permute-start.2 = (bf16[4,96,128]{2,1,0:T(8,128)(2,1)S(1)}, bf16[4,96,128]{2,1,0:T(8,128)(2,1)S(1)}, u32[]{:S(2)}, u32[]{:S(2)}) collective-permute-start(bf16[4,96,128]{2,1,0:T(8,128)(2,1)S(1)} %stack.3.after_ref.refs_0_), channel_id=1, source_target_pairs={{0,1},{1,0},{2,3},{3,2},{4,5},{5,4},{6,7},{7,6},{8,9},{9,8},{10,11... | collective-permute-start | bytes 294920 | tf_op jit(solution)/shard_map/ppermute | solution.py:61
  23.2 1.3 %collective-permute-start.3 = (f32[128,128]{1,0:T(8,128)S(1)}, f32[128,128]{1,0:T(8,128)S(1)}, u32[]{:S(2)}, u32[]{:S(2)}) collective-permute-start(f32[128,128]{1,0:T(8,128)S(1)} %project.1.a_ref), channel_id=1, source_target_pairs={{0,8},{1,9},{2,10},{3,11},{4,12},{5,13},{6,14},{7,15},{8,0},{9,1},... | collective-permute-start | bytes 196616 | tf_op jit(solution)/shard_map/ppermute | solution.py:61
  24.6 6.1 %collective-permute-start.4 = (f32[128,128]{1,0:T(8,128)S(1)}, f32[128,128]{1,0:T(8,128)S(1)}, u32[]{:S(2)}, u32[]{:S(2)}) collective-permute-start(f32[128,128]{1,0:T(8,128)S(1)} %get-tuple-element.52.refs_0_), channel_id=1, source_target_pairs={{0,24},{1,25},{2,26},{3,27},{4,28},{5,29},{6,30},{7,31},{8,16},{9,... | collective-permute-start | bytes 196616 | tf_op jit(solution)/shard_map/ppermute | solution.py:61
  25.9 4.2 %collective-permute-start.6 = (f32[64,128]{1,0:T(8,128)S(1)}, f32[64,128]{1,0:T(8,128)S(1)}, u32[]{:S(2)}, u32[]{:S(2)}) collective-permute-start(f32[64,128]{1,0:T(8,128)S(1)} %get-tuple-element.53), channel_id=1, source_target_pairs={{0,25},{1,24},{2,27},{3,26},{4,29},{5,28},{6,31},{7,30},{8,17},{9,... | collective-permute-start | bytes 98312 | tf_op jit(solution)/shard_map/ppermute | solution.py:61
  27.3 3.4 %collective-permute-start.5 = (f32[64,128]{1,0:T(8,128)S(1)}, f32[64,128]{1,0:T(8,128)S(1)}, u32[]{:S(2)}, u32[]{:S(2)}) collective-permute-start(f32[64,128]{1,0:T(8,128)S(1)} %get-tuple-element.53), channel_id=1, source_target_pairs={{0,9},{1,8},{2,11},{3,10},{4,13},{5,12},{6,15},{7,14},{8,1},{9,0},... | collective-permute-start | bytes 98312 | tf_op jit(solution)/shard_map/ppermute | solution.py:61
  30.7 3.4 %collective-permute-start.7 = (f32[64,128]{1,0:T(8,128)S(1)}, f32[64,128]{1,0:T(8,128)S(1)}, u32[]{:S(2)}, u32[]{:S(2)}) collective-permute-start(f32[64,128]{1,0:T(8,128)S(1)} %get-tuple-element.56.refs_2_.refs_0_), channel_id=1, source_target_pairs={{0,10},{1,11},{2,8},{3,9},{4,14},{5,15},{6,12},{7,13},{8,2},{9,3},... | collective-permute-start | bytes 98312 | tf_op jit(solution)/shard_map/ppermute | solution.py:61
  34.1 4.2 %collective-permute-start.8 = (f32[64,128]{1,0:T(8,128)S(1)}, f32[64,128]{1,0:T(8,128)S(1)}, u32[]{:S(2)}, u32[]{:S(2)}) collective-permute-start(f32[64,128]{1,0:T(8,128)S(1)} %add.13.refs_1_.refs_0_), channel_id=1, source_target_pairs={{0,12},{1,13},{2,14},{3,15},{4,8},{5,9},{6,10},{7,11},{8,4},{9,5},... | collective-permute-start | bytes 98312 | tf_op jit(solution)/shard_map/ppermute | solution.py:61
  44.6 7.3 %collective-permute-start.9 = (f32[2,64,128]{2,1,0:T(8,128)S(1)}, f32[2,64,128]{2,1,0:T(8,128)S(1)}, u32[]{:S(2)}, u32[]{:S(2)}) collective-permute-start(f32[2,64,128]{2,1,0:T(8,128)S(1)} %get-tuple-element.64), channel_id=1, source_target_pairs={{0,1},{1,0},{2,3},{3,2},{4,5},{5,4},{6,7},{7,6},{8,9},{9,8},{10,11... | collective-permute-start | bytes 196616 | tf_op jit(solution)/shard_map/ppermute | solution.py:61
  45.6 6.3 %collective-permute-start.10 = (f32[2,64,128]{2,1,0:T(8,128)S(1)}, f32[2,64,128]{2,1,0:T(8,128)S(1)}, u32[]{:S(2)}, u32[]{:S(2)}) collective-permute-start(f32[2,64,128]{2,1,0:T(8,128)S(1)} %get-tuple-element.65), channel_id=1, source_target_pairs={{0,2},{1,3},{2,0},{3,1},{4,6},{5,7},{6,4},{7,5},{8,10},{9,11},{10,... | collective-permute-start | bytes 196616 | tf_op jit(solution)/shard_map/ppermute | solution.py:61
  46.9 5.2 %collective-permute-start.11 = (f32[2,64,128]{2,1,0:T(8,128)S(1)}, f32[2,64,128]{2,1,0:T(8,128)S(1)}, u32[]{:S(2)}, u32[]{:S(2)}) collective-permute-start(f32[2,64,128]{2,1,0:T(8,128)S(1)} %get-tuple-element.66), channel_id=1, source_target_pairs={{0,3},{1,2},{2,1},{3,0},{4,7},{5,6},{6,5},{7,4},{8,11},{9,10},{10,... | collective-permute-start | bytes 196616 | tf_op jit(solution)/shard_map/ppermute | solution.py:61
  52.0 5.2 %collective-permute-start.12 = (f32[2,64,128]{2,1,0:T(8,128)S(1)}, f32[2,64,128]{2,1,0:T(8,128)S(1)}, u32[]{:S(2)}, u32[]{:S(2)}) collective-permute-start(f32[2,64,128]{2,1,0:T(8,128)S(1)} %add.15.refs_1_.refs_0_), channel_id=1, source_target_pairs={{0,4},{1,5},{2,6},{3,7},{4,0},{5,1},{6,2},{7,3},{8,12},{9,13},{10,... | collective-permute-start | bytes 196616 | tf_op jit(solution)/shard_map/ppermute | solution.py:61
  57.5 5.0 %collective-permute-start.15 = (bf16[2,64,128]{2,1,0:T(8,128)(2,1)S(1)}, bf16[2,64,128]{2,1,0:T(8,128)(2,1)S(1)}, u32[]{:S(2)}, u32[]{:S(2)}) collective-permute-start(bf16[2,64,128]{2,1,0:T(8,128)(2,1)S(1)} %update.1.refs_0_), channel_id=1, source_target_pairs={{0,3},{1,2},{2,1},{3,0},{4,7},{5,6},{6,5},{7,4},{8,11},{9,10},{10,... | collective-permute-start | bytes 98312 | tf_op jit(solution)/shard_map/ppermute | solution.py:61
  59.2 4.1 %collective-permute-start.14 = (bf16[2,64,128]{2,1,0:T(8,128)(2,1)S(1)}, bf16[2,64,128]{2,1,0:T(8,128)(2,1)S(1)}, u32[]{:S(2)}, u32[]{:S(2)}) collective-permute-start(bf16[2,64,128]{2,1,0:T(8,128)(2,1)S(1)} %update.1.refs_0_), channel_id=1, source_target_pairs={{0,2},{1,3},{2,0},{3,1},{4,6},{5,7},{6,4},{7,5},{8,10},{9,11},{10,... | collective-permute-start | bytes 98312 | tf_op jit(solution)/shard_map/ppermute | solution.py:61
  61.1 3.9 %collective-permute-start.13 = (bf16[2,64,128]{2,1,0:T(8,128)(2,1)S(1)}, bf16[2,64,128]{2,1,0:T(8,128)(2,1)S(1)}, u32[]{:S(2)}, u32[]{:S(2)}) collective-permute-start(bf16[2,64,128]{2,1,0:T(8,128)(2,1)S(1)} %update.1.refs_0_), channel_id=1, source_target_pairs={{0,1},{1,0},{2,3},{3,2},{4,5},{5,4},{6,7},{7,6},{8,9},{9,8},{10,11... | collective-permute-start | bytes 98312 | tf_op jit(solution)/shard_map/ppermute | solution.py:61
  66.7 1.3 %collective-permute-start.16 = (f32[64,128]{1,0:T(8,128)S(1)}, f32[64,128]{1,0:T(8,128)S(1)}, u32[]{:S(2)}, u32[]{:S(2)}) collective-permute-start(f32[64,128]{1,0:T(8,128)S(1)} %second.1.refs_0_.refs_2_), channel_id=1, source_target_pairs={{0,8},{1,9},{2,10},{3,11},{4,12},{5,13},{6,14},{7,15},{8,0},{9,1},... | collective-permute-start | bytes 98312 | tf_op jit(solution)/shard_map/ppermute | solution.py:61
  67.9 3.3 %collective-permute-start.17 = (f32[64,128]{1,0:T(8,128)S(1)}, f32[64,128]{1,0:T(8,128)S(1)}, u32[]{:S(2)}, u32[]{:S(2)}) collective-permute-start(f32[64,128]{1,0:T(8,128)S(1)} %add.16.mine_ref), channel_id=1, source_target_pairs={{0,24},{1,25},{2,26},{3,27},{4,28},{5,29},{6,30},{7,31},{8,16},{9,... | collective-permute-start | bytes 98312 | tf_op jit(solution)/shard_map/ppermute | solution.py:61
  74.8 4.8 %collective-permute-start.19 = (bf16[2,64,128]{2,1,0:T(8,128)(2,1)S(1)}, bf16[2,64,128]{2,1,0:T(8,128)(2,1)S(1)}, u32[]{:S(2)}, u32[]{:S(2)}) collective-permute-start(bf16[2,64,128]{2,1,0:T(8,128)(2,1)S(1)} %get-tuple-element.72), channel_id=1, source_target_pairs={{0,2},{1,3},{2,0},{3,1},{4,6},{5,7},{6,4},{7,5},{8,10},{9,11},{10,... | collective-permute-start | bytes 98312 | tf_op jit(solution)/shard_map/ppermute | solution.py:61
  75.0 4.8 %collective-permute-start.20 = (bf16[2,64,128]{2,1,0:T(8,128)(2,1)S(1)}, bf16[2,64,128]{2,1,0:T(8,128)(2,1)S(1)}, u32[]{:S(2)}, u32[]{:S(2)}) collective-permute-start(bf16[2,64,128]{2,1,0:T(8,128)(2,1)S(1)} %get-tuple-element.73), channel_id=1, source_target_pairs={{0,3},{1,2},{2,1},{3,0},{4,7},{5,6},{6,5},{7,4},{8,11},{9,10},{10,... | collective-permute-start | bytes 98312 | tf_op jit(solution)/shard_map/ppermute | solution.py:61
  76.3 3.9 %collective-permute-start.18 = (bf16[2,64,128]{2,1,0:T(8,128)(2,1)S(1)}, bf16[2,64,128]{2,1,0:T(8,128)(2,1)S(1)}, u32[]{:S(2)}, u32[]{:S(2)}) collective-permute-start(bf16[2,64,128]{2,1,0:T(8,128)(2,1)S(1)} %get-tuple-element.71.after_ref), channel_id=1, source_target_pairs={{0,1},{1,0},{2,3},{3,2},{4,5},{5,4},{6,7},{7,6},{8,9},{9,8},{10,11... | collective-permute-start | bytes 98312 | tf_op jit(solution)/shard_map/ppermute | solution.py:61
  80.3 4.7 %collective-permute-start.21 = (bf16[64,128]{1,0:T(8,128)(2,1)S(1)}, bf16[64,128]{1,0:T(8,128)(2,1)S(1)}, u32[]{:S(2)}, u32[]{:S(2)}) collective-permute-start(bf16[64,128]{1,0:T(8,128)(2,1)S(1)} %get-tuple-element.75), channel_id=1, source_target_pairs={{0,4},{1,5},{2,6},{3,7},{4,0},{5,1},{6,2},{7,3},{8,12},{9,13},{10,... | collective-permute-start | bytes 49160 | tf_op jit(solution)/shard_map/ppermute | solution.py:61

commit v12 on v11

--- a/solution.py
+++ b/solution.py
@@ -154,25 +154,23 @@
 
 def prepare_body(at, cols, here, ahead, t_ref, b_ref, after_ref, *refs):
     del after_ref
-    slab_ref = refs[0] if here else None
-    refs = list(refs[1:] if here else refs)
+    refs = list(refs)
+    early_ref = refs.pop(0) if here else None
     out_ref, wide_ref, token_ref = refs[:3]
     next_ref = refs.pop(3) if ahead else None
     sems = refs[-1]
-    slab_ref = slab_ref if here else refs[3]
-    blocks = slab_ref.shape[0]
-
-    def fetch(n, to_ref, start, sem):
+    blocks = t_ref.shape[0] // GROUP
+    slab_ref = refs[3] if here < blocks else None
+
+    def fetch(n, to_ref, slot, start, sem):
         return pltpu.make_async_copy(
-            t_ref.at[pl.ds(n * GROUP, GROUP), pl.ds(start, to_ref.shape[2])], to_ref.at[n], sems.at[sem, n]
+            t_ref.at[pl.ds(n * GROUP, GROUP), pl.ds(start, to_ref.shape[2])], to_ref.at[slot], sems.at[sem, n]
         )
 
-    if not here:
-        for n in range(blocks):
-            fetch(n, slab_ref, at, 0).start()
-    if ahead:
-        for n in range(blocks):
-            fetch(n, next_ref, at + cols, 1).start()
+    for n in range(here, blocks):
+        fetch(n, slab_ref, n - here, at, 0).start()
+    for n in range(ahead):
+        fetch(n, next_ref, n, at + cols, 1).start()
     token_ref[...] = jnp.zeros_like(token_ref)
     for j in range(cols):
         wide_ref[j] = jnp.broadcast_to(b_ref[:, at + j : at + j + 1], wide_ref.shape[1:])
@@ -180,31 +178,41 @@
     of = lax.broadcasted_iota(jnp.int32, (256, 256), 1)
     turn = jnp.where((to // GROUP) + (to % GROUP) * GROUP == of, 1.0, 0.0).astype(BF16)
 
-    def step(n, _):
-        if not here:
-            fetch(n, slab_ref, at, 0).wait()
+    def turn_block(n, from_ref, slot):
         for g in range(0, cols, GROUP):
-            block = slab_ref[n, :, g : g + GROUP, :].reshape(GROUP * GROUP, -1)
+            block = from_ref[slot, :, g : g + GROUP, :].reshape(GROUP * GROUP, -1)
             turned = dot(turn, block, ((1,), (0,))).astype(BF16).reshape(GROUP, GROUP, -1)
             out_ref[g : g + GROUP, pl.ds(pl.multiple_of(n * GROUP, GROUP), GROUP), :] = turned
+
+    def early(n, _):
+        turn_block(n, early_ref, n)
         return 0
 
-    lax.fori_loop(0, blocks, step, 0)
-    if ahead:
-        for n in range(blocks):
-            fetch(n, next_ref, at + cols, 1).wait()
+    def late(n, _):
+        fetch(n, slab_ref, n - here, at, 0).wait()
+        turn_block(n, slab_ref, n - here)
+        return 0
+
+    if here:
+        lax.fori_loop(0, here, early, 0)
+    if here < blocks:
+        lax.fori_loop(here, blocks, late, 0)
+    for n in range(ahead):
+        fetch(n, next_ref, n, at + cols, 1).wait()
 
 
 def prepare(tensor, second, at, cols, fetched, next_cols, after):
     frames, _, rows = tensor.shape
     components = second.shape[0]
     blocks = frames // GROUP
+    here = fetched[0].shape[0] if fetched else 0
+    ahead = 0 if not next_cols else blocks if here else blocks // 2
     outs = (VM((cols, frames, rows), BF16), VM((cols, components, 128), F32), shaped((8, 128)))
-    if next_cols:
-        outs += (VM((blocks, GROUP, next_cols, rows), BF16),)
-    scratch = [] if fetched else [VM((blocks, GROUP, cols, rows), BF16)]
+    if ahead:
+        outs += (VM((ahead, GROUP, next_cols, rows), BF16),)
+    scratch = [VM((blocks - here, GROUP, cols, rows), BF16)] if here < blocks else []
     got = call(
-        functools.partial(prepare_body, at, cols, bool(fetched), bool(next_cols)),
+        functools.partial(prepare_body, at, cols, here, ahead),
         outs,
         [anywhere(), vmem(), anywhere()] + [vmem()] * len(fetched),
         (tensor, second, after, *fetched),

time: 86 us -> 87.3 us (1.015)
  waiting for transfers between devices: 21.7 us -> 24.6 us
  starting transfers between devices: 27.7 us -> 25.9 us
    ppermute x22, waiting for transfers between devices: 21.7 us -> 24.6 us  [swap(): return lax.ppermute(x, axes, [(n, n ^ offset) for n in range(count)])]
    ppermute x22, starting transfers between devices: 27.7 us -> 25.9 us  [swap(): return lax.ppermute(x, axes, [(n, n ^ offset) for n in range(count)])]
  transfers between devices with their start and end apart: 22 -> 22, of which waited for: 16 -> 15; matrix products, arithmetic and copies ran while one was open for 0% -> 0% of each run, Pallas kernels for 20% -> 20%
where the time goes in v12:
time: 87.3 us; the launch traced here: 86.9 us
  Pallas kernels  34.9 us (40%)
  starting transfers between devices  25.9 us (30%)
  waiting for transfers between devices  24.6 us (28%)
    pallas_call x25, Pallas kernels, call(): pl.pallas_call(body, out_shape=outs, in_specs=ins, out_specs=(vmem(),) *...  34.9 us
    ppermute x22, starting transfers between devices, swap(): return lax.ppermute(x, axes, [(n, n ^ offset) for n in range(count)])  25.9 us
    ppermute x22, waiting for transfers between devices, swap(): return lax.ppermute(x, axes, [(n, n ^ offset) for n in range(count)])  24.6 us
  transfers between devices with their start and end apart: 22, of which 15 were waited for; matrix products, arithmetic and copies ran while one was open for 0% of the time, Pallas kernels for 20%

profile of v12, /device:TPU:0, one launch (start us, length us, event | category | flops | bytes accessed | tf_op | source)
XLA Modules:
  0.0 86.9 jit_solution(11363019085604303117)
XLA Ops:
  1.5 4.1 %collective-permute-start = (bf16[1,96,128]{2,1,0:T(8,128)(2,1)S(1)}, bf16[1,96,128]{2,1,0:T(8,128)(2,1)S(1)}, u32[]{:S(2)}, u32[]{:S(2)}) collective-permute-start(bf16[1,96,128]{2,1,0:T(8,128)(2,1)S(1)} %get-tuple-element.39.after_ref.refs_0_), channel_id=1, source_target_pairs={{0,4},{1,5},{2,6},{3,7},{4,0},{5,1},{6,2},{7,3},{8,12},{9,13},{10,... | collective-permute-start | bytes 73736 | tf_op jit(solution)/shard_map/ppermute | solution.py:61
  5.6 3.6 %prepare.3 = (bf16[16,128,1024]{2,1,0:T(8,128)(2,1)S(1)}, f32[16,64,128]{2,1,0:T(8,128)S(1)}, f32[8,128]{1,0:T(8,128)S(1)}, bf16[4,16,16,1024]{3,2,1,0:T(8,128)(2,1)S(1)}) custom-call(bf16[128,48,1024]{2,1,0:T(8,128)(2,1)} %t_ref.5, f32[64,128]{1,0:T(8,128)S(1)} %get-tuple-element.40.b_ref, bf16[1,96,128]{2,1,0:T(8,128)(2,1)S(1)} %get-tuple-element.39.after_ref.refs_0_), custom_call_target="tpu_custom_call" | custom-call | bytes 6000000 | tf_op jit(solution)/shard_map/prepare/pallas_call | solution.py:37
  9.2 1.6 %collective-permute-start.1 = (bf16[2,96,128]{2,1,0:T(8,128)(2,1)S(1)}, bf16[2,96,128]{2,1,0:T(8,128)(2,1)S(1)}, u32[]{:S(2)}, u32[]{:S(2)}) collective-permute-start(bf16[2,96,128]{2,1,0:T(8,128)(2,1)S(1)} %stack.2.after_ref.refs_0_), channel_id=1, source_target_pairs={{0,2},{1,3},{2,0},{3,1},{4,6},{5,7},{6,4},{7,5},{8,10},{9,11},{10,... | collective-permute-start | bytes 147464 | tf_op jit(solution)/shard_map/ppermute | solution.py:61
  10.9 3.0 %prepare.4 = (bf16[16,128,1024]{2,1,0:T(8,128)(2,1)S(1)}, f32[16,64,128]{2,1,0:T(8,128)S(1)}, f32[8,128]{1,0:T(8,128)S(1)}, bf16[8,16,16,1024]{3,2,1,0:T(8,128)(2,1)S(1)}) custom-call(bf16[128,48,1024]{2,1,0:T(8,128)(2,1)} %t_ref.5, f32[64,128]{1,0:T(8,128)S(1)} %get-tuple-element.40.b_ref, bf16[2,96,128]{2,1,0:T(8,128)(2,1)S(1)} %stack.2.after_ref.refs_0_, ...), custom_call_target="tpu_custom_call" | custom-call | bytes 6000000 | tf_op jit(solution)/shard_map/prepare/pallas_call | solution.py:37
  13.9 1.6 %collective-permute-start.2 = (bf16[4,96,128]{2,1,0:T(8,128)(2,1)S(1)}, bf16[4,96,128]{2,1,0:T(8,128)(2,1)S(1)}, u32[]{:S(2)}, u32[]{:S(2)}) collective-permute-start(bf16[4,96,128]{2,1,0:T(8,128)(2,1)S(1)} %stack.3.after_ref.refs_0_), channel_id=1, source_target_pairs={{0,1},{1,0},{2,3},{3,2},{4,5},{5,4},{6,7},{7,6},{8,9},{9,8},{10,11... | collective-permute-start | bytes 294920 | tf_op jit(solution)/shard_map/ppermute | solution.py:61
  15.4 2.8 %prepare.5 = (bf16[16,128,1024]{2,1,0:T(8,128)(2,1)S(1)}, f32[16,64,128]{2,1,0:T(8,128)S(1)}, f32[8,128]{1,0:T(8,128)S(1)}) custom-call(bf16[128,48,1024]{2,1,0:T(8,128)(2,1)} %t_ref.5, f32[64,128]{1,0:T(8,128)S(1)} %get-tuple-element.40.b_ref, bf16[4,96,128]{2,1,0:T(8,128)(2,1)S(1)} %stack.3.after_ref.refs_0_, ...), custom_call_target="tpu_custom_call" | custom-call | bytes 6000000 | tf_op jit(solution)/shard_map/prepare/pallas_call | solution.py:37
  18.9 4.4 %project.1.a_ref = f32[128,128]{1,0:T(8,128)S(1)} custom-call(bf16[1024,64]{1,0:T(8,128)(2,1)S(1)} %get-tuple-element.46.turned_ref, f32[48,64]{1,0:T(8,128)S(1)} %get-tuple-element.47.second_ref, f32[64,64]{1,0:T(8,128)S(1)} %get-tuple-element.48.gram_ref, bf16[16,128,1024]{2,1,0:T(8,128)(2,1)S(1)} %get-tuple-element.49.refs_0_.refs_2_.refs_1_, ...), custom_call_target="tpu_custom_call" | custom-call | bytes 15000000 | tf_op jit(solution)/shard_map/project/pallas_call | solution.py:37
  26.0 1.4 %collective-permute-start.6 = (f32[64,128]{1,0:T(8,128)S(1)}, f32[64,128]{1,0:T(8,128)S(1)}, u32[]{:S(2)}, u32[]{:S(2)}) collective-permute-start(f32[64,128]{1,0:T(8,128)S(1)} %get-tuple-element.53), channel_id=1, source_target_pairs={{0,25},{1,24},{2,27},{3,26},{4,29},{5,28},{6,31},{7,30},{8,17},{9,... | collective-permute-start | bytes 98312 | tf_op jit(solution)/shard_map/ppermute | solution.py:61
  27.7 2.5 %collective-permute-done.6.refs_3_ = f32[64,128]{1,0:T(8,128)S(1)} collective-permute-done((f32[64,128]{1,0:T(8,128)S(1)}, f32[64,128]{1,0:T(8,128)S(1)}, u32[]{:S(2)}, u32[]{:S(2)}) %collective-permute-start.6) | collective-permute-done | bytes 32800 | tf_op jit(solution)/shard_map/ppermute | solution.py:61
  31.7 1.7 %eliminate.3.refs_2_.refs_0_ = f32[64,64]{1,0:T(8,128)S(1)} custom-call(f32[64,64]{1,0:T(8,128)S(1)} %get-tuple-element.54.refs_0_, f32[64,64]{1,0:T(8,128)S(1)} %get-tuple-element.55.refs_1_.other_ref, f32[64,128]{1,0:T(8,128)S(1)} %get-tuple-element.56.refs_2_.refs_0_), custom_call_target="tpu_custom_call" | custom-call | bytes 3000000 | tf_op jit(solution)/shard_map/eliminate/pallas_call | solution.py:37
  35.8 2.6 %collective-permute-done.8.refs_1_ = f32[64,128]{1,0:T(8,128)S(1)} collective-permute-done((f32[64,128]{1,0:T(8,128)S(1)}, f32[64,128]{1,0:T(8,128)S(1)}, u32[]{:S(2)}, u32[]{:S(2)}) %collective-permute-start.8) | collective-permute-done | bytes 32800 | tf_op jit(solution)/shard_map/ppermute | solution.py:61
  38.4 6.3 %slab.2 = (f32[64,128]{1,0:T(8,128)}, f32[64,128]{1,0:T(8,128)S(1)}, f32[48,64,768]{2,1,0:T(8,128)S(1)}, f32[2,64,128]{2,1,0:T(8,128)S(1)}, f32[2,64,128]{2,1,0:T(8,128)S(1)}, /*index=5*/f32[2,64,128]{2,1,0:T(8,128)S(1)}) custom-call(s32[1]{0:T(128)} %bitcast.me_ref, f32[64,64]{1,0:T(8,128)S(1)} %eliminate.4.refs_2_.refs_0_, f32[64,128]{1,0:T(8,128)S(1)} %add.14.refs_1_, ...), custom_call_target="tpu_custom_call" | custom-call | bytes 18000000 | tf_op jit(solution)/shard_map/slab/pallas_call | solution.py:37
  46.8 1.4 %collective-permute-start.11 = (f32[2,64,128]{2,1,0:T(8,128)S(1)}, f32[2,64,128]{2,1,0:T(8,128)S(1)}, u32[]{:S(2)}, u32[]{:S(2)}) collective-permute-start(f32[2,64,128]{2,1,0:T(8,128)S(1)} %get-tuple-element.66), channel_id=1, source_target_pairs={{0,3},{1,2},{2,1},{3,0},{4,7},{5,6},{6,5},{7,4},{8,11},{9,10},{10,... | collective-permute-start | bytes 196616 | tf_op jit(solution)/shard_map/ppermute | solution.py:61
  48.2 1.9 %slab.3 = (f32[48,64,256]{2,1,0:T(8,128)S(1)}, f32[2,64,128]{2,1,0:T(8,128)S(1)}) custom-call(s32[1]{0:T(128)} %bitcast.me_ref, f32[64,128]{1,0:T(8,128)S(1)} %get-tuple-element.61.refs_0_.frames_ref, bf16[16,128,1024]{2,1,0:T(8,128)(2,1)S(1)} %get-tuple-element.49.refs_0_.refs_2_.refs_1_, ...), custom_call_target="tpu_custom_call" | custom-call | bytes 6000000 | tf_op jit(solution)/shard_map/slab/pallas_call | solution.py:37
  50.1 1.9 %frames_gram.1 = (f32[64,64]{1,0:T(8,128)S(1)}, f32[64,64]{1,0:T(8,128)S(1)}) custom-call(f32[64,128]{1,0:T(8,128)S(1)} %get-tuple-element.61.refs_0_.frames_ref, f32[64,64]{1,0:T(8,128)S(1)} %get-tuple-element.55.refs_1_.other_ref, f32[2,64,128]{2,1,0:T(8,128)S(1)} %get-tuple-element.62.after_ref.refs_0_), custom_call_target="tpu_custom_call" | custom-call | bytes 6000000 | tf_op jit(solution)/shard_map/frames_gram/pallas_call | solution.py:37
  54.0 4.4 %collective-permute-done.12.refs_1_ = f32[2,64,128]{2,1,0:T(8,128)S(1)} collective-permute-done((f32[2,64,128]{2,1,0:T(8,128)S(1)}, f32[2,64,128]{2,1,0:T(8,128)S(1)}, u32[]{:S(2)}, u32[]{:S(2)}) %collective-permute-start.12) | collective-permute-done | bytes 65568 | tf_op jit(solution)/shard_map/ppermute | solution.py:61
  59.1 1.9 %collective-permute-start.14 = (bf16[2,64,128]{2,1,0:T(8,128)(2,1)S(1)}, bf16[2,64,128]{2,1,0:T(8,128)(2,1)S(1)}, u32[]{:S(2)}, u32[]{:S(2)}) collective-permute-start(bf16[2,64,128]{2,1,0:T(8,128)(2,1)S(1)} %update.1.refs_0_), channel_id=1, source_target_pairs={{0,2},{1,3},{2,0},{3,1},{4,6},{5,7},{6,4},{7,5},{8,10},{9,11},{10,... | collective-permute-start | bytes 98312 | tf_op jit(solution)/shard_map/ppermute | solution.py:61
  63.6 1.4 %collective-permute-done.13.refs_1_ = bf16[2,64,128]{2,1,0:T(8,128)(2,1)S(1)} collective-permute-done((bf16[2,64,128]{2,1,0:T(8,128)(2,1)S(1)}, bf16[2,64,128]{2,1,0:T(8,128)(2,1)S(1)}, u32[]{:S(2)}, u32[]{:S(2)}) %collective-permute-start.13) | collective-permute-done | bytes 32800 | tf_op jit(solution)/shard_map/ppermute | solution.py:61
  65.0 1.7 %second.1.refs_0_.refs_2_ = f32[64,128]{1,0:T(8,128)S(1)} custom-call(bf16[2,64,128]{2,1,0:T(8,128)(2,1)S(1)} %update.1.refs_0_, bf16[2,64,128]{2,1,0:T(8,128)(2,1)S(1)} %collective-permute-done.13.refs_1_, bf16[2,64,128]{2,1,0:T(8,128)(2,1)S(1)} %collective-permute-done.14.refs_2_, bf16[2,64,128]{2,1,0:T(8,128)(2,1)S(1)} %collective-permute-done.15.refs_3_, ...), custom_call_target="tpu_custom_call" | custom-call | bytes 6000000 | tf_op jit(solution)/shard_map/second/pallas_call | solution.py:37
  69.2 2.1 %collective-permute-done.17.got_ref = f32[64,128]{1,0:T(8,128)S(1)} collective-permute-done((f32[64,128]{1,0:T(8,128)S(1)}, f32[64,128]{1,0:T(8,128)S(1)}, u32[]{:S(2)}, u32[]{:S(2)}) %collective-permute-start.17) | collective-permute-done | bytes 32800 | tf_op jit(solution)/shard_map/ppermute | solution.py:61
  71.3 3.5 %mode_send.1 = (f32[64,128]{1,0:T(8,128)S(1)}, bf16[2,64,128]{2,1,0:T(8,128)(2,1)S(1)}, bf16[2,64,128]{2,1,0:T(8,128)(2,1)S(1)}, bf16[2,64,128]{2,1,0:T(8,128)(2,1)S(1)}) custom-call(f32[64,128]{1,0:T(8,128)S(1)} %add.16.mine_ref, f32[64,128]{1,0:T(8,128)S(1)} %collective-permute-done.17.got_ref, f32[64,64]{1,0:T(8,128)S(1)} %get-tuple-element.69.gram_frames_ref, ...), custom_call_target="tpu_custom_call" | custom-call | bytes 12000000 | tf_op jit(solution)/shard_map/mode_send/pallas_call | solution.py:37
  75.0 2.5 %collective-permute-start.20 = (bf16[2,64,128]{2,1,0:T(8,128)(2,1)S(1)}, bf16[2,64,128]{2,1,0:T(8,128)(2,1)S(1)}, u32[]{:S(2)}, u32[]{:S(2)}) collective-permute-start(bf16[2,64,128]{2,1,0:T(8,128)(2,1)S(1)} %get-tuple-element.73), channel_id=1, source_target_pairs={{0,3},{1,2},{2,1},{3,0},{4,7},{5,6},{6,5},{7,4},{8,11},{9,10},{10,... | collective-permute-start | bytes 98312 | tf_op jit(solution)/shard_map/ppermute | solution.py:61
  79.8 1.6 %collective-permute-done.18.refs_1_ = bf16[2,64,128]{2,1,0:T(8,128)(2,1)S(1)} collective-permute-done((bf16[2,64,128]{2,1,0:T(8,128)(2,1)S(1)}, bf16[2,64,128]{2,1,0:T(8,128)(2,1)S(1)}, u32[]{:S(2)}, u32[]{:S(2)}) %collective-permute-start.18) | collective-permute-done | bytes 32800 | tf_op jit(solution)/shard_map/ppermute | solution.py:61
  82.0 4.3 %collective-permute-done.21 = bf16[64,128]{1,0:T(8,128)(2,1)S(1)} collective-permute-done((bf16[64,128]{1,0:T(8,128)(2,1)S(1)}, bf16[64,128]{1,0:T(8,128)(2,1)S(1)}, u32[]{:S(2)}, u32[]{:S(2)}) %collective-permute-start.21) | collective-permute-done | bytes 16416 | tf_op jit(solution)/shard_map/ppermute | solution.py:61
  (46 shorter events, 21.7 us)
Async XLA Ops:
  1.5 7.7 %collective-permute-start = (bf16[1,96,128]{2,1,0:T(8,128)(2,1)S(1)}, bf16[1,96,128]{2,1,0:T(8,128)(2,1)S(1)}, u32[]{:S(2)}, u32[]{:S(2)}) collective-permute-start(bf16[1,96,128]{2,1,0:T(8,128)(2,1)S(1)} %get-tuple-element.39.after_ref.refs_0_), channel_id=1, source_target_pairs={{0,4},{1,5},{2,6},{3,7},{4,0},{5,1},{6,2},{7,3},{8,12},{9,13},{10,... | collective-permute-start | bytes 73736 | tf_op jit(solution)/shard_map/ppermute | solution.py:61
  9.2 4.6 %collective-permute-start.1 = (bf16[2,96,128]{2,1,0:T(8,128)(2,1)S(1)}, bf16[2,96,128]{2,1,0:T(8,128)(2,1)S(1)}, u32[]{:S(2)}, u32[]{:S(2)}) collective-permute-start(bf16[2,96,128]{2,1,0:T(8,128)(2,1)S(1)} %stack.2.after_ref.refs_0_), channel_id=1, source_target_pairs={{0,2},{1,3},{2,0},{3,1},{4,6},{5,7},{6,4},{7,5},{8,10},{9,11},{10,... | collective-permute-start | bytes 147464 | tf_op jit(solution)/shard_map/ppermute | solution.py:61
  13.9 4.7 %collective-permute-start.2 = (bf16[4,96,128]{2,1,0:T(8,128)(2,1)S(1)}, bf16[4,96,128]{2,1,0:T(8,128)(2,1)S(1)}, u32[]{:S(2)}, u32[]{:S(2)}) collective-permute-start(bf16[4,96,128]{2,1,0:T(8,128)(2,1)S(1)} %stack.3.after_ref.refs_0_), channel_id=1, source_target_pairs={{0,1},{1,0},{2,3},{3,2},{4,5},{5,4},{6,7},{7,6},{8,9},{9,8},{10,11... | collective-permute-start | bytes 294920 | tf_op jit(solution)/shard_map/ppermute | solution.py:61
  23.3 1.3 %collective-permute-start.3 = (f32[128,128]{1,0:T(8,128)S(1)}, f32[128,128]{1,0:T(8,128)S(1)}, u32[]{:S(2)}, u32[]{:S(2)}) collective-permute-start(f32[128,128]{1,0:T(8,128)S(1)} %project.1.a_ref), channel_id=1, source_target_pairs={{0,8},{1,9},{2,10},{3,11},{4,12},{5,13},{6,14},{7,15},{8,0},{9,1},... | collective-permute-start | bytes 196616 | tf_op jit(solution)/shard_map/ppermute | solution.py:61
  24.7 6.1 %collective-permute-start.4 = (f32[128,128]{1,0:T(8,128)S(1)}, f32[128,128]{1,0:T(8,128)S(1)}, u32[]{:S(2)}, u32[]{:S(2)}) collective-permute-start(f32[128,128]{1,0:T(8,128)S(1)} %get-tuple-element.52.refs_0_), channel_id=1, source_target_pairs={{0,24},{1,25},{2,26},{3,27},{4,28},{5,29},{6,30},{7,31},{8,16},{9,... | collective-permute-start | bytes 196616 | tf_op jit(solution)/shard_map/ppermute | solution.py:61
  26.0 4.2 %collective-permute-start.6 = (f32[64,128]{1,0:T(8,128)S(1)}, f32[64,128]{1,0:T(8,128)S(1)}, u32[]{:S(2)}, u32[]{:S(2)}) collective-permute-start(f32[64,128]{1,0:T(8,128)S(1)} %get-tuple-element.53), channel_id=1, source_target_pairs={{0,25},{1,24},{2,27},{3,26},{4,29},{5,28},{6,31},{7,30},{8,17},{9,... | collective-permute-start | bytes 98312 | tf_op jit(solution)/shard_map/ppermute | solution.py:61
  27.4 3.4 %collective-permute-start.5 = (f32[64,128]{1,0:T(8,128)S(1)}, f32[64,128]{1,0:T(8,128)S(1)}, u32[]{:S(2)}, u32[]{:S(2)}) collective-permute-start(f32[64,128]{1,0:T(8,128)S(1)} %get-tuple-element.53), channel_id=1, source_target_pairs={{0,9},{1,8},{2,11},{3,10},{4,13},{5,12},{6,15},{7,14},{8,1},{9,0},... | collective-permute-start | bytes 98312 | tf_op jit(solution)/shard_map/ppermute | solution.py:61
  30.8 3.4 %collective-permute-start.7 = (f32[64,128]{1,0:T(8,128)S(1)}, f32[64,128]{1,0:T(8,128)S(1)}, u32[]{:S(2)}, u32[]{:S(2)}) collective-permute-start(f32[64,128]{1,0:T(8,128)S(1)} %get-tuple-element.56.refs_2_.refs_0_), channel_id=1, source_target_pairs={{0,10},{1,11},{2,8},{3,9},{4,14},{5,15},{6,12},{7,13},{8,2},{9,3},... | collective-permute-start | bytes 98312 | tf_op jit(solution)/shard_map/ppermute | solution.py:61
  34.2 4.2 %collective-permute-start.8 = (f32[64,128]{1,0:T(8,128)S(1)}, f32[64,128]{1,0:T(8,128)S(1)}, u32[]{:S(2)}, u32[]{:S(2)}) collective-permute-start(f32[64,128]{1,0:T(8,128)S(1)} %add.13.refs_1_.refs_0_), channel_id=1, source_target_pairs={{0,12},{1,13},{2,14},{3,15},{4,8},{5,9},{6,10},{7,11},{8,4},{9,5},... | collective-permute-start | bytes 98312 | tf_op jit(solution)/shard_map/ppermute | solution.py:61
  44.7 7.3 %collective-permute-start.9 = (f32[2,64,128]{2,1,0:T(8,128)S(1)}, f32[2,64,128]{2,1,0:T(8,128)S(1)}, u32[]{:S(2)}, u32[]{:S(2)}) collective-permute-start(f32[2,64,128]{2,1,0:T(8,128)S(1)} %get-tuple-element.64), channel_id=1, source_target_pairs={{0,1},{1,0},{2,3},{3,2},{4,5},{5,4},{6,7},{7,6},{8,9},{9,8},{10,11... | collective-permute-start | bytes 196616 | tf_op jit(solution)/shard_map/ppermute | solution.py:61
  45.7 6.3 %collective-permute-start.10 = (f32[2,64,128]{2,1,0:T(8,128)S(1)}, f32[2,64,128]{2,1,0:T(8,128)S(1)}, u32[]{:S(2)}, u32[]{:S(2)}) collective-permute-start(f32[2,64,128]{2,1,0:T(8,128)S(1)} %get-tuple-element.65), channel_id=1, source_target_pairs={{0,2},{1,3},{2,0},{3,1},{4,6},{5,7},{6,4},{7,5},{8,10},{9,11},{10,... | collective-permute-start | bytes 196616 | tf_op jit(solution)/shard_map/ppermute | solution.py:61
  46.8 5.3 %collective-permute-start.11 = (f32[2,64,128]{2,1,0:T(8,128)S(1)}, f32[2,64,128]{2,1,0:T(8,128)S(1)}, u32[]{:S(2)}, u32[]{:S(2)}) collective-permute-start(f32[2,64,128]{2,1,0:T(8,128)S(1)} %get-tuple-element.66), channel_id=1, source_target_pairs={{0,3},{1,2},{2,1},{3,0},{4,7},{5,6},{6,5},{7,4},{8,11},{9,10},{10,... | collective-permute-start | bytes 196616 | tf_op jit(solution)/shard_map/ppermute | solution.py:61
  52.2 6.3 %collective-permute-start.12 = (f32[2,64,128]{2,1,0:T(8,128)S(1)}, f32[2,64,128]{2,1,0:T(8,128)S(1)}, u32[]{:S(2)}, u32[]{:S(2)}) collective-permute-start(f32[2,64,128]{2,1,0:T(8,128)S(1)} %add.15.refs_1_.refs_0_), channel_id=1, source_target_pairs={{0,4},{1,5},{2,6},{3,7},{4,0},{5,1},{6,2},{7,3},{8,12},{9,13},{10,... | collective-permute-start | bytes 196616 | tf_op jit(solution)/shard_map/ppermute | solution.py:61
  58.7 4.9 %collective-permute-start.15 = (bf16[2,64,128]{2,1,0:T(8,128)(2,1)S(1)}, bf16[2,64,128]{2,1,0:T(8,128)(2,1)S(1)}, u32[]{:S(2)}, u32[]{:S(2)}) collective-permute-start(bf16[2,64,128]{2,1,0:T(8,128)(2,1)S(1)} %update.1.refs_0_), channel_id=1, source_target_pairs={{0,3},{1,2},{2,1},{3,0},{4,7},{5,6},{6,5},{7,4},{8,11},{9,10},{10,... | collective-permute-start | bytes 98312 | tf_op jit(solution)/shard_map/ppermute | solution.py:61
  59.1 4.4 %collective-permute-start.14 = (bf16[2,64,128]{2,1,0:T(8,128)(2,1)S(1)}, bf16[2,64,128]{2,1,0:T(8,128)(2,1)S(1)}, u32[]{:S(2)}, u32[]{:S(2)}) collective-permute-start(bf16[2,64,128]{2,1,0:T(8,128)(2,1)S(1)} %update.1.refs_0_), channel_id=1, source_target_pairs={{0,2},{1,3},{2,0},{3,1},{4,6},{5,7},{6,4},{7,5},{8,10},{9,11},{10,... | collective-permute-start | bytes 98312 | tf_op jit(solution)/shard_map/ppermute | solution.py:61
  61.1 3.9 %collective-permute-start.13 = (bf16[2,64,128]{2,1,0:T(8,128)(2,1)S(1)}, bf16[2,64,128]{2,1,0:T(8,128)(2,1)S(1)}, u32[]{:S(2)}, u32[]{:S(2)}) collective-permute-start(bf16[2,64,128]{2,1,0:T(8,128)(2,1)S(1)} %update.1.refs_0_), channel_id=1, source_target_pairs={{0,1},{1,0},{2,3},{3,2},{4,5},{5,4},{6,7},{7,6},{8,9},{9,8},{10,11... | collective-permute-start | bytes 98312 | tf_op jit(solution)/shard_map/ppermute | solution.py:61
  66.7 1.3 %collective-permute-start.16 = (f32[64,128]{1,0:T(8,128)S(1)}, f32[64,128]{1,0:T(8,128)S(1)}, u32[]{:S(2)}, u32[]{:S(2)}) collective-permute-start(f32[64,128]{1,0:T(8,128)S(1)} %second.1.refs_0_.refs_2_), channel_id=1, source_target_pairs={{0,8},{1,9},{2,10},{3,11},{4,12},{5,13},{6,14},{7,15},{8,0},{9,1},... | collective-permute-start | bytes 98312 | tf_op jit(solution)/shard_map/ppermute | solution.py:61
  68.0 3.3 %collective-permute-start.17 = (f32[64,128]{1,0:T(8,128)S(1)}, f32[64,128]{1,0:T(8,128)S(1)}, u32[]{:S(2)}, u32[]{:S(2)}) collective-permute-start(f32[64,128]{1,0:T(8,128)S(1)} %add.16.mine_ref), channel_id=1, source_target_pairs={{0,24},{1,25},{2,26},{3,27},{4,28},{5,29},{6,30},{7,31},{8,16},{9,... | collective-permute-start | bytes 98312 | tf_op jit(solution)/shard_map/ppermute | solution.py:61
  74.8 4.8 %collective-permute-start.19 = (bf16[2,64,128]{2,1,0:T(8,128)(2,1)S(1)}, bf16[2,64,128]{2,1,0:T(8,128)(2,1)S(1)}, u32[]{:S(2)}, u32[]{:S(2)}) collective-permute-start(bf16[2,64,128]{2,1,0:T(8,128)(2,1)S(1)} %get-tuple-element.72), channel_id=1, source_target_pairs={{0,2},{1,3},{2,0},{3,1},{4,6},{5,7},{6,4},{7,5},{8,10},{9,11},{10,... | collective-permute-start | bytes 98312 | tf_op jit(solution)/shard_map/ppermute | solution.py:61
  75.0 4.8 %collective-permute-start.20 = (bf16[2,64,128]{2,1,0:T(8,128)(2,1)S(1)}, bf16[2,64,128]{2,1,0:T(8,128)(2,1)S(1)}, u32[]{:S(2)}, u32[]{:S(2)}) collective-permute-start(bf16[2,64,128]{2,1,0:T(8,128)(2,1)S(1)} %get-tuple-element.73), channel_id=1, source_target_pairs={{0,3},{1,2},{2,1},{3,0},{4,7},{5,6},{6,5},{7,4},{8,11},{9,10},{10,... | collective-permute-start | bytes 98312 | tf_op jit(solution)/shard_map/ppermute | solution.py:61
  77.5 3.9 %collective-permute-start.18 = (bf16[2,64,128]{2,1,0:T(8,128)(2,1)S(1)}, bf16[2,64,128]{2,1,0:T(8,128)(2,1)S(1)}, u32[]{:S(2)}, u32[]{:S(2)}) collective-permute-start(bf16[2,64,128]{2,1,0:T(8,128)(2,1)S(1)} %get-tuple-element.71.after_ref), channel_id=1, source_target_pairs={{0,1},{1,0},{2,3},{3,2},{4,5},{5,4},{6,7},{7,6},{8,9},{9,8},{10,11... | collective-permute-start | bytes 98312 | tf_op jit(solution)/shard_map/ppermute | solution.py:61
  81.5 4.8 %collective-permute-start.21 = (bf16[64,128]{1,0:T(8,128)(2,1)S(1)}, bf16[64,128]{1,0:T(8,128)(2,1)S(1)}, u32[]{:S(2)}, u32[]{:S(2)}) collective-permute-start(bf16[64,128]{1,0:T(8,128)(2,1)S(1)} %get-tuple-element.75), channel_id=1, source_target_pairs={{0,4},{1,5},{2,6},{3,7},{4,0},{5,1},{6,2},{7,3},{8,12},{9,13},{10,... | collective-permute-start | bytes 49160 | tf_op jit(solution)/shard_map/ppermute | solution.py:61
